TPU v7x, 32 devices: a whole 2x2x4 slice. The times are simulated.
32 devices in a mesh: tm: 8 (over z, core), sta: 4 (over y, x).
Axes of the slice: x: 2, y: 2, z: 4, core: 2. Of those that a mesh axis runs over, the one named last changes fastest.
Arguments:
- waveforms: bfloat16 [120, 4096], P('sta', 'tm'), may hold values from -6 to 6
- templates: bfloat16 [16, 64, 120, 100], P('tm', None, 'sta'), may hold values from -6 to 6
- available: int32 [16, 64, 120], P('tm', None, 'sta'), may hold values 0 or 1
- moveout: int32 [16, 64, 120], P('tm', None, 'sta'), may hold values from 0 to 63
- bank_blocks: int32 [2], replicated, may hold values from 0 to 15
Outputs:
- detect_sum: float32 [128, 4096], P('sta', 'tm')
Inputs may be any that keep to these rules, and one draw needn't show every extreme that they name: `bank_blocks`: block b is stored at index b // 2 of tm.
All inputs are finite; a program needn't handle non-finite values. No bound on the sum of `available` on one device may be relied on, other than what follows from the above.
Results may differ from a plain program's by a relative error of at most 0.0029.
Values may be sent and summed in bfloat16 or wider, within the bound.
No kernel may reach another device: no remote copies, remote signals or barrier semaphores. Data moves between devices by JAX's collectives and lax.ppermute only.
A program may use at most 128 MiB of HBM per device.

v0:
```python
import jax
import jax.numpy as jnp
from jax import lax
from jax.sharding import PartitionSpec as P

MOVE = 64


epsilon = 1e-06
block_span = 512


def shifted(block, axis, distance):
    devices = range(lax.axis_size(axis))
    route = [(i - distance, i) for i in devices if i - distance in devices]
    return lax.ppermute(block, axis, route)


def spread_2(array, axis, root):
    mine = lax.axis_index(axis) == root
    return lax.psum(jnp.where(mine, array, jnp.zeros_like(array)), axis)


def normalize_bank(bank):
    values = bank.astype(jnp.float32)
    center = jnp.mean(values, axis=-1, keepdims=True)
    deviate = values - center
    spread = jnp.sqrt(jnp.mean(deviate * deviate, axis=-1, keepdims=True) + epsilon)
    return (deviate / (spread * bank.shape[-1])).astype(jnp.bfloat16)


def window_sigma(padded, length, tlen):
    first_sum = jnp.zeros((padded.shape[0], length), jnp.float32)
    second_sum = jnp.zeros((padded.shape[0], length), jnp.float32)
    for lag in range(tlen):
        piece = padded[:, lag : lag + length].astype(jnp.float32)
        first_sum = first_sum + piece
        second_sum = second_sum + piece * piece
    mean_value = first_sum / tlen
    return jnp.sqrt(second_sum / tlen - mean_value * mean_value + epsilon)


def shards(waveforms, templates, available, moveout, bank_blocks):
    channels_dev = waveforms.shape[0]
    samples = waveforms.shape[1]
    blocks_dev = templates.shape[0]
    events = templates.shape[1]
    tlen = templates.shape[3]
    rim_span = MOVE + tlen - 1
    rim_cells = shifted(waveforms[:, :rim_span], "tm", -1)
    extended = jnp.concatenate([waveforms, rim_cells], axis=1)
    sigma = window_sigma(extended, samples + MOVE, tlen)
    owners = bank_blocks // blocks_dev
    slots = bank_blocks % blocks_dev
    bank_list = []
    flag_list = []
    for which in range(2):
        slot_now = slots[which]
        template_portion = lax.dynamic_index_in_dim(templates, slot_now, 0, keepdims=False)
        flag_piece = jnp.stack(
            [
                lax.dynamic_index_in_dim(available, slot_now, 0, keepdims=False),
                lax.dynamic_index_in_dim(moveout, slot_now, 0, keepdims=False),
            ]
        ).astype(jnp.bfloat16)
        template_portion, flag_piece = (template_portion, flag_piece)
        got_bank, got_flags = (
            spread_2(template_portion, "tm", owners[which]),
            spread_2(flag_piece, "tm", owners[which]),
        )
        bank_list.append(got_bank)
        flag_list.append(got_flags.astype(jnp.float32))
    bank_all = jnp.stack(bank_list)
    flag_all = jnp.stack(flag_list)
    unit_norm_templates = normalize_bank(bank_all.reshape(2 * events, channels_dev, tlen))
    weights = flag_all[:, 0].reshape(2 * events, channels_dev)
    shifts = flag_all[:, 1].reshape(2 * events, channels_dev).astype(jnp.int32)
    offsets = jnp.arange(MOVE, dtype=jnp.int32)
    coefficients = jnp.where(shifts[:, :, None] == offsets[None, None, :], weights[:, :, None], 0.0)
    window_width = block_span + MOVE
    own_rows = 2 * events // lax.axis_size("sta")

    def one_window(block):
        reference_sample = block * block_span
        stacked_correlation = jnp.stack(
            [extended[:, lag : lag + window_width] for lag in range(tlen)], axis=1
        )
        correlation_values = jnp.einsum(
            "ofn,fnw->ofw",
            unit_norm_templates,
            stacked_correlation,
            preferred_element_type=jnp.float32,
        )
        scaled_traces = (
            correlation_values
            / lax.dynamic_slice_in_dim(sigma, reference_sample, window_width, 1)[None]
        )
        by_offset = jnp.einsum(
            "tcm,tcw->tmw", coefficients, scaled_traces, precision=lax.Precision.HIGHEST
        )
        flat_rows = by_offset.reshape(own_rows * lax.axis_size("sta"), MOVE * window_width)
        flat_rows = jnp.pad(flat_rows, ((0, 0), (0, MOVE)))
        skewed = flat_rows.reshape(own_rows * lax.axis_size("sta"), MOVE, window_width + 1)
        return jnp.sum(skewed[:, :, :block_span], axis=1)

    result = lax.map(one_window, jnp.arange(samples // block_span, dtype=jnp.int32))
    return lax.psum_scatter(
        jnp.transpose(result, (1, 0, 2)).reshape(own_rows * lax.axis_size("sta"), samples),
        "sta",
        scatter_dimension=0,
        tiled=True,
    )


def solution(mesh):
    in_specs = (
        P("sta", "tm"),
        P("tm", None, "sta", None),
        P("tm", None, "sta"),
        P("tm", None, "sta"),
        P(),
    )
    out_specs = P("sta", "tm")
    return jax.shard_map(shards, mesh=mesh, in_specs=in_specs, out_specs=out_specs, check_vma=False)
```

profile of v0, /device:TPU:7, one launch (start us, length us, event | category | flops | bytes accessed | tf_op | source)
XLA Modules:
  0.0 269.0 jit_solution(7973490313279327693)
XLA Ops:
  6.5 0.7 slice.533
  7.3 2.6 collective-permute-start
  16.1 2.3 dynamic-slice_select_fusion.1
  18.6 0.9 dynamic-slice_convert_fusion.2
  19.4 0.9 dynamic-slice_convert_fusion.3
  20.5 26.5 %all-reduce.1 = (bf16[1,2,64,30]{2,0,3,1:T(2,128)(2,1)S(1)}, bf16[1,2,64,30]{2,0,3,1:T(2,128)(2,1)S(1)}) all-reduce(bf16[1,2,64,30]{2,0,3,1:T(2,128)(2,1)S(1)} %copy.3426, bf16[1,2,64,30]{2,0,3,1:T(2,128)(2,1)S(1)} %copy.3425), channel_id=1, replica_groups=mesh['tm'=8,'sta'=4] {'tm'}, use_global_device_ids=true, to_apply=%region_1.2 | all-reduce | flops 7680 | bytes 30720 | tf_op jit(solution)/shard_map/psum | solution.py:21
  47.1 0.8 constant_dynamic-update-slice_fusion.1
  53.3 0.7 copy.3470
  54.0 0.7 copy.3469
  54.7 0.7 copy.3468
  55.4 0.7 copy.3467
  57.5 0.7 copy.3464
  58.2 0.7 copy.3463
  59.5 0.7 copy.3461
  61.6 0.7 copy.3458
  64.3 0.7 copy.3454
  65.0 0.7 copy.3453
  67.8 0.7 copy.3506
  68.5 0.7 copy.3505
  71.2 0.7 copy.3501
  71.9 0.7 copy.3500
  75.3 0.7 copy.3495
  78.1 0.7 copy.3491
  78.8 0.7 copy.3490
  80.1 0.7 copy.3488
  80.8 0.7 copy.3487
  82.9 0.7 copy.3484
  84.3 0.7 copy.3482
  85.0 0.7 copy.3481
  85.7 0.7 copy.3480
  86.4 0.7 copy.3479
  87.1 0.7 copy.3478
  87.8 0.7 copy.3477
  91.9 33.3 %stack.545 = bf16[30,100,576]{2,1,0:T(8,128)(2,1)} concatenate(bf16[30,1,576]{2,1,0:T(2,128)(2,1)S(1)} %copy.3429, bf16[30,1,576]{2,1,0:T(2,128)(2,1)S(1)} %copy.3430, bf16[30,1,576]{2,1,0:T(2,128)(2,1)S(1)} %copy.3431, bf16[30,1,576]{2,1,0:T(2,128)(2,1)S(1)} %copy.3432, bf16[30,1,576]{2,1,0:T(2,128)(2,1)S(1)} %copy.3433, bf16[30,1,576]{2,1,0:T(2,128)(2,1)S(1)} %copy.3434, ...), dimensions={1} | concatenate | bytes 6912000 | tf_op jit(solution)/shard_map/while/body/eval_jaxpr/stack | solution.py:85
  125.2 1.6 fusion.111
  126.8 1.8 fusion.7
  128.6 2.3 multiply_reduce_fusion
  131.0 1.5 maximum_convert_fusion
  132.8 1.4 fusion.3
  134.8 6.3 %divide_bitcast_fusion = f32[128,30,576]{0,2,1:T(8,128)} fusion(f32[30,576]{1,0:T(8,128)S(1)} %fusion.111, bf16[30,100,576]{2,1,0:T(8,128)(2,1)S(1)} %copy-done, bf16[128,30,100]{2,0,1:T(8,128)(2,1)S(1)} %fusion.3), kind=kOutput, calls=%fused_computation.1 | convolution fusion | flops 444579840 | bytes 13140480 | tf_op jit(solution)/shard_map/while/body/eval_jaxpr/ofn,fnw->ofw/dot_general | solution.py:88
  141.1 12.0 %copy.3533 = f32[128,30,576]{2,1,0:T(8,128)} copy(f32[128,30,576]{0,2,1:T(8,128)} %divide_bitcast_fusion) | data formatting | bytes 17694720 | tf_op jit(solution)/shard_map/while/body/eval_jaxpr/div | solution.py:95
  153.1 25.3 %fusion = f32[128,64,576]{2,1,0:T(8,128)} fusion(f32[128,30,576]{2,1,0:T(8,128)} %copy.3533, f32[128,30]{1,0:T(8,128)S(1)} %bitcast.231, s32[128,30]{1,0:T(8,128)S(1)} %bitcast.230), kind=kOutput, calls=%fused_computation.2 | convolution fusion | flops 1699184640 | bytes 27752448 | tf_op jit(solution)/shard_map/while/body/eval_jaxpr/tcm,tcw->tmw/dot_general | solution.py:98
  178.4 22.3 %copy.3534 = f32[128,64,576]{0,2,1:T(8,128)} copy(f32[128,64,576]{2,1,0:T(8,128)} %fusion) | data formatting | bytes 37748736 | tf_op jit(solution)/shard_map/while/body/eval_jaxpr/tcm,tcw->tmw/dot_general | solution.py:98
  200.7 14.5 %pad.5 = f32[128,36928]{0,1:T(8,128)} pad(f32[128,36864]{0,1:T(8,128)} %bitcast.229, f32[]{:T(128)} %constant.78.clone.1), padding=0_0x0_64 | pad | bytes 37781508 | tf_op jit(solution)/shard_map/while/body/eval_jaxpr/jit(_pad)/pad | solution.py:102
  215.2 15.1 %reshape.60 = f32[128,64,577]{0,2,1:T(8,128)} reshape(f32[128,36928]{0,1:T(8,128)} %pad.5) | data formatting | bytes 37814272 | tf_op jit(solution)/shard_map/while/body/eval_jaxpr/reshape | solution.py:103
  230.3 6.6 %slice_reduce_fusion = f32[128,512]{0,1:T(8,128)S(1)} fusion(f32[128,64,577]{0,2,1:T(8,128)} %reshape.60), kind=kLoop, calls=%fused_computation | loop fusion | flops 4128768 | bytes 17039360 | tf_op jit(solution)/shard_map/while/body/eval_jaxpr/reduce_sum | solution.py:104
  236.8 0.8 copy.3539
  237.7 24.5 %reduce-scatter.4.cloned.1.call-done = f32[32,512]{1,0:T(8,128)} async-done(((f32[128,512]{1,0:T(8,128)}), f32[32,512]{1,0:T(8,128)}) %reduce-scatter.4.cloned.1.call-update) | async-done | bytes 65552 | tf_op jit(solution)/shard_map/reduce_scatter | solution.py:107
  (106 shorter events, 28.1 us)
Async XLA Ops:
  6.5 120.3 %all-reduce.5.cloned.1.call-start = ((), (), s32[]{:S(2)}) async-start(), calls=%async_computation.2 | async-start | bytes 1966080 | tf_op jit(solution)/shard_map/psum | solution.py:21
  7.3 40.8 %collective-permute-start = (bf16[30,163]{1,0:T(8,128)(2,1)S(1)}, bf16[30,163]{1,0:T(8,128)(2,1)S(1)}, u32[]{:S(2)}, u32[]{:S(2)}) collective-permute-start(bf16[30,163]{1,0:T(8,128)(2,1)S(1)} %slice.533), channel_id=1, source_target_pairs={{4,0},{8,4},{12,8},{16,12},{20,16},{24,20},{28,24},{5,1},{9,5},{13... | collective-permute-start | bytes 29348 | tf_op jit(solution)/shard_map/ppermute | solution.py:16
  18.5 243.7 %reduce-scatter.4.cloned.1.call-start = ((), (), s32[]{:S(2)}) async-start(), calls=%async_computation.1 | async-start | bytes 327680 | tf_op jit(solution)/shard_map/reduce_scatter | solution.py:107
  132.7 2.1 copy-start
Sparse Core Ops, SparseCore 0:
  18.6 57.6 all-reduce.4
  237.8 24.3 reduce-scatter.3
where the time goes:
time: 274 us; the launch traced here: 269 us
  local copies, waits for them, and re-layouts  145 us (53%)
  matrix products  31.5 us (11%)
  blocking collectives  26.5 us (10%)
  waiting for transfers between devices  24.5 us (9%)
  other arithmetic  20.2 us (7%)
  between operations  18.9 us (7%)
    another operation x107, local copies, waits for them, and re-layouts, one_window(): jnp.stack([extended[:, lag:lag + window_width] for lag in range(tlen)], a...  76.6 us
    psum x1, blocking collectives, spread_2(): return lax.psum(jnp.where(mine, array, jnp.zeros_like(array)), axis)  26.5 us
    dot_general x1, matrix products, one_window(): jnp.einsum('tcm,tcw->tmw', coefficients, scaled_traces, precision=lax.Pre...  25.3 us
    reduce_scatter x1, waiting for transfers between devices, shards(): lax.psum_scatter(jnp.transpose(result, (1, 0, 2)).reshape(own_rows * lax....  24.5 us
    dot_general x1, local copies, waits for them, and re-layouts, one_window(): jnp.einsum('tcm,tcw->tmw', coefficients, scaled_traces, precision=lax.Pre...  22.3 us
    reshape x1, local copies, waits for them, and re-layouts, one_window(): flat_rows.reshape(own_rows * lax.axis_size('sta'), MOVE, window_width + 1)  15.1 us
    pad x1, local copies, waits for them, and re-layouts, one_window(): flat_rows = jnp.pad(flat_rows, ((0, 0), (0, MOVE)))  14.5 us
    div x1, local copies, waits for them, and re-layouts, one_window(): correlation_values / lax.dynamic_slice_in_dim(sigma, reference_sample, wi...  12 us
  transfers between devices with their start and end apart: 3, of which 1 were waited for; matrix products, arithmetic and copies ran while one was open for 32% of the time, Pallas kernels for 0%

commit v1 on v0

v1 whole, which is shorter than its diff:
```python
import functools

import jax
import jax.numpy as jnp
from jax import lax
from jax.experimental import pallas as pl
from jax.experimental.pallas import tpu as pltpu
from jax.sharding import PartitionSpec as P

MOVE = 64
EPSILON = 1e-06
LANES = 128
OFFSETS = 16
CODE = 100
VMEM_LIMIT = 40 * 1024 * 1024


def pack_kernel(chips, group, scalars, templates, available, moveout, mine, theirs, raw, packed, sems):
    blocks, events = templates.shape[:2]
    channels, tlen = templates.shape[2:]
    fetch = [
        pltpu.make_async_copy(templates.at[scalars[which]], raw.at[which], sems.at[which])
        for which in range(2)
    ]
    for copy in fetch:
        copy.start()
    packed[...] = jnp.zeros_like(packed)
    flags = jnp.where(available[...] > 0, moveout[...] + 1, 0).astype(jnp.float32)
    for which in range(2):
        code = flags[:, 0, :]
        for block in range(1, blocks):
            code = jnp.where(scalars[which] == block, flags[:, block, :], code)
        code = code.astype(jnp.bfloat16)
        fetch[which].wait()
        for event in range(events):
            row = which * events + event
            dest, item = divmod(row, group)
            chip, core = divmod(dest, 2)
            packed[core, chip, item, 0:channels, 0:tlen] = raw[which, event]
            packed[core, chip, item, 0:channels, CODE : CODE + 1] = code[:, event : event + 1]
    me = scalars[2]
    send = [
        pltpu.make_async_copy(packed.at[me], mine, sems.at[0]),
        pltpu.make_async_copy(packed.at[1 - me], theirs, sems.at[1]),
    ]
    for copy in send:
        copy.start()
    for copy in send:
        copy.wait()


def pack(chips, group, scalars, templates, available, moveout):
    _, events, channels, tlen = templates.shape
    shape = (chips, group, 32, LANES)
    return pl.pallas_call(
        functools.partial(pack_kernel, chips, group),
        out_shape=[jax.ShapeDtypeStruct(shape, jnp.bfloat16)] * 2,
        in_specs=[
            pl.BlockSpec(memory_space=pltpu.SMEM),
            pl.BlockSpec(memory_space=pl.ANY),
            pl.BlockSpec(memory_space=pltpu.VMEM),
            pl.BlockSpec(memory_space=pltpu.VMEM),
        ],
        out_specs=[pl.BlockSpec(memory_space=pl.ANY)] * 2,
        scratch_shapes=[
            pltpu.VMEM((2, events, channels, tlen), jnp.bfloat16),
            pltpu.VMEM((2,) + shape, jnp.bfloat16),
            pltpu.SemaphoreType.DMA((2,)),
        ],
        compiler_params=pltpu.CompilerParams(vmem_limit_bytes=VMEM_LIMIT),
        name="pack",
    )(scalars, templates, available, moveout)


def merge_kernel(chips, scalars, mine, other, *rest):
    outs, sems = rest[:-1], rest[-1]
    chip, core = scalars[0], scalars[1]
    for step in range(chips):
        dest = jnp.bitwise_xor(chip, step)
        owner = jnp.where(dest < chips // 2, scalars[2], scalars[3])
        here = owner % 2 == core

        @pl.when(here)
        def _():
            pltpu.make_async_copy(mine.at[dest], outs[step], sems.at[step]).start()

        @pl.when(jnp.logical_not(here))
        def _():
            pltpu.make_async_copy(other.at[dest], outs[step], sems.at[step]).start()

    for step in range(chips):
        pltpu.make_async_copy(mine.at[0], outs[step], sems.at[step]).wait()


def merge(chips, scalars, mine, other):
    return pl.pallas_call(
        functools.partial(merge_kernel, chips),
        out_shape=[jax.ShapeDtypeStruct(mine.shape[1:], mine.dtype)] * chips,
        in_specs=[pl.BlockSpec(memory_space=pltpu.SMEM)] + [pl.BlockSpec(memory_space=pl.ANY)] * 2,
        out_specs=[pl.BlockSpec(memory_space=pl.ANY)] * chips,
        scratch_shapes=[pltpu.SemaphoreType.DMA((chips,))],
        compiler_params=pltpu.CompilerParams(vmem_limit_bytes=VMEM_LIMIT),
        name="merge",
    )(scalars, mine, other)


def left(values, count):
    return pltpu.roll(values, values.shape[1] - count, 1)


def window_sums(values):
    sums = {1: values}
    width = 1
    while width < 64:
        sums[2 * width] = sums[width] + left(sums[width], width)
        width *= 2
    return sums[64] + left(sums[32], 64) + left(sums[4], 96)


def stacked(row, span):
    copies = jnp.broadcast_to(row, (8, row.shape[1]))
    return pltpu.roll(copies, row.shape[1] - 112, 1, stride=16, stride_axis=0)


def tiles(values, first, count):
    return jnp.concatenate(
        [values[:, LANES * m : LANES * (m + 1)] for m in range(first, first + count)], axis=0
    )


def main_kernel(sources, channels, tlen, group, scalars, waves, *rest):
    pieces = rest[:sources]
    outs = rest[sources:-8]
    padded, inverse, piece, bank, weight_a, weight_r, total, sem = rest[-8:]
    length = waves.shape[1]
    span = padded.shape[1]
    per_tile = LANES // group
    tile_count = OFFSETS // per_tile
    row_tiles = length // LANES

    source = scalars[0]
    for index in range(sources):

        @pl.when(source == index)
        def _():
            pltpu.make_async_copy(pieces[index], piece, sem).start()

    padded[...] = jnp.zeros_like(padded)
    padded[0:channels, 0:length] = waves[...].astype(jnp.float32)

    @pl.loop(0, 4)
    def _(part):
        rows = pl.ds(pl.multiple_of(part * 8, 8), 8)
        values = padded[rows, :]
        first_sum = window_sums(values)
        second_sum = window_sums(values * values)
        mean = first_sum / tlen
        inverse[rows, :] = lax.rsqrt(second_sum / tlen - mean * mean + EPSILON)

    pltpu.make_async_copy(pieces[0], piece, sem).wait()

    lag = lax.broadcasted_iota(jnp.int32, (LANES, 8 * group), 0)
    for part in range(4):
        half = piece[:, 16 * (part // 2) : 16 * (part // 2) + 16, :].astype(jnp.float32)
        values = half[:, 8 * (part % 2) : 8 * (part % 2) + 8, :].reshape(8 * group, LANES).T
        used = lag < tlen
        center = jnp.sum(jnp.where(used, values, 0.0), axis=0, keepdims=True) / tlen
        deviate = jnp.where(used, values - center, 0.0)
        spread = jnp.sqrt(jnp.sum(deviate * deviate, axis=0, keepdims=True) / tlen + EPSILON)
        unit = jnp.where(lag == CODE, values, deviate / (spread * tlen))
        bank[part] = unit.astype(jnp.bfloat16)

    @pl.loop(0, channels)
    def _(channel):
        part, item = channel // 8, channel % 8
        source_lane = lax.broadcasted_iota(jnp.int32, (8 * group, LANES), 0)
        target_lane = lax.broadcasted_iota(jnp.int32, (8 * group, LANES), 1)
        expand = (source_lane == (target_lane % group) * 8 + item).astype(jnp.float32)
        spreaded = jnp.dot(
            bank[part], expand.astype(jnp.bfloat16), preferred_element_type=jnp.float32
        )
        code = spreaded[CODE : CODE + 1, :].astype(jnp.int32)
        usable = code > 0
        shift = code - 1 + lax.broadcasted_iota(jnp.int32, (1, LANES), 1) // group
        rows = lax.broadcasted_iota(jnp.int32, (112, LANES), 0)
        taps = jnp.where(jnp.logical_and(rows < tlen, usable), spreaded[0:112, :], 0.0)
        for bit in (1, 2, 4):
            taps = jnp.where(jnp.bitwise_and(shift, bit) > 0, pltpu.roll(taps, bit, 0), taps)
        for bit in (8, 16, 32, 64):
            gap = jnp.zeros((bit, LANES), jnp.float32)
            taps = jnp.where(
                jnp.bitwise_and(shift, bit) > 0,
                jnp.concatenate([gap, taps], axis=0),
                jnp.concatenate([taps, gap], axis=0),
            )[0:184]
        offset_rows = lax.broadcasted_iota(jnp.int32, (LANES, LANES), 0)
        for index in range(tile_count):
            ahead = index * per_tile
            column = [taps, jnp.zeros((256 - 184 - ahead, LANES), jnp.float32)]
            if ahead:
                column = [jnp.zeros((ahead, LANES), jnp.float32)] + column
            lanes = slice(LANES * index, LANES * (index + 1))
            weight_a[channel, :, lanes] = jnp.concatenate(column, axis=0).astype(jnp.bfloat16)
            pick = jnp.logical_and(offset_rows == shift + ahead, usable)
            pick = jnp.where(pick, 1.0, 0.0).astype(jnp.bfloat16)
            weight_r[channel, 0:LANES, lanes] = pick
            weight_r[channel, LANES : 2 * LANES, lanes] = pick

    total[...] = jnp.zeros_like(total)

    @pl.loop(0, channels)
    def _(channel):
        samples = stacked(padded[pl.ds(channel, 1), :], span)
        left_a = jnp.concatenate(
            [tiles(samples, 0, row_tiles), tiles(samples, 1, row_tiles)], axis=1
        ).astype(jnp.bfloat16)
        scale = tiles(stacked(inverse[pl.ds(channel, 1), :], span), 0, row_tiles)
        high = scale.astype(jnp.bfloat16)
        low = (scale - high.astype(jnp.float32)).astype(jnp.bfloat16)
        left_r = jnp.concatenate([high, low], axis=1)
        corr = jnp.dot(left_a, weight_a[channel], preferred_element_type=jnp.float32)
        factor = jnp.dot(left_r, weight_r[channel], preferred_element_type=jnp.float32)
        total[...] += corr * factor

    rows_out = outs[0].shape[0]
    for step, out in enumerate(outs):
        segment = jnp.bitwise_xor(scalars[1], step)
        out[...] = total[pl.ds(pl.multiple_of(segment * rows_out, rows_out), rows_out), :].astype(
            jnp.bfloat16
        )


def correlate(channels, tlen, group, samples, scalars, waves, pieces):
    length = waves.shape[1]
    segments = length // samples
    span = length + 2 * LANES
    rows = length // OFFSETS
    width = OFFSETS * group
    out = jax.ShapeDtypeStruct((samples // OFFSETS, width), jnp.bfloat16)
    return pl.pallas_call(
        functools.partial(main_kernel, len(pieces), channels, tlen, group),
        out_shape=[out] * segments,
        in_specs=[
            pl.BlockSpec(memory_space=pltpu.SMEM),
            pl.BlockSpec(memory_space=pltpu.VMEM),
        ]
        + [pl.BlockSpec(memory_space=pl.ANY)] * len(pieces),
        out_specs=[pl.BlockSpec(memory_space=pltpu.VMEM)] * segments,
        scratch_shapes=[
            pltpu.VMEM((32, span), jnp.float32),
            pltpu.VMEM((32, span), jnp.float32),
            pltpu.VMEM((group, 32, LANES), jnp.bfloat16),
            pltpu.VMEM((4, LANES, 8 * group), jnp.bfloat16),
            pltpu.VMEM((channels, 256, width), jnp.bfloat16),
            pltpu.VMEM((channels, 256, width), jnp.bfloat16),
            pltpu.VMEM((rows, width), jnp.float32),
            pltpu.SemaphoreType.DMA(()),
        ],
        compiler_params=pltpu.CompilerParams(vmem_limit_bytes=VMEM_LIMIT),
        name="correlate",
    )(scalars, waves, *pieces)


def finish_kernel(group, scalars, *rest):
    parts, out = rest[:-1], rest[-1]
    rows, width = parts[0].shape
    samples = out.shape[1]
    sums = []
    for parity in range(2):
        value = parts[parity][...].astype(jnp.float32)
        for part in parts[parity + 2 :: 2]:
            value = value + part[...].astype(jnp.float32)
        sums.append(value)
    swapped = scalars[0] == 1
    halves = [jnp.where(swapped, sums[1], sums[0]), jnp.where(swapped, sums[0], sums[1])]
    row = lax.broadcasted_iota(jnp.int32, (rows, samples), 0)
    lane = lax.broadcasted_iota(jnp.int32, (rows, samples), 1)
    place = (lane // OFFSETS == 8 * (row // 8) + 7 - row % 8).astype(jnp.float32)
    lane = lax.broadcasted_iota(jnp.int32, (group, samples), 1) % OFFSETS
    for index, half in enumerate(halves):
        wide = jnp.dot(
            half.T, place, precision=lax.Precision.HIGHEST, preferred_element_type=jnp.float32
        )
        value = jnp.zeros((group, samples), jnp.float32)
        for offset in range(OFFSETS):
            value = jnp.where(lane == offset, wide[offset * group : (offset + 1) * group], value)
        out[index * group : (index + 1) * group, :] = value


def finish(group, samples, scalars, parts):
    return pl.pallas_call(
        functools.partial(finish_kernel, group),
        out_shape=jax.ShapeDtypeStruct((2 * group, samples), jnp.float32),
        in_specs=[pl.BlockSpec(memory_space=pltpu.SMEM)]
        + [pl.BlockSpec(memory_space=pltpu.VMEM)] * len(parts),
        out_specs=pl.BlockSpec(memory_space=pltpu.VMEM),
        compiler_params=pltpu.CompilerParams(vmem_limit_bytes=VMEM_LIMIT),
        name="finish",
    )(scalars, *parts)


def shards(waveforms, templates, available, moveout, bank_blocks):
    channels, samples = waveforms.shape
    blocks, events, _, tlen = templates.shape
    count_tm = lax.axis_size("tm")
    count_sta = lax.axis_size("sta")
    chips = count_tm // 2
    group = 2 * events // count_tm
    me = lax.axis_index("tm").astype(jnp.int32)
    station = lax.axis_index("sta").astype(jnp.int32)
    chip, core = me // 2, me % 2

    owners = bank_blocks // blocks
    slots = bank_blocks % blocks
    waves = lax.all_gather(waveforms, "tm", axis=1, tiled=True)

    mine, theirs = pack(
        chips,
        group,
        jnp.stack([slots[0], slots[1], core]),
        templates,
        jnp.transpose(available, (2, 0, 1)),
        jnp.transpose(moveout, (2, 0, 1)),
    )
    other = lax.ppermute(theirs, "tm", [(i, i ^ 1) for i in range(count_tm)])
    merged = merge(chips, jnp.stack([chip, core, owners[0], owners[1]]), mine, other)
    pieces = [merged[0]]
    for step in range(1, chips):
        pieces.append(
            lax.ppermute(merged[step], "tm", [(i, i ^ (2 * step)) for i in range(count_tm)])
        )
    owner = jnp.where(chip < chips // 2, owners[0], owners[1])
    slot = 2 * station + core
    parts = correlate(
        channels, tlen, group, samples, jnp.stack([(owner // 2) ^ chip, slot]), waves, pieces
    )
    gathered = []
    for step in range(count_tm):
        route = [
            (d * count_sta + s, ((2 * s + d % 2) ^ step) * count_sta + d // 2)
            for d in range(count_tm)
            for s in range(count_sta)
        ]
        gathered.append(lax.ppermute(parts[step], ("tm", "sta"), route))
    return finish(group, samples, core[None], gathered)


def solution(mesh):
    in_specs = (
        P("sta", "tm"),
        P("tm", None, "sta", None),
        P("tm", None, "sta"),
        P("tm", None, "sta"),
        P(),
    )
    out_specs = P("sta", "tm")
    return jax.shard_map(shards, mesh=mesh, in_specs=in_specs, out_specs=out_specs, check_vma=False)
```

time: 274 us -> 77 us (0.28)
  the two profiles are of different devices: /device:TPU:7 before, /device:TPU:9 now
where the time goes in v1:
time: 77 us; the launch traced here: 76.8 us
  Pallas kernels  24.2 us (31%)
  starting transfers between devices  22.1 us (29%)
  blocking collectives  20 us (26%)
  waiting for transfers between devices  5.82 us (8%)
  local copies, waits for them, and re-layouts  3.12 us (4%)
  between operations  1.39 us (2%)
    all_gather x1, blocking collectives, shards(): waves = lax.all_gather(waveforms, 'tm', axis=1, tiled=True)  20 us
    pallas_call x1, Pallas kernels, correlate(): pl.pallas_call(functools.partial(main_kernel, len(pieces), channels, tlen...  19.7 us
    ppermute x8, starting transfers between devices, shards(): gathered.append(lax.ppermute(parts[step], ('tm', 'sta'), route))  18.6 us
    ppermute x8, waiting for transfers between devices, shards(): gathered.append(lax.ppermute(parts[step], ('tm', 'sta'), route))  4.95 us
    ppermute x3, starting transfers between devices, shards(): lax.ppermute(merged[step], 'tm', [(i, i ^ 2 * step) for i in range(count_...  2.71 us
    unnamed x9, local copies, waits for them, and re-layouts  2.53 us
    pallas_call x1, Pallas kernels, finish(): pl.pallas_call(functools.partial(finish_kernel, group), out_shape=jax.Sha...  1.66 us
    pallas_call x1, Pallas kernels, pack(): pl.pallas_call(functools.partial(pack_kernel, chips, group), out_shape=[j...  1.56 us
  transfers between devices with their start and end apart: 12, of which 3 were waited for; matrix products, arithmetic and copies ran while one was open for 1% of the time, Pallas kernels for 0%

profile of v1, /device:TPU:9, one launch (start us, length us, event | category | flops | bytes accessed | tf_op | source)
XLA Modules:
  0.0 76.8 jit_solution(18131639080246289923)
XLA Ops:
  0.0 0.0 copy-start.3
  0.0 0.7 copy-done.3
  0.7 0.0 copy-start
  0.7 0.0 copy-start.1
  0.7 1.9 %copy.6.templates = bf16[2,64,30,100]{3,2,1,0:T(8,128)(2,1)S(1)} copy(bf16[2,64,30,100]{3,1,2,0:T(8,128)(2,1)} %param.6) | data formatting | bytes 1536000 | tf_op args[1]
  2.6 0.1 pad_add_fusion.2.scalars
  2.6 0.0 copy-done
  2.6 0.0 copy-done.1
  2.6 1.6 %pack.1 = (bf16[4,16,32,128]{3,2,1,0:T(8,128)(2,1)S(1)}, bf16[4,16,32,128]{3,2,1,0:T(8,128)(2,1)S(1)}) custom-call(s32[3]{0:T(128)S(1)} %pad_add_fusion.2.scalars, bf16[2,64,30,100]{3,2,1,0:T(8,128)(2,1)S(1)} %copy.6.templates, s32[30,2,64]{2,1,0:T(2,128)S(1)} %bitcast.8, s32[30,2,64]{2,1,0:T(2,128)S(1)} %bitcast.9), custom_call_target="tpu_custom_call" | custom-call | tf_op jit(solution)/shard_map/pack/pallas_call | solution.py:55
  4.2 0.7 collective-permute-start
  4.9 0.1 pad_add_fusion.1.scalars
  5.0 0.6 fusion
  5.6 0.9 %collective-permute-done.other = bf16[4,16,32,128]{3,2,1,0:T(8,128)(2,1)S(1)} collective-permute-done((bf16[4,16,32,128]{3,2,1,0:T(8,128)(2,1)S(1)}, bf16[4,16,32,128]{3,2,1,0:T(8,128)(2,1)S(1)}, u32[]{:S(2)}, u32[]{:S(2)}) %collective-permute-start) | collective-permute-done | bytes 524320 | tf_op jit(solution)/shard_map/ppermute | solution.py:325
  6.5 0.0 copy-start.2
  6.5 1.3 %merge.1 = (bf16[16,32,128]{2,1,0:T(8,128)(2,1)S(1)}, bf16[16,32,128]{2,1,0:T(8,128)(2,1)S(1)}, bf16[16,32,128]{2,1,0:T(8,128)(2,1)S(1)}, bf16[16,32,128]{2,1,0:T(8,128)(2,1)S(1)}) custom-call(s32[4]{0:T(128)S(1)} %pad_add_fusion.1.scalars, bf16[4,16,32,128]{3,2,1,0:T(8,128)(2,1)S(1)} %get-tuple-element.19.mine, ...), custom_call_target="tpu_custom_call" | custom-call | tf_op jit(solution)/shard_map/merge/pallas_call | solution.py:96
  7.8 0.1 collective-permute-start.1
  7.9 2.5 %collective-permute-start.2 = (bf16[16,32,128]{2,1,0:T(8,128)(2,1)S(1)}, bf16[16,32,128]{2,1,0:T(8,128)(2,1)S(1)}, u32[]{:S(2)}, u32[]{:S(2)}) collective-permute-start(bf16[16,32,128]{2,1,0:T(8,128)(2,1)S(1)} %get-tuple-element.23), channel_id=1, source_target_pairs={{0,16},{4,20},{8,24},{12,28},{16,0},{20,4},{24,8},{28,12},{1,17},{... | collective-permute-start | bytes 393224 | tf_op jit(solution)/shard_map/ppermute | solution.py:330
  10.4 0.2 collective-permute-start.3
  10.5 0.0 copy-done.2
  10.5 20.0 %all_gather.3.waves = bf16[30,4096]{1,0:T(8,128)(2,1)S(1)} all-gather(bf16[30,512]{1,0:T(8,128)(2,1)S(1)} %copy-done.2), channel_id=1, replica_groups=mesh['tm'=8,'sta'=4] {'tm'}, dimensions={1}, use_global_device_ids=true | all-gather | bytes 276480 | tf_op jit(solution)/shard_map/all_gather | solution.py:315
  31.8 0.1 pad_add_fusion.scalars
  31.9 0.0 collective-permute-done.1.rest_1_
  31.9 0.0 collective-permute-done.2.rest_2_
  31.9 0.0 collective-permute-done.3.rest_3_
  31.9 19.7 %correlate.1 = (bf16[32,256]{1,0:T(8,128)(2,1)S(1)}, bf16[32,256]{1,0:T(8,128)(2,1)S(1)}, bf16[32,256]{1,0:T(8,128)(2,1)S(1)}, bf16[32,256]{1,0:T(8,128)(2,1)S(1...) custom-call(s32[2]{0:T(128)S(1)} %pad_add_fusion.scalars, ...), custom_call_target="tpu_custom_call" | custom-call | tf_op jit(solution)/shard_map/correlate/pallas_call | solution.py:240
  51.6 3.1 %collective-permute-start.10 = (bf16[32,256]{1,0:T(8,128)(2,1)S(1)}, bf16[32,256]{1,0:T(8,128)(2,1)S(1)}, u32[]{:S(2)}, u32[]{:S(2)}) collective-permute-start(bf16[32,256]{1,0:T(8,128)(2,1)S(1)} %get-tuple-element.31), channel_id=1, source_target_pairs={{0,24},{1,16},{2,8},{3,0},{4,28},{5,20},{6,12},{7,4},{8,25},{9,17}... | collective-permute-start | bytes 49160 | tf_op jit(solution)/shard_map/ppermute | solution.py:344
  54.7 1.7 %collective-permute-start.11 = (bf16[32,256]{1,0:T(8,128)(2,1)S(1)}, bf16[32,256]{1,0:T(8,128)(2,1)S(1)}, u32[]{:S(2)}, u32[]{:S(2)}) collective-permute-start(bf16[32,256]{1,0:T(8,128)(2,1)S(1)} %get-tuple-element.32), channel_id=1, source_target_pairs={{0,28},{1,20},{2,12},{3,4},{4,24},{5,16},{6,8},{7,0},{8,29},{9,21}... | collective-permute-start | bytes 49160 | tf_op jit(solution)/shard_map/ppermute | solution.py:344
  56.4 3.0 %collective-permute-start.4 = (bf16[32,256]{1,0:T(8,128)(2,1)S(1)}, bf16[32,256]{1,0:T(8,128)(2,1)S(1)}, u32[]{:S(2)}, u32[]{:S(2)}) collective-permute-start(bf16[32,256]{1,0:T(8,128)(2,1)S(1)} %get-tuple-element.25), channel_id=1, source_target_pairs={{0,0},{1,8},{2,16},{3,24},{4,4},{5,12},{6,20},{7,28},{8,1},{9,9},{... | collective-permute-start | bytes 49160 | tf_op jit(solution)/shard_map/ppermute | solution.py:344
  59.3 1.6 %collective-permute-start.5 = (bf16[32,256]{1,0:T(8,128)(2,1)S(1)}, bf16[32,256]{1,0:T(8,128)(2,1)S(1)}, u32[]{:S(2)}, u32[]{:S(2)}) collective-permute-start(bf16[32,256]{1,0:T(8,128)(2,1)S(1)} %get-tuple-element.26), channel_id=1, source_target_pairs={{0,4},{1,12},{2,20},{3,28},{4,0},{5,8},{6,16},{7,24},{8,5},{9,13},... | collective-permute-start | bytes 49160 | tf_op jit(solution)/shard_map/ppermute | solution.py:344
  60.9 0.0 collective-permute-start.6
  60.9 0.0 collective-permute-done.10.rest_6_
  60.9 1.7 %collective-permute-start.7 = (bf16[32,256]{1,0:T(8,128)(2,1)S(1)}, bf16[32,256]{1,0:T(8,128)(2,1)S(1)}, u32[]{:S(2)}, u32[]{:S(2)}) collective-permute-start(bf16[32,256]{1,0:T(8,128)(2,1)S(1)} %get-tuple-element.28), channel_id=1, source_target_pairs={{0,12},{1,4},{2,28},{3,20},{4,8},{5,0},{6,24},{7,16},{8,13},{9,5},... | collective-permute-start | bytes 49160 | tf_op jit(solution)/shard_map/ppermute | solution.py:344
  62.6 0.0 collective-permute-done.11.rest_7_
  62.6 7.6 %collective-permute-start.8 = (bf16[32,256]{1,0:T(8,128)(2,1)S(1)}, bf16[32,256]{1,0:T(8,128)(2,1)S(1)}, u32[]{:S(2)}, u32[]{:S(2)}) collective-permute-start(bf16[32,256]{1,0:T(8,128)(2,1)S(1)} %get-tuple-element.29), channel_id=1, source_target_pairs={{0,16},{1,24},{2,0},{3,8},{4,20},{5,28},{6,4},{7,12},{8,17},{9,25}... | collective-permute-start | bytes 49160 | tf_op jit(solution)/shard_map/ppermute | solution.py:344
  70.2 0.0 collective-permute-done.4.rest_0_
  70.2 0.0 collective-permute-start.9
  70.2 0.0 collective-permute-done.5.rest_1_
  70.2 0.0 collective-permute-done.6.rest_2_
  70.2 0.0 collective-permute-done.7.rest_3_
  70.2 0.8 %collective-permute-done.8.rest_4_ = bf16[32,256]{1,0:T(8,128)(2,1)S(1)} collective-permute-done((bf16[32,256]{1,0:T(8,128)(2,1)S(1)}, bf16[32,256]{1,0:T(8,128)(2,1)S(1)}, u32[]{:S(2)}, u32[]{:S(2)}) %collective-permute-start.8) | collective-permute-done | bytes 16416 | tf_op jit(solution)/shard_map/ppermute | solution.py:344
  71.1 4.1 %collective-permute-done.9.rest_5_ = bf16[32,256]{1,0:T(8,128)(2,1)S(1)} collective-permute-done((bf16[32,256]{1,0:T(8,128)(2,1)S(1)}, bf16[32,256]{1,0:T(8,128)(2,1)S(1)}, u32[]{:S(2)}, u32[]{:S(2)}) %collective-permute-start.9) | collective-permute-done | bytes 16416 | tf_op jit(solution)/shard_map/ppermute | solution.py:344
  75.2 1.7 %finish.1 = f32[32,512]{1,0:T(8,128)} custom-call(s32[1]{0:T(128)} %bitcast.scalars, bf16[32,256]{1,0:T(8,128)(2,1)S(1)} %collective-permute-done.4.rest_0_, bf16[32,256]{1,0:T(8,128)(2,1)S(1)} %collective-permute-done.5.rest_1_, bf16[32,256]{1,0:T(8,128)(2,1)S(1)} %collective-permute-done.6.rest_2_, bf16[32,256]{1,0:T(8,128)(2,1)S(1)} %collective-permute-done.7.rest_3_, ...), custom_call_target="tpu_custom_call" | custom-call | tf_op jit(solution)/shard_map/finish/pallas_call | solution.py:291
  (1 shorter events, 0.0 us)
Async XLA Ops:
  0.0 0.7 copy-start.3
  0.7 2.0 %copy-start = (s32[2,64,30]{1,0,2:T(2,128)S(1)}, s32[2,64,30]{1,0,2:T(2,128)}, u32[]{:S(2)}) copy-start(s32[2,64,30]{1,0,2:T(2,128)} %param.7) | copy-start | bytes 46084
  0.7 2.0 %copy-start.1 = (s32[2,64,30]{1,0,2:T(2,128)S(1)}, s32[2,64,30]{1,0,2:T(2,128)}, u32[]{:S(2)}) copy-start(s32[2,64,30]{1,0,2:T(2,128)} %param.8) | copy-start | bytes 46084
  4.2 2.3 %collective-permute-start = (bf16[4,16,32,128]{3,2,1,0:T(8,128)(2,1)S(1)}, bf16[4,16,32,128]{3,2,1,0:T(8,128)(2,1)S(1)}, u32[]{:S(2)}, u32[]{:S(2)}) collective-permute-start(bf16[4,16,32,128]{3,2,1,0:T(8,128)(2,1)S(1)} %get-tuple-element.20), channel_id=1, source_target_pairs={{0,4},{4,0},{8,12},{12,8},{16,20},{20,16},{24,28},{28,24},{1,5},{5... | collective-permute-start | bytes 1572872 | tf_op jit(solution)/shard_map/ppermute | solution.py:325
  6.5 4.0 %copy-start.2 = (bf16[30,512]{1,0:T(8,128)(2,1)S(1)}, bf16[30,512]{1,0:T(8,128)(2,1)}, u32[]{:S(2)}) copy-start(bf16[30,512]{1,0:T(8,128)(2,1)} %param.5) | copy-start | bytes 92164
  7.8 24.0 %collective-permute-start.1 = (bf16[16,32,128]{2,1,0:T(8,128)(2,1)S(1)}, bf16[16,32,128]{2,1,0:T(8,128)(2,1)S(1)}, u32[]{:S(2)}, u32[]{:S(2)}) collective-permute-start(bf16[16,32,128]{2,1,0:T(8,128)(2,1)S(1)} %get-tuple-element.22), channel_id=1, source_target_pairs={{0,8},{4,12},{8,0},{12,4},{16,24},{20,28},{24,16},{28,20},{1,9},{5... | collective-permute-start | bytes 393224 | tf_op jit(solution)/shard_map/ppermute | solution.py:330
  7.9 24.0 %collective-permute-start.2 = (bf16[16,32,128]{2,1,0:T(8,128)(2,1)S(1)}, bf16[16,32,128]{2,1,0:T(8,128)(2,1)S(1)}, u32[]{:S(2)}, u32[]{:S(2)}) collective-permute-start(bf16[16,32,128]{2,1,0:T(8,128)(2,1)S(1)} %get-tuple-element.23), channel_id=1, source_target_pairs={{0,16},{4,20},{8,24},{12,28},{16,0},{20,4},{24,8},{28,12},{1,17},{... | collective-permute-start | bytes 393224 | tf_op jit(solution)/shard_map/ppermute | solution.py:330
  10.4 21.5 %collective-permute-start.3 = (bf16[16,32,128]{2,1,0:T(8,128)(2,1)S(1)}, bf16[16,32,128]{2,1,0:T(8,128)(2,1)S(1)}, u32[]{:S(2)}, u32[]{:S(2)}) collective-permute-start(bf16[16,32,128]{2,1,0:T(8,128)(2,1)S(1)} %get-tuple-element.24), channel_id=1, source_target_pairs={{0,24},{4,28},{8,16},{12,20},{16,8},{20,12},{24,0},{28,4},{1,25},{... | collective-permute-start | bytes 393224 | tf_op jit(solution)/shard_map/ppermute | solution.py:330
  51.6 9.4 %collective-permute-start.10 = (bf16[32,256]{1,0:T(8,128)(2,1)S(1)}, bf16[32,256]{1,0:T(8,128)(2,1)S(1)}, u32[]{:S(2)}, u32[]{:S(2)}) collective-permute-start(bf16[32,256]{1,0:T(8,128)(2,1)S(1)} %get-tuple-element.31), channel_id=1, source_target_pairs={{0,24},{1,16},{2,8},{3,0},{4,28},{5,20},{6,12},{7,4},{8,25},{9,17}... | collective-permute-start | bytes 49160 | tf_op jit(solution)/shard_map/ppermute | solution.py:344
  54.7 7.9 %collective-permute-start.11 = (bf16[32,256]{1,0:T(8,128)(2,1)S(1)}, bf16[32,256]{1,0:T(8,128)(2,1)S(1)}, u32[]{:S(2)}, u32[]{:S(2)}) collective-permute-start(bf16[32,256]{1,0:T(8,128)(2,1)S(1)} %get-tuple-element.32), channel_id=1, source_target_pairs={{0,28},{1,20},{2,12},{3,4},{4,24},{5,16},{6,8},{7,0},{8,29},{9,21}... | collective-permute-start | bytes 49160 | tf_op jit(solution)/shard_map/ppermute | solution.py:344
  56.4 13.8 %collective-permute-start.4 = (bf16[32,256]{1,0:T(8,128)(2,1)S(1)}, bf16[32,256]{1,0:T(8,128)(2,1)S(1)}, u32[]{:S(2)}, u32[]{:S(2)}) collective-permute-start(bf16[32,256]{1,0:T(8,128)(2,1)S(1)} %get-tuple-element.25), channel_id=1, source_target_pairs={{0,0},{1,8},{2,16},{3,24},{4,4},{5,12},{6,20},{7,28},{8,1},{9,9},{... | collective-permute-start | bytes 49160 | tf_op jit(solution)/shard_map/ppermute | solution.py:344
  59.3 10.9 %collective-permute-start.5 = (bf16[32,256]{1,0:T(8,128)(2,1)S(1)}, bf16[32,256]{1,0:T(8,128)(2,1)S(1)}, u32[]{:S(2)}, u32[]{:S(2)}) collective-permute-start(bf16[32,256]{1,0:T(8,128)(2,1)S(1)} %get-tuple-element.26), channel_id=1, source_target_pairs={{0,4},{1,12},{2,20},{3,28},{4,0},{5,8},{6,16},{7,24},{8,5},{9,13},... | collective-permute-start | bytes 49160 | tf_op jit(solution)/shard_map/ppermute | solution.py:344
  60.9 9.3 %collective-permute-start.6 = (bf16[32,256]{1,0:T(8,128)(2,1)S(1)}, bf16[32,256]{1,0:T(8,128)(2,1)S(1)}, u32[]{:S(2)}, u32[]{:S(2)}) collective-permute-start(bf16[32,256]{1,0:T(8,128)(2,1)S(1)} %get-tuple-element.27), channel_id=1, source_target_pairs={{0,8},{1,0},{2,24},{3,16},{4,12},{5,4},{6,28},{7,20},{8,9},{9,1},{... | collective-permute-start | bytes 49160 | tf_op jit(solution)/shard_map/ppermute | solution.py:344
  60.9 9.3 %collective-permute-start.7 = (bf16[32,256]{1,0:T(8,128)(2,1)S(1)}, bf16[32,256]{1,0:T(8,128)(2,1)S(1)}, u32[]{:S(2)}, u32[]{:S(2)}) collective-permute-start(bf16[32,256]{1,0:T(8,128)(2,1)S(1)} %get-tuple-element.28), channel_id=1, source_target_pairs={{0,12},{1,4},{2,28},{3,20},{4,8},{5,0},{6,24},{7,16},{8,13},{9,5},... | collective-permute-start | bytes 49160 | tf_op jit(solution)/shard_map/ppermute | solution.py:344
  62.6 8.5 %collective-permute-start.8 = (bf16[32,256]{1,0:T(8,128)(2,1)S(1)}, bf16[32,256]{1,0:T(8,128)(2,1)S(1)}, u32[]{:S(2)}, u32[]{:S(2)}) collective-permute-start(bf16[32,256]{1,0:T(8,128)(2,1)S(1)} %get-tuple-element.29), channel_id=1, source_target_pairs={{0,16},{1,24},{2,0},{3,8},{4,20},{5,28},{6,4},{7,12},{8,17},{9,25}... | collective-permute-start | bytes 49160 | tf_op jit(solution)/shard_map/ppermute | solution.py:344
  70.2 5.0 %collective-permute-start.9 = (bf16[32,256]{1,0:T(8,128)(2,1)S(1)}, bf16[32,256]{1,0:T(8,128)(2,1)S(1)}, u32[]{:S(2)}, u32[]{:S(2)}) collective-permute-start(bf16[32,256]{1,0:T(8,128)(2,1)S(1)} %get-tuple-element.30), channel_id=1, source_target_pairs={{0,20},{1,28},{2,4},{3,12},{4,16},{5,24},{6,0},{7,8},{8,21},{9,29}... | collective-permute-start | bytes 49160 | tf_op jit(solution)/shard_map/ppermute | solution.py:344

commit v2 on v1

v2 whole, which is shorter than its diff:
```python
import functools

import jax
import jax.numpy as jnp
from jax import lax
from jax.experimental import pallas as pl
from jax.experimental.pallas import tpu as pltpu
from jax.sharding import PartitionSpec as P

MOVE = 64
EPSILON = 1e-06
LANES = 128
OFFSETS = 8
STRIDE = 64
DEPTH = 256
VMEM_LIMIT = 28 * 1024 * 1024

SMEM = pl.BlockSpec(memory_space=pltpu.SMEM)
VMEM = pl.BlockSpec(memory_space=pltpu.VMEM)
ANY = pl.BlockSpec(memory_space=pl.ANY)


def params():
    return pltpu.CompilerParams(vmem_limit_bytes=VMEM_LIMIT)


def cost(micros):
    return pl.CostEstimate(
        flops=int(micros * 1e9), bytes_accessed=int(micros * 1e6), transcendentals=0
    )


def pack_kernel(scalars, templates, available, moveout, mine, theirs, square, sems):
    blocks, channels, events, tlen = templates.shape
    chips, _, group, _ = mine.shape
    half = channels // 2
    me = scalars[2]
    copies = []
    for chip in range(chips):
        which, part = divmod(chip * group, events)
        for side, out in enumerate((mine, theirs)):
            first = half * jnp.where(me == side, 0, 1)
            copy = pltpu.make_async_copy(
                templates.at[scalars[which], pl.ds(first, half), pl.ds(part, group), :],
                out.at[chip, pl.ds(0, half)],
                sems.at[chip, side],
            )
            copy.start()
            copies.append(copy)
    flags = jnp.where(available[...] > 0, moveout[...] + 1, 0).astype(jnp.float32)
    for which in range(2):
        code = flags[:, 0, :]
        for block in range(1, blocks):
            code = jnp.where(scalars[which] == block, flags[:, block, :], code)
        square[...] = jnp.zeros_like(square)
        square[0:channels, 0:events] = code
        turned = square[...].T
        other = pltpu.roll(turned, LANES - half, 1)
        here = jnp.where(me == 0, turned, other)[:, 0:tlen].astype(jnp.bfloat16)
        there = jnp.where(me == 0, other, turned)[:, 0:tlen].astype(jnp.bfloat16)
        for index in range(events // group):
            chip = which * (events // group) + index
            rows = slice(index * group, (index + 1) * group)
            mine[chip, half] = here[rows]
            theirs[chip, half] = there[rows]
    for copy in copies:
        copy.wait()


def pack(chips, group, scalars, templates, available, moveout):
    channels, tlen = templates.shape[1], templates.shape[3]
    shape = (chips, channels // 2 + 1, group, tlen)
    return pl.pallas_call(
        pack_kernel,
        out_shape=[jax.ShapeDtypeStruct(shape, jnp.bfloat16)] * 2,
        in_specs=[SMEM, ANY, VMEM, VMEM],
        out_specs=[VMEM] * 2,
        scratch_shapes=[
            pltpu.VMEM((LANES, LANES), jnp.float32),
            pltpu.SemaphoreType.DMA((chips, 2)),
        ],
        compiler_params=params(),
        cost_estimate=cost(1.5),
        name="pack",
    )(scalars, templates, available, moveout)


def merge_kernel(chips, scalars, mine, other, *rest):
    outs, sems = rest[:-1], rest[-1]
    chip, core = scalars[0], scalars[1]
    for step in range(chips):
        dest = jnp.bitwise_xor(chip, step)
        owner = jnp.where(dest < chips // 2, scalars[2], scalars[3])
        here = owner % 2 == core

        @pl.when(here)
        def _():
            pltpu.make_async_copy(mine.at[dest], outs[step], sems.at[step]).start()

        @pl.when(jnp.logical_not(here))
        def _():
            pltpu.make_async_copy(other.at[dest], outs[step], sems.at[step]).start()

    for step in range(chips):
        pltpu.make_async_copy(mine.at[0], outs[step], sems.at[step]).wait()


def merge(chips, scalars, mine, other):
    return pl.pallas_call(
        functools.partial(merge_kernel, chips),
        out_shape=[jax.ShapeDtypeStruct(mine.shape[1:], mine.dtype)] * chips,
        in_specs=[SMEM, ANY, ANY],
        out_specs=[ANY] * chips,
        scratch_shapes=[pltpu.SemaphoreType.DMA((chips,))],
        compiler_params=params(),
        cost_estimate=cost(1),
        name="merge",
    )(scalars, mine, other)


def left(values, count):
    return pltpu.roll(values, values.shape[1] - count, 1)


def window_sums(values):
    sums = {1: values}
    width = 1
    while width < 64:
        sums[2 * width] = sums[width] + left(sums[width], width)
        width *= 2
    return sums[64] + left(sums[32], 64) + left(sums[4], 96)


def lagged(row, ahead):
    copies = jnp.broadcast_to(row, (8, row.shape[1]))
    return pltpu.roll(copies, row.shape[1] - 7 - ahead, 1, stride=1, stride_axis=0)


def waves_kernel(channels, samples, tlen, *rest):
    waves = rest[:-4]
    left_a, left_r, padded, inverse = rest[-4:]
    span = waves[0].shape[1]
    steps = samples // STRIDE
    padded[...] = jnp.zeros_like(padded)
    for index, wave in enumerate(waves):
        padded[0:channels, span * index : span * (index + 1)] = wave[...].astype(jnp.float32)

    @pl.loop(0, 4)
    def _(part):
        rows = pl.ds(pl.multiple_of(part * 8, 8), 8)
        values = padded[rows, :]
        first_sum = window_sums(values)
        second_sum = window_sums(values * values)
        mean = first_sum / tlen
        inverse[rows, :] = lax.rsqrt(second_sum / tlen - mean * mean + EPSILON)

    @pl.loop(0, channels)
    def _(channel):
        row = padded[pl.ds(channel, 1), :]
        scale = inverse[pl.ds(channel, 1), :]
        even, odd = lagged(row, 0), lagged(row, STRIDE)
        even_scale, odd_scale = lagged(scale, 0), lagged(scale, STRIDE)
        columns = ([], [], [])
        for index in range(len(waves)):
            for step in range(steps):
                start = span * index + STRIDE * (step - step % 2)
                values = odd if step % 2 else even
                columns[0].append(values[:, start : start + LANES])
                columns[1].append(values[:, start + LANES : start + 2 * LANES])
                values = odd_scale if step % 2 else even_scale
                columns[2].append(values[:, start : start + LANES])
        left_a[channel, :, 0:LANES] = jnp.concatenate(columns[0], axis=0).astype(jnp.bfloat16)
        left_a[channel, :, LANES:] = jnp.concatenate(columns[1], axis=0).astype(jnp.bfloat16)
        value = jnp.concatenate(columns[2], axis=0)
        high = value.astype(jnp.bfloat16)
        left_r[channel, :, 0:LANES] = high
        left_r[channel, :, LANES:] = (value - high.astype(jnp.float32)).astype(jnp.bfloat16)


def prepare_waves(samples, tlen, waves):
    channels, span = waves[0].shape
    rows = len(waves) * samples // OFFSETS
    out = jax.ShapeDtypeStruct((channels, rows, DEPTH), jnp.bfloat16)
    return pl.pallas_call(
        functools.partial(waves_kernel, channels, samples, tlen),
        out_shape=[out, out],
        in_specs=[VMEM] * len(waves),
        out_specs=[VMEM, VMEM],
        scratch_shapes=[
            pltpu.VMEM((32, span * len(waves)), jnp.float32),
            pltpu.VMEM((32, span * len(waves)), jnp.float32),
        ],
        compiler_params=params(),
        cost_estimate=cost(5),
        name="prepare_waves",
    )(*waves)


def main_kernel(channels, tlen, group, scalars, first, second, left_a, left_r, *rest):
    outs = rest[:-4]
    bank, weight_a, weight_r, total = rest[-4:]
    half = channels // 2
    slots = LANES // group
    banks = (half + 1) // slots
    offset_count = LANES // group
    tile_count = OFFSETS // offset_count
    code_lane = (half % slots) * group
    top = 112 + 8 * (7 + offset_count - 1)

    lag = lax.broadcasted_iota(jnp.int32, (LANES, LANES), 0)
    lane = lax.broadcasted_iota(jnp.int32, (1, LANES), 1)
    used = lag < tlen
    for side, piece in enumerate((first, second)):
        turned = []
        for index in range(banks):
            values = piece[slots * index : slots * (index + 1)].astype(jnp.float32)
            values = values.reshape(LANES, tlen)
            values = jnp.concatenate([values, jnp.zeros((LANES, LANES - tlen), jnp.float32)], axis=1)
            turned.append(values.T)
        codes = turned[-1]
        for index, values in enumerate(turned):
            code = jnp.zeros((1, LANES), jnp.float32)
            for slot in range(slots):
                item = slots * index + slot
                if item < half:
                    moved = pltpu.roll(
                        codes[item : item + 1, :], (group * slot - code_lane) % LANES, 1
                    )
                    code = jnp.where(lane // group == slot, moved, code)
            center = jnp.sum(jnp.where(used, values, 0.0), axis=0, keepdims=True) / tlen
            deviate = jnp.where(used, values - center, 0.0)
            spread = jnp.sqrt(jnp.sum(deviate * deviate, axis=0, keepdims=True) / tlen + EPSILON)
            unit = (deviate / (spread * tlen)).astype(jnp.bfloat16).astype(jnp.float32)
            unit = jnp.where(code > 0, unit, 0.0)
            shift = code.astype(jnp.int32) - 1
            for bit in (1, 2, 4):
                unit = jnp.where(jnp.bitwise_and(shift, bit) > 0, pltpu.roll(unit, bit, 0), unit)
            unit = jnp.where(lag == 112, code, unit)
            bank[side * banks + index] = unit.astype(jnp.bfloat16)

    source_lane = lax.broadcasted_iota(jnp.int32, (LANES, LANES), 0)
    target_lane = lax.broadcasted_iota(jnp.int32, (LANES, LANES), 1)
    ahead = lane // group
    for side in range(2):
        base = half * jnp.where(scalars[1] == side, 0, 1)

        @pl.loop(0, half)
        def _(item):
            slot = item % slots
            expand = (source_lane == target_lane % group + slot * group).astype(jnp.float32)
            spreaded = jnp.dot(
                bank[side * banks + item // slots],
                expand.astype(jnp.bfloat16),
                preferred_element_type=jnp.float32,
            )
            code = spreaded[112:113, :].astype(jnp.int32)
            usable = code > 0
            shift = code - 1
            moves = shift // 8 + ahead
            taps = spreaded[0:112, :]
            for bit in (1, 2, 4, 8):
                gap = jnp.zeros((8 * bit, LANES), jnp.float32)
                taps = jnp.where(
                    jnp.bitwise_and(moves, bit) > 0,
                    jnp.concatenate([gap, taps], axis=0),
                    jnp.concatenate([taps, gap], axis=0),
                )[0:top]
            channel = base + item
            reach = shift + 8 * ahead
            for index in range(tile_count):
                skip = 8 * offset_count * index
                column = [taps, jnp.zeros((DEPTH - top - skip, LANES), jnp.float32)]
                if skip:
                    column = [jnp.zeros((skip, LANES), jnp.float32)] + column
                lanes = slice(LANES * index, LANES * (index + 1))
                weight_a[channel, :, lanes] = jnp.concatenate(column, axis=0).astype(jnp.bfloat16)
                pick = jnp.logical_and(source_lane == reach + skip, usable)
                pick = jnp.where(pick, 1.0, 0.0).astype(jnp.bfloat16)
                weight_r[channel, 0:LANES, lanes] = pick
                weight_r[channel, LANES : 2 * LANES, lanes] = pick

    total[...] = jnp.zeros_like(total)

    @pl.loop(0, channels // 2)
    def _(pair):
        for channel in (2 * pair, 2 * pair + 1):
            corr = jnp.dot(left_a[channel], weight_a[channel], preferred_element_type=jnp.float32)
            factor = jnp.dot(left_r[channel], weight_r[channel], preferred_element_type=jnp.float32)
            total[...] += corr * factor

    rows_out = outs[0].shape[0]
    for step, out in enumerate(outs):
        segment = jnp.bitwise_xor(scalars[0], step)
        out[...] = total[pl.ds(pl.multiple_of(segment * rows_out, rows_out), rows_out), :].astype(
            jnp.bfloat16
        )


def correlate(channels, tlen, group, samples, scalars, first, second, left_a, left_r):
    rows = left_a.shape[1]
    width = OFFSETS * group
    rows_out = samples // OFFSETS
    out = jax.ShapeDtypeStruct((rows_out, width), jnp.bfloat16)
    banks = 2 * (channels // 2 + 1) * group // LANES
    return pl.pallas_call(
        functools.partial(main_kernel, channels, tlen, group),
        out_shape=[out] * (rows // rows_out),
        in_specs=[SMEM, VMEM, VMEM, VMEM, VMEM],
        out_specs=[VMEM] * (rows // rows_out),
        scratch_shapes=[
            pltpu.VMEM((banks, LANES, LANES), jnp.bfloat16),
            pltpu.VMEM((channels, DEPTH, width), jnp.bfloat16),
            pltpu.VMEM((channels, DEPTH, width), jnp.bfloat16),
            pltpu.VMEM((rows, width), jnp.float32),
        ],
        compiler_params=params(),
        cost_estimate=cost(9),
        name="correlate",
    )(scalars, first, second, left_a, left_r)


def finish_kernel(group, *rest):
    parts, out = rest[:-1], rest[-1]
    samples = out.shape[1]
    rows = parts[0].shape[0]
    value = parts[0][...].astype(jnp.float32)
    for part in parts[1:]:
        value = value + part[...].astype(jnp.float32)
    high = value.astype(jnp.bfloat16).astype(jnp.float32)
    both = jnp.concatenate([high, value - high], axis=0).T.astype(jnp.bfloat16)
    row = lax.broadcasted_iota(jnp.int32, (2 * rows, samples), 0) % rows
    lane = lax.broadcasted_iota(jnp.int32, (2 * rows, samples), 1)
    place = jnp.logical_and(lane // STRIDE == row // 8, lane % 8 == 7 - row % 8)
    place = jnp.where(place, 1.0, 0.0).astype(jnp.bfloat16)
    wide = jnp.dot(both, place, preferred_element_type=jnp.float32)
    lane = lax.broadcasted_iota(jnp.int32, (group, samples), 1) // 8 % OFFSETS
    result = jnp.zeros((group, samples), jnp.float32)
    for offset in range(OFFSETS):
        result = jnp.where(lane == offset, wide[offset * group : (offset + 1) * group], result)
    out[...] = result


def finish(group, samples, parts):
    return pl.pallas_call(
        functools.partial(finish_kernel, group),
        out_shape=jax.ShapeDtypeStruct((group, samples), jnp.float32),
        in_specs=[VMEM] * len(parts),
        out_specs=VMEM,
        compiler_params=params(),
        cost_estimate=cost(1),
        name="finish",
    )(*parts)


def shards(waveforms, templates, available, moveout, bank_blocks):
    channels, samples = waveforms.shape
    blocks, events, _, tlen = templates.shape
    count_tm = lax.axis_size("tm")
    count_sta = lax.axis_size("sta")
    chips = count_tm // 2
    group = 2 * events // chips
    rim = MOVE + tlen - 1
    me = lax.axis_index("tm").astype(jnp.int32)
    station = lax.axis_index("sta").astype(jnp.int32)
    chip, core = me // 2, me % 2
    swap = [(i, i ^ 1) for i in range(count_tm)]

    def across(array, step):
        return lax.ppermute(array, "tm", [(i, i ^ (2 * step)) for i in range(count_tm)])

    owners = bank_blocks // blocks
    slots = bank_blocks % blocks

    next_rim = lax.ppermute(
        waveforms[:, :rim], "tm", [(i, i - 1) for i in range(1, count_tm)]
    )
    tail = jnp.zeros((channels, 2 * LANES - rim), waveforms.dtype)
    segment = jnp.concatenate([waveforms, next_rim, tail], axis=1)
    segments = [segment] + [across(segment, step) for step in range(1, chips)]

    mine, theirs = pack(
        chips,
        group,
        jnp.stack([slots[0], slots[1], core]),
        jnp.transpose(templates, (0, 2, 1, 3)),
        jnp.transpose(available, (2, 0, 1)),
        jnp.transpose(moveout, (2, 0, 1)),
    )
    other = lax.ppermute(theirs, "tm", swap)
    merged = merge(chips, jnp.stack([chip, core, owners[0], owners[1]]), mine, other)
    pieces = [merged[0]] + [across(merged[step], step) for step in range(1, chips)]
    left_a, left_r = prepare_waves(samples, tlen, segments)

    source = (jnp.where(chip < chips // 2, owners[0], owners[1]) // 2) ^ chip
    first = pieces[0]
    for step in range(1, chips):
        first = jnp.where(source == step, pieces[step], first)
    second = lax.ppermute(first, "tm", swap)
    parts = correlate(
        channels, tlen, group, samples, jnp.stack([chip ^ station, core]), first, second, left_a, left_r
    )
    gathered = []
    for step in range(chips):
        route = [
            (d * count_sta + s, (2 * (s ^ step) + d % 2) * count_sta + d // 2)
            for d in range(count_tm)
            for s in range(count_sta)
        ]
        gathered.append(lax.ppermute(parts[step], ("tm", "sta"), route))
    return finish(group, samples, gathered)


def solution(mesh):
    in_specs = (
        P("sta", "tm"),
        P("tm", None, "sta", None),
        P("tm", None, "sta"),
        P("tm", None, "sta"),
        P(),
    )
    out_specs = P("sta", "tm")
    return jax.shard_map(shards, mesh=mesh, in_specs=in_specs, out_specs=out_specs, check_vma=False)
```

time: 77 us -> 63 us (0.82)
  the two profiles are of different devices: /device:TPU:9 before, /device:TPU:2 now
where the time goes in v2:
time: 63 us; the launch traced here: 62.7 us
  starting transfers between devices  26 us (41%)
  Pallas kernels  21.3 us (34%)
  waiting for transfers between devices  9.55 us (15%)
  local copies, waits for them, and re-layouts  3.44 us (5%)
  between operations  1.44 us (2%)
  other arithmetic  0.96 us (2%)
    ppermute x6, starting transfers between devices, across(): lax.ppermute(array, 'tm', [(i, i ^ 2 * step) for i in range(count_tm)])  15.4 us
    pallas_call x1, Pallas kernels, correlate(): pl.pallas_call(functools.partial(main_kernel, channels, tlen, group), out...  11.3 us
    ppermute x4, starting transfers between devices, shards(): gathered.append(lax.ppermute(parts[step], ('tm', 'sta'), route))  9.17 us
    pallas_call x1, Pallas kernels, prepare_waves(): pl.pallas_call(functools.partial(waves_kernel, channels, samples, tlen),...  6.73 us
    ppermute x4, waiting for transfers between devices, shards(): gathered.append(lax.ppermute(parts[step], ('tm', 'sta'), route))  4.81 us
    ppermute x6, waiting for transfers between devices, across(): lax.ppermute(array, 'tm', [(i, i ^ 2 * step) for i in range(count_tm)])  4.73 us
    unnamed x8, local copies, waits for them, and re-layouts  2.71 us
    pallas_call x1, Pallas kernels, merge(): pl.pallas_call(functools.partial(merge_kernel, chips), out_shape=[jax.Sha...  1.32 us
  transfers between devices with their start and end apart: 13, of which 4 were waited for; matrix products, arithmetic and copies ran while one was open for 1% of the time, Pallas kernels for 13%

profile of v2, /device:TPU:2, one launch (start us, length us, event | category | flops | bytes accessed | tf_op | source)
XLA Modules:
  0.0 62.7 jit_solution(14237769705325374319)
XLA Ops:
  0.0 0.0 copy-start.3
  0.0 0.7 %and_select_fusion = (s32[2]{0:T(128)S(1)}, s32[2]{0:T(128)S(1)}) fusion(s32[2]{0:T(128)} %param.9), kind=kLoop, calls=%fused_computation.2 | loop fusion | flops 38 | bytes 24 | tf_op jit(solution)/shard_map/jit(remainder)/select_n | solution.py:372
  0.7 0.1 pad_add_fusion.2.scalars
  0.8 0.0 copy-start
  0.8 1.2 %copy-done = bf16[2,64,30,100]{3,1,2,0:T(8,128)(2,1)S(1)} copy-done((bf16[2,64,30,100]{3,1,2,0:T(8,128)(2,1)S(1)}, bf16[2,64,30,100]{3,1,2,0:T(8,128)(2,1)}, u32[]{:S(2)}) %copy-start) | copy-done | bytes 768024
  2.0 0.0 copy-start.1
  2.0 0.8 %copy-done.1 = s32[2,64,30]{1,0,2:T(2,128)S(1)} copy-done((s32[2,64,30]{1,0,2:T(2,128)S(1)}, s32[2,64,30]{1,0,2:T(2,128)}, u32[]{:S(2)}) %copy-start.1) | copy-done | bytes 15384
  2.7 0.0 copy-start.2
  2.7 0.8 %copy-done.2 = s32[2,64,30]{1,0,2:T(2,128)S(1)} copy-done((s32[2,64,30]{1,0,2:T(2,128)S(1)}, s32[2,64,30]{1,0,2:T(2,128)}, u32[]{:S(2)}) %copy-start.2) | copy-done | bytes 15384
  3.5 1.0 %pack.1 = (bf16[4,16,32,100]{3,2,1,0:T(8,128)(2,1)S(1)}, bf16[4,16,32,100]{3,2,1,0:T(8,128)(2,1)S(1)}) custom-call(s32[3]{0:T(128)S(1)} %pad_add_fusion.2.scalars, bf16[2,30,64,100]{3,2,1,0:T(8,128)(2,1)S(1)} %bitcast.8, s32[30,2,64]{2,1,0:T(2,128)S(1)} %bitcast.9, s32[30,2,64]{2,1,0:T(2,128)S(1)} %bitcast.10), custom_call_target="tpu_custom_call" | custom-call | flops 1500000000 | bytes 1500000 | tf_op jit(solution)/shard_map/pack/pallas_call | solution.py:73
  4.5 0.1 collective-permute-start
  4.6 0.0 copy-done.3
  4.6 1.3 %collective-permute-start.5 = (bf16[30,163]{1,0:T(8,128)(2,1)S(1)}, bf16[30,163]{1,0:T(8,128)(2,1)S(1)}, u32[]{:S(2)}, u32[]{:S(2)}) collective-permute-start(bf16[30,163]{1,0:T(8,128)(2,1)S(1)} %slice.17), channel_id=1, source_target_pairs={{4,0},{8,4},{12,8},{16,12},{20,16},{24,20},{28,24},{5,1},{9,5},{13... | collective-permute-start | bytes 29348 | tf_op jit(solution)/shard_map/ppermute | solution.py:374
  5.9 0.6 %fusion = (s32[1]{0:T(128)}, s32[1]{0:T(128)}) fusion(s32[2]{0:T(128)S(1)} %get-tuple-element.32), kind=kLoop, calls=%fused_computation.10 | loop fusion | bytes 16 | tf_op jit(solution)/shard_map/slice | solution.py:394
  7.9 0.1 pad.2.clone
  7.9 0.1 pad_add_fusion.scalars
  8.0 0.1 pad_add_fusion.1.scalars
  8.1 0.0 collective-permute-done.other
  8.1 1.3 %merge.1 = (bf16[16,32,100]{2,1,0:T(8,128)(2,1)S(1)}, bf16[16,32,100]{2,1,0:T(8,128)(2,1)S(1)}, bf16[16,32,100]{2,1,0:T(8,128)(2,1)S(1)}, bf16[16,32,100]{2,1,0:T(8,128)(2,1)S(1)}) custom-call(s32[4]{0:T(128)S(1)} %pad_add_fusion.1.scalars, bf16[4,16,32,100]{3,2,1,0:T(8,128)(2,1)S(1)} %get-tuple-element.17.mine, ...), custom_call_target="tpu_custom_call" | custom-call | flops 1000000000 | bytes 1000000 | tf_op jit(solution)/shard_map/merge/pallas_call | solution.py:109
  9.4 4.8 %collective-permute-start.1 = (bf16[16,32,100]{2,1,0:T(8,128)(2,1)S(1)}, bf16[16,32,100]{2,1,0:T(8,128)(2,1)S(1)}, u32[]{:S(2)}, u32[]{:S(2)}) collective-permute-start(bf16[16,32,100]{2,1,0:T(8,128)(2,1)S(1)} %get-tuple-element.19), channel_id=1, source_target_pairs={{0,24},{4,28},{8,16},{12,20},{16,8},{20,12},{24,0},{28,4},{1,25},{... | collective-permute-start | bytes 307208 | tf_op jit(solution)/shard_map/ppermute | solution.py:369
  14.2 0.0 collective-permute-start.2
  14.2 0.6 %collective-permute-start.3 = (bf16[16,32,100]{2,1,0:T(8,128)(2,1)S(1)}, bf16[16,32,100]{2,1,0:T(8,128)(2,1)S(1)}, u32[]{:S(2)}, u32[]{:S(2)}) collective-permute-start(bf16[16,32,100]{2,1,0:T(8,128)(2,1)S(1)} %get-tuple-element.21), channel_id=1, source_target_pairs={{0,8},{4,12},{8,0},{12,4},{16,24},{20,28},{24,16},{28,20},{1,9},{5... | collective-permute-start | bytes 307208 | tf_op jit(solution)/shard_map/ppermute | solution.py:369
  14.9 0.0 collective-permute-done.5
  14.9 3.8 %collective-permute-start.8 = (bf16[30,768]{1,0:T(8,128)(2,1)S(1)}, bf16[30,768]{1,0:T(8,128)(2,1)S(1)}, u32[]{:S(2)}, u32[]{:S(2)}) collective-permute-start(bf16[30,768]{1,0:T(8,128)(2,1)S(1)} %maximum_maximum_fusion.rest_0_), channel_id=1, source_target_pairs={{0,24},{4,28},{8,16},{12,20},{16,8},{20,12},{24,0},{28,4},{1,25},{... | collective-permute-start | bytes 138248 | tf_op jit(solution)/shard_map/ppermute | solution.py:369
  18.7 0.0 collective-permute-start.7
  18.7 0.0 collective-permute-done.1
  18.7 6.1 %collective-permute-start.6 = (bf16[30,768]{1,0:T(8,128)(2,1)S(1)}, bf16[30,768]{1,0:T(8,128)(2,1)S(1)}, u32[]{:S(2)}, u32[]{:S(2)}) collective-permute-start(bf16[30,768]{1,0:T(8,128)(2,1)S(1)} %maximum_maximum_fusion.rest_0_), channel_id=1, source_target_pairs={{0,8},{4,12},{8,0},{12,4},{16,24},{20,28},{24,16},{28,20},{1,9},{5... | collective-permute-start | bytes 138248 | tf_op jit(solution)/shard_map/ppermute | solution.py:369
  24.8 3.7 %collective-permute-done.2 = bf16[16,32,100]{2,1,0:T(8,128)(2,1)S(1)} collective-permute-done((bf16[16,32,100]{2,1,0:T(8,128)(2,1)S(1)}, bf16[16,32,100]{2,1,0:T(8,128)(2,1)S(1)}, u32[]{:S(2)}, u32[]{:S(2)}) %collective-permute-start.2) | collective-permute-done | bytes 102432 | tf_op jit(solution)/shard_map/ppermute | solution.py:369
  28.5 0.0 collective-permute-done.3
  28.5 0.1 collective-permute-start.4
  28.6 0.0 collective-permute-done.8.rest_3_
  28.6 1.0 %collective-permute-done.7.rest_2_ = bf16[30,768]{1,0:T(8,128)(2,1)S(1)} collective-permute-done((bf16[30,768]{1,0:T(8,128)(2,1)S(1)}, bf16[30,768]{1,0:T(8,128)(2,1)S(1)}, u32[]{:S(2)}, u32[]{:S(2)}) %collective-permute-start.7) | collective-permute-done | bytes 46112 | tf_op jit(solution)/shard_map/ppermute | solution.py:369
  29.7 0.0 collective-permute-done.6.rest_1_
  29.7 6.7 %prepare_waves.1 = (bf16[30,256,256]{2,1,0:T(8,128)(2,1)S(1)}, bf16[30,256,256]{2,1,0:T(8,128)(2,1)S(1)}) custom-call(bf16[30,768]{1,0:T(8,128)(2,1)S(1)} %maximum_maximum_fusion.rest_0_, bf16[30,768]{1,0:T(8,128)(2,1)S(1)} %collective-permute-done.6.rest_1_, bf16[30,768]{1,0:T(8,128)(2,1)S(1)} %collective-permute-done.7.rest_2_, ...), custom_call_target="tpu_custom_call" | custom-call | flops 5000000000 | bytes 5000000 | tf_op jit(solution)/shard_map/prepare_waves/pallas_call | solution.py:184
  36.4 0.0 collective-permute-done.4.second
  36.4 11.3 %correlate.1 = (bf16[64,256]{1,0:T(8,128)(2,1)S(1)}, bf16[64,256]{1,0:T(8,128)(2,1)S(1)}, bf16[64,256]{1,0:T(8,128)(2,1)S(1)}, bf16[64,256]{1,0:T(8,128)(2,1)S(1)}) custom-call(s32[2]{0:T(128)S(1)} %pad_add_fusion.scalars, bf16[16,32,100]{2,1,0:T(8,128)(2,1)S(1)} %select_select_fusion.first, bf16[16,32,100]{2,1,0:T(8,128)(2,1)S(1)} %collective-permute-done.4.second, ...), custom_call_target="tpu_custom_call" | custom-call | flops 8999999488 | bytes 9000000 | tf_op jit(solution)/shard_map/correlate/pallas_call | solution.py:305
  47.8 1.9 %collective-permute-start.9 = (bf16[64,256]{1,0:T(8,128)(2,1)S(1)}, bf16[64,256]{1,0:T(8,128)(2,1)S(1)}, u32[]{:S(2)}, u32[]{:S(2)}) collective-permute-start(bf16[64,256]{1,0:T(8,128)(2,1)S(1)} %get-tuple-element.25), channel_id=1, source_target_pairs={{0,0},{1,8},{2,16},{3,24},{4,4},{5,12},{6,20},{7,28},{8,1},{9,9},{... | collective-permute-start | bytes 98312 | tf_op jit(solution)/shard_map/ppermute | solution.py:409
  49.7 0.1 collective-permute-start.10
  49.8 7.2 %collective-permute-start.11 = (bf16[64,256]{1,0:T(8,128)(2,1)S(1)}, bf16[64,256]{1,0:T(8,128)(2,1)S(1)}, u32[]{:S(2)}, u32[]{:S(2)}) collective-permute-start(bf16[64,256]{1,0:T(8,128)(2,1)S(1)} %get-tuple-element.27), channel_id=1, source_target_pairs={{0,16},{1,24},{2,0},{3,8},{4,20},{5,28},{6,4},{7,12},{8,17},{9,25}... | collective-permute-start | bytes 98312 | tf_op jit(solution)/shard_map/ppermute | solution.py:409
  57.0 0.0 collective-permute-start.12
  57.0 0.0 collective-permute-done.9.rest_0_
  57.0 0.0 collective-permute-done.10.rest_1_
  57.0 1.6 %collective-permute-done.11.rest_2_ = bf16[64,256]{1,0:T(8,128)(2,1)S(1)} collective-permute-done((bf16[64,256]{1,0:T(8,128)(2,1)S(1)}, bf16[64,256]{1,0:T(8,128)(2,1)S(1)}, u32[]{:S(2)}, u32[]{:S(2)}) %collective-permute-start.11) | collective-permute-done | bytes 32800 | tf_op jit(solution)/shard_map/ppermute | solution.py:409
  58.6 3.2 %collective-permute-done.12.rest_3_ = bf16[64,256]{1,0:T(8,128)(2,1)S(1)} collective-permute-done((bf16[64,256]{1,0:T(8,128)(2,1)S(1)}, bf16[64,256]{1,0:T(8,128)(2,1)S(1)}, u32[]{:S(2)}, u32[]{:S(2)}) %collective-permute-start.12) | collective-permute-done | bytes 32800 | tf_op jit(solution)/shard_map/ppermute | solution.py:409
  61.8 0.9 %finish.1 = f32[32,512]{1,0:T(8,128)} custom-call(bf16[64,256]{1,0:T(8,128)(2,1)S(1)} %collective-permute-done.9.rest_0_, bf16[64,256]{1,0:T(8,128)(2,1)S(1)} %collective-permute-done.10.rest_1_, bf16[64,256]{1,0:T(8,128)(2,1)S(1)} %collective-permute-done.11.rest_2_, bf16[64,256]{1,0:T(8,128)(2,1)S(1)} %collective-permute-done.12.rest_3_), custom_call_target="tpu_custom_call" | custom-call | flops 1000000000 | bytes 1000000 | tf_op jit(solution)/shard_map/finish/pallas_call | solution.py:344
  (4 shorter events, 0.1 us)
Async XLA Ops:
  0.0 4.6 %copy-start.3 = (bf16[30,512]{1,0:T(8,128)(2,1)S(1)}, bf16[30,512]{1,0:T(8,128)(2,1)}, u32[]{:S(2)}) copy-start(bf16[30,512]{1,0:T(8,128)(2,1)} %param.5) | copy-start | bytes 92164
  0.8 1.2 %copy-start = (bf16[2,64,30,100]{3,1,2,0:T(8,128)(2,1)S(1)}, bf16[2,64,30,100]{3,1,2,0:T(8,128)(2,1)}, u32[]{:S(2)}) copy-start(bf16[2,64,30,100]{3,1,2,0:T(8,128)(2,1)} %param.6) | copy-start | bytes 2304004
  2.0 0.8 %copy-start.1 = (s32[2,64,30]{1,0,2:T(2,128)S(1)}, s32[2,64,30]{1,0,2:T(2,128)}, u32[]{:S(2)}) copy-start(s32[2,64,30]{1,0,2:T(2,128)} %param.7) | copy-start | bytes 46084
  2.7 0.8 %copy-start.2 = (s32[2,64,30]{1,0,2:T(2,128)S(1)}, s32[2,64,30]{1,0,2:T(2,128)}, u32[]{:S(2)}) copy-start(s32[2,64,30]{1,0,2:T(2,128)} %param.8) | copy-start | bytes 46084
  4.5 3.6 %collective-permute-start = (bf16[4,16,32,100]{3,2,1,0:T(8,128)(2,1)S(1)}, bf16[4,16,32,100]{3,2,1,0:T(8,128)(2,1)S(1)}, u32[]{:S(2)}, u32[]{:S(2)}) collective-permute-start(bf16[4,16,32,100]{3,2,1,0:T(8,128)(2,1)S(1)} %get-tuple-element.18), channel_id=1, source_target_pairs={{0,4},{4,0},{8,12},{12,8},{16,20},{20,16},{24,28},{28,24},{1,5},{5... | collective-permute-start | bytes 1228808 | tf_op jit(solution)/shard_map/ppermute | solution.py:389
  4.6 10.3 %collective-permute-start.5 = (bf16[30,163]{1,0:T(8,128)(2,1)S(1)}, bf16[30,163]{1,0:T(8,128)(2,1)S(1)}, u32[]{:S(2)}, u32[]{:S(2)}) collective-permute-start(bf16[30,163]{1,0:T(8,128)(2,1)S(1)} %slice.17), channel_id=1, source_target_pairs={{4,0},{8,4},{12,8},{16,12},{20,16},{24,20},{28,24},{5,1},{9,5},{13... | collective-permute-start | bytes 29348 | tf_op jit(solution)/shard_map/ppermute | solution.py:374
  9.4 9.3 %collective-permute-start.1 = (bf16[16,32,100]{2,1,0:T(8,128)(2,1)S(1)}, bf16[16,32,100]{2,1,0:T(8,128)(2,1)S(1)}, u32[]{:S(2)}, u32[]{:S(2)}) collective-permute-start(bf16[16,32,100]{2,1,0:T(8,128)(2,1)S(1)} %get-tuple-element.19), channel_id=1, source_target_pairs={{0,24},{4,28},{8,16},{12,20},{16,8},{20,12},{24,0},{28,4},{1,25},{... | collective-permute-start | bytes 307208 | tf_op jit(solution)/shard_map/ppermute | solution.py:369
  14.2 14.3 %collective-permute-start.2 = (bf16[16,32,100]{2,1,0:T(8,128)(2,1)S(1)}, bf16[16,32,100]{2,1,0:T(8,128)(2,1)S(1)}, u32[]{:S(2)}, u32[]{:S(2)}) collective-permute-start(bf16[16,32,100]{2,1,0:T(8,128)(2,1)S(1)} %get-tuple-element.20), channel_id=1, source_target_pairs={{0,16},{4,20},{8,24},{12,28},{16,0},{20,4},{24,8},{28,12},{1,17},{... | collective-permute-start | bytes 307208 | tf_op jit(solution)/shard_map/ppermute | solution.py:369
  14.2 14.3 %collective-permute-start.3 = (bf16[16,32,100]{2,1,0:T(8,128)(2,1)S(1)}, bf16[16,32,100]{2,1,0:T(8,128)(2,1)S(1)}, u32[]{:S(2)}, u32[]{:S(2)}) collective-permute-start(bf16[16,32,100]{2,1,0:T(8,128)(2,1)S(1)} %get-tuple-element.21), channel_id=1, source_target_pairs={{0,8},{4,12},{8,0},{12,4},{16,24},{20,28},{24,16},{28,20},{1,9},{5... | collective-permute-start | bytes 307208 | tf_op jit(solution)/shard_map/ppermute | solution.py:369
  14.9 13.7 %collective-permute-start.8 = (bf16[30,768]{1,0:T(8,128)(2,1)S(1)}, bf16[30,768]{1,0:T(8,128)(2,1)S(1)}, u32[]{:S(2)}, u32[]{:S(2)}) collective-permute-start(bf16[30,768]{1,0:T(8,128)(2,1)S(1)} %maximum_maximum_fusion.rest_0_), channel_id=1, source_target_pairs={{0,24},{4,28},{8,16},{12,20},{16,8},{20,12},{24,0},{28,4},{1,25},{... | collective-permute-start | bytes 138248 | tf_op jit(solution)/shard_map/ppermute | solution.py:369
  18.7 11.0 %collective-permute-start.7 = (bf16[30,768]{1,0:T(8,128)(2,1)S(1)}, bf16[30,768]{1,0:T(8,128)(2,1)S(1)}, u32[]{:S(2)}, u32[]{:S(2)}) collective-permute-start(bf16[30,768]{1,0:T(8,128)(2,1)S(1)} %maximum_maximum_fusion.rest_0_), channel_id=1, source_target_pairs={{0,16},{4,20},{8,24},{12,28},{16,0},{20,4},{24,8},{28,12},{1,17},{... | collective-permute-start | bytes 138248 | tf_op jit(solution)/shard_map/ppermute | solution.py:369
  18.7 11.0 %collective-permute-start.6 = (bf16[30,768]{1,0:T(8,128)(2,1)S(1)}, bf16[30,768]{1,0:T(8,128)(2,1)S(1)}, u32[]{:S(2)}, u32[]{:S(2)}) collective-permute-start(bf16[30,768]{1,0:T(8,128)(2,1)S(1)} %maximum_maximum_fusion.rest_0_), channel_id=1, source_target_pairs={{0,8},{4,12},{8,0},{12,4},{16,24},{20,28},{24,16},{28,20},{1,9},{5... | collective-permute-start | bytes 138248 | tf_op jit(solution)/shard_map/ppermute | solution.py:369
  28.5 7.9 %collective-permute-start.4 = (bf16[16,32,100]{2,1,0:T(8,128)(2,1)S(1)}, bf16[16,32,100]{2,1,0:T(8,128)(2,1)S(1)}, u32[]{:S(2)}, u32[]{:S(2)}) collective-permute-start(bf16[16,32,100]{2,1,0:T(8,128)(2,1)S(1)} %select_select_fusion.first), channel_id=1, source_target_pairs={{0,4},{4,0},{8,12},{12,8},{16,20},{20,16},{24,28},{28,24},{1,5},{5... | collective-permute-start | bytes 307208 | tf_op jit(solution)/shard_map/ppermute | solution.py:398
  47.8 9.2 %collective-permute-start.9 = (bf16[64,256]{1,0:T(8,128)(2,1)S(1)}, bf16[64,256]{1,0:T(8,128)(2,1)S(1)}, u32[]{:S(2)}, u32[]{:S(2)}) collective-permute-start(bf16[64,256]{1,0:T(8,128)(2,1)S(1)} %get-tuple-element.25), channel_id=1, source_target_pairs={{0,0},{1,8},{2,16},{3,24},{4,4},{5,12},{6,20},{7,28},{8,1},{9,9},{... | collective-permute-start | bytes 98312 | tf_op jit(solution)/shard_map/ppermute | solution.py:409
  49.7 7.3 %collective-permute-start.10 = (bf16[64,256]{1,0:T(8,128)(2,1)S(1)}, bf16[64,256]{1,0:T(8,128)(2,1)S(1)}, u32[]{:S(2)}, u32[]{:S(2)}) collective-permute-start(bf16[64,256]{1,0:T(8,128)(2,1)S(1)} %get-tuple-element.26), channel_id=1, source_target_pairs={{0,8},{1,0},{2,24},{3,16},{4,12},{5,4},{6,28},{7,20},{8,9},{9,1},{... | collective-permute-start | bytes 98312 | tf_op jit(solution)/shard_map/ppermute | solution.py:409
  49.8 8.8 %collective-permute-start.11 = (bf16[64,256]{1,0:T(8,128)(2,1)S(1)}, bf16[64,256]{1,0:T(8,128)(2,1)S(1)}, u32[]{:S(2)}, u32[]{:S(2)}) collective-permute-start(bf16[64,256]{1,0:T(8,128)(2,1)S(1)} %get-tuple-element.27), channel_id=1, source_target_pairs={{0,16},{1,24},{2,0},{3,8},{4,20},{5,28},{6,4},{7,12},{8,17},{9,25}... | collective-permute-start | bytes 98312 | tf_op jit(solution)/shard_map/ppermute | solution.py:409
  57.0 4.8 %collective-permute-start.12 = (bf16[64,256]{1,0:T(8,128)(2,1)S(1)}, bf16[64,256]{1,0:T(8,128)(2,1)S(1)}, u32[]{:S(2)}, u32[]{:S(2)}) collective-permute-start(bf16[64,256]{1,0:T(8,128)(2,1)S(1)} %get-tuple-element.28), channel_id=1, source_target_pairs={{0,24},{1,16},{2,8},{3,0},{4,28},{5,20},{6,12},{7,4},{8,25},{9,17}... | collective-permute-start | bytes 98312 | tf_op jit(solution)/shard_map/ppermute | solution.py:409

commit v3 on v2

--- a/solution.py
+++ b/solution.py
@@ -7,7 +7,6 @@
 from jax.experimental.pallas import tpu as pltpu
 from jax.sharding import PartitionSpec as P
 
-MOVE = 64
 EPSILON = 1e-06
 LANES = 128
 OFFSETS = 8
@@ -18,6 +17,7 @@
 SMEM = pl.BlockSpec(memory_space=pltpu.SMEM)
 VMEM = pl.BlockSpec(memory_space=pltpu.VMEM)
 ANY = pl.BlockSpec(memory_space=pl.ANY)
+HBM = pl.BlockSpec(memory_space=pltpu.HBM)
 
 
 def params():
@@ -30,11 +30,17 @@
     )
 
 
-def pack_kernel(scalars, templates, available, moveout, mine, theirs, square, sems):
+def pack_kernel(scalars, templates, available, moveout, mine, theirs, usable, shifts, square, sems, fetched):
     blocks, channels, events, tlen = templates.shape
     chips, _, group, _ = mine.shape
     half = channels // 2
     me = scalars[2]
+    flag_copies = [
+        pltpu.make_async_copy(available, usable, fetched.at[0]),
+        pltpu.make_async_copy(moveout, shifts, fetched.at[1]),
+    ]
+    for copy in flag_copies:
+        copy.start()
     copies = []
     for chip in range(chips):
         which, part = divmod(chip * group, events)
@@ -47,7 +53,9 @@
             )
             copy.start()
             copies.append(copy)
-    flags = jnp.where(available[...] > 0, moveout[...] + 1, 0).astype(jnp.float32)
+    for copy in flag_copies:
+        copy.wait()
+    flags = jnp.where(usable[...] > 0, shifts[...] + 1, 0).astype(jnp.float32)
     for which in range(2):
         code = flags[:, 0, :]
         for block in range(1, blocks):
@@ -73,11 +81,14 @@
     return pl.pallas_call(
         pack_kernel,
         out_shape=[jax.ShapeDtypeStruct(shape, jnp.bfloat16)] * 2,
-        in_specs=[SMEM, ANY, VMEM, VMEM],
+        in_specs=[SMEM, HBM, HBM, HBM],
         out_specs=[VMEM] * 2,
         scratch_shapes=[
+            pltpu.VMEM(available.shape, jnp.int32),
+            pltpu.VMEM(moveout.shape, jnp.int32),
             pltpu.VMEM((LANES, LANES), jnp.float32),
             pltpu.SemaphoreType.DMA((chips, 2)),
+            pltpu.SemaphoreType.DMA((2,)),
         ],
         compiler_params=params(),
         cost_estimate=cost(1.5),
@@ -85,32 +96,30 @@
     )(scalars, templates, available, moveout)
 
 
-def merge_kernel(chips, scalars, mine, other, *rest):
-    outs, sems = rest[:-1], rest[-1]
-    chip, core = scalars[0], scalars[1]
-    for step in range(chips):
-        dest = jnp.bitwise_xor(chip, step)
-        owner = jnp.where(dest < chips // 2, scalars[2], scalars[3])
+def merge_kernel(chips, scalars, mine, other, out, sems):
+    core = scalars[0]
+    for chip in range(chips):
+        owner = scalars[1] if chip < chips // 2 else scalars[2]
         here = owner % 2 == core
 
         @pl.when(here)
         def _():
-            pltpu.make_async_copy(mine.at[dest], outs[step], sems.at[step]).start()
+            pltpu.make_async_copy(mine.at[chip], out.at[chip], sems.at[chip]).start()
 
         @pl.when(jnp.logical_not(here))
         def _():
-            pltpu.make_async_copy(other.at[dest], outs[step], sems.at[step]).start()
-
-    for step in range(chips):
-        pltpu.make_async_copy(mine.at[0], outs[step], sems.at[step]).wait()
+            pltpu.make_async_copy(other.at[chip], out.at[chip], sems.at[chip]).start()
+
+    for chip in range(chips):
+        pltpu.make_async_copy(mine.at[chip], out.at[chip], sems.at[chip]).wait()
 
 
 def merge(chips, scalars, mine, other):
     return pl.pallas_call(
         functools.partial(merge_kernel, chips),
-        out_shape=[jax.ShapeDtypeStruct(mine.shape[1:], mine.dtype)] * chips,
+        out_shape=jax.ShapeDtypeStruct(mine.shape, mine.dtype),
         in_specs=[SMEM, ANY, ANY],
-        out_specs=[ANY] * chips,
+        out_specs=ANY,
         scratch_shapes=[pltpu.SemaphoreType.DMA((chips,))],
         compiler_params=params(),
         cost_estimate=cost(1),
@@ -136,14 +145,22 @@
     return pltpu.roll(copies, row.shape[1] - 7 - ahead, 1, stride=1, stride_axis=0)
 
 
-def waves_kernel(channels, samples, tlen, *rest):
+def waves_kernel(channels, samples, tlen, scalars, rims, *rest):
     waves = rest[:-4]
     left_a, left_r, padded, inverse = rest[-4:]
-    span = waves[0].shape[1]
+    chips = len(waves)
+    span = padded.shape[1] // chips
     steps = samples // STRIDE
+    chip, core = scalars[0], scalars[1]
     padded[...] = jnp.zeros_like(padded)
     for index, wave in enumerate(waves):
-        padded[0:channels, span * index : span * (index + 1)] = wave[...].astype(jnp.float32)
+        start = span * index
+        padded[0:channels, start : start + samples] = wave[...].astype(jnp.float32)
+        following = jnp.bitwise_xor(chip, index) + core
+        inside = following < chips
+        rim = rims[jnp.bitwise_xor(chip, jnp.where(inside, following, chips - 1))]
+        rim = jnp.where(inside, rim.astype(jnp.float32), 0.0)
+        padded[0:channels, start + samples : start + span] = rim
 
     @pl.loop(0, 4)
     def _(part):
@@ -161,7 +178,7 @@
         even, odd = lagged(row, 0), lagged(row, STRIDE)
         even_scale, odd_scale = lagged(scale, 0), lagged(scale, STRIDE)
         columns = ([], [], [])
-        for index in range(len(waves)):
+        for index in range(chips):
             for step in range(steps):
                 start = span * index + STRIDE * (step - step % 2)
                 values = odd if step % 2 else even
@@ -177,14 +194,15 @@
         left_r[channel, :, LANES:] = (value - high.astype(jnp.float32)).astype(jnp.bfloat16)
 
 
-def prepare_waves(samples, tlen, waves):
-    channels, span = waves[0].shape
+def prepare_waves(tlen, scalars, rims, waves):
+    channels, samples = waves[0].shape
+    span = samples + rims.shape[2]
     rows = len(waves) * samples // OFFSETS
     out = jax.ShapeDtypeStruct((channels, rows, DEPTH), jnp.bfloat16)
     return pl.pallas_call(
         functools.partial(waves_kernel, channels, samples, tlen),
         out_shape=[out, out],
-        in_specs=[VMEM] * len(waves),
+        in_specs=[SMEM, VMEM] + [VMEM] * len(waves),
         out_specs=[VMEM, VMEM],
         scratch_shapes=[
             pltpu.VMEM((32, span * len(waves)), jnp.float32),
@@ -193,12 +211,11 @@
         compiler_params=params(),
         cost_estimate=cost(5),
         name="prepare_waves",
-    )(*waves)
-
-
-def main_kernel(channels, tlen, group, scalars, first, second, left_a, left_r, *rest):
-    outs = rest[:-4]
-    bank, weight_a, weight_r, total = rest[-4:]
+    )(scalars, rims, *waves)
+
+
+def main_kernel(channels, tlen, group, scalars, first, second, left_a, left_r, out, *scratch):
+    bank, expand, weight_a, weight_r, total = scratch
     half = channels // 2
     slots = LANES // group
     banks = (half + 1) // slots
@@ -206,10 +223,15 @@
     tile_count = OFFSETS // offset_count
     code_lane = (half % slots) * group
     top = 112 + 8 * (7 + offset_count - 1)
+    top = top + top % 16
 
     lag = lax.broadcasted_iota(jnp.int32, (LANES, LANES), 0)
+    target = lax.broadcasted_iota(jnp.int32, (LANES, LANES), 1)
     lane = lax.broadcasted_iota(jnp.int32, (1, LANES), 1)
     used = lag < tlen
+    for slot in range(slots):
+        chosen = jnp.where(lag == target % group + slot * group, 1.0, 0.0)
+        expand[:, slot * LANES : (slot + 1) * LANES] = chosen.astype(jnp.bfloat16)
     for side, piece in enumerate((first, second)):
         turned = []
         for index in range(banks):
@@ -238,21 +260,18 @@
             unit = jnp.where(lag == 112, code, unit)
             bank[side * banks + index] = unit.astype(jnp.bfloat16)
 
-    source_lane = lax.broadcasted_iota(jnp.int32, (LANES, LANES), 0)
-    target_lane = lax.broadcasted_iota(jnp.int32, (LANES, LANES), 1)
     ahead = lane // group
-    for side in range(2):
+
+    def channel_of(number, slot):
+        side = number // banks
+        item = (number % banks) * slots + slot
         base = half * jnp.where(scalars[1] == side, 0, 1)
-
-        @pl.loop(0, half)
-        def _(item):
-            slot = item % slots
-            expand = (source_lane == target_lane % group + slot * group).astype(jnp.float32)
-            spreaded = jnp.dot(
-                bank[side * banks + item // slots],
-                expand.astype(jnp.bfloat16),
-                preferred_element_type=jnp.float32,
-            )
+        return jnp.where(item < half, base + item, channels + side)
+
+    def build(number):
+        wide = jnp.dot(bank[number], expand[...], preferred_element_type=jnp.float32)
+        for slot in range(slots):
+            spreaded = wide[:, slot * LANES : (slot + 1) * LANES]
             code = spreaded[112:113, :].astype(jnp.int32)
             usable = code > 0
             shift = code - 1
@@ -265,33 +284,47 @@
                     jnp.concatenate([gap, taps], axis=0),
                     jnp.concatenate([taps, gap], axis=0),
                 )[0:top]
-            channel = base + item
-            reach = shift + 8 * ahead
+            taps = taps.astype(jnp.bfloat16)
+            channel = channel_of(number, slot)
+            pick = jnp.logical_and(lag == shift + 8 * ahead, usable)
+            pick = jnp.where(pick, 1.0, 0.0).astype(jnp.bfloat16)
             for index in range(tile_count):
                 skip = 8 * offset_count * index
-                column = [taps, jnp.zeros((DEPTH - top - skip, LANES), jnp.float32)]
+                lanes = slice(LANES * index, LANES * (index + 1))
                 if skip:
-                    column = [jnp.zeros((skip, LANES), jnp.float32)] + column
-                lanes = slice(LANES * index, LANES * (index + 1))
-                weight_a[channel, :, lanes] = jnp.concatenate(column, axis=0).astype(jnp.bfloat16)
-                pick = jnp.logical_and(source_lane == reach + skip, usable)
-                pick = jnp.where(pick, 1.0, 0.0).astype(jnp.bfloat16)
+                    weight_a[channel, 0:skip, lanes] = jnp.zeros((skip, LANES), jnp.bfloat16)
+                    pick = jnp.concatenate(
+                        [jnp.zeros((skip, LANES), jnp.bfloat16), pick[0 : LANES - skip]], axis=0
+                    )
+                weight_a[channel, skip : skip + top, lanes] = taps
+                rest = DEPTH - top - skip
+                if rest:
+                    weight_a[channel, skip + top :, lanes] = jnp.zeros((rest, LANES), jnp.bfloat16)
                 weight_r[channel, 0:LANES, lanes] = pick
                 weight_r[channel, LANES : 2 * LANES, lanes] = pick
 
+    def apply(number):
+        for slot in range(slots):
+            channel = channel_of(number, slot)
+            samples = jnp.minimum(channel, channels - 1)
+            corr = jnp.dot(left_a[samples], weight_a[channel], preferred_element_type=jnp.float32)
+            factor = jnp.dot(left_r[samples], weight_r[channel], preferred_element_type=jnp.float32)
+            total[...] += corr * factor
+
     total[...] = jnp.zeros_like(total)
-
-    @pl.loop(0, channels // 2)
-    def _(pair):
-        for channel in (2 * pair, 2 * pair + 1):
-            corr = jnp.dot(left_a[channel], weight_a[channel], preferred_element_type=jnp.float32)
-            factor = jnp.dot(left_r[channel], weight_r[channel], preferred_element_type=jnp.float32)
-            total[...] += corr * factor
-
-    rows_out = outs[0].shape[0]
-    for step, out in enumerate(outs):
-        segment = jnp.bitwise_xor(scalars[0], step)
-        out[...] = total[pl.ds(pl.multiple_of(segment * rows_out, rows_out), rows_out), :].astype(
+    build(0)
+
+    @pl.loop(1, 2 * banks)
+    def _(number):
+        apply(number - 1)
+        build(number)
+
+    apply(2 * banks - 1)
+
+    rows_out = out.shape[1]
+    for chip in range(out.shape[0]):
+        segment = jnp.bitwise_xor(scalars[0], chip)
+        out[chip] = total[pl.ds(pl.multiple_of(segment * rows_out, rows_out), rows_out), :].astype(
             jnp.bfloat16
         )
 
@@ -300,17 +333,17 @@
     rows = left_a.shape[1]
     width = OFFSETS * group
     rows_out = samples // OFFSETS
-    out = jax.ShapeDtypeStruct((rows_out, width), jnp.bfloat16)
     banks = 2 * (channels // 2 + 1) * group // LANES
     return pl.pallas_call(
         functools.partial(main_kernel, channels, tlen, group),
-        out_shape=[out] * (rows // rows_out),
+        out_shape=jax.ShapeDtypeStruct((rows // rows_out, rows_out, width), jnp.bfloat16),
         in_specs=[SMEM, VMEM, VMEM, VMEM, VMEM],
-        out_specs=[VMEM] * (rows // rows_out),
+        out_specs=VMEM,
         scratch_shapes=[
             pltpu.VMEM((banks, LANES, LANES), jnp.bfloat16),
-            pltpu.VMEM((channels, DEPTH, width), jnp.bfloat16),
-            pltpu.VMEM((channels, DEPTH, width), jnp.bfloat16),
+            pltpu.VMEM((LANES, LANES // group * LANES), jnp.bfloat16),
+            pltpu.VMEM((channels + 2, DEPTH, width), jnp.bfloat16),
+            pltpu.VMEM((channels + 2, DEPTH, width), jnp.bfloat16),
             pltpu.VMEM((rows, width), jnp.float32),
         ],
         compiler_params=params(),
@@ -319,13 +352,12 @@
     )(scalars, first, second, left_a, left_r)
 
 
-def finish_kernel(group, *rest):
-    parts, out = rest[:-1], rest[-1]
+def finish_kernel(group, parts, out):
     samples = out.shape[1]
-    rows = parts[0].shape[0]
-    value = parts[0][...].astype(jnp.float32)
-    for part in parts[1:]:
-        value = value + part[...].astype(jnp.float32)
+    count, rows, _ = parts.shape
+    value = parts[0].astype(jnp.float32)
+    for index in range(1, count):
+        value = value + parts[index].astype(jnp.float32)
     high = value.astype(jnp.bfloat16).astype(jnp.float32)
     both = jnp.concatenate([high, value - high], axis=0).T.astype(jnp.bfloat16)
     row = lax.broadcasted_iota(jnp.int32, (2 * rows, samples), 0) % rows
@@ -344,24 +376,21 @@
     return pl.pallas_call(
         functools.partial(finish_kernel, group),
         out_shape=jax.ShapeDtypeStruct((group, samples), jnp.float32),
-        in_specs=[VMEM] * len(parts),
+        in_specs=[VMEM],
         out_specs=VMEM,
         compiler_params=params(),
         cost_estimate=cost(1),
         name="finish",
-    )(*parts)
+    )(parts)
 
 
 def shards(waveforms, templates, available, moveout, bank_blocks):
     channels, samples = waveforms.shape
     blocks, events, _, tlen = templates.shape
     count_tm = lax.axis_size("tm")
-    count_sta = lax.axis_size("sta")
     chips = count_tm // 2
     group = 2 * events // chips
-    rim = MOVE + tlen - 1
     me = lax.axis_index("tm").astype(jnp.int32)
-    station = lax.axis_index("sta").astype(jnp.int32)
     chip, core = me // 2, me % 2
     swap = [(i, i ^ 1) for i in range(count_tm)]
 
@@ -371,13 +400,7 @@
     owners = bank_blocks // blocks
     slots = bank_blocks % blocks
 
-    next_rim = lax.ppermute(
-        waveforms[:, :rim], "tm", [(i, i - 1) for i in range(1, count_tm)]
-    )
-    tail = jnp.zeros((channels, 2 * LANES - rim), waveforms.dtype)
-    segment = jnp.concatenate([waveforms, next_rim, tail], axis=1)
-    segments = [segment] + [across(segment, step) for step in range(1, chips)]
-
+    segments = [waveforms] + [across(waveforms, step) for step in range(1, chips)]
     mine, theirs = pack(
         chips,
         group,
@@ -387,27 +410,22 @@
         jnp.transpose(moveout, (2, 0, 1)),
     )
     other = lax.ppermute(theirs, "tm", swap)
-    merged = merge(chips, jnp.stack([chip, core, owners[0], owners[1]]), mine, other)
-    pieces = [merged[0]] + [across(merged[step], step) for step in range(1, chips)]
-    left_a, left_r = prepare_waves(samples, tlen, segments)
-
-    source = (jnp.where(chip < chips // 2, owners[0], owners[1]) // 2) ^ chip
-    first = pieces[0]
-    for step in range(1, chips):
-        first = jnp.where(source == step, pieces[step], first)
+    rims = lax.ppermute(jnp.stack([s[:, : 2 * LANES] for s in segments]), "tm", swap)
+    other, rims, *segments = lax.optimization_barrier((other, rims, *segments))
+    merged = merge(chips, jnp.stack([core, owners[0], owners[1]]), mine, other)
+    lines = [[2 * z + c for z in range(chips)] for c in range(2)]
+    pieces = lax.all_to_all(merged, "tm", 0, 0, axis_index_groups=lines, tiled=True)
+    left_a, left_r = prepare_waves(tlen, jnp.stack([chip, core]), rims, segments)
+
+    source = jnp.where(chip < chips // 2, owners[0], owners[1]) // 2
+    first = lax.dynamic_index_in_dim(pieces, source, 0, keepdims=False)
     second = lax.ppermute(first, "tm", swap)
     parts = correlate(
-        channels, tlen, group, samples, jnp.stack([chip ^ station, core]), first, second, left_a, left_r
+        channels, tlen, group, samples, jnp.stack([chip, core]), first, second, left_a, left_r
     )
-    gathered = []
-    for step in range(chips):
-        route = [
-            (d * count_sta + s, (2 * (s ^ step) + d % 2) * count_sta + d // 2)
-            for d in range(count_tm)
-            for s in range(count_sta)
-        ]
-        gathered.append(lax.ppermute(parts[step], ("tm", "sta"), route))
-    return finish(group, samples, gathered)
+    parts = lax.all_to_all(parts, "tm", 0, 0, axis_index_groups=lines, tiled=True)
+    parts = lax.all_to_all(parts, "sta", 0, 0, tiled=True)
+    return finish(group, samples, parts)
 
 
 def solution(mesh):

time: 63 us -> 66.3 us (1.052)
  the two profiles are of different devices: /device:TPU:2 before, /device:TPU:0 now
where the time goes in v3:
time: 66.3 us; the launch traced here: 65.9 us
  blocking collectives  17.6 us (27%)
  Pallas kernels  17.2 us (26%)
  waiting for transfers between devices  15.3 us (23%)
  starting transfers between devices  10.3 us (16%)
  local copies, waits for them, and re-layouts  3.34 us (5%)
  between operations  1.42 us (2%)
  other arithmetic  0.83 us (1%)
    all_to_all x1, waiting for transfers between devices, shards(): lax.all_to_all(merged, 'tm', 0, 0, axis_index_groups=lines, tiled=True)  12.8 us
    all_to_all x1, blocking collectives, shards(): lax.all_to_all(parts, 'tm', 0, 0, axis_index_groups=lines, tiled=True)  9.04 us
    all_to_all x1, blocking collectives, shards(): parts = lax.all_to_all(parts, 'sta', 0, 0, tiled=True)  8.53 us
    pallas_call x1, Pallas kernels, prepare_waves(): pl.pallas_call(functools.partial(waves_kernel, channels, samples, tlen),...  7.27 us
    pallas_call x1, Pallas kernels, correlate(): pl.pallas_call(functools.partial(main_kernel, channels, tlen, group), out...  6.46 us
    ppermute x3, starting transfers between devices, across(): lax.ppermute(array, 'tm', [(i, i ^ 2 * step) for i in range(count_tm)])  5.62 us
    all_to_all x1, starting transfers between devices, shards(): lax.all_to_all(merged, 'tm', 0, 0, axis_index_groups=lines, tiled=True)  4.51 us
    unnamed x8, local copies, waits for them, and re-layouts  2.71 us
  transfers between devices with their start and end apart: 7, of which 3 were waited for; matrix products, arithmetic and copies ran while one was open for 2% of the time, Pallas kernels for 13%

profile of v3, /device:TPU:0, one launch (start us, length us, event | category | flops | bytes accessed | tf_op | source)
XLA Modules:
  0.0 65.9 jit_solution(11287111750418749313)
XLA Ops:
  0.0 0.0 copy-start
  0.0 4.0 %collective-permute-start.2 = (bf16[30,512]{1,0:T(8,128)(2,1)}, bf16[30,512]{1,0:T(8,128)(2,1)S(1)}, u32[]{:S(2)}, u32[]{:S(2)}) collective-permute-start(bf16[30,512]{1,0:T(8,128)(2,1)} %rest_0_), channel_id=1, source_target_pairs={{0,16},{4,20},{8,24},{12,28},{16,0},{20,4},{24,8},{28,12},{1,17},{... | collective-permute-start | bytes 92168 | tf_op jit(solution)/shard_map/ppermute | solution.py:398
  4.0 1.6 %collective-permute-start.1 = (bf16[30,512]{1,0:T(8,128)(2,1)}, bf16[30,512]{1,0:T(8,128)(2,1)S(1)}, u32[]{:S(2)}, u32[]{:S(2)}) collective-permute-start(bf16[30,512]{1,0:T(8,128)(2,1)} %rest_0_), channel_id=1, source_target_pairs={{0,8},{4,12},{8,0},{12,4},{16,24},{20,28},{24,16},{28,20},{1,9},{5... | collective-permute-start | bytes 92168 | tf_op jit(solution)/shard_map/ppermute | solution.py:398
  5.6 0.0 collective-permute-start.3
  5.6 0.7 %and_select_fusion = (s32[2]{0:T(128)S(1)}, s32[2]{0:T(128)S(1)}) fusion(s32[2]{0:T(128)} %param.9), kind=kLoop, calls=%fused_computation.6 | loop fusion | flops 38 | bytes 24 | tf_op jit(solution)/shard_map/jit(remainder)/select_n | solution.py:401
  6.3 0.1 pad_add_fusion.1
  6.4 0.0 copy-start.1
  6.4 1.2 %copy-done.1 = bf16[2,64,30,100]{3,1,2,0:T(8,128)(2,1)S(1)} copy-done((bf16[2,64,30,100]{3,1,2,0:T(8,128)(2,1)S(1)}, bf16[2,64,30,100]{3,1,2,0:T(8,128)(2,1)}, u32[]{:S(2)}) %copy-start.1) | copy-done | bytes 768024
  7.6 0.0 copy-start.2
  7.6 0.8 %copy-done.2 = s32[2,64,30]{1,0,2:T(2,128)S(1)} copy-done((s32[2,64,30]{1,0,2:T(2,128)S(1)}, s32[2,64,30]{1,0,2:T(2,128)}, u32[]{:S(2)}) %copy-start.2) | copy-done | bytes 15384
  8.3 0.0 copy-start.3
  8.3 0.8 %copy-done.3 = s32[2,64,30]{1,0,2:T(2,128)S(1)} copy-done((s32[2,64,30]{1,0,2:T(2,128)S(1)}, s32[2,64,30]{1,0,2:T(2,128)}, u32[]{:S(2)}) %copy-start.3) | copy-done | bytes 15384
  9.1 1.1 %pack.1 = (bf16[4,16,32,100]{3,2,1,0:T(8,128)(2,1)S(1)}, bf16[4,16,32,100]{3,2,1,0:T(8,128)(2,1)S(1)}) custom-call(s32[3]{0:T(128)S(1)} %get-tuple-element.30.scalars, bf16[2,30,64,100]{3,2,1,0:T(8,128)(2,1)S(1)} %bitcast.17, s32[30,2,64]{2,1,0:T(2,128)S(1)} %bitcast.18, s32[30,2,64]{2,1,0:T(2,128)S(1)} %bitcast.19), custom_call_target="tpu_custom_call" | custom-call | flops 1500000000 | bytes 1500000 | tf_op jit(solution)/shard_map/pack/pallas_call | solution.py:81
  10.2 0.1 collective-permute-start
  10.3 0.0 copy-done
  10.3 0.0 collective-permute-done.2.rest_2_
  10.3 0.0 collective-permute-done.1.rest_1_
  10.4 1.2 %collective-permute-done.3.rest_3_ = bf16[30,512]{1,0:T(8,128)(2,1)S(1)} collective-permute-done((bf16[30,512]{1,0:T(8,128)(2,1)}, bf16[30,512]{1,0:T(8,128)(2,1)S(1)}, u32[]{:S(2)}, u32[]{:S(2)}) %collective-permute-start.3) | collective-permute-done | bytes 30752 | tf_op jit(solution)/shard_map/ppermute | solution.py:398
  11.6 0.1 collective-permute-start.4
  11.6 1.2 %collective-permute-done.4.rims = bf16[4,30,256]{2,1,0:T(8,128)(2,1)S(1)} collective-permute-done((bf16[4,30,256]{2,1,0:T(8,128)(2,1)S(1)}, bf16[4,30,256]{2,1,0:T(8,128)(2,1)S(1)}, u32[]{:S(2)}, u32[]{:S(2)}) %collective-permute-start.4) | collective-permute-done | bytes 61472 | tf_op jit(solution)/shard_map/ppermute | solution.py:413
  12.9 0.0 collective-permute-done.other
  12.9 1.4 %merge.1 = bf16[4,16,32,100]{3,2,1,0:T(8,128)(2,1)} custom-call(s32[3]{0:T(128)S(1)} %get-tuple-element.29.scalars, bf16[4,16,32,100]{3,2,1,0:T(8,128)(2,1)S(1)} %get-tuple-element.15.mine, bf16[4,16,32,100]{3,2,1,0:T(8,128)(2,1)S(1)} %collective-permute-done.other), custom_call_target="tpu_custom_call" | custom-call | flops 1000000000 | bytes 1000000 | tf_op jit(solution)/shard_map/merge/pallas_call | solution.py:118
  14.3 4.5 %all-to-all-start = ((bf16[4,16,32,100]{3,2,1,0:T(8,128)(2,1)}), bf16[4,16,32,100]{3,2,1,0:T(8,128)(2,1)S(1)}, u32[]{:S(2)}, u32[]{:S(2)}) async-start(bf16[4,16,32,100]{3,2,1,0:T(8,128)(2,1)} %merge.1), calls=%async_computation | async-start | bytes 1048576 | tf_op jit(solution)/shard_map/all_to_all | solution.py:417
  18.8 0.6 fusion
  20.7 0.1 pad_add_fusion.scalars
  20.7 12.8 %all-to-all-done = bf16[4,16,32,100]{3,2,1,0:T(8,128)(2,1)S(1)} async-done(((bf16[4,16,32,100]{3,2,1,0:T(8,128)(2,1)}), bf16[4,16,32,100]{3,2,1,0:T(8,128)(2,1)S(1)}, u32[]{:S(2)}, u32[]{:S(2)}) %all-to-all-start) | async-done | bytes 409632 | tf_op jit(solution)/shard_map/all_to_all | solution.py:417
  33.6 0.1 collective-permute-start.5
  33.7 7.3 %prepare_waves.1 = (bf16[30,256,256]{2,1,0:T(8,128)(2,1)S(1)}, bf16[30,256,256]{2,1,0:T(8,128)(2,1)S(1)}) custom-call(s32[2]{0:T(128)S(1)} %pad_add_fusion.scalars, bf16[4,30,256]{2,1,0:T(8,128)(2,1)S(1)} %collective-permute-done.4.rims, bf16[30,512]{1,0:T(8,128)(2,1)S(1)} %copy-done, bf16[30,512]{1,0:T(8,128)(2,1)S(1)} %collective-permute-done.1.rest_1_, ...), custom_call_target="tpu_custom_call" | custom-call | flops 5000000000 | bytes 5000000 | tf_op jit(solution)/shard_map/prepare_waves/pallas_call | solution.py:202
  40.9 0.0 collective-permute-done.5.second
  40.9 6.5 %correlate.1 = bf16[4,64,256]{2,1,0:T(8,128)(2,1)S(1)} custom-call(s32[2]{0:T(128)S(1)} %pad_add_fusion.scalars, bf16[16,32,100]{2,1,0:T(8,128)(2,1)S(1)} %dynamic-slice_bitcast_fusion.first, bf16[16,32,100]{2,1,0:T(8,128)(2,1)S(1)} %collective-permute-done.5.second, bf16[30,256,256]{2,1,0:T(8,128)(2,1)S(1)} %get-tuple-element.23.left_a, ...), custom_call_target="tpu_custom_call" | custom-call | flops 8999999488 | bytes 9000000 | tf_op jit(solution)/shard_map/correlate/pallas_call | solution.py:337
  47.4 9.0 %all_to_all.15 = bf16[4,64,256]{2,1,0:T(8,128)(2,1)S(1)} all-to-all(bf16[4,64,256]{2,1,0:T(8,128)(2,1)S(1)} %correlate.1), channel_id=1, replica_groups={{0,8,16,24},{4,12,20,28},{1,9,17,25},{5,13,21,29},{2,10,18,26},{6,14,22..., dimensions={0} | all-to-all | bytes 262144 | tf_op jit(solution)/shard_map/all_to_all | solution.py:426
  56.5 8.5 %all_to_all.16.parts = bf16[4,64,256]{2,1,0:T(8,128)(2,1)S(1)} all-to-all(bf16[4,64,256]{2,1,0:T(8,128)(2,1)S(1)} %all_to_all.15), channel_id=1, replica_groups=mesh['tm'=8,'sta'=4] {'sta'}, dimensions={0} | all-to-all | bytes 262144 | tf_op jit(solution)/shard_map/all_to_all | solution.py:427
  65.0 0.9 %finish.1 = f32[32,512]{1,0:T(8,128)} custom-call(bf16[4,64,256]{2,1,0:T(8,128)(2,1)S(1)} %all_to_all.16.parts), custom_call_target="tpu_custom_call" | custom-call | flops 1000000000 | bytes 1000000 | tf_op jit(solution)/shard_map/finish/pallas_call | solution.py:376
  (6 shorter events, 0.0 us)
Async XLA Ops:
  0.0 10.3 %copy-start = (bf16[30,512]{1,0:T(8,128)(2,1)S(1)}, bf16[30,512]{1,0:T(8,128)(2,1)}, u32[]{:S(2)}) copy-start(bf16[30,512]{1,0:T(8,128)(2,1)} %rest_0_) | copy-start | bytes 92164
  0.0 10.3 %collective-permute-start.2 = (bf16[30,512]{1,0:T(8,128)(2,1)}, bf16[30,512]{1,0:T(8,128)(2,1)S(1)}, u32[]{:S(2)}, u32[]{:S(2)}) collective-permute-start(bf16[30,512]{1,0:T(8,128)(2,1)} %rest_0_), channel_id=1, source_target_pairs={{0,16},{4,20},{8,24},{12,28},{16,0},{20,4},{24,8},{28,12},{1,17},{... | collective-permute-start | bytes 92168 | tf_op jit(solution)/shard_map/ppermute | solution.py:398
  4.0 6.3 %collective-permute-start.1 = (bf16[30,512]{1,0:T(8,128)(2,1)}, bf16[30,512]{1,0:T(8,128)(2,1)S(1)}, u32[]{:S(2)}, u32[]{:S(2)}) collective-permute-start(bf16[30,512]{1,0:T(8,128)(2,1)} %rest_0_), channel_id=1, source_target_pairs={{0,8},{4,12},{8,0},{12,4},{16,24},{20,28},{24,16},{28,20},{1,9},{5... | collective-permute-start | bytes 92168 | tf_op jit(solution)/shard_map/ppermute | solution.py:398
  5.6 5.9 %collective-permute-start.3 = (bf16[30,512]{1,0:T(8,128)(2,1)}, bf16[30,512]{1,0:T(8,128)(2,1)S(1)}, u32[]{:S(2)}, u32[]{:S(2)}) collective-permute-start(bf16[30,512]{1,0:T(8,128)(2,1)} %rest_0_), channel_id=1, source_target_pairs={{0,24},{4,28},{8,16},{12,20},{16,8},{20,12},{24,0},{28,4},{1,25},{... | collective-permute-start | bytes 92168 | tf_op jit(solution)/shard_map/ppermute | solution.py:398
  6.4 1.2 %copy-start.1 = (bf16[2,64,30,100]{3,1,2,0:T(8,128)(2,1)S(1)}, bf16[2,64,30,100]{3,1,2,0:T(8,128)(2,1)}, u32[]{:S(2)}) copy-start(bf16[2,64,30,100]{3,1,2,0:T(8,128)(2,1)} %param.6) | copy-start | bytes 2304004
  7.6 0.8 %copy-start.2 = (s32[2,64,30]{1,0,2:T(2,128)S(1)}, s32[2,64,30]{1,0,2:T(2,128)}, u32[]{:S(2)}) copy-start(s32[2,64,30]{1,0,2:T(2,128)} %param.7) | copy-start | bytes 46084
  8.3 0.8 %copy-start.3 = (s32[2,64,30]{1,0,2:T(2,128)S(1)}, s32[2,64,30]{1,0,2:T(2,128)}, u32[]{:S(2)}) copy-start(s32[2,64,30]{1,0,2:T(2,128)} %param.8) | copy-start | bytes 46084
  10.2 2.7 %collective-permute-start = (bf16[4,16,32,100]{3,2,1,0:T(8,128)(2,1)S(1)}, bf16[4,16,32,100]{3,2,1,0:T(8,128)(2,1)S(1)}, u32[]{:S(2)}, u32[]{:S(2)}) collective-permute-start(bf16[4,16,32,100]{3,2,1,0:T(8,128)(2,1)S(1)} %get-tuple-element.16), channel_id=1, source_target_pairs={{0,4},{4,0},{8,12},{12,8},{16,20},{20,16},{24,28},{28,24},{1,5},{5... | collective-permute-start | bytes 1228808 | tf_op jit(solution)/shard_map/ppermute | solution.py:412
  11.6 1.3 %collective-permute-start.4 = (bf16[4,30,256]{2,1,0:T(8,128)(2,1)S(1)}, bf16[4,30,256]{2,1,0:T(8,128)(2,1)S(1)}, u32[]{:S(2)}, u32[]{:S(2)}) collective-permute-start(bf16[4,30,256]{2,1,0:T(8,128)(2,1)S(1)} %pad_maximum_fusion), channel_id=1, source_target_pairs={{0,4},{4,0},{8,12},{12,8},{16,20},{20,16},{24,28},{28,24},{1,5},{5... | collective-permute-start | bytes 184328 | tf_op jit(solution)/shard_map/ppermute | solution.py:413
  14.3 19.3 %all-to-all-start = ((bf16[4,16,32,100]{3,2,1,0:T(8,128)(2,1)}), bf16[4,16,32,100]{3,2,1,0:T(8,128)(2,1)S(1)}, u32[]{:S(2)}, u32[]{:S(2)}) async-start(bf16[4,16,32,100]{3,2,1,0:T(8,128)(2,1)} %merge.1), calls=%async_computation | async-start | bytes 1048576 | tf_op jit(solution)/shard_map/all_to_all | solution.py:417
  33.6 7.4 %collective-permute-start.5 = (bf16[16,32,100]{2,1,0:T(8,128)(2,1)S(1)}, bf16[16,32,100]{2,1,0:T(8,128)(2,1)S(1)}, u32[]{:S(2)}, u32[]{:S(2)}) collective-permute-start(bf16[16,32,100]{2,1,0:T(8,128)(2,1)S(1)} %dynamic-slice_bitcast_fusion.first), channel_id=1, source_target_pairs={{0,4},{4,0},{8,12},{12,8},{16,20},{20,16},{24,28},{28,24},{1,5},{5... | collective-permute-start | bytes 307208 | tf_op jit(solution)/shard_map/ppermute | solution.py:422

commit v4 on v3

--- a/solution.py
+++ b/solution.py
@@ -17,7 +17,6 @@
 SMEM = pl.BlockSpec(memory_space=pltpu.SMEM)
 VMEM = pl.BlockSpec(memory_space=pltpu.VMEM)
 ANY = pl.BlockSpec(memory_space=pl.ANY)
-HBM = pl.BlockSpec(memory_space=pltpu.HBM)
 
 
 def params():
@@ -30,11 +29,12 @@
     )
 
 
-def pack_kernel(scalars, templates, available, moveout, mine, theirs, usable, shifts, square, sems, fetched):
+def pack_kernel(bank_blocks, templates, available, moveout, mine, theirs, usable, shifts, square, codes, sems, fetched):
     blocks, channels, events, tlen = templates.shape
     chips, _, group, _ = mine.shape
     half = channels // 2
-    me = scalars[2]
+    me = lax.axis_index("tm") % 2
+    slots = [bank_blocks[which] % blocks for which in range(2)]
     flag_copies = [
         pltpu.make_async_copy(available, usable, fetched.at[0]),
         pltpu.make_async_copy(moveout, shifts, fetched.at[1]),
@@ -44,10 +44,10 @@
     copies = []
     for chip in range(chips):
         which, part = divmod(chip * group, events)
-        for side, out in enumerate((mine, theirs)):
-            first = half * jnp.where(me == side, 0, 1)
+        for side, out in enumerate((theirs, mine)):
+            first = half * jnp.where(me == 1 - side, 0, 1)
             copy = pltpu.make_async_copy(
-                templates.at[scalars[which], pl.ds(first, half), pl.ds(part, group), :],
+                templates.at[slots[which], pl.ds(first, half), pl.ds(part, group), :],
                 out.at[chip, pl.ds(0, half)],
                 sems.at[chip, side],
             )
@@ -59,7 +59,7 @@
     for which in range(2):
         code = flags[:, 0, :]
         for block in range(1, blocks):
-            code = jnp.where(scalars[which] == block, flags[:, block, :], code)
+            code = jnp.where(slots[which] == block, flags[:, block, :], code)
         square[...] = jnp.zeros_like(square)
         square[0:channels, 0:events] = code
         turned = square[...].T
@@ -69,62 +69,67 @@
         for index in range(events // group):
             chip = which * (events // group) + index
             rows = slice(index * group, (index + 1) * group)
-            mine[chip, half] = here[rows]
-            theirs[chip, half] = there[rows]
+            codes[0, chip, 0] = there[rows]
+            codes[1, chip, 0] = here[rows]
+    for side, out in enumerate((theirs, mine)):
+        copy = pltpu.make_async_copy(
+            codes.at[side], out.at[pl.ds(0, chips), pl.ds(half, 1)], fetched.at[side]
+        )
+        copy.start()
+        copies.append(copy)
     for copy in copies:
         copy.wait()
 
 
-def pack(chips, group, scalars, templates, available, moveout):
+def pack(chips, group, bank_blocks, templates, available, moveout):
     channels, tlen = templates.shape[1], templates.shape[3]
     shape = (chips, channels // 2 + 1, group, tlen)
     return pl.pallas_call(
         pack_kernel,
         out_shape=[jax.ShapeDtypeStruct(shape, jnp.bfloat16)] * 2,
-        in_specs=[SMEM, HBM, HBM, HBM],
-        out_specs=[VMEM] * 2,
+        in_specs=[SMEM, ANY, ANY, ANY],
+        out_specs=[ANY] * 2,
         scratch_shapes=[
             pltpu.VMEM(available.shape, jnp.int32),
             pltpu.VMEM(moveout.shape, jnp.int32),
             pltpu.VMEM((LANES, LANES), jnp.float32),
+            pltpu.VMEM((2, chips, 1, group, tlen), jnp.bfloat16),
             pltpu.SemaphoreType.DMA((chips, 2)),
             pltpu.SemaphoreType.DMA((2,)),
         ],
-        compiler_params=params(),
         cost_estimate=cost(1.5),
         name="pack",
-    )(scalars, templates, available, moveout)
-
-
-def merge_kernel(chips, scalars, mine, other, out, sems):
-    core = scalars[0]
-    for chip in range(chips):
-        owner = scalars[1] if chip < chips // 2 else scalars[2]
-        here = owner % 2 == core
+    )(bank_blocks, templates, available, moveout)
+
+
+def merge_kernel(blocks, bank_blocks, mine, other, *outs):
+    chips = len(outs)
+    me = lax.axis_index("tm")
+    for step, out in enumerate(outs):
+        dest = jnp.bitwise_xor(me // 2, step)
+        owner = jnp.where(dest < chips // 2, bank_blocks[0], bank_blocks[1]) // blocks
+        here = owner % 2 == me % 2
 
         @pl.when(here)
         def _():
-            pltpu.make_async_copy(mine.at[chip], out.at[chip], sems.at[chip]).start()
+            out[...] = mine[dest]
 
         @pl.when(jnp.logical_not(here))
         def _():
-            pltpu.make_async_copy(other.at[chip], out.at[chip], sems.at[chip]).start()
-
-    for chip in range(chips):
-        pltpu.make_async_copy(mine.at[chip], out.at[chip], sems.at[chip]).wait()
-
-
-def merge(chips, scalars, mine, other):
-    return pl.pallas_call(
-        functools.partial(merge_kernel, chips),
-        out_shape=jax.ShapeDtypeStruct(mine.shape, mine.dtype),
-        in_specs=[SMEM, ANY, ANY],
-        out_specs=ANY,
-        scratch_shapes=[pltpu.SemaphoreType.DMA((chips,))],
+            out[...] = other[dest]
+
+
+def merge(blocks, bank_blocks, mine, other):
+    chips = mine.shape[0]
+    return pl.pallas_call(
+        functools.partial(merge_kernel, blocks),
+        out_shape=[jax.ShapeDtypeStruct(mine.shape[1:], mine.dtype)] * chips,
+        in_specs=[SMEM, VMEM, VMEM],
+        out_specs=[VMEM] * chips,
         compiler_params=params(),
         cost_estimate=cost(1),
         name="merge",
-    )(scalars, mine, other)
+    )(bank_blocks, mine, other)
 
 
 def left(values, count):
@@ -145,22 +150,20 @@
     return pltpu.roll(copies, row.shape[1] - 7 - ahead, 1, stride=1, stride_axis=0)
 
 
-def waves_kernel(channels, samples, tlen, scalars, rims, *rest):
-    waves = rest[:-4]
-    left_a, left_r, padded, inverse = rest[-4:]
-    chips = len(waves)
-    span = padded.shape[1] // chips
-    steps = samples // STRIDE
-    chip, core = scalars[0], scalars[1]
+def waves_kernel(channels, tlen, swapped, local, left_a, left_r, padded, inverse):
+    chips, _, samples = local.shape
+    near = chips // 2
+    steps = 2 * near * samples // STRIDE
+    me = lax.axis_index("tm")
+    chip, core = me // 2, me % 2
     padded[...] = jnp.zeros_like(padded)
-    for index, wave in enumerate(waves):
-        start = span * index
-        padded[0:channels, start : start + samples] = wave[...].astype(jnp.float32)
-        following = jnp.bitwise_xor(chip, index) + core
-        inside = following < chips
-        rim = rims[jnp.bitwise_xor(chip, jnp.where(inside, following, chips - 1))]
-        rim = jnp.where(inside, rim.astype(jnp.float32), 0.0)
-        padded[0:channels, start + samples : start + span] = rim
+    for index in range(2 * near):
+        source = jnp.bitwise_xor(chip, near * core + index // 2)
+        wave = jnp.where(core == index % 2, local[source], swapped[index // 2])
+        padded[0:channels, samples * index : samples * (index + 1)] = wave.astype(jnp.float32)
+    rim = local[jnp.bitwise_xor(chip, near)][:, 0 : padded.shape[1] - 2 * near * samples]
+    rim = jnp.where(core == 0, rim.astype(jnp.float32), 0.0)
+    padded[0:channels, 2 * near * samples :] = rim
 
     @pl.loop(0, 4)
     def _(part):
@@ -178,14 +181,13 @@
         even, odd = lagged(row, 0), lagged(row, STRIDE)
         even_scale, odd_scale = lagged(scale, 0), lagged(scale, STRIDE)
         columns = ([], [], [])
-        for index in range(chips):
-            for step in range(steps):
-                start = span * index + STRIDE * (step - step % 2)
-                values = odd if step % 2 else even
-                columns[0].append(values[:, start : start + LANES])
-                columns[1].append(values[:, start + LANES : start + 2 * LANES])
-                values = odd_scale if step % 2 else even_scale
-                columns[2].append(values[:, start : start + LANES])
+        for step in range(steps):
+            start = STRIDE * (step - step % 2)
+            values = odd if step % 2 else even
+            columns[0].append(values[:, start : start + LANES])
+            columns[1].append(values[:, start + LANES : start + 2 * LANES])
+            values = odd_scale if step % 2 else even_scale
+            columns[2].append(values[:, start : start + LANES])
         left_a[channel, :, 0:LANES] = jnp.concatenate(columns[0], axis=0).astype(jnp.bfloat16)
         left_a[channel, :, LANES:] = jnp.concatenate(columns[1], axis=0).astype(jnp.bfloat16)
         value = jnp.concatenate(columns[2], axis=0)
@@ -194,28 +196,29 @@
         left_r[channel, :, LANES:] = (value - high.astype(jnp.float32)).astype(jnp.bfloat16)
 
 
-def prepare_waves(tlen, scalars, rims, waves):
-    channels, samples = waves[0].shape
-    span = samples + rims.shape[2]
-    rows = len(waves) * samples // OFFSETS
-    out = jax.ShapeDtypeStruct((channels, rows, DEPTH), jnp.bfloat16)
-    return pl.pallas_call(
-        functools.partial(waves_kernel, channels, samples, tlen),
+def prepare_waves(tlen, swapped, local):
+    chips, channels, samples = local.shape
+    length = chips * samples
+    out = jax.ShapeDtypeStruct((channels, length // OFFSETS, DEPTH), jnp.bfloat16)
+    return pl.pallas_call(
+        functools.partial(waves_kernel, channels, tlen),
         out_shape=[out, out],
-        in_specs=[SMEM, VMEM] + [VMEM] * len(waves),
+        in_specs=[VMEM, VMEM],
         out_specs=[VMEM, VMEM],
         scratch_shapes=[
-            pltpu.VMEM((32, span * len(waves)), jnp.float32),
-            pltpu.VMEM((32, span * len(waves)), jnp.float32),
+            pltpu.VMEM((32, length + 2 * LANES), jnp.float32),
+            pltpu.VMEM((32, length + 2 * LANES), jnp.float32),
         ],
         compiler_params=params(),
-        cost_estimate=cost(5),
+        cost_estimate=cost(7),
         name="prepare_waves",
-    )(scalars, rims, *waves)
-
-
-def main_kernel(channels, tlen, group, scalars, first, second, left_a, left_r, out, *scratch):
-    bank, expand, weight_a, weight_r, total = scratch
+    )(swapped, local)
+
+
+def main_kernel(channels, tlen, group, first, second, left_a, left_r, *rest):
+    outs = rest[:-5]
+    bank, expand, weight_a, weight_r, total = rest[-5:]
+    core = lax.axis_index("tm") % 2
     half = channels // 2
     slots = LANES // group
     banks = (half + 1) // slots
@@ -265,7 +268,7 @@
     def channel_of(number, slot):
         side = number // banks
         item = (number % banks) * slots + slot
-        base = half * jnp.where(scalars[1] == side, 0, 1)
+        base = half * jnp.where(core == side, 0, 1)
         return jnp.where(item < half, base + item, channels + side)
 
     def build(number):
@@ -321,24 +324,24 @@
 
     apply(2 * banks - 1)
 
-    rows_out = out.shape[1]
-    for chip in range(out.shape[0]):
-        segment = jnp.bitwise_xor(scalars[0], chip)
-        out[chip] = total[pl.ds(pl.multiple_of(segment * rows_out, rows_out), rows_out), :].astype(
+    rows_out = outs[0].shape[0]
+    station = lax.axis_index("sta") % len(outs)
+    for step, out in enumerate(outs):
+        part = jnp.bitwise_xor(station, step)
+        out[...] = total[pl.ds(pl.multiple_of(part * rows_out, rows_out), rows_out), :].astype(
             jnp.bfloat16
         )
 
 
-def correlate(channels, tlen, group, samples, scalars, first, second, left_a, left_r):
+def correlate(channels, tlen, group, count, first, second, left_a, left_r):
     rows = left_a.shape[1]
     width = OFFSETS * group
-    rows_out = samples // OFFSETS
     banks = 2 * (channels // 2 + 1) * group // LANES
     return pl.pallas_call(
         functools.partial(main_kernel, channels, tlen, group),
-        out_shape=jax.ShapeDtypeStruct((rows // rows_out, rows_out, width), jnp.bfloat16),
-        in_specs=[SMEM, VMEM, VMEM, VMEM, VMEM],
-        out_specs=VMEM,
+        out_shape=[jax.ShapeDtypeStruct((rows // count, width), jnp.bfloat16)] * count,
+        in_specs=[VMEM, VMEM, VMEM, VMEM],
+        out_specs=[VMEM] * count,
         scratch_shapes=[
             pltpu.VMEM((banks, LANES, LANES), jnp.bfloat16),
             pltpu.VMEM((LANES, LANES // group * LANES), jnp.bfloat16),
@@ -347,17 +350,41 @@
             pltpu.VMEM((rows, width), jnp.float32),
         ],
         compiler_params=params(),
-        cost_estimate=cost(9),
+        cost_estimate=cost(6),
         name="correlate",
-    )(scalars, first, second, left_a, left_r)
-
-
-def finish_kernel(group, parts, out):
+    )(first, second, left_a, left_r)
+
+
+def add_kernel(*refs):
+    parts, keep, send = refs[:-2], refs[-2], refs[-1]
+    rows = keep.shape[0]
+    core = lax.axis_index("tm") % 2
+    for out, which in ((keep, core), (send, 1 - core)):
+        place = pl.ds(pl.multiple_of(which * rows, rows), rows)
+        value = parts[0][place, :].astype(jnp.float32)
+        for part in parts[1:]:
+            value = value + part[place, :].astype(jnp.float32)
+        out[...] = value
+
+
+def add(parts):
+    rows, width = parts[0].shape
+    out = jax.ShapeDtypeStruct((rows // 2, width), jnp.float32)
+    return pl.pallas_call(
+        add_kernel,
+        out_shape=[out, out],
+        in_specs=[VMEM] * len(parts),
+        out_specs=[VMEM, VMEM],
+        compiler_params=params(),
+        cost_estimate=cost(0.5),
+        name="add",
+    )(*parts)
+
+
+def finish_kernel(group, ours, received, out):
     samples = out.shape[1]
-    count, rows, _ = parts.shape
-    value = parts[0].astype(jnp.float32)
-    for index in range(1, count):
-        value = value + parts[index].astype(jnp.float32)
+    rows = ours.shape[0]
+    value = ours[...] + received[...]
     high = value.astype(jnp.bfloat16).astype(jnp.float32)
     both = jnp.concatenate([high, value - high], axis=0).T.astype(jnp.bfloat16)
     row = lax.broadcasted_iota(jnp.int32, (2 * rows, samples), 0) % rows
@@ -372,60 +399,75 @@
     out[...] = result
 
 
-def finish(group, samples, parts):
+def finish(group, samples, ours, received):
     return pl.pallas_call(
         functools.partial(finish_kernel, group),
         out_shape=jax.ShapeDtypeStruct((group, samples), jnp.float32),
-        in_specs=[VMEM],
+        in_specs=[VMEM, VMEM],
         out_specs=VMEM,
         compiler_params=params(),
         cost_estimate=cost(1),
         name="finish",
-    )(parts)
+    )(ours, received)
 
 
 def shards(waveforms, templates, available, moveout, bank_blocks):
     channels, samples = waveforms.shape
     blocks, events, _, tlen = templates.shape
     count_tm = lax.axis_size("tm")
+    count_sta = lax.axis_size("sta")
     chips = count_tm // 2
+    near = chips // 2
     group = 2 * events // chips
     me = lax.axis_index("tm").astype(jnp.int32)
     chip, core = me // 2, me % 2
-    swap = [(i, i ^ 1) for i in range(count_tm)]
+
+    def swap(array):
+        return lax.ppermute(array, "tm", [(i, i ^ 1) for i in range(count_tm)])
 
     def across(array, step):
         return lax.ppermute(array, "tm", [(i, i ^ (2 * step)) for i in range(count_tm)])
 
-    owners = bank_blocks // blocks
-    slots = bank_blocks % blocks
-
-    segments = [waveforms] + [across(waveforms, step) for step in range(1, chips)]
     mine, theirs = pack(
         chips,
         group,
-        jnp.stack([slots[0], slots[1], core]),
+        bank_blocks,
         jnp.transpose(templates, (0, 2, 1, 3)),
         jnp.transpose(available, (2, 0, 1)),
         jnp.transpose(moveout, (2, 0, 1)),
     )
-    other = lax.ppermute(theirs, "tm", swap)
-    rims = lax.ppermute(jnp.stack([s[:, : 2 * LANES] for s in segments]), "tm", swap)
-    other, rims, *segments = lax.optimization_barrier((other, rims, *segments))
-    merged = merge(chips, jnp.stack([core, owners[0], owners[1]]), mine, other)
-    lines = [[2 * z + c for z in range(chips)] for c in range(2)]
-    pieces = lax.all_to_all(merged, "tm", 0, 0, axis_index_groups=lines, tiled=True)
-    left_a, left_r = prepare_waves(tlen, jnp.stack([chip, core]), rims, segments)
-
-    source = jnp.where(chip < chips // 2, owners[0], owners[1]) // 2
-    first = lax.dynamic_index_in_dim(pieces, source, 0, keepdims=False)
-    second = lax.ppermute(first, "tm", swap)
-    parts = correlate(
-        channels, tlen, group, samples, jnp.stack([chip, core]), first, second, left_a, left_r
-    )
-    parts = lax.all_to_all(parts, "tm", 0, 0, axis_index_groups=lines, tiled=True)
-    parts = lax.all_to_all(parts, "sta", 0, 0, tiled=True)
-    return finish(group, samples, parts)
+    other = swap(theirs)
+    waveforms, mine = lax.optimization_barrier((waveforms, mine))
+    local = jnp.stack([waveforms] + [across(waveforms, step) for step in range(1, chips)])
+    other, local = lax.optimization_barrier((other, local))
+    merged = merge(blocks, bank_blocks, mine, other)
+    pieces = [merged[0]] + [across(merged[step], step) for step in range(1, chips)]
+
+    wanted = [
+        lax.dynamic_index_in_dim(local, chip ^ (near * (1 - core) + step), 0, keepdims=False)
+        for step in range(near)
+    ]
+    swapped = swap(jnp.stack(wanted))
+    left_a, left_r = prepare_waves(tlen, swapped, local)
+
+    left_a, left_r, *pieces = lax.optimization_barrier((left_a, left_r, *pieces))
+    owner = jnp.where(chip < near, bank_blocks[0], bank_blocks[1]) // blocks
+    source = (owner // 2) ^ chip
+    first = pieces[0]
+    for step in range(1, chips):
+        first = jnp.where(source == step, pieces[step], first)
+    second = swap(first)
+    parts = correlate(channels, tlen, group, near, first, second, left_a, left_r)
+    gathered = []
+    for step in range(near):
+        route = []
+        for d in range(count_tm):
+            for s in range(count_sta):
+                dest = near * (d % 2) + (s % near ^ step)
+                route.append((d * count_sta + s, (2 * dest + s // near) * count_sta + d // 2))
+        gathered.append(lax.ppermute(parts[step], ("tm", "sta"), route))
+    ours, send = add(gathered)
+    return finish(group, samples, ours, swap(send))
 
 
 def solution(mesh):

time: 66.3 us -> 77.7 us (1.17)
  the two profiles are of different devices: /device:TPU:0 before, /device:TPU:7 now
where the time goes in v4:
time: 77.7 us; the launch traced here: 77 us
  Pallas kernels  45.6 us (59%)
  starting transfers between devices  19.6 us (25%)
  waiting for transfers between devices  8.81 us (11%)
  local copies, waits for them, and re-layouts  1.65 us (2%)
  between operations  1.36 us (2%)
    pallas_call x1, Pallas kernels, pack(): pl.pallas_call(pack_kernel, out_shape=[jax.ShapeDtypeStruct(shape, jnp.bf...  31.8 us
    ppermute x2, starting transfers between devices, shards(): gathered.append(lax.ppermute(parts[step], ('tm', 'sta'), route))  7.37 us
    ppermute x6, starting transfers between devices, across(): lax.ppermute(array, 'tm', [(i, i ^ 2 * step) for i in range(count_tm)])  7.22 us
    pallas_call x1, Pallas kernels, prepare_waves(): pl.pallas_call(functools.partial(waves_kernel, channels, tlen), out_shape...  6.19 us
    pallas_call x1, Pallas kernels, correlate(): pl.pallas_call(functools.partial(main_kernel, channels, tlen, group), out...  5.95 us
    ppermute x4, starting transfers between devices, swap(): return lax.ppermute(array, 'tm', [(i, i ^ 1) for i in range(count_tm)])  5.01 us
    ppermute x6, waiting for transfers between devices, across(): lax.ppermute(array, 'tm', [(i, i ^ 2 * step) for i in range(count_tm)])  4.28 us
    ppermute x2, waiting for transfers between devices, shards(): gathered.append(lax.ppermute(parts[step], ('tm', 'sta'), route))  2.64 us
  transfers between devices with their start and end apart: 12, of which 6 were waited for; matrix products, arithmetic and copies ran while one was open for 1% of the time, Pallas kernels for 9%

profile of v4, /device:TPU:7, one launch (start us, length us, event | category | flops | bytes accessed | tf_op | source)
XLA Modules:
  0.0 77.0 jit_solution(9141988528442913876)
XLA Ops:
  0.0 0.0 copy-start
  0.0 0.0 copy-start.2
  0.0 31.8 %pack.1 = (bf16[4,16,32,100]{3,2,1,0:T(8,128)(2,1)}, bf16[4,16,32,100]{3,2,1,0:T(8,128)(2,1)}) custom-call(s32[2]{0:T(128)} %bank_blocks.3, bf16[2,30,64,100]{3,2,1,0:T(8,128)(2,1)} %bitcast.13, s32[30,2,64]{2,1,0:T(2,128)} %bitcast.14, s32[30,2,64]{2,1,0:T(2,128)} %bitcast.15), custom_call_target="tpu_custom_call" | custom-call | flops 1500000000 | bytes 1500000 | tf_op jit(solution)/shard_map/pack/pallas_call | solution.py:87
  31.8 0.7 collective-permute-start
  32.5 0.0 copy-done.2
  32.5 3.3 %collective-permute-start.3 = (bf16[30,512]{1,0:T(8,128)(2,1)S(1)}, bf16[30,512]{1,0:T(8,128)(2,1)S(1)}, u32[]{:S(2)}, u32[]{:S(2)}) collective-permute-start(bf16[30,512]{1,0:T(8,128)(2,1)S(1)} %copy-done.2), channel_id=1, source_target_pairs={{0,24},{4,28},{8,16},{12,20},{16,8},{20,12},{24,0},{28,4},{1,25},{... | collective-permute-start | bytes 92168 | tf_op jit(solution)/shard_map/ppermute | solution.py:429
  35.9 0.0 collective-permute-start.2
  35.9 0.3 collective-permute-start.1
  36.2 0.0 copy-done
  36.2 0.6 fusion
  38.0 0.0 collective-permute-done.3
  38.0 1.8 %collective-permute-done.2 = bf16[30,512]{1,0:T(8,128)(2,1)S(1)} collective-permute-done((bf16[30,512]{1,0:T(8,128)(2,1)S(1)}, bf16[30,512]{1,0:T(8,128)(2,1)S(1)}, u32[]{:S(2)}, u32[]{:S(2)}) %collective-permute-start.2) | collective-permute-done | bytes 30752 | tf_op jit(solution)/shard_map/ppermute | solution.py:429
  39.8 0.0 collective-permute-done.1
  39.8 0.0 collective-permute-done.other
  39.9 1.3 %collective-permute-start.4 = (bf16[2,30,512]{2,1,0:T(8,128)(2,1)S(1)}, bf16[2,30,512]{2,1,0:T(8,128)(2,1)S(1)}, u32[]{:S(2)}, u32[]{:S(2)}) collective-permute-start(bf16[2,30,512]{2,1,0:T(8,128)(2,1)S(1)} %pad_maximum_fusion.1), channel_id=1, source_target_pairs={{0,4},{4,0},{8,12},{12,8},{16,20},{20,16},{24,28},{28,24},{1,5},{5... | collective-permute-start | bytes 184328 | tf_op jit(solution)/shard_map/ppermute | solution.py:426
  41.2 0.0 copy-start.1
  41.2 1.0 %copy-done.1 = bf16[4,16,32,100]{3,2,1,0:T(8,128)(2,1)S(1)} copy-done((bf16[4,16,32,100]{3,2,1,0:T(8,128)(2,1)S(1)}, bf16[4,16,32,100]{3,2,1,0:T(8,128)(2,1)}, u32[]{:S(2)}) %copy-start.1) | copy-done | bytes 409624
  42.2 0.7 merge.1
  43.0 0.1 collective-permute-start.5
  43.1 1.8 %collective-permute-start.6 = (bf16[16,32,100]{2,1,0:T(8,128)(2,1)S(1)}, bf16[16,32,100]{2,1,0:T(8,128)(2,1)S(1)}, u32[]{:S(2)}, u32[]{:S(2)}) collective-permute-start(bf16[16,32,100]{2,1,0:T(8,128)(2,1)S(1)} %get-tuple-element.37), channel_id=1, source_target_pairs={{0,16},{4,20},{8,24},{12,28},{16,0},{20,4},{24,8},{28,12},{1,17},{... | collective-permute-start | bytes 307208 | tf_op jit(solution)/shard_map/ppermute | solution.py:429
  44.9 1.7 %collective-permute-start.7 = (bf16[16,32,100]{2,1,0:T(8,128)(2,1)S(1)}, bf16[16,32,100]{2,1,0:T(8,128)(2,1)S(1)}, u32[]{:S(2)}, u32[]{:S(2)}) collective-permute-start(bf16[16,32,100]{2,1,0:T(8,128)(2,1)S(1)} %get-tuple-element.38), channel_id=1, source_target_pairs={{0,24},{4,28},{8,16},{12,20},{16,8},{20,12},{24,0},{28,4},{1,25},{... | collective-permute-start | bytes 307208 | tf_op jit(solution)/shard_map/ppermute | solution.py:429
  46.6 0.0 collective-permute-done.4.swapped
  46.6 6.2 %prepare_waves.1 = (bf16[30,256,256]{2,1,0:T(8,128)(2,1)S(1)}, bf16[30,256,256]{2,1,0:T(8,128)(2,1)S(1)}) custom-call(bf16[2,30,512]{2,1,0:T(8,128)(2,1)S(1)} %collective-permute-done.4.swapped, bf16[4,30,512]{2,1,0:T(8,128)(2,1)S(1)} %pad_maximum_fusion.local), custom_call_target="tpu_custom_call" | custom-call | flops 7000000000 | bytes 7000000 | tf_op jit(solution)/shard_map/prepare_waves/pallas_call | solution.py:203
  52.8 0.0 collective-permute-done.5
  52.8 0.0 collective-permute-done.6
  52.8 2.5 %collective-permute-done.7 = bf16[16,32,100]{2,1,0:T(8,128)(2,1)S(1)} collective-permute-done((bf16[16,32,100]{2,1,0:T(8,128)(2,1)S(1)}, bf16[16,32,100]{2,1,0:T(8,128)(2,1)S(1)}, u32[]{:S(2)}, u32[]{:S(2)}) %collective-permute-start.7) | collective-permute-done | bytes 102432 | tf_op jit(solution)/shard_map/ppermute | solution.py:429
  55.3 1.1 %collective-permute-start.8 = (bf16[16,32,100]{2,1,0:T(8,128)(2,1)S(1)}, bf16[16,32,100]{2,1,0:T(8,128)(2,1)S(1)}, u32[]{:S(2)}, u32[]{:S(2)}) collective-permute-start(bf16[16,32,100]{2,1,0:T(8,128)(2,1)S(1)} %select_select_fusion.first), channel_id=1, source_target_pairs={{0,4},{4,0},{8,12},{12,8},{16,20},{20,16},{24,28},{28,24},{1,5},{5... | collective-permute-start | bytes 307208 | tf_op jit(solution)/shard_map/ppermute | solution.py:426
  56.4 1.0 %collective-permute-done.8.second = bf16[16,32,100]{2,1,0:T(8,128)(2,1)S(1)} collective-permute-done((bf16[16,32,100]{2,1,0:T(8,128)(2,1)S(1)}, bf16[16,32,100]{2,1,0:T(8,128)(2,1)S(1)}, u32[]{:S(2)}, u32[]{:S(2)}) %collective-permute-start.8) | collective-permute-done | bytes 102432 | tf_op jit(solution)/shard_map/ppermute | solution.py:426
  57.4 5.9 %correlate.1 = (bf16[128,256]{1,0:T(8,128)(2,1)S(1)}, bf16[128,256]{1,0:T(8,128)(2,1)S(1)}) custom-call(bf16[16,32,100]{2,1,0:T(8,128)(2,1)S(1)} %select_select_fusion.first, bf16[16,32,100]{2,1,0:T(8,128)(2,1)S(1)} %collective-permute-done.8.second, bf16[30,256,256]{2,1,0:T(8,128)(2,1)S(1)} %get-tuple-element.43.left_a, ...), custom_call_target="tpu_custom_call" | custom-call | flops 6000000000 | bytes 6000000 | tf_op jit(solution)/shard_map/correlate/pallas_call | solution.py:340
  63.3 4.5 %collective-permute-start.9 = (bf16[128,256]{1,0:T(8,128)(2,1)S(1)}, bf16[128,256]{1,0:T(8,128)(2,1)S(1)}, u32[]{:S(2)}, u32[]{:S(2)}) collective-permute-start(bf16[128,256]{1,0:T(8,128)(2,1)S(1)} %get-tuple-element.45), channel_id=1, source_target_pairs={{0,0},{1,8},{2,4},{3,12},{4,16},{5,24},{6,20},{7,28},{8,1},{9,9},{... | collective-permute-start | bytes 196616 | tf_op jit(solution)/shard_map/ppermute | solution.py:468
  67.8 2.9 %collective-permute-start.10 = (bf16[128,256]{1,0:T(8,128)(2,1)S(1)}, bf16[128,256]{1,0:T(8,128)(2,1)S(1)}, u32[]{:S(2)}, u32[]{:S(2)}) collective-permute-start(bf16[128,256]{1,0:T(8,128)(2,1)S(1)} %get-tuple-element.46), channel_id=1, source_target_pairs={{0,8},{1,0},{2,12},{3,4},{4,24},{5,16},{6,28},{7,20},{8,9},{9,1},{... | collective-permute-start | bytes 196616 | tf_op jit(solution)/shard_map/ppermute | solution.py:468
  70.7 1.0 %collective-permute-done.9.refs_0_ = bf16[128,256]{1,0:T(8,128)(2,1)S(1)} collective-permute-done((bf16[128,256]{1,0:T(8,128)(2,1)S(1)}, bf16[128,256]{1,0:T(8,128)(2,1)S(1)}, u32[]{:S(2)}, u32[]{:S(2)}) %collective-permute-start.9) | collective-permute-done | bytes 65568 | tf_op jit(solution)/shard_map/ppermute | solution.py:468
  71.7 1.6 %collective-permute-done.10.refs_1_ = bf16[128,256]{1,0:T(8,128)(2,1)S(1)} collective-permute-done((bf16[128,256]{1,0:T(8,128)(2,1)S(1)}, bf16[128,256]{1,0:T(8,128)(2,1)S(1)}, u32[]{:S(2)}, u32[]{:S(2)}) %collective-permute-start.10) | collective-permute-done | bytes 65568 | tf_op jit(solution)/shard_map/ppermute | solution.py:468
  73.4 1.9 %collective-permute-start.11 = (f32[64,256]{1,0:T(8,128)S(1)}, f32[64,256]{1,0:T(8,128)S(1)}, u32[]{:S(2)}, u32[]{:S(2)}) collective-permute-start(f32[64,256]{1,0:T(8,128)S(1)} %get-tuple-element.48), channel_id=1, source_target_pairs={{0,4},{4,0},{8,12},{12,8},{16,20},{20,16},{24,28},{28,24},{1,5},{5... | collective-permute-start | bytes 196616 | tf_op jit(solution)/shard_map/ppermute | solution.py:426
  75.2 0.9 %collective-permute-done.11.received = f32[64,256]{1,0:T(8,128)S(1)} collective-permute-done((f32[64,256]{1,0:T(8,128)S(1)}, f32[64,256]{1,0:T(8,128)S(1)}, u32[]{:S(2)}, u32[]{:S(2)}) %collective-permute-start.11) | collective-permute-done | bytes 65568 | tf_op jit(solution)/shard_map/ppermute | solution.py:426
  76.1 0.9 %finish.1 = f32[32,512]{1,0:T(8,128)} custom-call(f32[64,256]{1,0:T(8,128)S(1)} %get-tuple-element.47.ours, f32[64,256]{1,0:T(8,128)S(1)} %collective-permute-done.11.received), custom_call_target="tpu_custom_call" | custom-call | flops 1000000000 | bytes 1000000 | tf_op jit(solution)/shard_map/finish/pallas_call | solution.py:403
  (5 shorter events, 0.1 us)
Async XLA Ops:
  0.0 36.2 %copy-start = (s32[2]{0:T(128)S(1)}, s32[2]{0:T(128)}, u32[]{:S(2)}) copy-start(s32[2]{0:T(128)} %bank_blocks.3) | copy-start | bytes 28
  0.0 32.5 %copy-start.2 = (bf16[30,512]{1,0:T(8,128)(2,1)S(1)}, bf16[30,512]{1,0:T(8,128)(2,1)}, u32[]{:S(2)}) copy-start(bf16[30,512]{1,0:T(8,128)(2,1)} %param.5) | copy-start | bytes 92164
  31.8 8.0 %collective-permute-start = (bf16[4,16,32,100]{3,2,1,0:T(8,128)(2,1)}, bf16[4,16,32,100]{3,2,1,0:T(8,128)(2,1)S(1)}, u32[]{:S(2)}, u32[]{:S(2)}) collective-permute-start(bf16[4,16,32,100]{3,2,1,0:T(8,128)(2,1)} %get-tuple-element.27), channel_id=1, source_target_pairs={{0,4},{4,0},{8,12},{12,8},{16,20},{20,16},{24,28},{28,24},{1,5},{5... | collective-permute-start | bytes 1228808 | tf_op jit(solution)/shard_map/ppermute | solution.py:426
  32.5 5.5 %collective-permute-start.3 = (bf16[30,512]{1,0:T(8,128)(2,1)S(1)}, bf16[30,512]{1,0:T(8,128)(2,1)S(1)}, u32[]{:S(2)}, u32[]{:S(2)}) collective-permute-start(bf16[30,512]{1,0:T(8,128)(2,1)S(1)} %copy-done.2), channel_id=1, source_target_pairs={{0,24},{4,28},{8,16},{12,20},{16,8},{20,12},{24,0},{28,4},{1,25},{... | collective-permute-start | bytes 92168 | tf_op jit(solution)/shard_map/ppermute | solution.py:429
  35.9 3.9 %collective-permute-start.2 = (bf16[30,512]{1,0:T(8,128)(2,1)S(1)}, bf16[30,512]{1,0:T(8,128)(2,1)S(1)}, u32[]{:S(2)}, u32[]{:S(2)}) collective-permute-start(bf16[30,512]{1,0:T(8,128)(2,1)S(1)} %copy-done.2), channel_id=1, source_target_pairs={{0,16},{4,20},{8,24},{12,28},{16,0},{20,4},{24,8},{28,12},{1,17},{... | collective-permute-start | bytes 92168 | tf_op jit(solution)/shard_map/ppermute | solution.py:429
  35.9 3.9 %collective-permute-start.1 = (bf16[30,512]{1,0:T(8,128)(2,1)S(1)}, bf16[30,512]{1,0:T(8,128)(2,1)S(1)}, u32[]{:S(2)}, u32[]{:S(2)}) collective-permute-start(bf16[30,512]{1,0:T(8,128)(2,1)S(1)} %copy-done.2), channel_id=1, source_target_pairs={{0,8},{4,12},{8,0},{12,4},{16,24},{20,28},{24,16},{28,20},{1,9},{5... | collective-permute-start | bytes 92168 | tf_op jit(solution)/shard_map/ppermute | solution.py:429
  39.9 6.7 %collective-permute-start.4 = (bf16[2,30,512]{2,1,0:T(8,128)(2,1)S(1)}, bf16[2,30,512]{2,1,0:T(8,128)(2,1)S(1)}, u32[]{:S(2)}, u32[]{:S(2)}) collective-permute-start(bf16[2,30,512]{2,1,0:T(8,128)(2,1)S(1)} %pad_maximum_fusion.1), channel_id=1, source_target_pairs={{0,4},{4,0},{8,12},{12,8},{16,20},{20,16},{24,28},{28,24},{1,5},{5... | collective-permute-start | bytes 184328 | tf_op jit(solution)/shard_map/ppermute | solution.py:426
  41.2 1.0 %copy-start.1 = (bf16[4,16,32,100]{3,2,1,0:T(8,128)(2,1)S(1)}, bf16[4,16,32,100]{3,2,1,0:T(8,128)(2,1)}, u32[]{:S(2)}) copy-start(bf16[4,16,32,100]{3,2,1,0:T(8,128)(2,1)} %get-tuple-element.33.mine) | copy-start | bytes 1228804
  43.0 9.8 %collective-permute-start.5 = (bf16[16,32,100]{2,1,0:T(8,128)(2,1)S(1)}, bf16[16,32,100]{2,1,0:T(8,128)(2,1)S(1)}, u32[]{:S(2)}, u32[]{:S(2)}) collective-permute-start(bf16[16,32,100]{2,1,0:T(8,128)(2,1)S(1)} %get-tuple-element.36), channel_id=1, source_target_pairs={{0,8},{4,12},{8,0},{12,4},{16,24},{20,28},{24,16},{28,20},{1,9},{5... | collective-permute-start | bytes 307208 | tf_op jit(solution)/shard_map/ppermute | solution.py:429
  43.1 9.7 %collective-permute-start.6 = (bf16[16,32,100]{2,1,0:T(8,128)(2,1)S(1)}, bf16[16,32,100]{2,1,0:T(8,128)(2,1)S(1)}, u32[]{:S(2)}, u32[]{:S(2)}) collective-permute-start(bf16[16,32,100]{2,1,0:T(8,128)(2,1)S(1)} %get-tuple-element.37), channel_id=1, source_target_pairs={{0,16},{4,20},{8,24},{12,28},{16,0},{20,4},{24,8},{28,12},{1,17},{... | collective-permute-start | bytes 307208 | tf_op jit(solution)/shard_map/ppermute | solution.py:429
  44.9 10.4 %collective-permute-start.7 = (bf16[16,32,100]{2,1,0:T(8,128)(2,1)S(1)}, bf16[16,32,100]{2,1,0:T(8,128)(2,1)S(1)}, u32[]{:S(2)}, u32[]{:S(2)}) collective-permute-start(bf16[16,32,100]{2,1,0:T(8,128)(2,1)S(1)} %get-tuple-element.38), channel_id=1, source_target_pairs={{0,24},{4,28},{8,16},{12,20},{16,8},{20,12},{24,0},{28,4},{1,25},{... | collective-permute-start | bytes 307208 | tf_op jit(solution)/shard_map/ppermute | solution.py:429
  55.3 2.1 %collective-permute-start.8 = (bf16[16,32,100]{2,1,0:T(8,128)(2,1)S(1)}, bf16[16,32,100]{2,1,0:T(8,128)(2,1)S(1)}, u32[]{:S(2)}, u32[]{:S(2)}) collective-permute-start(bf16[16,32,100]{2,1,0:T(8,128)(2,1)S(1)} %select_select_fusion.first), channel_id=1, source_target_pairs={{0,4},{4,0},{8,12},{12,8},{16,20},{20,16},{24,28},{28,24},{1,5},{5... | collective-permute-start | bytes 307208 | tf_op jit(solution)/shard_map/ppermute | solution.py:426
  63.3 8.4 %collective-permute-start.9 = (bf16[128,256]{1,0:T(8,128)(2,1)S(1)}, bf16[128,256]{1,0:T(8,128)(2,1)S(1)}, u32[]{:S(2)}, u32[]{:S(2)}) collective-permute-start(bf16[128,256]{1,0:T(8,128)(2,1)S(1)} %get-tuple-element.45), channel_id=1, source_target_pairs={{0,0},{1,8},{2,4},{3,12},{4,16},{5,24},{6,20},{7,28},{8,1},{9,9},{... | collective-permute-start | bytes 196616 | tf_op jit(solution)/shard_map/ppermute | solution.py:468
  67.8 5.5 %collective-permute-start.10 = (bf16[128,256]{1,0:T(8,128)(2,1)S(1)}, bf16[128,256]{1,0:T(8,128)(2,1)S(1)}, u32[]{:S(2)}, u32[]{:S(2)}) collective-permute-start(bf16[128,256]{1,0:T(8,128)(2,1)S(1)} %get-tuple-element.46), channel_id=1, source_target_pairs={{0,8},{1,0},{2,12},{3,4},{4,24},{5,16},{6,28},{7,20},{8,9},{9,1},{... | collective-permute-start | bytes 196616 | tf_op jit(solution)/shard_map/ppermute | solution.py:468
  73.4 2.8 %collective-permute-start.11 = (f32[64,256]{1,0:T(8,128)S(1)}, f32[64,256]{1,0:T(8,128)S(1)}, u32[]{:S(2)}, u32[]{:S(2)}) collective-permute-start(f32[64,256]{1,0:T(8,128)S(1)} %get-tuple-element.48), channel_id=1, source_target_pairs={{0,4},{4,0},{8,12},{12,8},{16,20},{20,16},{24,28},{28,24},{1,5},{5... | collective-permute-start | bytes 196616 | tf_op jit(solution)/shard_map/ppermute | solution.py:426

commit v5 on v4

--- a/solution.py
+++ b/solution.py
@@ -29,11 +29,12 @@
     )
 
 
-def pack_kernel(bank_blocks, templates, available, moveout, mine, theirs, usable, shifts, square, codes, sems, fetched):
+def pack_kernel(bank_blocks, templates, available, moveout, mine, theirs, usable, shifts, square, sems, fetched):
     blocks, channels, events, tlen = templates.shape
     chips, _, group, _ = mine.shape
     half = channels // 2
     me = lax.axis_index("tm") % 2
+    station = lax.axis_index("sta")
     slots = [bank_blocks[which] % blocks for which in range(2)]
     flag_copies = [
         pltpu.make_async_copy(available, usable, fetched.at[0]),
@@ -42,14 +43,15 @@
     for copy in flag_copies:
         copy.start()
     copies = []
-    for chip in range(chips):
-        which, part = divmod(chip * group, events)
+    for index in range(chips):
+        which, part = divmod(index * group, events)
+        chip = jnp.bitwise_xor(station, index)
         for side, out in enumerate((theirs, mine)):
             first = half * jnp.where(me == 1 - side, 0, 1)
             copy = pltpu.make_async_copy(
                 templates.at[slots[which], pl.ds(first, half), pl.ds(part, group), :],
                 out.at[chip, pl.ds(0, half)],
-                sems.at[chip, side],
+                sems.at[index, side],
             )
             copy.start()
             copies.append(copy)
@@ -67,16 +69,10 @@
         here = jnp.where(me == 0, turned, other)[:, 0:tlen].astype(jnp.bfloat16)
         there = jnp.where(me == 0, other, turned)[:, 0:tlen].astype(jnp.bfloat16)
         for index in range(events // group):
-            chip = which * (events // group) + index
+            chip = jnp.bitwise_xor(station, which * (events // group) + index)
             rows = slice(index * group, (index + 1) * group)
-            codes[0, chip, 0] = there[rows]
-            codes[1, chip, 0] = here[rows]
-    for side, out in enumerate((theirs, mine)):
-        copy = pltpu.make_async_copy(
-            codes.at[side], out.at[pl.ds(0, chips), pl.ds(half, 1)], fetched.at[side]
-        )
-        copy.start()
-        copies.append(copy)
+            mine[chip, half] = here[rows]
+            theirs[chip, half] = there[rows]
     for copy in copies:
         copy.wait()
 
@@ -84,30 +80,36 @@
 def pack(chips, group, bank_blocks, templates, available, moveout):
     channels, tlen = templates.shape[1], templates.shape[3]
     shape = (chips, channels // 2 + 1, group, tlen)
+    held = [
+        pltpu.with_memory_space_constraint(array, pltpu.HBM)
+        for array in (templates, available, moveout)
+    ]
     return pl.pallas_call(
         pack_kernel,
         out_shape=[jax.ShapeDtypeStruct(shape, jnp.bfloat16)] * 2,
         in_specs=[SMEM, ANY, ANY, ANY],
-        out_specs=[ANY] * 2,
+        out_specs=[VMEM] * 2,
         scratch_shapes=[
             pltpu.VMEM(available.shape, jnp.int32),
             pltpu.VMEM(moveout.shape, jnp.int32),
             pltpu.VMEM((LANES, LANES), jnp.float32),
-            pltpu.VMEM((2, chips, 1, group, tlen), jnp.bfloat16),
             pltpu.SemaphoreType.DMA((chips, 2)),
             pltpu.SemaphoreType.DMA((2,)),
         ],
+        compiler_params=params(),
         cost_estimate=cost(1.5),
         name="pack",
-    )(bank_blocks, templates, available, moveout)
+    )(bank_blocks, *held)
 
 
 def merge_kernel(blocks, bank_blocks, mine, other, *outs):
     chips = len(outs)
     me = lax.axis_index("tm")
+    station = lax.axis_index("sta")
     for step, out in enumerate(outs):
         dest = jnp.bitwise_xor(me // 2, step)
-        owner = jnp.where(dest < chips // 2, bank_blocks[0], bank_blocks[1]) // blocks
+        first = jnp.bitwise_xor(dest, station) < chips // 2
+        owner = jnp.where(first, bank_blocks[0], bank_blocks[1]) // blocks
         here = owner % 2 == me % 2
 
         @pl.when(here)
@@ -150,20 +152,19 @@
     return pltpu.roll(copies, row.shape[1] - 7 - ahead, 1, stride=1, stride_axis=0)
 
 
-def waves_kernel(channels, tlen, swapped, local, left_a, left_r, padded, inverse):
-    chips, _, samples = local.shape
+def waves_kernel(channels, tlen, rim, local, left_a, left_r, padded, inverse):
+    chips, _, _, samples = local.shape
     near = chips // 2
-    steps = 2 * near * samples // STRIDE
+    length = chips * samples
+    steps = length // STRIDE
     me = lax.axis_index("tm")
     chip, core = me // 2, me % 2
     padded[...] = jnp.zeros_like(padded)
-    for index in range(2 * near):
+    for index in range(chips):
         source = jnp.bitwise_xor(chip, near * core + index // 2)
-        wave = jnp.where(core == index % 2, local[source], swapped[index // 2])
-        padded[0:channels, samples * index : samples * (index + 1)] = wave.astype(jnp.float32)
-    rim = local[jnp.bitwise_xor(chip, near)][:, 0 : padded.shape[1] - 2 * near * samples]
-    rim = jnp.where(core == 0, rim.astype(jnp.float32), 0.0)
-    padded[0:channels, 2 * near * samples :] = rim
+        wave = local[source, index % 2].astype(jnp.float32)
+        padded[0:channels, samples * index : samples * (index + 1)] = wave
+    padded[0:channels, length:] = rim[...].astype(jnp.float32)
 
     @pl.loop(0, 4)
     def _(part):
@@ -196,8 +197,8 @@
         left_r[channel, :, LANES:] = (value - high.astype(jnp.float32)).astype(jnp.bfloat16)
 
 
-def prepare_waves(tlen, swapped, local):
-    chips, channels, samples = local.shape
+def prepare_waves(tlen, rim, local):
+    chips, _, channels, samples = local.shape
     length = chips * samples
     out = jax.ShapeDtypeStruct((channels, length // OFFSETS, DEPTH), jnp.bfloat16)
     return pl.pallas_call(
@@ -212,14 +213,18 @@
         compiler_params=params(),
         cost_estimate=cost(7),
         name="prepare_waves",
-    )(swapped, local)
-
-
-def main_kernel(channels, tlen, group, first, second, left_a, left_r, *rest):
+    )(rim, local)
+
+
+def main_kernel(side, tlen, group, piece, left_a, left_r, *rest):
     outs = rest[:-5]
+    if side:
+        before, outs = outs[0], outs[1:]
     bank, expand, weight_a, weight_r, total = rest[-5:]
     core = lax.axis_index("tm") % 2
+    channels = left_a.shape[0]
     half = channels // 2
+    base = half * jnp.where(core == side, 0, 1)
     slots = LANES // group
     banks = (half + 1) // slots
     offset_count = LANES // group
@@ -232,44 +237,34 @@
     target = lax.broadcasted_iota(jnp.int32, (LANES, LANES), 1)
     lane = lax.broadcasted_iota(jnp.int32, (1, LANES), 1)
     used = lag < tlen
+    ahead = lane // group
     for slot in range(slots):
         chosen = jnp.where(lag == target % group + slot * group, 1.0, 0.0)
         expand[:, slot * LANES : (slot + 1) * LANES] = chosen.astype(jnp.bfloat16)
-    for side, piece in enumerate((first, second)):
-        turned = []
-        for index in range(banks):
-            values = piece[slots * index : slots * (index + 1)].astype(jnp.float32)
-            values = values.reshape(LANES, tlen)
-            values = jnp.concatenate([values, jnp.zeros((LANES, LANES - tlen), jnp.float32)], axis=1)
-            turned.append(values.T)
-        codes = turned[-1]
-        for index, values in enumerate(turned):
-            code = jnp.zeros((1, LANES), jnp.float32)
-            for slot in range(slots):
-                item = slots * index + slot
-                if item < half:
-                    moved = pltpu.roll(
-                        codes[item : item + 1, :], (group * slot - code_lane) % LANES, 1
-                    )
-                    code = jnp.where(lane // group == slot, moved, code)
-            center = jnp.sum(jnp.where(used, values, 0.0), axis=0, keepdims=True) / tlen
-            deviate = jnp.where(used, values - center, 0.0)
-            spread = jnp.sqrt(jnp.sum(deviate * deviate, axis=0, keepdims=True) / tlen + EPSILON)
-            unit = (deviate / (spread * tlen)).astype(jnp.bfloat16).astype(jnp.float32)
-            unit = jnp.where(code > 0, unit, 0.0)
-            shift = code.astype(jnp.int32) - 1
-            for bit in (1, 2, 4):
-                unit = jnp.where(jnp.bitwise_and(shift, bit) > 0, pltpu.roll(unit, bit, 0), unit)
-            unit = jnp.where(lag == 112, code, unit)
-            bank[side * banks + index] = unit.astype(jnp.bfloat16)
-
-    ahead = lane // group
-
-    def channel_of(number, slot):
-        side = number // banks
-        item = (number % banks) * slots + slot
-        base = half * jnp.where(core == side, 0, 1)
-        return jnp.where(item < half, base + item, channels + side)
+    turned = []
+    for index in range(banks):
+        values = piece[slots * index : slots * (index + 1)].astype(jnp.float32)
+        values = values.reshape(LANES, tlen)
+        values = jnp.concatenate([values, jnp.zeros((LANES, LANES - tlen), jnp.float32)], axis=1)
+        turned.append(values.T)
+    codes = turned[-1]
+    for index, values in enumerate(turned):
+        code = jnp.zeros((1, LANES), jnp.float32)
+        for slot in range(slots):
+            item = slots * index + slot
+            if item < half:
+                moved = pltpu.roll(codes[item : item + 1, :], (group * slot - code_lane) % LANES, 1)
+                code = jnp.where(ahead == slot, moved, code)
+        center = jnp.sum(jnp.where(used, values, 0.0), axis=0, keepdims=True) / tlen
+        deviate = jnp.where(used, values - center, 0.0)
+        spread = jnp.sqrt(jnp.sum(deviate * deviate, axis=0, keepdims=True) / tlen + EPSILON)
+        unit = (deviate / (spread * tlen)).astype(jnp.bfloat16).astype(jnp.float32)
+        unit = jnp.where(code > 0, unit, 0.0)
+        shift = code.astype(jnp.int32) - 1
+        for bit in (1, 2, 4):
+            unit = jnp.where(jnp.bitwise_and(shift, bit) > 0, pltpu.roll(unit, bit, 0), unit)
+        unit = jnp.where(lag == 112, code, unit)
+        bank[index] = unit.astype(jnp.bfloat16)
 
     def build(number):
         wide = jnp.dot(bank[number], expand[...], preferred_element_type=jnp.float32)
@@ -288,42 +283,46 @@
                     jnp.concatenate([taps, gap], axis=0),
                 )[0:top]
             taps = taps.astype(jnp.bfloat16)
-            channel = channel_of(number, slot)
+            item = number * slots + slot
             pick = jnp.logical_and(lag == shift + 8 * ahead, usable)
             pick = jnp.where(pick, 1.0, 0.0).astype(jnp.bfloat16)
             for index in range(tile_count):
                 skip = 8 * offset_count * index
                 lanes = slice(LANES * index, LANES * (index + 1))
                 if skip:
-                    weight_a[channel, 0:skip, lanes] = jnp.zeros((skip, LANES), jnp.bfloat16)
+                    weight_a[item, 0:skip, lanes] = jnp.zeros((skip, LANES), jnp.bfloat16)
                     pick = jnp.concatenate(
                         [jnp.zeros((skip, LANES), jnp.bfloat16), pick[0 : LANES - skip]], axis=0
                     )
-                weight_a[channel, skip : skip + top, lanes] = taps
+                weight_a[item, skip : skip + top, lanes] = taps
                 rest = DEPTH - top - skip
                 if rest:
-                    weight_a[channel, skip + top :, lanes] = jnp.zeros((rest, LANES), jnp.bfloat16)
-                weight_r[channel, 0:LANES, lanes] = pick
-                weight_r[channel, LANES : 2 * LANES, lanes] = pick
-
-    def apply(number):
-        for slot in range(slots):
-            channel = channel_of(number, slot)
-            samples = jnp.minimum(channel, channels - 1)
-            corr = jnp.dot(left_a[samples], weight_a[channel], preferred_element_type=jnp.float32)
-            factor = jnp.dot(left_r[samples], weight_r[channel], preferred_element_type=jnp.float32)
+                    weight_a[item, skip + top :, lanes] = jnp.zeros((rest, LANES), jnp.bfloat16)
+                weight_r[item, 0:LANES, lanes] = pick
+                weight_r[item, LANES : 2 * LANES, lanes] = pick
+
+    def apply(number, count):
+        for slot in range(count):
+            item = number * slots + slot
+            corr = jnp.dot(left_a[base + item], weight_a[item], preferred_element_type=jnp.float32)
+            factor = jnp.dot(
+                left_r[base + item], weight_r[item], preferred_element_type=jnp.float32
+            )
             total[...] += corr * factor
 
-    total[...] = jnp.zeros_like(total)
+    total[...] = before[...] if side else jnp.zeros_like(total)
     build(0)
 
-    @pl.loop(1, 2 * banks)
+    @pl.loop(1, banks)
     def _(number):
-        apply(number - 1)
+        apply(number - 1, slots)
         build(number)
 
-    apply(2 * banks - 1)
-
+    apply(banks - 1, half - slots * (banks - 1))
+
+    if not side:
+        outs[0][...] = total[...]
+        return
     rows_out = outs[0].shape[0]
     station = lax.axis_index("sta") % len(outs)
     for step, out in enumerate(outs):
@@ -333,26 +332,30 @@
         )
 
 
-def correlate(channels, tlen, group, count, first, second, left_a, left_r):
-    rows = left_a.shape[1]
+def correlate(side, group, count, piece, left_a, left_r, *before):
+    channels, rows, _ = left_a.shape
     width = OFFSETS * group
-    banks = 2 * (channels // 2 + 1) * group // LANES
-    return pl.pallas_call(
-        functools.partial(main_kernel, channels, tlen, group),
-        out_shape=[jax.ShapeDtypeStruct((rows // count, width), jnp.bfloat16)] * count,
-        in_specs=[VMEM, VMEM, VMEM, VMEM],
-        out_specs=[VMEM] * count,
+    half = channels // 2
+    if side:
+        out = [jax.ShapeDtypeStruct((rows // count, width), jnp.bfloat16)] * count
+    else:
+        out = [jax.ShapeDtypeStruct((rows, width), jnp.float32)]
+    return pl.pallas_call(
+        functools.partial(main_kernel, side, piece.shape[2], group),
+        out_shape=out,
+        in_specs=[VMEM] * (3 + len(before)),
+        out_specs=[VMEM] * len(out),
         scratch_shapes=[
-            pltpu.VMEM((banks, LANES, LANES), jnp.bfloat16),
+            pltpu.VMEM(((half + 1) * group // LANES, LANES, LANES), jnp.bfloat16),
             pltpu.VMEM((LANES, LANES // group * LANES), jnp.bfloat16),
-            pltpu.VMEM((channels + 2, DEPTH, width), jnp.bfloat16),
-            pltpu.VMEM((channels + 2, DEPTH, width), jnp.bfloat16),
+            pltpu.VMEM((half + 1, DEPTH, width), jnp.bfloat16),
+            pltpu.VMEM((half + 1, DEPTH, width), jnp.bfloat16),
             pltpu.VMEM((rows, width), jnp.float32),
         ],
         compiler_params=params(),
-        cost_estimate=cost(6),
-        name="correlate",
-    )(first, second, left_a, left_r)
+        cost_estimate=cost(3),
+        name="correlate_" + ("second" if side else "first"),
+    )(piece, left_a, left_r, *before)
 
 
 def add_kernel(*refs):
@@ -420,6 +423,7 @@
     near = chips // 2
     group = 2 * events // chips
     me = lax.axis_index("tm").astype(jnp.int32)
+    station = lax.axis_index("sta").astype(jnp.int32)
     chip, core = me // 2, me % 2
 
     def swap(array):
@@ -427,6 +431,10 @@
 
     def across(array, step):
         return lax.ppermute(array, "tm", [(i, i ^ (2 * step)) for i in range(count_tm)])
+
+    def spread(array, step):
+        route = [(2 * z + z // near, 2 * (z ^ step) + z // near) for z in range(chips)]
+        return lax.ppermute(array, "tm", route)
 
     mine, theirs = pack(
         chips,
@@ -436,35 +444,39 @@
         jnp.transpose(available, (2, 0, 1)),
         jnp.transpose(moveout, (2, 0, 1)),
     )
+    waveforms, theirs = lax.optimization_barrier((waveforms, theirs))
+    paired = swap(waveforms)
     other = swap(theirs)
-    waveforms, mine = lax.optimization_barrier((waveforms, mine))
-    local = jnp.stack([waveforms] + [across(waveforms, step) for step in range(1, chips)])
+    both = jnp.where(
+        core == 0, jnp.stack([waveforms, paired]), jnp.stack([paired, waveforms])
+    )
+    far = [spread(both, step) for step in range(near, chips)]
+    local = jnp.stack([both] + [spread(both, step) for step in range(1, near)] + far)
     other, local = lax.optimization_barrier((other, local))
     merged = merge(blocks, bank_blocks, mine, other)
     pieces = [merged[0]] + [across(merged[step], step) for step in range(1, chips)]
 
-    wanted = [
-        lax.dynamic_index_in_dim(local, chip ^ (near * (1 - core) + step), 0, keepdims=False)
-        for step in range(near)
-    ]
-    swapped = swap(jnp.stack(wanted))
-    left_a, left_r = prepare_waves(tlen, swapped, local)
+    rim = lax.dynamic_index_in_dim(local, chip ^ near, 0, keepdims=False)[0, :, : 2 * LANES]
+    rim = lax.ppermute(rim, "tm", [(2 * z + 1, 2 * z) for z in range(chips)])
+    left_a, left_r = prepare_waves(tlen, rim, local)
 
     left_a, left_r, *pieces = lax.optimization_barrier((left_a, left_r, *pieces))
-    owner = jnp.where(chip < near, bank_blocks[0], bank_blocks[1]) // blocks
+    owner = jnp.where(chip ^ station < near, bank_blocks[0], bank_blocks[1]) // blocks
     source = (owner // 2) ^ chip
     first = pieces[0]
     for step in range(1, chips):
         first = jnp.where(source == step, pieces[step], first)
     second = swap(first)
-    parts = correlate(channels, tlen, group, near, first, second, left_a, left_r)
+    total = correlate(0, group, near, first, left_a, left_r)
+    parts = correlate(1, group, near, second, left_a, left_r, *total)
     gathered = []
     for step in range(near):
         route = []
         for d in range(count_tm):
             for s in range(count_sta):
                 dest = near * (d % 2) + (s % near ^ step)
-                route.append((d * count_sta + s, (2 * dest + s // near) * count_sta + d // 2))
+                sta = d // 2 ^ s
+                route.append((d * count_sta + s, (2 * dest + s // near) * count_sta + sta))
         gathered.append(lax.ppermute(parts[step], ("tm", "sta"), route))
     ours, send = add(gathered)
     return finish(group, samples, ours, swap(send))

time: 77.7 us -> 57.5 us (0.74)
  the two profiles are of different devices: /device:TPU:7 before, /device:TPU:0 now
where the time goes in v5:
time: 57.5 us; the launch traced here: 57.2 us
  starting transfers between devices  27.5 us (48%)
  Pallas kernels  15.7 us (27%)
  waiting for transfers between devices  11.1 us (19%)
  between operations  1.56 us (3%)
  local copies, waits for them, and re-layouts  1.33 us (2%)
    ppermute x3, starting transfers between devices, spread(): return lax.ppermute(array, 'tm', route)  10.7 us
    ppermute x2, starting transfers between devices, shards(): gathered.append(lax.ppermute(parts[step], ('tm', 'sta'), route))  7.07 us
    pallas_call x1, Pallas kernels, prepare_waves(): pl.pallas_call(functools.partial(waves_kernel, channels, tlen), out_shape...  6.19 us
    pallas_call x2, Pallas kernels, correlate(): pl.pallas_call(functools.partial(main_kernel, side, piece.shape[2], group...  5.73 us
    ppermute x3, starting transfers between devices, across(): lax.ppermute(array, 'tm', [(i, i ^ 2 * step) for i in range(count_tm)])  4.45 us
    ppermute x4, starting transfers between devices, swap(): return lax.ppermute(array, 'tm', [(i, i ^ 1) for i in range(count_tm)])  3.91 us
    ppermute x2, waiting for transfers between devices, shards(): gathered.append(lax.ppermute(parts[step], ('tm', 'sta'), route))  3.67 us
    ppermute x3, waiting for transfers between devices, spread(): return lax.ppermute(array, 'tm', route)  3.64 us
  transfers between devices with their start and end apart: 13, of which 4 were waited for; matrix products, arithmetic and copies ran while one was open for 1% of the time, Pallas kernels for 17%

profile of v5, /device:TPU:0, one launch (start us, length us, event | category | flops | bytes accessed | tf_op | source)
XLA Modules:
  0.0 57.2 jit_solution(708133782586734333)
XLA Ops:
  0.0 0.0 copy-start.1
  0.0 0.0 copy-start
  0.0 0.7 %copy-done = s32[2]{0:T(128)S(1)} copy-done((s32[2]{0:T(128)S(1)}, s32[2]{0:T(128)}, u32[]{:S(2)}) %copy-start) | copy-done | bytes 32
  0.7 0.0 copy-start.2
  0.7 2.2 %pack.1 = (bf16[4,16,32,100]{3,2,1,0:T(8,128)(2,1)S(1)}, bf16[4,16,32,100]{3,2,1,0:T(8,128)(2,1)S(1)}) custom-call(s32[2]{0:T(128)S(1)} %copy-done, bf16[2,30,64,100]{3,2,1,0:T(8,128)(2,1)} %bitcast.23, s32[30,2,64]{2,1,0:T(2,128)} %bitcast.24, s32[30,2,64]{2,1,0:T(2,128)} %bitcast.25), custom_call_target="tpu_custom_call" | custom-call | flops 1500000000 | bytes 1500000 | tf_op jit(solution)/shard_map/pack/pallas_call | solution.py:87
  2.9 0.0 copy-done.2
  2.9 0.4 collective-permute-start.1
  3.3 0.2 collective-permute-start
  3.5 0.6 %fusion = (s32[1]{0:T(128)}, s32[1]{0:T(128)}) fusion(s32[2]{0:T(128)S(1)} %copy-done), kind=kLoop, calls=%fused_computation.6 | loop fusion | bytes 16 | tf_op jit(solution)/shard_map/slice | solution.py:464
  5.4 0.0 collective-permute-done.1
  5.4 7.0 %collective-permute-start.4 = (bf16[2,30,512]{2,1,0:T(8,128)(2,1)S(1)}, bf16[2,30,512]{2,1,0:T(8,128)(2,1)S(1)}, u32[]{:S(2)}, u32[]{:S(2)}) collective-permute-start(bf16[2,30,512]{2,1,0:T(8,128)(2,1)S(1)} %maximum_select_fusion.1), channel_id=1, source_target_pairs={{0,24},{8,16},{20,12},{28,4},{1,25},{9,17},{21,13},{29,5},{2,26},{... | collective-permute-start | bytes 184328 | tf_op jit(solution)/shard_map/ppermute | solution.py:437
  12.4 1.3 %collective-permute-start.3 = (bf16[2,30,512]{2,1,0:T(8,128)(2,1)S(1)}, bf16[2,30,512]{2,1,0:T(8,128)(2,1)S(1)}, u32[]{:S(2)}, u32[]{:S(2)}) collective-permute-start(bf16[2,30,512]{2,1,0:T(8,128)(2,1)S(1)} %maximum_select_fusion.1), channel_id=1, source_target_pairs={{0,16},{8,24},{20,4},{28,12},{1,17},{9,25},{21,5},{29,13},{2,18},{... | collective-permute-start | bytes 184328 | tf_op jit(solution)/shard_map/ppermute | solution.py:437
  13.7 2.5 %collective-permute-start.2 = (bf16[2,30,512]{2,1,0:T(8,128)(2,1)S(1)}, bf16[2,30,512]{2,1,0:T(8,128)(2,1)S(1)}, u32[]{:S(2)}, u32[]{:S(2)}) collective-permute-start(bf16[2,30,512]{2,1,0:T(8,128)(2,1)S(1)} %maximum_select_fusion.1), channel_id=1, source_target_pairs={{0,8},{8,0},{20,28},{28,20},{1,9},{9,1},{21,29},{29,21},{2,10},{10... | collective-permute-start | bytes 184328 | tf_op jit(solution)/shard_map/ppermute | solution.py:437
  16.2 0.0 collective-permute-done.4
  16.2 0.0 collective-permute-done.3
  16.2 3.6 %collective-permute-done.2 = bf16[2,30,512]{2,1,0:T(8,128)(2,1)S(1)} collective-permute-done((bf16[2,30,512]{2,1,0:T(8,128)(2,1)S(1)}, bf16[2,30,512]{2,1,0:T(8,128)(2,1)S(1)}, u32[]{:S(2)}, u32[]{:S(2)}) %collective-permute-start.2) | collective-permute-done | bytes 61472 | tf_op jit(solution)/shard_map/ppermute | solution.py:437
  19.9 0.0 collective-permute-done.other
  19.9 1.3 %collective-permute-start.5 = (bf16[30,256]{1,0:T(8,128)(2,1)S(1)}, bf16[30,256]{1,0:T(8,128)(2,1)S(1)}, u32[]{:S(2)}, u32[]{:S(2)}) collective-permute-start(bf16[30,256]{1,0:T(8,128)(2,1)S(1)} %slice_bitcast_fusion), channel_id=1, source_target_pairs={{4,0},{12,8},{20,16},{28,24},{5,1},{13,9},{21,17},{29,25},{6,2},{1... | collective-permute-start | bytes 46088 | tf_op jit(solution)/shard_map/ppermute | solution.py:460
  21.2 0.0 copy-done.1
  21.3 0.7 %merge.1 = (bf16[16,32,100]{2,1,0:T(8,128)(2,1)S(1)}, bf16[16,32,100]{2,1,0:T(8,128)(2,1)S(1)}, bf16[16,32,100]{2,1,0:T(8,128)(2,1)S(1)}, bf16[16,32,100]{2,1,0:T(8,128)(2,1)S(1)}) custom-call(s32[2]{0:T(128)S(1)} %copy-done.1, bf16[4,16,32,100]{3,2,1,0:T(8,128)(2,1)S(1)} %get-tuple-element.33.mine, bf16[4,16,32,100]{3,2,1,0:T(8,128)(2,1)S(1)} %collective-permute-done.other), custom_call_target="tpu_custom_call" | custom-call | flops 1000000000 | bytes 1000000 | tf_op jit(solution)/shard_map/merge/pallas_call | solution.py:126
  22.0 0.6 %collective-permute-start.6 = (bf16[16,32,100]{2,1,0:T(8,128)(2,1)S(1)}, bf16[16,32,100]{2,1,0:T(8,128)(2,1)S(1)}, u32[]{:S(2)}, u32[]{:S(2)}) collective-permute-start(bf16[16,32,100]{2,1,0:T(8,128)(2,1)S(1)} %get-tuple-element.36), channel_id=1, source_target_pairs={{0,8},{4,12},{8,0},{12,4},{16,24},{20,28},{24,16},{28,20},{1,9},{5... | collective-permute-start | bytes 307208 | tf_op jit(solution)/shard_map/ppermute | solution.py:433
  22.6 0.0 collective-permute-start.7
  22.6 3.8 %collective-permute-start.8 = (bf16[16,32,100]{2,1,0:T(8,128)(2,1)S(1)}, bf16[16,32,100]{2,1,0:T(8,128)(2,1)S(1)}, u32[]{:S(2)}, u32[]{:S(2)}) collective-permute-start(bf16[16,32,100]{2,1,0:T(8,128)(2,1)S(1)} %get-tuple-element.38), channel_id=1, source_target_pairs={{0,24},{4,28},{8,16},{12,20},{16,8},{20,12},{24,0},{28,4},{1,25},{... | collective-permute-start | bytes 307208 | tf_op jit(solution)/shard_map/ppermute | solution.py:433
  26.4 0.0 collective-permute-done.5.rim
  26.5 6.2 %prepare_waves.1 = (bf16[30,256,256]{2,1,0:T(8,128)(2,1)S(1)}, bf16[30,256,256]{2,1,0:T(8,128)(2,1)S(1)}) custom-call(bf16[30,256]{1,0:T(8,128)(2,1)S(1)} %collective-permute-done.5.rim, bf16[4,2,30,512]{3,2,1,0:T(8,128)(2,1)S(1)} %pad_maximum_fusion.local), custom_call_target="tpu_custom_call" | custom-call | flops 7000000000 | bytes 7000000 | tf_op jit(solution)/shard_map/prepare_waves/pallas_call | solution.py:204
  32.6 0.0 collective-permute-done.6
  32.7 2.9 %collective-permute-done.7 = bf16[16,32,100]{2,1,0:T(8,128)(2,1)S(1)} collective-permute-done((bf16[16,32,100]{2,1,0:T(8,128)(2,1)S(1)}, bf16[16,32,100]{2,1,0:T(8,128)(2,1)S(1)}, u32[]{:S(2)}, u32[]{:S(2)}) %collective-permute-start.7) | collective-permute-done | bytes 102432 | tf_op jit(solution)/shard_map/ppermute | solution.py:433
  35.5 0.0 collective-permute-done.8
  35.5 0.1 collective-permute-start.9
  35.6 2.8 %correlate_first.1.rest_0_ = f32[256,256]{1,0:T(8,128)S(1)} custom-call(bf16[16,32,100]{2,1,0:T(8,128)(2,1)S(1)} %select_select_fusion.piece, bf16[30,256,256]{2,1,0:T(8,128)(2,1)S(1)} %get-tuple-element.43.left_a, bf16[30,256,256]{2,1,0:T(8,128)(2,1)S(1)} %get-tuple-element.44.left_r), custom_call_target="tpu_custom_call" | custom-call | flops 3000000000 | bytes 3000000 | tf_op jit(solution)/shard_map/correlate_first/pallas_call | solution.py:343
  38.5 0.0 collective-permute-done.9.piece
  38.5 2.9 %correlate_second.1 = (bf16[128,256]{1,0:T(8,128)(2,1)S(1)}, bf16[128,256]{1,0:T(8,128)(2,1)S(1)}) custom-call(bf16[16,32,100]{2,1,0:T(8,128)(2,1)S(1)} %collective-permute-done.9.piece, bf16[30,256,256]{2,1,0:T(8,128)(2,1)S(1)} %get-tuple-element.43.left_a, bf16[30,256,256]{2,1,0:T(8,128)(2,1)S(1)} %get-tuple-element.44.left_r, ...), custom_call_target="tpu_custom_call" | custom-call | flops 3000000000 | bytes 3000000 | tf_op jit(solution)/shard_map/correlate_second/pallas_call | solution.py:343
  41.4 0.7 %collective-permute-start.10 = (bf16[128,256]{1,0:T(8,128)(2,1)S(1)}, bf16[128,256]{1,0:T(8,128)(2,1)S(1)}, u32[]{:S(2)}, u32[]{:S(2)}) collective-permute-start(bf16[128,256]{1,0:T(8,128)(2,1)S(1)} %get-tuple-element.45), channel_id=1, source_target_pairs={{0,0},{1,9},{2,6},{3,15},{4,16},{5,25},{6,22},{7,31},{8,1},{9,8},{... | collective-permute-start | bytes 196616 | tf_op jit(solution)/shard_map/ppermute | solution.py:480
  42.0 6.4 %collective-permute-start.11 = (bf16[128,256]{1,0:T(8,128)(2,1)S(1)}, bf16[128,256]{1,0:T(8,128)(2,1)S(1)}, u32[]{:S(2)}, u32[]{:S(2)}) collective-permute-start(bf16[128,256]{1,0:T(8,128)(2,1)S(1)} %get-tuple-element.46), channel_id=1, source_target_pairs={{0,8},{1,1},{2,14},{3,7},{4,24},{5,17},{6,30},{7,23},{8,9},{9,0},{... | collective-permute-start | bytes 196616 | tf_op jit(solution)/shard_map/ppermute | solution.py:480
  48.5 0.0 collective-permute-done.10.refs_0_
  48.5 3.7 %collective-permute-done.11.refs_1_ = bf16[128,256]{1,0:T(8,128)(2,1)S(1)} collective-permute-done((bf16[128,256]{1,0:T(8,128)(2,1)S(1)}, bf16[128,256]{1,0:T(8,128)(2,1)S(1)}, u32[]{:S(2)}, u32[]{:S(2)}) %collective-permute-start.11) | collective-permute-done | bytes 65568 | tf_op jit(solution)/shard_map/ppermute | solution.py:480
  52.2 3.3 %collective-permute-start.12 = (f32[64,256]{1,0:T(8,128)S(1)}, f32[64,256]{1,0:T(8,128)S(1)}, u32[]{:S(2)}, u32[]{:S(2)}) collective-permute-start(f32[64,256]{1,0:T(8,128)S(1)} %get-tuple-element.48), channel_id=1, source_target_pairs={{0,4},{4,0},{8,12},{12,8},{16,20},{20,16},{24,28},{28,24},{1,5},{5... | collective-permute-start | bytes 196616 | tf_op jit(solution)/shard_map/ppermute | solution.py:430
  55.4 0.9 %collective-permute-done.12.received = f32[64,256]{1,0:T(8,128)S(1)} collective-permute-done((f32[64,256]{1,0:T(8,128)S(1)}, f32[64,256]{1,0:T(8,128)S(1)}, u32[]{:S(2)}, u32[]{:S(2)}) %collective-permute-start.12) | collective-permute-done | bytes 65568 | tf_op jit(solution)/shard_map/ppermute | solution.py:430
  56.3 0.9 %finish.1 = f32[32,512]{1,0:T(8,128)} custom-call(f32[64,256]{1,0:T(8,128)S(1)} %get-tuple-element.47.ours, f32[64,256]{1,0:T(8,128)S(1)} %collective-permute-done.12.received), custom_call_target="tpu_custom_call" | custom-call | flops 1000000000 | bytes 1000000 | tf_op jit(solution)/shard_map/finish/pallas_call | solution.py:406
  (7 shorter events, 0.1 us)
Async XLA Ops:
  0.0 21.2 %copy-start.1 = (s32[2]{0:T(128)S(1)}, s32[2]{0:T(128)}, u32[]{:S(2)}) copy-start(s32[2]{0:T(128)} %bank_blocks.3) | copy-start | bytes 28
  0.0 0.7 %copy-start = (s32[2]{0:T(128)S(1)}, s32[2]{0:T(128)}, u32[]{:S(2)}) copy-start(s32[2]{0:T(128)} %bank_blocks.3) | copy-start | bytes 28
  0.7 2.2 %copy-start.2 = (bf16[30,512]{1,0:T(8,128)(2,1)S(1)}, bf16[30,512]{1,0:T(8,128)(2,1)}, u32[]{:S(2)}) copy-start(bf16[30,512]{1,0:T(8,128)(2,1)} %param.5) | copy-start | bytes 92164
  2.9 2.5 %collective-permute-start.1 = (bf16[30,512]{1,0:T(8,128)(2,1)S(1)}, bf16[30,512]{1,0:T(8,128)(2,1)S(1)}, u32[]{:S(2)}, u32[]{:S(2)}) collective-permute-start(bf16[30,512]{1,0:T(8,128)(2,1)S(1)} %copy-done.2), channel_id=1, source_target_pairs={{0,4},{4,0},{8,12},{12,8},{16,20},{20,16},{24,28},{28,24},{1,5},{5... | collective-permute-start | bytes 92168 | tf_op jit(solution)/shard_map/ppermute | solution.py:430
  3.3 16.6 %collective-permute-start = (bf16[4,16,32,100]{3,2,1,0:T(8,128)(2,1)S(1)}, bf16[4,16,32,100]{3,2,1,0:T(8,128)(2,1)S(1)}, u32[]{:S(2)}, u32[]{:S(2)}) collective-permute-start(bf16[4,16,32,100]{3,2,1,0:T(8,128)(2,1)S(1)} %get-tuple-element.28), channel_id=1, source_target_pairs={{0,4},{4,0},{8,12},{12,8},{16,20},{20,16},{24,28},{28,24},{1,5},{5... | collective-permute-start | bytes 1228808 | tf_op jit(solution)/shard_map/ppermute | solution.py:430
  5.4 10.8 %collective-permute-start.4 = (bf16[2,30,512]{2,1,0:T(8,128)(2,1)S(1)}, bf16[2,30,512]{2,1,0:T(8,128)(2,1)S(1)}, u32[]{:S(2)}, u32[]{:S(2)}) collective-permute-start(bf16[2,30,512]{2,1,0:T(8,128)(2,1)S(1)} %maximum_select_fusion.1), channel_id=1, source_target_pairs={{0,24},{8,16},{20,12},{28,4},{1,25},{9,17},{21,13},{29,5},{2,26},{... | collective-permute-start | bytes 184328 | tf_op jit(solution)/shard_map/ppermute | solution.py:437
  12.4 3.8 %collective-permute-start.3 = (bf16[2,30,512]{2,1,0:T(8,128)(2,1)S(1)}, bf16[2,30,512]{2,1,0:T(8,128)(2,1)S(1)}, u32[]{:S(2)}, u32[]{:S(2)}) collective-permute-start(bf16[2,30,512]{2,1,0:T(8,128)(2,1)S(1)} %maximum_select_fusion.1), channel_id=1, source_target_pairs={{0,16},{8,24},{20,4},{28,12},{1,17},{9,25},{21,5},{29,13},{2,18},{... | collective-permute-start | bytes 184328 | tf_op jit(solution)/shard_map/ppermute | solution.py:437
  13.7 6.2 %collective-permute-start.2 = (bf16[2,30,512]{2,1,0:T(8,128)(2,1)S(1)}, bf16[2,30,512]{2,1,0:T(8,128)(2,1)S(1)}, u32[]{:S(2)}, u32[]{:S(2)}) collective-permute-start(bf16[2,30,512]{2,1,0:T(8,128)(2,1)S(1)} %maximum_select_fusion.1), channel_id=1, source_target_pairs={{0,8},{8,0},{20,28},{28,20},{1,9},{9,1},{21,29},{29,21},{2,10},{10... | collective-permute-start | bytes 184328 | tf_op jit(solution)/shard_map/ppermute | solution.py:437
  19.9 6.5 %collective-permute-start.5 = (bf16[30,256]{1,0:T(8,128)(2,1)S(1)}, bf16[30,256]{1,0:T(8,128)(2,1)S(1)}, u32[]{:S(2)}, u32[]{:S(2)}) collective-permute-start(bf16[30,256]{1,0:T(8,128)(2,1)S(1)} %slice_bitcast_fusion), channel_id=1, source_target_pairs={{4,0},{12,8},{20,16},{28,24},{5,1},{13,9},{21,17},{29,25},{6,2},{1... | collective-permute-start | bytes 46088 | tf_op jit(solution)/shard_map/ppermute | solution.py:460
  22.0 10.7 %collective-permute-start.6 = (bf16[16,32,100]{2,1,0:T(8,128)(2,1)S(1)}, bf16[16,32,100]{2,1,0:T(8,128)(2,1)S(1)}, u32[]{:S(2)}, u32[]{:S(2)}) collective-permute-start(bf16[16,32,100]{2,1,0:T(8,128)(2,1)S(1)} %get-tuple-element.36), channel_id=1, source_target_pairs={{0,8},{4,12},{8,0},{12,4},{16,24},{20,28},{24,16},{28,20},{1,9},{5... | collective-permute-start | bytes 307208 | tf_op jit(solution)/shard_map/ppermute | solution.py:433
  22.6 12.9 %collective-permute-start.7 = (bf16[16,32,100]{2,1,0:T(8,128)(2,1)S(1)}, bf16[16,32,100]{2,1,0:T(8,128)(2,1)S(1)}, u32[]{:S(2)}, u32[]{:S(2)}) collective-permute-start(bf16[16,32,100]{2,1,0:T(8,128)(2,1)S(1)} %get-tuple-element.37), channel_id=1, source_target_pairs={{0,16},{4,20},{8,24},{12,28},{16,0},{20,4},{24,8},{28,12},{1,17},{... | collective-permute-start | bytes 307208 | tf_op jit(solution)/shard_map/ppermute | solution.py:433
  22.6 12.9 %collective-permute-start.8 = (bf16[16,32,100]{2,1,0:T(8,128)(2,1)S(1)}, bf16[16,32,100]{2,1,0:T(8,128)(2,1)S(1)}, u32[]{:S(2)}, u32[]{:S(2)}) collective-permute-start(bf16[16,32,100]{2,1,0:T(8,128)(2,1)S(1)} %get-tuple-element.38), channel_id=1, source_target_pairs={{0,24},{4,28},{8,16},{12,20},{16,8},{20,12},{24,0},{28,4},{1,25},{... | collective-permute-start | bytes 307208 | tf_op jit(solution)/shard_map/ppermute | solution.py:433
  35.5 2.9 %collective-permute-start.9 = (bf16[16,32,100]{2,1,0:T(8,128)(2,1)S(1)}, bf16[16,32,100]{2,1,0:T(8,128)(2,1)S(1)}, u32[]{:S(2)}, u32[]{:S(2)}) collective-permute-start(bf16[16,32,100]{2,1,0:T(8,128)(2,1)S(1)} %select_select_fusion.piece), channel_id=1, source_target_pairs={{0,4},{4,0},{8,12},{12,8},{16,20},{20,16},{24,28},{28,24},{1,5},{5... | collective-permute-start | bytes 307208 | tf_op jit(solution)/shard_map/ppermute | solution.py:430
  41.4 7.1 %collective-permute-start.10 = (bf16[128,256]{1,0:T(8,128)(2,1)S(1)}, bf16[128,256]{1,0:T(8,128)(2,1)S(1)}, u32[]{:S(2)}, u32[]{:S(2)}) collective-permute-start(bf16[128,256]{1,0:T(8,128)(2,1)S(1)} %get-tuple-element.45), channel_id=1, source_target_pairs={{0,0},{1,9},{2,6},{3,15},{4,16},{5,25},{6,22},{7,31},{8,1},{9,8},{... | collective-permute-start | bytes 196616 | tf_op jit(solution)/shard_map/ppermute | solution.py:480
  42.0 10.1 %collective-permute-start.11 = (bf16[128,256]{1,0:T(8,128)(2,1)S(1)}, bf16[128,256]{1,0:T(8,128)(2,1)S(1)}, u32[]{:S(2)}, u32[]{:S(2)}) collective-permute-start(bf16[128,256]{1,0:T(8,128)(2,1)S(1)} %get-tuple-element.46), channel_id=1, source_target_pairs={{0,8},{1,1},{2,14},{3,7},{4,24},{5,17},{6,30},{7,23},{8,9},{9,0},{... | collective-permute-start | bytes 196616 | tf_op jit(solution)/shard_map/ppermute | solution.py:480
  52.2 4.2 %collective-permute-start.12 = (f32[64,256]{1,0:T(8,128)S(1)}, f32[64,256]{1,0:T(8,128)S(1)}, u32[]{:S(2)}, u32[]{:S(2)}) collective-permute-start(f32[64,256]{1,0:T(8,128)S(1)} %get-tuple-element.48), channel_id=1, source_target_pairs={{0,4},{4,0},{8,12},{12,8},{16,20},{20,16},{24,28},{28,24},{1,5},{5... | collective-permute-start | bytes 196616 | tf_op jit(solution)/shard_map/ppermute | solution.py:430

commit v6 on v5

--- a/solution.py
+++ b/solution.py
@@ -10,6 +10,8 @@
 EPSILON = 1e-06
 LANES = 128
 OFFSETS = 8
+TILES = 12
+QUARTER = 25
 STRIDE = 64
 DEPTH = 256
 VMEM_LIMIT = 28 * 1024 * 1024
@@ -29,87 +31,86 @@
     )
 
 
-def pack_kernel(bank_blocks, templates, available, moveout, mine, theirs, usable, shifts, square, sems, fetched):
+def pack_kernel(bank_blocks, templates, available, moveout, mine, theirs, chosen, raw, usable, shifts, square, packed, sems):
     blocks, channels, events, tlen = templates.shape
     chips, _, group, _ = mine.shape
     half = channels // 2
     me = lax.axis_index("tm") % 2
-    station = lax.axis_index("sta")
-    slots = [bank_blocks[which] % blocks for which in range(2)]
-    flag_copies = [
-        pltpu.make_async_copy(available, usable, fetched.at[0]),
-        pltpu.make_async_copy(moveout, shifts, fetched.at[1]),
+    fetch = [
+        pltpu.make_async_copy(source, target, sems.at[index])
+        for index, (source, target) in enumerate(
+            ((bank_blocks, chosen), (available, usable), (moveout, shifts), (templates, raw))
+        )
     ]
-    for copy in flag_copies:
+    for copy in fetch:
         copy.start()
-    copies = []
-    for index in range(chips):
-        which, part = divmod(index * group, events)
-        chip = jnp.bitwise_xor(station, index)
-        for side, out in enumerate((theirs, mine)):
-            first = half * jnp.where(me == 1 - side, 0, 1)
-            copy = pltpu.make_async_copy(
-                templates.at[slots[which], pl.ds(first, half), pl.ds(part, group), :],
-                out.at[chip, pl.ds(0, half)],
-                sems.at[index, side],
-            )
-            copy.start()
-            copies.append(copy)
-    for copy in flag_copies:
+    packed[...] = jnp.zeros_like(packed)
+    square[...] = jnp.zeros_like(square)
+    for copy in fetch[:3]:
         copy.wait()
+    slots = [chosen[which] % blocks for which in range(2)]
     flags = jnp.where(usable[...] > 0, shifts[...] + 1, 0).astype(jnp.float32)
+    turned = []
     for which in range(2):
         code = flags[:, 0, :]
         for block in range(1, blocks):
             code = jnp.where(slots[which] == block, flags[:, block, :], code)
-        square[...] = jnp.zeros_like(square)
         square[0:channels, 0:events] = code
-        turned = square[...].T
-        other = pltpu.roll(turned, LANES - half, 1)
-        here = jnp.where(me == 0, turned, other)[:, 0:tlen].astype(jnp.bfloat16)
-        there = jnp.where(me == 0, other, turned)[:, 0:tlen].astype(jnp.bfloat16)
-        for index in range(events // group):
-            chip = jnp.bitwise_xor(station, which * (events // group) + index)
-            rows = slice(index * group, (index + 1) * group)
-            mine[chip, half] = here[rows]
-            theirs[chip, half] = there[rows]
-    for copy in copies:
-        copy.wait()
+        turned.append(square[...].T.astype(jnp.bfloat16))
+    fetch[3].wait()
+    for which in range(2):
+        for core in range(2):
+            for tile in range(TILES):
+                channel = half * core + tile
+                extra = half * core + TILES + tile // 4
+                start = QUARTER * (tile % 4)
+                for index in range(events // group):
+                    chip = which * (events // group) + index
+                    rows = slice(index * group, (index + 1) * group)
+                    packed[core, chip, tile, :, 0:tlen] = raw[slots[which], channel, rows, :]
+                    packed[core, chip, tile, :, tlen : tlen + QUARTER] = raw[
+                        slots[which], extra, rows, start : start + QUARTER
+                    ]
+                    packed[core, chip, tile, :, 125:126] = turned[which][rows, channel : channel + 1]
+                    if tile < half - TILES:
+                        beyond = channel + TILES
+                        packed[core, chip, tile, :, 126:127] = turned[which][rows, beyond : beyond + 1]
+    mine[...] = packed[me]
+    theirs[...] = packed[1 - me]
 
 
 def pack(chips, group, bank_blocks, templates, available, moveout):
-    channels, tlen = templates.shape[1], templates.shape[3]
-    shape = (chips, channels // 2 + 1, group, tlen)
+    shape = (chips, TILES, group, LANES)
     held = [
         pltpu.with_memory_space_constraint(array, pltpu.HBM)
-        for array in (templates, available, moveout)
+        for array in (bank_blocks, templates, available, moveout)
     ]
     return pl.pallas_call(
         pack_kernel,
         out_shape=[jax.ShapeDtypeStruct(shape, jnp.bfloat16)] * 2,
-        in_specs=[SMEM, ANY, ANY, ANY],
+        in_specs=[ANY] * 4,
         out_specs=[VMEM] * 2,
         scratch_shapes=[
+            pltpu.SMEM(bank_blocks.shape, jnp.int32),
+            pltpu.VMEM(templates.shape, jnp.bfloat16),
             pltpu.VMEM(available.shape, jnp.int32),
             pltpu.VMEM(moveout.shape, jnp.int32),
             pltpu.VMEM((LANES, LANES), jnp.float32),
-            pltpu.SemaphoreType.DMA((chips, 2)),
-            pltpu.SemaphoreType.DMA((2,)),
+            pltpu.VMEM((2,) + shape, jnp.bfloat16),
+            pltpu.SemaphoreType.DMA((4,)),
         ],
         compiler_params=params(),
-        cost_estimate=cost(1.5),
+        cost_estimate=cost(2),
         name="pack",
-    )(bank_blocks, *held)
+    )(*held)
 
 
 def merge_kernel(blocks, bank_blocks, mine, other, *outs):
     chips = len(outs)
     me = lax.axis_index("tm")
-    station = lax.axis_index("sta")
     for step, out in enumerate(outs):
         dest = jnp.bitwise_xor(me // 2, step)
-        first = jnp.bitwise_xor(dest, station) < chips // 2
-        owner = jnp.where(first, bank_blocks[0], bank_blocks[1]) // blocks
+        owner = jnp.where(dest < chips // 2, bank_blocks[0], bank_blocks[1]) // blocks
         here = owner % 2 == me % 2
 
         @pl.when(here)
@@ -152,8 +153,8 @@
     return pltpu.roll(copies, row.shape[1] - 7 - ahead, 1, stride=1, stride_axis=0)
 
 
-def waves_kernel(channels, tlen, rim, local, left_a, left_r, padded, inverse):
-    chips, _, _, samples = local.shape
+def waves_kernel(channels, tlen, swapped, local, left_a, left_r, padded, inverse):
+    chips, _, samples = local.shape
     near = chips // 2
     length = chips * samples
     steps = length // STRIDE
@@ -162,9 +163,10 @@
     padded[...] = jnp.zeros_like(padded)
     for index in range(chips):
         source = jnp.bitwise_xor(chip, near * core + index // 2)
-        wave = local[source, index % 2].astype(jnp.float32)
-        padded[0:channels, samples * index : samples * (index + 1)] = wave
-    padded[0:channels, length:] = rim[...].astype(jnp.float32)
+        wave = jnp.where(core == index % 2, local[source], swapped[index // 2])
+        padded[0:channels, samples * index : samples * (index + 1)] = wave.astype(jnp.float32)
+    rim = local[jnp.bitwise_xor(chip, near)][:, 0 : padded.shape[1] - length]
+    padded[0:channels, length:] = jnp.where(core == 0, rim.astype(jnp.float32), 0.0)
 
     @pl.loop(0, 4)
     def _(part):
@@ -197,8 +199,8 @@
         left_r[channel, :, LANES:] = (value - high.astype(jnp.float32)).astype(jnp.bfloat16)
 
 
-def prepare_waves(tlen, rim, local):
-    chips, _, channels, samples = local.shape
+def prepare_waves(tlen, swapped, local):
+    chips, channels, samples = local.shape
     length = chips * samples
     out = jax.ShapeDtypeStruct((channels, length // OFFSETS, DEPTH), jnp.bfloat16)
     return pl.pallas_call(
@@ -213,7 +215,7 @@
         compiler_params=params(),
         cost_estimate=cost(7),
         name="prepare_waves",
-    )(rim, local)
+    )(swapped, local)
 
 
 def main_kernel(side, tlen, group, piece, left_a, left_r, *rest):
@@ -229,7 +231,6 @@
     banks = (half + 1) // slots
     offset_count = LANES // group
     tile_count = OFFSETS // offset_count
-    code_lane = (half % slots) * group
     top = 112 + 8 * (7 + offset_count - 1)
     top = top + top % 16
 
@@ -243,19 +244,45 @@
         expand[:, slot * LANES : (slot + 1) * LANES] = chosen.astype(jnp.bfloat16)
     turned = []
     for index in range(banks):
-        values = piece[slots * index : slots * (index + 1)].astype(jnp.float32)
-        values = values.reshape(LANES, tlen)
-        values = jnp.concatenate([values, jnp.zeros((LANES, LANES - tlen), jnp.float32)], axis=1)
-        turned.append(values.T)
-    codes = turned[-1]
-    for index, values in enumerate(turned):
-        code = jnp.zeros((1, LANES), jnp.float32)
-        for slot in range(slots):
-            item = slots * index + slot
-            if item < half:
-                moved = pltpu.roll(codes[item : item + 1, :], (group * slot - code_lane) % LANES, 1)
-                code = jnp.where(ahead == slot, moved, code)
-        center = jnp.sum(jnp.where(used, values, 0.0), axis=0, keepdims=True) / tlen
+        count = min(slots, max(TILES - slots * index, 0))
+        values = jnp.zeros((LANES, LANES), jnp.float32)
+        if count:
+            values = piece[slots * index : slots * index + count].astype(jnp.float32)
+            values = values.reshape(count * group, LANES)
+            if count < slots:
+                gap = jnp.zeros((LANES - count * group, LANES), jnp.float32)
+                values = jnp.concatenate([values, gap], axis=0)
+            values = values.T
+        turned.append(values)
+    codes = [values[125:126, :] for values in turned]
+    heads = [jnp.where(used, values, 0.0) for values in turned]
+    for extra in range(half - TILES):
+        place, slot = divmod(TILES + extra, slots)
+        mask = ahead == slot
+        code = pltpu.roll(turned[0][126:127, :], (slot - extra) * group % LANES, 1)
+        codes[place] = jnp.where(mask, code, codes[place])
+        for quarter in range(4):
+            source, lanes = divmod(4 * extra + quarter, slots)
+            values = turned[source][96:128]
+            rows = lag[96:128]
+            inside = jnp.logical_and(rows >= tlen, rows < tlen + QUARTER)
+            values = jnp.where(inside, values, 0.0)
+            values = pltpu.roll(values, (slot - lanes) * group % LANES, 1)
+            start = QUARTER * quarter - (tlen - 96)
+            values = jnp.concatenate([values, jnp.zeros((8, LANES), jnp.float32)], axis=0)
+            values = pltpu.roll(values, start % 8, 0)
+            start -= start % 8
+            if start < 0:
+                values, start = values[8:], 0
+            below = LANES - start - values.shape[0]
+            if start:
+                values = jnp.concatenate([jnp.zeros((start, LANES), jnp.float32), values], axis=0)
+            if below > 0:
+                values = jnp.concatenate([values, jnp.zeros((below, LANES), jnp.float32)], axis=0)
+            heads[place] = heads[place] + jnp.where(mask, values[0:LANES], 0.0)
+    for index, (values, code) in enumerate(zip(heads, codes)):
+        code = jnp.where(slots * index + ahead < half, code, 0.0)
+        center = jnp.sum(values, axis=0, keepdims=True) / tlen
         deviate = jnp.where(used, values - center, 0.0)
         spread = jnp.sqrt(jnp.sum(deviate * deviate, axis=0, keepdims=True) / tlen + EPSILON)
         unit = (deviate / (spread * tlen)).astype(jnp.bfloat16).astype(jnp.float32)
@@ -332,7 +359,7 @@
         )
 
 
-def correlate(side, group, count, piece, left_a, left_r, *before):
+def correlate(side, tlen, group, count, piece, left_a, left_r, *before):
     channels, rows, _ = left_a.shape
     width = OFFSETS * group
     half = channels // 2
@@ -341,7 +368,7 @@
     else:
         out = [jax.ShapeDtypeStruct((rows, width), jnp.float32)]
     return pl.pallas_call(
-        functools.partial(main_kernel, side, piece.shape[2], group),
+        functools.partial(main_kernel, side, tlen, group),
         out_shape=out,
         in_specs=[VMEM] * (3 + len(before)),
         out_specs=[VMEM] * len(out),
@@ -423,7 +450,6 @@
     near = chips // 2
     group = 2 * events // chips
     me = lax.axis_index("tm").astype(jnp.int32)
-    station = lax.axis_index("sta").astype(jnp.int32)
     chip, core = me // 2, me % 2
 
     def swap(array):
@@ -432,10 +458,7 @@
     def across(array, step):
         return lax.ppermute(array, "tm", [(i, i ^ (2 * step)) for i in range(count_tm)])
 
-    def spread(array, step):
-        route = [(2 * z + z // near, 2 * (z ^ step) + z // near) for z in range(chips)]
-        return lax.ppermute(array, "tm", route)
-
+    local = jnp.stack([waveforms] + [across(waveforms, step) for step in range(1, chips)])
     mine, theirs = pack(
         chips,
         group,
@@ -444,39 +467,34 @@
         jnp.transpose(available, (2, 0, 1)),
         jnp.transpose(moveout, (2, 0, 1)),
     )
-    waveforms, theirs = lax.optimization_barrier((waveforms, theirs))
-    paired = swap(waveforms)
     other = swap(theirs)
-    both = jnp.where(
-        core == 0, jnp.stack([waveforms, paired]), jnp.stack([paired, waveforms])
-    )
-    far = [spread(both, step) for step in range(near, chips)]
-    local = jnp.stack([both] + [spread(both, step) for step in range(1, near)] + far)
     other, local = lax.optimization_barrier((other, local))
     merged = merge(blocks, bank_blocks, mine, other)
     pieces = [merged[0]] + [across(merged[step], step) for step in range(1, chips)]
 
-    rim = lax.dynamic_index_in_dim(local, chip ^ near, 0, keepdims=False)[0, :, : 2 * LANES]
-    rim = lax.ppermute(rim, "tm", [(2 * z + 1, 2 * z) for z in range(chips)])
-    left_a, left_r = prepare_waves(tlen, rim, local)
+    wanted = [
+        lax.dynamic_index_in_dim(local, chip ^ (near * (1 - core) + step), 0, keepdims=False)
+        for step in range(near)
+    ]
+    swapped = swap(jnp.stack(wanted))
+    left_a, left_r = prepare_waves(tlen, swapped, local)
 
     left_a, left_r, *pieces = lax.optimization_barrier((left_a, left_r, *pieces))
-    owner = jnp.where(chip ^ station < near, bank_blocks[0], bank_blocks[1]) // blocks
+    owner = jnp.where(chip < near, bank_blocks[0], bank_blocks[1]) // blocks
     source = (owner // 2) ^ chip
     first = pieces[0]
     for step in range(1, chips):
         first = jnp.where(source == step, pieces[step], first)
     second = swap(first)
-    total = correlate(0, group, near, first, left_a, left_r)
-    parts = correlate(1, group, near, second, left_a, left_r, *total)
+    total = correlate(0, tlen, group, near, first, left_a, left_r)
+    parts = correlate(1, tlen, group, near, second, left_a, left_r, *total)
     gathered = []
     for step in range(near):
         route = []
         for d in range(count_tm):
             for s in range(count_sta):
                 dest = near * (d % 2) + (s % near ^ step)
-                sta = d // 2 ^ s
-                route.append((d * count_sta + s, (2 * dest + s // near) * count_sta + sta))
+                route.append((d * count_sta + s, (2 * dest + s // near) * count_sta + d // 2))
         gathered.append(lax.ppermute(parts[step], ("tm", "sta"), route))
     ours, send = add(gathered)
     return finish(group, samples, ours, swap(send))

time: 57.5 us -> 43.5 us (0.76)
  the two profiles are of different devices: /device:TPU:0 before, /device:TPU:7 now
where the time goes in v6:
time: 43.5 us; the launch traced here: 43.4 us
  starting transfers between devices  18.3 us (42%)
  Pallas kernels  16.1 us (37%)
  waiting for transfers between devices  6.96 us (16%)
  between operations  1.4 us (3%)
  local copies, waits for them, and re-layouts  0.6 us (1%)
    ppermute x6, starting transfers between devices, across(): lax.ppermute(array, 'tm', [(i, i ^ 2 * step) for i in range(count_tm)])  7.23 us
    pallas_call x1, Pallas kernels, prepare_waves(): pl.pallas_call(functools.partial(waves_kernel, channels, tlen), out_shape...  6.19 us
    ppermute x4, starting transfers between devices, swap(): return lax.ppermute(array, 'tm', [(i, i ^ 1) for i in range(count_tm)])  6.06 us
    pallas_call x2, Pallas kernels, correlate(): pl.pallas_call(functools.partial(main_kernel, side, tlen, group), out_sha...  5.81 us
    ppermute x2, starting transfers between devices, shards(): gathered.append(lax.ppermute(parts[step], ('tm', 'sta'), route))  5 us
    ppermute x2, waiting for transfers between devices, shards(): gathered.append(lax.ppermute(parts[step], ('tm', 'sta'), route))  4.01 us
    pallas_call x1, Pallas kernels, pack(): pl.pallas_call(pack_kernel, out_shape=[jax.ShapeDtypeStruct(shape, jnp.bf...  2.48 us
    ppermute x6, waiting for transfers between devices, across(): lax.ppermute(array, 'tm', [(i, i ^ 2 * step) for i in range(count_tm)])  2.05 us
  transfers between devices with their start and end apart: 12, of which 5 were waited for; matrix products, arithmetic and copies ran while one was open for 1% of the time, Pallas kernels for 22%

profile of v6, /device:TPU:7, one launch (start us, length us, event | category | flops | bytes accessed | tf_op | source)
XLA Modules:
  0.0 43.4 jit_solution(12636272005226872434)
XLA Ops:
  0.0 0.0 copy-start
  0.0 0.0 copy-start.1
  0.0 2.5 %pack.1 = (bf16[4,12,32,128]{3,2,1,0:T(8,128)(2,1)S(1)}, bf16[4,12,32,128]{3,2,1,0:T(8,128)(2,1)S(1)}) custom-call(s32[2]{0:T(128)} %bank_blocks.3, bf16[2,30,64,100]{3,2,1,0:T(8,128)(2,1)} %bitcast.13, s32[30,2,64]{2,1,0:T(2,128)} %bitcast.14, s32[30,2,64]{2,1,0:T(2,128)} %bitcast.15), custom_call_target="tpu_custom_call" | custom-call | flops 2000000000 | bytes 2000000 | tf_op jit(solution)/shard_map/pack/pallas_call | solution.py:88
  2.5 0.7 %collective-permute-start = (bf16[4,12,32,128]{3,2,1,0:T(8,128)(2,1)S(1)}, bf16[4,12,32,128]{3,2,1,0:T(8,128)(2,1)S(1)}, u32[]{:S(2)}, u32[]{:S(2)}) collective-permute-start(bf16[4,12,32,128]{3,2,1,0:T(8,128)(2,1)S(1)} %get-tuple-element.25), channel_id=1, source_target_pairs={{0,4},{4,0},{8,12},{12,8},{16,20},{20,16},{24,28},{28,24},{1,5},{5... | collective-permute-start | bytes 1179656 | tf_op jit(solution)/shard_map/ppermute | solution.py:456
  3.2 0.0 copy-done.1
  3.2 1.3 %collective-permute-start.1 = (bf16[30,512]{1,0:T(8,128)(2,1)S(1)}, bf16[30,512]{1,0:T(8,128)(2,1)S(1)}, u32[]{:S(2)}, u32[]{:S(2)}) collective-permute-start(bf16[30,512]{1,0:T(8,128)(2,1)S(1)} %copy-done.1), channel_id=1, source_target_pairs={{0,8},{4,12},{8,0},{12,4},{16,24},{20,28},{24,16},{28,20},{1,9},{5... | collective-permute-start | bytes 92168 | tf_op jit(solution)/shard_map/ppermute | solution.py:459
  4.5 2.2 %collective-permute-start.3 = (bf16[30,512]{1,0:T(8,128)(2,1)S(1)}, bf16[30,512]{1,0:T(8,128)(2,1)S(1)}, u32[]{:S(2)}, u32[]{:S(2)}) collective-permute-start(bf16[30,512]{1,0:T(8,128)(2,1)S(1)} %copy-done.1), channel_id=1, source_target_pairs={{0,24},{4,28},{8,16},{12,20},{16,8},{20,12},{24,0},{28,4},{1,25},{... | collective-permute-start | bytes 92168 | tf_op jit(solution)/shard_map/ppermute | solution.py:459
  6.7 0.1 collective-permute-start.2
  6.9 0.0 copy-done
  6.9 0.6 %fusion = (s32[1]{0:T(128)}, s32[1]{0:T(128)}) fusion(s32[2]{0:T(128)S(1)} %copy-done), kind=kLoop, calls=%fused_computation.5 | loop fusion | bytes 16 | tf_op jit(solution)/shard_map/slice | solution.py:483
  8.7 0.0 collective-permute-done.1
  8.7 0.4 collective-permute-done.3
  9.1 1.6 %collective-permute-done.2 = bf16[30,512]{1,0:T(8,128)(2,1)S(1)} collective-permute-done((bf16[30,512]{1,0:T(8,128)(2,1)S(1)}, bf16[30,512]{1,0:T(8,128)(2,1)S(1)}, u32[]{:S(2)}, u32[]{:S(2)}) %collective-permute-start.2) | collective-permute-done | bytes 30752 | tf_op jit(solution)/shard_map/ppermute | solution.py:459
  10.8 0.0 collective-permute-done.other
  10.8 1.8 %collective-permute-start.4 = (bf16[2,30,512]{2,1,0:T(8,128)(2,1)S(1)}, bf16[2,30,512]{2,1,0:T(8,128)(2,1)S(1)}, u32[]{:S(2)}, u32[]{:S(2)}) collective-permute-start(bf16[2,30,512]{2,1,0:T(8,128)(2,1)S(1)} %pad_maximum_fusion.1), channel_id=1, source_target_pairs={{0,4},{4,0},{8,12},{12,8},{16,20},{20,16},{24,28},{28,24},{1,5},{5... | collective-permute-start | bytes 184328 | tf_op jit(solution)/shard_map/ppermute | solution.py:456
  12.7 0.7 %merge.1 = (bf16[12,32,128]{2,1,0:T(8,128)(2,1)S(1)}, bf16[12,32,128]{2,1,0:T(8,128)(2,1)S(1)}, bf16[12,32,128]{2,1,0:T(8,128)(2,1)S(1)}, bf16[12,32,128]{2,1,0:T(8,128)(2,1)S(1)}) custom-call(s32[2]{0:T(128)S(1)} %copy-done, bf16[4,12,32,128]{3,2,1,0:T(8,128)(2,1)S(1)} %get-tuple-element.29.mine, bf16[4,12,32,128]{3,2,1,0:T(8,128)(2,1)S(1)} %collective-permute-done.other), custom_call_target="tpu_custom_call" | custom-call | flops 1000000000 | bytes 1000000 | tf_op jit(solution)/shard_map/merge/pallas_call | solution.py:127
  13.4 0.2 collective-permute-start.5
  13.6 1.7 %collective-permute-start.6 = (bf16[12,32,128]{2,1,0:T(8,128)(2,1)S(1)}, bf16[12,32,128]{2,1,0:T(8,128)(2,1)S(1)}, u32[]{:S(2)}, u32[]{:S(2)}) collective-permute-start(bf16[12,32,128]{2,1,0:T(8,128)(2,1)S(1)} %get-tuple-element.33), channel_id=1, source_target_pairs={{0,16},{4,20},{8,24},{12,28},{16,0},{20,4},{24,8},{28,12},{1,17},{... | collective-permute-start | bytes 294920 | tf_op jit(solution)/shard_map/ppermute | solution.py:459
  15.3 1.7 %collective-permute-start.7 = (bf16[12,32,128]{2,1,0:T(8,128)(2,1)S(1)}, bf16[12,32,128]{2,1,0:T(8,128)(2,1)S(1)}, u32[]{:S(2)}, u32[]{:S(2)}) collective-permute-start(bf16[12,32,128]{2,1,0:T(8,128)(2,1)S(1)} %get-tuple-element.34), channel_id=1, source_target_pairs={{0,24},{4,28},{8,16},{12,20},{16,8},{20,12},{24,0},{28,4},{1,25},{... | collective-permute-start | bytes 294920 | tf_op jit(solution)/shard_map/ppermute | solution.py:459
  17.0 0.0 collective-permute-done.4.swapped
  17.0 6.2 %prepare_waves.1 = (bf16[30,256,256]{2,1,0:T(8,128)(2,1)S(1)}, bf16[30,256,256]{2,1,0:T(8,128)(2,1)S(1)}) custom-call(bf16[2,30,512]{2,1,0:T(8,128)(2,1)S(1)} %collective-permute-done.4.swapped, bf16[4,30,512]{2,1,0:T(8,128)(2,1)S(1)} %pad_maximum_fusion.local), custom_call_target="tpu_custom_call" | custom-call | flops 7000000000 | bytes 7000000 | tf_op jit(solution)/shard_map/prepare_waves/pallas_call | solution.py:206
  23.2 0.0 collective-permute-done.5
  23.2 0.0 collective-permute-done.6
  23.2 0.0 collective-permute-done.7
  23.2 1.5 %collective-permute-start.8 = (bf16[12,32,128]{2,1,0:T(8,128)(2,1)S(1)}, bf16[12,32,128]{2,1,0:T(8,128)(2,1)S(1)}, u32[]{:S(2)}, u32[]{:S(2)}) collective-permute-start(bf16[12,32,128]{2,1,0:T(8,128)(2,1)S(1)} %select_select_fusion.piece), channel_id=1, source_target_pairs={{0,4},{4,0},{8,12},{12,8},{16,20},{20,16},{24,28},{28,24},{1,5},{5... | collective-permute-start | bytes 294920 | tf_op jit(solution)/shard_map/ppermute | solution.py:456
  24.7 2.9 %correlate_first.1.rest_0_ = f32[256,256]{1,0:T(8,128)S(1)} custom-call(bf16[12,32,128]{2,1,0:T(8,128)(2,1)S(1)} %select_select_fusion.piece, bf16[30,256,256]{2,1,0:T(8,128)(2,1)S(1)} %get-tuple-element.39.left_a, bf16[30,256,256]{2,1,0:T(8,128)(2,1)S(1)} %get-tuple-element.40.left_r), custom_call_target="tpu_custom_call" | custom-call | flops 3000000000 | bytes 3000000 | tf_op jit(solution)/shard_map/correlate_first/pallas_call | solution.py:370
  27.6 0.0 collective-permute-done.8.piece
  27.6 2.9 %correlate_second.1 = (bf16[128,256]{1,0:T(8,128)(2,1)S(1)}, bf16[128,256]{1,0:T(8,128)(2,1)S(1)}) custom-call(bf16[12,32,128]{2,1,0:T(8,128)(2,1)S(1)} %collective-permute-done.8.piece, bf16[30,256,256]{2,1,0:T(8,128)(2,1)S(1)} %get-tuple-element.39.left_a, bf16[30,256,256]{2,1,0:T(8,128)(2,1)S(1)} %get-tuple-element.40.left_r, ...), custom_call_target="tpu_custom_call" | custom-call | flops 3000000000 | bytes 3000000 | tf_op jit(solution)/shard_map/correlate_second/pallas_call | solution.py:370
  30.6 3.2 %collective-permute-start.9 = (bf16[128,256]{1,0:T(8,128)(2,1)S(1)}, bf16[128,256]{1,0:T(8,128)(2,1)S(1)}, u32[]{:S(2)}, u32[]{:S(2)}) collective-permute-start(bf16[128,256]{1,0:T(8,128)(2,1)S(1)} %get-tuple-element.41), channel_id=1, source_target_pairs={{0,0},{1,8},{2,4},{3,12},{4,16},{5,24},{6,20},{7,28},{8,1},{9,9},{... | collective-permute-start | bytes 196616 | tf_op jit(solution)/shard_map/ppermute | solution.py:498
  33.7 1.8 %collective-permute-start.10 = (bf16[128,256]{1,0:T(8,128)(2,1)S(1)}, bf16[128,256]{1,0:T(8,128)(2,1)S(1)}, u32[]{:S(2)}, u32[]{:S(2)}) collective-permute-start(bf16[128,256]{1,0:T(8,128)(2,1)S(1)} %get-tuple-element.42), channel_id=1, source_target_pairs={{0,8},{1,0},{2,12},{3,4},{4,24},{5,16},{6,28},{7,20},{8,9},{9,1},{... | collective-permute-start | bytes 196616 | tf_op jit(solution)/shard_map/ppermute | solution.py:498
  35.6 3.4 %collective-permute-done.9.refs_0_ = bf16[128,256]{1,0:T(8,128)(2,1)S(1)} collective-permute-done((bf16[128,256]{1,0:T(8,128)(2,1)S(1)}, bf16[128,256]{1,0:T(8,128)(2,1)S(1)}, u32[]{:S(2)}, u32[]{:S(2)}) %collective-permute-start.9) | collective-permute-done | bytes 65568 | tf_op jit(solution)/shard_map/ppermute | solution.py:498
  38.9 0.6 %collective-permute-done.10.refs_1_ = bf16[128,256]{1,0:T(8,128)(2,1)S(1)} collective-permute-done((bf16[128,256]{1,0:T(8,128)(2,1)S(1)}, bf16[128,256]{1,0:T(8,128)(2,1)S(1)}, u32[]{:S(2)}, u32[]{:S(2)}) %collective-permute-start.10) | collective-permute-done | bytes 65568 | tf_op jit(solution)/shard_map/ppermute | solution.py:498
  39.6 2.0 %collective-permute-start.11 = (f32[64,256]{1,0:T(8,128)S(1)}, f32[64,256]{1,0:T(8,128)S(1)}, u32[]{:S(2)}, u32[]{:S(2)}) collective-permute-start(f32[64,256]{1,0:T(8,128)S(1)} %get-tuple-element.44), channel_id=1, source_target_pairs={{0,4},{4,0},{8,12},{12,8},{16,20},{20,16},{24,28},{28,24},{1,5},{5... | collective-permute-start | bytes 196616 | tf_op jit(solution)/shard_map/ppermute | solution.py:456
  41.6 0.9 %collective-permute-done.11.received = f32[64,256]{1,0:T(8,128)S(1)} collective-permute-done((f32[64,256]{1,0:T(8,128)S(1)}, f32[64,256]{1,0:T(8,128)S(1)}, u32[]{:S(2)}, u32[]{:S(2)}) %collective-permute-start.11) | collective-permute-done | bytes 65568 | tf_op jit(solution)/shard_map/ppermute | solution.py:456
  42.5 0.9 %finish.1 = f32[32,512]{1,0:T(8,128)} custom-call(f32[64,256]{1,0:T(8,128)S(1)} %get-tuple-element.43.ours, f32[64,256]{1,0:T(8,128)S(1)} %collective-permute-done.11.received), custom_call_target="tpu_custom_call" | custom-call | flops 1000000000 | bytes 1000000 | tf_op jit(solution)/shard_map/finish/pallas_call | solution.py:433
  (5 shorter events, 0.1 us)
Async XLA Ops:
  0.0 6.9 %copy-start = (s32[2]{0:T(128)S(1)}, s32[2]{0:T(128)}, u32[]{:S(2)}) copy-start(s32[2]{0:T(128)} %bank_blocks.3) | copy-start | bytes 28
  0.0 3.2 %copy-start.1 = (bf16[30,512]{1,0:T(8,128)(2,1)S(1)}, bf16[30,512]{1,0:T(8,128)(2,1)}, u32[]{:S(2)}) copy-start(bf16[30,512]{1,0:T(8,128)(2,1)} %param.5) | copy-start | bytes 92164
  2.5 8.3 %collective-permute-start = (bf16[4,12,32,128]{3,2,1,0:T(8,128)(2,1)S(1)}, bf16[4,12,32,128]{3,2,1,0:T(8,128)(2,1)S(1)}, u32[]{:S(2)}, u32[]{:S(2)}) collective-permute-start(bf16[4,12,32,128]{3,2,1,0:T(8,128)(2,1)S(1)} %get-tuple-element.25), channel_id=1, source_target_pairs={{0,4},{4,0},{8,12},{12,8},{16,20},{20,16},{24,28},{28,24},{1,5},{5... | collective-permute-start | bytes 1179656 | tf_op jit(solution)/shard_map/ppermute | solution.py:456
  3.2 5.5 %collective-permute-start.1 = (bf16[30,512]{1,0:T(8,128)(2,1)S(1)}, bf16[30,512]{1,0:T(8,128)(2,1)S(1)}, u32[]{:S(2)}, u32[]{:S(2)}) collective-permute-start(bf16[30,512]{1,0:T(8,128)(2,1)S(1)} %copy-done.1), channel_id=1, source_target_pairs={{0,8},{4,12},{8,0},{12,4},{16,24},{20,28},{24,16},{28,20},{1,9},{5... | collective-permute-start | bytes 92168 | tf_op jit(solution)/shard_map/ppermute | solution.py:459
  4.5 4.6 %collective-permute-start.3 = (bf16[30,512]{1,0:T(8,128)(2,1)S(1)}, bf16[30,512]{1,0:T(8,128)(2,1)S(1)}, u32[]{:S(2)}, u32[]{:S(2)}) collective-permute-start(bf16[30,512]{1,0:T(8,128)(2,1)S(1)} %copy-done.1), channel_id=1, source_target_pairs={{0,24},{4,28},{8,16},{12,20},{16,8},{20,12},{24,0},{28,4},{1,25},{... | collective-permute-start | bytes 92168 | tf_op jit(solution)/shard_map/ppermute | solution.py:459
  6.7 4.0 %collective-permute-start.2 = (bf16[30,512]{1,0:T(8,128)(2,1)S(1)}, bf16[30,512]{1,0:T(8,128)(2,1)S(1)}, u32[]{:S(2)}, u32[]{:S(2)}) collective-permute-start(bf16[30,512]{1,0:T(8,128)(2,1)S(1)} %copy-done.1), channel_id=1, source_target_pairs={{0,16},{4,20},{8,24},{12,28},{16,0},{20,4},{24,8},{28,12},{1,17},{... | collective-permute-start | bytes 92168 | tf_op jit(solution)/shard_map/ppermute | solution.py:459
  10.8 6.1 %collective-permute-start.4 = (bf16[2,30,512]{2,1,0:T(8,128)(2,1)S(1)}, bf16[2,30,512]{2,1,0:T(8,128)(2,1)S(1)}, u32[]{:S(2)}, u32[]{:S(2)}) collective-permute-start(bf16[2,30,512]{2,1,0:T(8,128)(2,1)S(1)} %pad_maximum_fusion.1), channel_id=1, source_target_pairs={{0,4},{4,0},{8,12},{12,8},{16,20},{20,16},{24,28},{28,24},{1,5},{5... | collective-permute-start | bytes 184328 | tf_op jit(solution)/shard_map/ppermute | solution.py:456
  13.4 9.8 %collective-permute-start.5 = (bf16[12,32,128]{2,1,0:T(8,128)(2,1)S(1)}, bf16[12,32,128]{2,1,0:T(8,128)(2,1)S(1)}, u32[]{:S(2)}, u32[]{:S(2)}) collective-permute-start(bf16[12,32,128]{2,1,0:T(8,128)(2,1)S(1)} %get-tuple-element.32), channel_id=1, source_target_pairs={{0,8},{4,12},{8,0},{12,4},{16,24},{20,28},{24,16},{28,20},{1,9},{5... | collective-permute-start | bytes 294920 | tf_op jit(solution)/shard_map/ppermute | solution.py:459
  13.6 9.6 %collective-permute-start.6 = (bf16[12,32,128]{2,1,0:T(8,128)(2,1)S(1)}, bf16[12,32,128]{2,1,0:T(8,128)(2,1)S(1)}, u32[]{:S(2)}, u32[]{:S(2)}) collective-permute-start(bf16[12,32,128]{2,1,0:T(8,128)(2,1)S(1)} %get-tuple-element.33), channel_id=1, source_target_pairs={{0,16},{4,20},{8,24},{12,28},{16,0},{20,4},{24,8},{28,12},{1,17},{... | collective-permute-start | bytes 294920 | tf_op jit(solution)/shard_map/ppermute | solution.py:459
  15.3 7.9 %collective-permute-start.7 = (bf16[12,32,128]{2,1,0:T(8,128)(2,1)S(1)}, bf16[12,32,128]{2,1,0:T(8,128)(2,1)S(1)}, u32[]{:S(2)}, u32[]{:S(2)}) collective-permute-start(bf16[12,32,128]{2,1,0:T(8,128)(2,1)S(1)} %get-tuple-element.34), channel_id=1, source_target_pairs={{0,24},{4,28},{8,16},{12,20},{16,8},{20,12},{24,0},{28,4},{1,25},{... | collective-permute-start | bytes 294920 | tf_op jit(solution)/shard_map/ppermute | solution.py:459
  23.2 4.4 %collective-permute-start.8 = (bf16[12,32,128]{2,1,0:T(8,128)(2,1)S(1)}, bf16[12,32,128]{2,1,0:T(8,128)(2,1)S(1)}, u32[]{:S(2)}, u32[]{:S(2)}) collective-permute-start(bf16[12,32,128]{2,1,0:T(8,128)(2,1)S(1)} %select_select_fusion.piece), channel_id=1, source_target_pairs={{0,4},{4,0},{8,12},{12,8},{16,20},{20,16},{24,28},{28,24},{1,5},{5... | collective-permute-start | bytes 294920 | tf_op jit(solution)/shard_map/ppermute | solution.py:456
  30.6 8.4 %collective-permute-start.9 = (bf16[128,256]{1,0:T(8,128)(2,1)S(1)}, bf16[128,256]{1,0:T(8,128)(2,1)S(1)}, u32[]{:S(2)}, u32[]{:S(2)}) collective-permute-start(bf16[128,256]{1,0:T(8,128)(2,1)S(1)} %get-tuple-element.41), channel_id=1, source_target_pairs={{0,0},{1,8},{2,4},{3,12},{4,16},{5,24},{6,20},{7,28},{8,1},{9,9},{... | collective-permute-start | bytes 196616 | tf_op jit(solution)/shard_map/ppermute | solution.py:498
  33.7 5.8 %collective-permute-start.10 = (bf16[128,256]{1,0:T(8,128)(2,1)S(1)}, bf16[128,256]{1,0:T(8,128)(2,1)S(1)}, u32[]{:S(2)}, u32[]{:S(2)}) collective-permute-start(bf16[128,256]{1,0:T(8,128)(2,1)S(1)} %get-tuple-element.42), channel_id=1, source_target_pairs={{0,8},{1,0},{2,12},{3,4},{4,24},{5,16},{6,28},{7,20},{8,9},{9,1},{... | collective-permute-start | bytes 196616 | tf_op jit(solution)/shard_map/ppermute | solution.py:498
  39.6 2.9 %collective-permute-start.11 = (f32[64,256]{1,0:T(8,128)S(1)}, f32[64,256]{1,0:T(8,128)S(1)}, u32[]{:S(2)}, u32[]{:S(2)}) collective-permute-start(f32[64,256]{1,0:T(8,128)S(1)} %get-tuple-element.44), channel_id=1, source_target_pairs={{0,4},{4,0},{8,12},{12,8},{16,20},{20,16},{24,28},{28,24},{1,5},{5... | collective-permute-start | bytes 196616 | tf_op jit(solution)/shard_map/ppermute | solution.py:456

commit v7 on v6

--- a/solution.py
+++ b/solution.py
@@ -153,8 +153,58 @@
     return pltpu.roll(copies, row.shape[1] - 7 - ahead, 1, stride=1, stride_axis=0)
 
 
-def waves_kernel(channels, tlen, swapped, local, left_a, left_r, padded, inverse):
-    chips, _, samples = local.shape
+def pick(arrays, index):
+    value = arrays[0][...]
+    for number, array in enumerate(arrays[1:], 1):
+        value = jnp.where(index == number, array[...], value)
+    return value
+
+
+def choose_kernel(near, *refs):
+    waves, out = refs[:-1], refs[-1]
+    me = lax.axis_index("tm")
+    for step in range(near):
+        out[step] = pick(waves, jnp.bitwise_xor(me // 2, near * (1 - me % 2) + step))
+
+
+def choose_waves(waves):
+    near = len(waves) // 2
+    return pl.pallas_call(
+        functools.partial(choose_kernel, near),
+        out_shape=jax.ShapeDtypeStruct((near,) + waves[0].shape, waves[0].dtype),
+        in_specs=[VMEM] * len(waves),
+        out_specs=VMEM,
+        compiler_params=params(),
+        cost_estimate=cost(0.3),
+        name="choose_waves",
+    )(*waves)
+
+
+def own_kernel(blocks, bank_blocks, *refs):
+    pieces, out = refs[:-1], refs[-1]
+    chip = lax.axis_index("tm") // 2
+    first = chip < len(pieces) // 2
+    owner = jnp.where(first, bank_blocks[0], bank_blocks[1]) // blocks
+    out[...] = pick(pieces, jnp.bitwise_xor(owner // 2, chip))
+
+
+def choose_piece(blocks, bank_blocks, pieces):
+    return pl.pallas_call(
+        functools.partial(own_kernel, blocks),
+        out_shape=jax.ShapeDtypeStruct(pieces[0].shape, pieces[0].dtype),
+        in_specs=[SMEM] + [VMEM] * len(pieces),
+        out_specs=VMEM,
+        compiler_params=params(),
+        cost_estimate=cost(0.3),
+        name="choose_piece",
+    )(bank_blocks, *pieces)
+
+
+def waves_kernel(channels, tlen, swapped, *rest):
+    local = rest[:-4]
+    left_a, left_r, padded, inverse = rest[-4:]
+    chips = len(local)
+    samples = local[0].shape[1]
     near = chips // 2
     length = chips * samples
     steps = length // STRIDE
@@ -162,10 +212,10 @@
     chip, core = me // 2, me % 2
     padded[...] = jnp.zeros_like(padded)
     for index in range(chips):
-        source = jnp.bitwise_xor(chip, near * core + index // 2)
-        wave = jnp.where(core == index % 2, local[source], swapped[index // 2])
+        wave = pick(local, jnp.bitwise_xor(chip, near * core + index // 2))
+        wave = jnp.where(core == index % 2, wave, swapped[index // 2])
         padded[0:channels, samples * index : samples * (index + 1)] = wave.astype(jnp.float32)
-    rim = local[jnp.bitwise_xor(chip, near)][:, 0 : padded.shape[1] - length]
+    rim = pick(local, jnp.bitwise_xor(chip, near))[:, 0 : padded.shape[1] - length]
     padded[0:channels, length:] = jnp.where(core == 0, rim.astype(jnp.float32), 0.0)
 
     @pl.loop(0, 4)
@@ -200,22 +250,22 @@
 
 
 def prepare_waves(tlen, swapped, local):
-    chips, channels, samples = local.shape
-    length = chips * samples
+    channels, samples = local[0].shape
+    length = len(local) * samples
     out = jax.ShapeDtypeStruct((channels, length // OFFSETS, DEPTH), jnp.bfloat16)
     return pl.pallas_call(
         functools.partial(waves_kernel, channels, tlen),
         out_shape=[out, out],
-        in_specs=[VMEM, VMEM],
+        in_specs=[VMEM] * (1 + len(local)),
         out_specs=[VMEM, VMEM],
         scratch_shapes=[
             pltpu.VMEM((32, length + 2 * LANES), jnp.float32),
             pltpu.VMEM((32, length + 2 * LANES), jnp.float32),
         ],
         compiler_params=params(),
-        cost_estimate=cost(7),
+        cost_estimate=cost(0.05),
         name="prepare_waves",
-    )(swapped, local)
+    )(swapped, *local)
 
 
 def main_kernel(side, tlen, group, piece, left_a, left_r, *rest):
@@ -449,8 +499,6 @@
     chips = count_tm // 2
     near = chips // 2
     group = 2 * events // chips
-    me = lax.axis_index("tm").astype(jnp.int32)
-    chip, core = me // 2, me % 2
 
     def swap(array):
         return lax.ppermute(array, "tm", [(i, i ^ 1) for i in range(count_tm)])
@@ -458,7 +506,7 @@
     def across(array, step):
         return lax.ppermute(array, "tm", [(i, i ^ (2 * step)) for i in range(count_tm)])
 
-    local = jnp.stack([waveforms] + [across(waveforms, step) for step in range(1, chips)])
+    local = [waveforms] + [across(waveforms, step) for step in range(1, chips)]
     mine, theirs = pack(
         chips,
         group,
@@ -468,23 +516,14 @@
         jnp.transpose(moveout, (2, 0, 1)),
     )
     other = swap(theirs)
-    other, local = lax.optimization_barrier((other, local))
     merged = merge(blocks, bank_blocks, mine, other)
-    pieces = [merged[0]] + [across(merged[step], step) for step in range(1, chips)]
-
-    wanted = [
-        lax.dynamic_index_in_dim(local, chip ^ (near * (1 - core) + step), 0, keepdims=False)
-        for step in range(near)
-    ]
-    swapped = swap(jnp.stack(wanted))
-    left_a, left_r = prepare_waves(tlen, swapped, local)
-
-    left_a, left_r, *pieces = lax.optimization_barrier((left_a, left_r, *pieces))
-    owner = jnp.where(chip < near, bank_blocks[0], bank_blocks[1]) // blocks
-    source = (owner // 2) ^ chip
-    first = pieces[0]
-    for step in range(1, chips):
-        first = jnp.where(source == step, pieces[step], first)
+    pieces = [across(merged[step], step) for step in reversed(range(1, chips))]
+    pieces = [merged[0]] + pieces[::-1]
+    left_a, left_r = prepare_waves(tlen, swap(choose_waves(local)), local)
+
+    left_a, left_r, *pieces = lax.optimization_barrier((left_a, left_r, *pieces[::-1]))
+    pieces = pieces[::-1]
+    first = choose_piece(blocks, bank_blocks, pieces)
     second = swap(first)
     total = correlate(0, tlen, group, near, first, left_a, left_r)
     parts = correlate(1, tlen, group, near, second, left_a, left_r, *total)

time: 43.5 us -> 40 us (0.920)
  starting transfers between devices: 18.3 us -> 15.4 us
  between operations: 1.4 us -> 0.11 us
  waiting for transfers between devices: 6.96 us -> 7.62 us
  Pallas kernels: 16.1 us -> 16.7 us
  local copies, waits for them, and re-layouts: 0.6 us -> 0.01 us
    ppermute x4, starting transfers between devices: 6.06 us -> 2.93 us  [swap(): return lax.ppermute(array, 'tm', [(i, i ^ 1) for i in range(count_tm)])]
    ppermute x6, waiting for transfers between devices: 2.05 us -> 0.02 us  [across(): lax.ppermute(array, 'tm', [(i, i ^ 2 * step) for i in range(count_tm)])]
    ppermute x2, waiting for transfers between devices: 4.01 us -> 5.47 us  [shards(): gathered.append(lax.ppermute(parts[step], ('tm', 'sta'), route))]
    ppermute x4, waiting for transfers between devices: 0.91 us -> 2.13 us  [swap(): return lax.ppermute(array, 'tm', [(i, i ^ 1) for i in range(count_tm)])]
    pallas_call x0 -> x2, Pallas kernels: none -> 0.63 us  [the longest x1 0.61 us: choose_piece(): pl.pallas_call(functools.partial(own_kernel, blocks), out_shape=jax.Shape...]
    slice x1 -> x0, local copies, waits for them, and re-layouts: 0.58 us -> none  [shards(): owner = jnp.where(chip < near, bank_blocks[0], bank_blocks[1]) // blocks]
  transfers between devices with their start and end apart: 12 -> 12, of which waited for: 5 -> 4; matrix products, arithmetic and copies ran while one was open for 1% -> 0% of each run, Pallas kernels for 22% -> 25%
where the time goes in v7:
time: 40 us; the launch traced here: 39.9 us
  Pallas kernels  16.7 us (42%)
  starting transfers between devices  15.4 us (38%)
  waiting for transfers between devices  7.62 us (19%)
    ppermute x6, starting transfers between devices, across(): lax.ppermute(array, 'tm', [(i, i ^ 2 * step) for i in range(count_tm)])  7.31 us
    pallas_call x1, Pallas kernels, prepare_waves(): pl.pallas_call(functools.partial(waves_kernel, channels, tlen), out_shape...  6.2 us
    pallas_call x2, Pallas kernels, correlate(): pl.pallas_call(functools.partial(main_kernel, side, tlen, group), out_sha...  5.81 us
    ppermute x2, waiting for transfers between devices, shards(): gathered.append(lax.ppermute(parts[step], ('tm', 'sta'), route))  5.47 us
    ppermute x2, starting transfers between devices, shards(): gathered.append(lax.ppermute(parts[step], ('tm', 'sta'), route))  5.2 us
    ppermute x4, starting transfers between devices, swap(): return lax.ppermute(array, 'tm', [(i, i ^ 1) for i in range(count_tm)])  2.93 us
    pallas_call x1, Pallas kernels, pack(): pl.pallas_call(pack_kernel, out_shape=[jax.ShapeDtypeStruct(shape, jnp.bf...  2.48 us
    ppermute x4, waiting for transfers between devices, swap(): return lax.ppermute(array, 'tm', [(i, i ^ 1) for i in range(count_tm)])  2.13 us
  transfers between devices with their start and end apart: 12, of which 4 were waited for; matrix products, arithmetic and copies ran while one was open for 0% of the time, Pallas kernels for 25%

profile of v7, /device:TPU:7, one launch (start us, length us, event | category | flops | bytes accessed | tf_op | source)
XLA Modules:
  0.0 39.9 jit_solution(15975432943129885128)
XLA Ops:
  0.0 0.0 copy-start.1
  0.0 0.0 copy-start
  0.0 2.5 %pack.1 = (bf16[4,12,32,128]{3,2,1,0:T(8,128)(2,1)S(1)}, bf16[4,12,32,128]{3,2,1,0:T(8,128)(2,1)S(1)}) custom-call(s32[2]{0:T(128)} %bank_blocks.5, bf16[2,30,64,100]{3,2,1,0:T(8,128)(2,1)} %bitcast.3, s32[30,2,64]{2,1,0:T(2,128)} %bitcast.4, s32[30,2,64]{2,1,0:T(2,128)} %bitcast.5), custom_call_target="tpu_custom_call" | custom-call | flops 2000000000 | bytes 2000000 | tf_op jit(solution)/shard_map/pack/pallas_call | solution.py:88
  2.5 0.7 %collective-permute-start.4 = (bf16[4,12,32,128]{3,2,1,0:T(8,128)(2,1)S(1)}, bf16[4,12,32,128]{3,2,1,0:T(8,128)(2,1)S(1)}, u32[]{:S(2)}, u32[]{:S(2)}) collective-permute-start(bf16[4,12,32,128]{3,2,1,0:T(8,128)(2,1)S(1)} %get-tuple-element.26), channel_id=1, source_target_pairs={{0,4},{4,0},{8,12},{12,8},{16,20},{20,16},{24,28},{28,24},{1,5},{5... | collective-permute-start | bytes 1179656 | tf_op jit(solution)/shard_map/ppermute | solution.py:504
  3.2 0.0 copy-done
  3.2 3.3 %collective-permute-start.2 = (bf16[30,512]{1,0:T(8,128)(2,1)S(1)}, bf16[30,512]{1,0:T(8,128)(2,1)S(1)}, u32[]{:S(2)}, u32[]{:S(2)}) collective-permute-start(bf16[30,512]{1,0:T(8,128)(2,1)S(1)} %copy-done), channel_id=1, source_target_pairs={{0,24},{4,28},{8,16},{12,20},{16,8},{20,12},{24,0},{28,4},{1,25},{... | collective-permute-start | bytes 92168 | tf_op jit(solution)/shard_map/ppermute | solution.py:507
  6.6 0.0 collective-permute-start.1
  6.6 0.3 collective-permute-start
  6.8 0.0 collective-permute-done.4.other
  6.8 0.0 copy-done.1
  6.8 0.7 %merge.1 = (bf16[12,32,128]{2,1,0:T(8,128)(2,1)S(1)}, bf16[12,32,128]{2,1,0:T(8,128)(2,1)S(1)}, bf16[12,32,128]{2,1,0:T(8,128)(2,1)S(1)}, bf16[12,32,128]{2,1,0:T(8,128)(2,1)S(1)}) custom-call(s32[2]{0:T(128)S(1)} %copy-done.1, bf16[4,12,32,128]{3,2,1,0:T(8,128)(2,1)S(1)} %get-tuple-element.25.mine, bf16[4,12,32,128]{3,2,1,0:T(8,128)(2,1)S(1)} %collective-permute-done.4.other), custom_call_target="tpu_custom_call" | custom-call | flops 1000000000 | bytes 1000000 | tf_op jit(solution)/shard_map/merge/pallas_call | solution.py:127
  7.5 3.3 %collective-permute-start.5 = (bf16[12,32,128]{2,1,0:T(8,128)(2,1)S(1)}, bf16[12,32,128]{2,1,0:T(8,128)(2,1)S(1)}, u32[]{:S(2)}, u32[]{:S(2)}) collective-permute-start(bf16[12,32,128]{2,1,0:T(8,128)(2,1)S(1)} %get-tuple-element.27), channel_id=1, source_target_pairs={{0,24},{4,28},{8,16},{12,20},{16,8},{20,12},{24,0},{28,4},{1,25},{... | collective-permute-start | bytes 294920 | tf_op jit(solution)/shard_map/ppermute | solution.py:507
  10.9 0.0 collective-permute-start.6
  10.9 0.0 collective-permute-done.2.refs_3_.rest_3_
  10.9 0.4 collective-permute-start.7
  11.2 0.0 collective-permute-done.1.refs_2_.rest_2_
  11.2 0.0 collective-permute-done.refs_1_.rest_1_
  11.3 1.7 %collective-permute-start.3 = (bf16[2,30,512]{2,1,0:T(8,128)(2,1)S(1)}, bf16[2,30,512]{2,1,0:T(8,128)(2,1)S(1)}, u32[]{:S(2)}, u32[]{:S(2)}) collective-permute-start(bf16[2,30,512]{2,1,0:T(8,128)(2,1)S(1)} %choose_waves.1), channel_id=1, source_target_pairs={{0,4},{4,0},{8,12},{12,8},{16,20},{20,16},{24,28},{28,24},{1,5},{5... | collective-permute-start | bytes 184328 | tf_op jit(solution)/shard_map/ppermute | solution.py:504
  13.0 0.9 %collective-permute-done.3.swapped = bf16[2,30,512]{2,1,0:T(8,128)(2,1)S(1)} collective-permute-done((bf16[2,30,512]{2,1,0:T(8,128)(2,1)S(1)}, bf16[2,30,512]{2,1,0:T(8,128)(2,1)S(1)}, u32[]{:S(2)}, u32[]{:S(2)}) %collective-permute-start.3) | collective-permute-done | bytes 61472 | tf_op jit(solution)/shard_map/ppermute | solution.py:504
  13.9 6.2 %prepare_waves.1 = (bf16[30,256,256]{2,1,0:T(8,128)(2,1)S(1)}, bf16[30,256,256]{2,1,0:T(8,128)(2,1)S(1)}) custom-call(bf16[2,30,512]{2,1,0:T(8,128)(2,1)S(1)} %collective-permute-done.3.swapped, bf16[30,512]{1,0:T(8,128)(2,1)S(1)} %copy-done, bf16[30,512]{1,0:T(8,128)(2,1)S(1)} %collective-permute-done.refs_1_.rest_1_, ...), custom_call_target="tpu_custom_call" | custom-call | flops 50000000 | bytes 50000 | tf_op jit(solution)/shard_map/prepare_waves/pallas_call | solution.py:256
  20.1 0.0 collective-permute-done.5.refs_3_
  20.1 0.0 collective-permute-done.6.refs_2_
  20.1 0.0 collective-permute-done.7.refs_1_
  20.1 0.6 %choose_piece.1.piece = bf16[12,32,128]{2,1,0:T(8,128)(2,1)S(1)} custom-call(s32[2]{0:T(128)S(1)} %copy-done.1, bf16[12,32,128]{2,1,0:T(8,128)(2,1)S(1)} %get-tuple-element.31.refs_0_, bf16[12,32,128]{2,1,0:T(8,128)(2,1)S(1)} %collective-permute-done.7.refs_1_, bf16[12,32,128]{2,1,0:T(8,128)(2,1)S(1)} %collective-permute-done.6.refs_2_, ...), custom_call_target="tpu_custom_call" | custom-call | flops 300000000 | bytes 300000 | tf_op jit(solution)/shard_map/choose_piece/pallas_call | solution.py:192
  20.7 0.4 %collective-permute-start.8 = (bf16[12,32,128]{2,1,0:T(8,128)(2,1)S(1)}, bf16[12,32,128]{2,1,0:T(8,128)(2,1)S(1)}, u32[]{:S(2)}, u32[]{:S(2)}) collective-permute-start(bf16[12,32,128]{2,1,0:T(8,128)(2,1)S(1)} %choose_piece.1.piece), channel_id=1, source_target_pairs={{0,4},{4,0},{8,12},{12,8},{16,20},{20,16},{24,28},{28,24},{1,5},{5... | collective-permute-start | bytes 294920 | tf_op jit(solution)/shard_map/ppermute | solution.py:504
  21.1 2.9 %correlate_first.1.rest_0_ = f32[256,256]{1,0:T(8,128)S(1)} custom-call(bf16[12,32,128]{2,1,0:T(8,128)(2,1)S(1)} %choose_piece.1.piece, bf16[30,256,256]{2,1,0:T(8,128)(2,1)S(1)} %get-tuple-element.35.left_a, bf16[30,256,256]{2,1,0:T(8,128)(2,1)S(1)} %get-tuple-element.36.left_r), custom_call_target="tpu_custom_call" | custom-call | flops 3000000000 | bytes 3000000 | tf_op jit(solution)/shard_map/correlate_first/pallas_call | solution.py:420
  24.0 0.0 collective-permute-done.8.piece
  24.0 2.9 %correlate_second.1 = (bf16[128,256]{1,0:T(8,128)(2,1)S(1)}, bf16[128,256]{1,0:T(8,128)(2,1)S(1)}) custom-call(bf16[12,32,128]{2,1,0:T(8,128)(2,1)S(1)} %collective-permute-done.8.piece, bf16[30,256,256]{2,1,0:T(8,128)(2,1)S(1)} %get-tuple-element.35.left_a, bf16[30,256,256]{2,1,0:T(8,128)(2,1)S(1)} %get-tuple-element.36.left_r, ...), custom_call_target="tpu_custom_call" | custom-call | flops 3000000000 | bytes 3000000 | tf_op jit(solution)/shard_map/correlate_second/pallas_call | solution.py:420
  27.0 5.1 %collective-permute-start.9 = (bf16[128,256]{1,0:T(8,128)(2,1)S(1)}, bf16[128,256]{1,0:T(8,128)(2,1)S(1)}, u32[]{:S(2)}, u32[]{:S(2)}) collective-permute-start(bf16[128,256]{1,0:T(8,128)(2,1)S(1)} %get-tuple-element.37), channel_id=1, source_target_pairs={{0,0},{1,8},{2,4},{3,12},{4,16},{5,24},{6,20},{7,28},{8,1},{9,9},{... | collective-permute-start | bytes 196616 | tf_op jit(solution)/shard_map/ppermute | solution.py:537
  32.1 0.1 collective-permute-start.10
  32.2 3.1 %collective-permute-done.9.refs_0_ = bf16[128,256]{1,0:T(8,128)(2,1)S(1)} collective-permute-done((bf16[128,256]{1,0:T(8,128)(2,1)S(1)}, bf16[128,256]{1,0:T(8,128)(2,1)S(1)}, u32[]{:S(2)}, u32[]{:S(2)}) %collective-permute-start.9) | collective-permute-done | bytes 65568 | tf_op jit(solution)/shard_map/ppermute | solution.py:537
  35.3 2.3 %collective-permute-done.10.refs_1_ = bf16[128,256]{1,0:T(8,128)(2,1)S(1)} collective-permute-done((bf16[128,256]{1,0:T(8,128)(2,1)S(1)}, bf16[128,256]{1,0:T(8,128)(2,1)S(1)}, u32[]{:S(2)}, u32[]{:S(2)}) %collective-permute-start.10) | collective-permute-done | bytes 65568 | tf_op jit(solution)/shard_map/ppermute | solution.py:537
  37.7 0.1 collective-permute-start.11
  37.8 1.2 %collective-permute-done.11.received = f32[64,256]{1,0:T(8,128)S(1)} collective-permute-done((f32[64,256]{1,0:T(8,128)S(1)}, f32[64,256]{1,0:T(8,128)S(1)}, u32[]{:S(2)}, u32[]{:S(2)}) %collective-permute-start.11) | collective-permute-done | bytes 65568 | tf_op jit(solution)/shard_map/ppermute | solution.py:504
  39.0 0.9 %finish.1 = f32[32,512]{1,0:T(8,128)} custom-call(f32[64,256]{1,0:T(8,128)S(1)} %get-tuple-element.39.ours, f32[64,256]{1,0:T(8,128)S(1)} %collective-permute-done.11.received), custom_call_target="tpu_custom_call" | custom-call | flops 1000000000 | bytes 1000000 | tf_op jit(solution)/shard_map/finish/pallas_call | solution.py:483
  (2 shorter events, 0.0 us)
Async XLA Ops:
  0.0 6.8 %copy-start.1 = (s32[2]{0:T(128)S(1)}, s32[2]{0:T(128)}, u32[]{:S(2)}) copy-start(s32[2]{0:T(128)} %bank_blocks.5) | copy-start | bytes 28
  0.0 3.2 %copy-start = (bf16[30,512]{1,0:T(8,128)(2,1)S(1)}, bf16[30,512]{1,0:T(8,128)(2,1)}, u32[]{:S(2)}) copy-start(bf16[30,512]{1,0:T(8,128)(2,1)} %rest_0_.1) | copy-start | bytes 92164
  2.5 4.4 %collective-permute-start.4 = (bf16[4,12,32,128]{3,2,1,0:T(8,128)(2,1)S(1)}, bf16[4,12,32,128]{3,2,1,0:T(8,128)(2,1)S(1)}, u32[]{:S(2)}, u32[]{:S(2)}) collective-permute-start(bf16[4,12,32,128]{3,2,1,0:T(8,128)(2,1)S(1)} %get-tuple-element.26), channel_id=1, source_target_pairs={{0,4},{4,0},{8,12},{12,8},{16,20},{20,16},{24,28},{28,24},{1,5},{5... | collective-permute-start | bytes 1179656 | tf_op jit(solution)/shard_map/ppermute | solution.py:504
  3.2 7.6 %collective-permute-start.2 = (bf16[30,512]{1,0:T(8,128)(2,1)S(1)}, bf16[30,512]{1,0:T(8,128)(2,1)S(1)}, u32[]{:S(2)}, u32[]{:S(2)}) collective-permute-start(bf16[30,512]{1,0:T(8,128)(2,1)S(1)} %copy-done), channel_id=1, source_target_pairs={{0,24},{4,28},{8,16},{12,20},{16,8},{20,12},{24,0},{28,4},{1,25},{... | collective-permute-start | bytes 92168 | tf_op jit(solution)/shard_map/ppermute | solution.py:507
  6.6 4.7 %collective-permute-start.1 = (bf16[30,512]{1,0:T(8,128)(2,1)S(1)}, bf16[30,512]{1,0:T(8,128)(2,1)S(1)}, u32[]{:S(2)}, u32[]{:S(2)}) collective-permute-start(bf16[30,512]{1,0:T(8,128)(2,1)S(1)} %copy-done), channel_id=1, source_target_pairs={{0,16},{4,20},{8,24},{12,28},{16,0},{20,4},{24,8},{28,12},{1,17},{... | collective-permute-start | bytes 92168 | tf_op jit(solution)/shard_map/ppermute | solution.py:507
  6.6 4.7 %collective-permute-start = (bf16[30,512]{1,0:T(8,128)(2,1)S(1)}, bf16[30,512]{1,0:T(8,128)(2,1)S(1)}, u32[]{:S(2)}, u32[]{:S(2)}) collective-permute-start(bf16[30,512]{1,0:T(8,128)(2,1)S(1)} %copy-done), channel_id=1, source_target_pairs={{0,8},{4,12},{8,0},{12,4},{16,24},{20,28},{24,16},{28,20},{1,9},{5... | collective-permute-start | bytes 92168 | tf_op jit(solution)/shard_map/ppermute | solution.py:507
  7.5 12.5 %collective-permute-start.5 = (bf16[12,32,128]{2,1,0:T(8,128)(2,1)S(1)}, bf16[12,32,128]{2,1,0:T(8,128)(2,1)S(1)}, u32[]{:S(2)}, u32[]{:S(2)}) collective-permute-start(bf16[12,32,128]{2,1,0:T(8,128)(2,1)S(1)} %get-tuple-element.27), channel_id=1, source_target_pairs={{0,24},{4,28},{8,16},{12,20},{16,8},{20,12},{24,0},{28,4},{1,25},{... | collective-permute-start | bytes 294920 | tf_op jit(solution)/shard_map/ppermute | solution.py:507
  10.9 9.2 %collective-permute-start.6 = (bf16[12,32,128]{2,1,0:T(8,128)(2,1)S(1)}, bf16[12,32,128]{2,1,0:T(8,128)(2,1)S(1)}, u32[]{:S(2)}, u32[]{:S(2)}) collective-permute-start(bf16[12,32,128]{2,1,0:T(8,128)(2,1)S(1)} %get-tuple-element.28), channel_id=1, source_target_pairs={{0,16},{4,20},{8,24},{12,28},{16,0},{20,4},{24,8},{28,12},{1,17},{... | collective-permute-start | bytes 294920 | tf_op jit(solution)/shard_map/ppermute | solution.py:507
  10.9 9.2 %collective-permute-start.7 = (bf16[12,32,128]{2,1,0:T(8,128)(2,1)S(1)}, bf16[12,32,128]{2,1,0:T(8,128)(2,1)S(1)}, u32[]{:S(2)}, u32[]{:S(2)}) collective-permute-start(bf16[12,32,128]{2,1,0:T(8,128)(2,1)S(1)} %get-tuple-element.29), channel_id=1, source_target_pairs={{0,8},{4,12},{8,0},{12,4},{16,24},{20,28},{24,16},{28,20},{1,9},{5... | collective-permute-start | bytes 294920 | tf_op jit(solution)/shard_map/ppermute | solution.py:507
  11.3 2.6 %collective-permute-start.3 = (bf16[2,30,512]{2,1,0:T(8,128)(2,1)S(1)}, bf16[2,30,512]{2,1,0:T(8,128)(2,1)S(1)}, u32[]{:S(2)}, u32[]{:S(2)}) collective-permute-start(bf16[2,30,512]{2,1,0:T(8,128)(2,1)S(1)} %choose_waves.1), channel_id=1, source_target_pairs={{0,4},{4,0},{8,12},{12,8},{16,20},{20,16},{24,28},{28,24},{1,5},{5... | collective-permute-start | bytes 184328 | tf_op jit(solution)/shard_map/ppermute | solution.py:504
  20.7 3.3 %collective-permute-start.8 = (bf16[12,32,128]{2,1,0:T(8,128)(2,1)S(1)}, bf16[12,32,128]{2,1,0:T(8,128)(2,1)S(1)}, u32[]{:S(2)}, u32[]{:S(2)}) collective-permute-start(bf16[12,32,128]{2,1,0:T(8,128)(2,1)S(1)} %choose_piece.1.piece), channel_id=1, source_target_pairs={{0,4},{4,0},{8,12},{12,8},{16,20},{20,16},{24,28},{28,24},{1,5},{5... | collective-permute-start | bytes 294920 | tf_op jit(solution)/shard_map/ppermute | solution.py:504
  27.0 8.3 %collective-permute-start.9 = (bf16[128,256]{1,0:T(8,128)(2,1)S(1)}, bf16[128,256]{1,0:T(8,128)(2,1)S(1)}, u32[]{:S(2)}, u32[]{:S(2)}) collective-permute-start(bf16[128,256]{1,0:T(8,128)(2,1)S(1)} %get-tuple-element.37), channel_id=1, source_target_pairs={{0,0},{1,8},{2,4},{3,12},{4,16},{5,24},{6,20},{7,28},{8,1},{9,9},{... | collective-permute-start | bytes 196616 | tf_op jit(solution)/shard_map/ppermute | solution.py:537
  32.1 5.5 %collective-permute-start.10 = (bf16[128,256]{1,0:T(8,128)(2,1)S(1)}, bf16[128,256]{1,0:T(8,128)(2,1)S(1)}, u32[]{:S(2)}, u32[]{:S(2)}) collective-permute-start(bf16[128,256]{1,0:T(8,128)(2,1)S(1)} %get-tuple-element.38), channel_id=1, source_target_pairs={{0,8},{1,0},{2,12},{3,4},{4,24},{5,16},{6,28},{7,20},{8,9},{9,1},{... | collective-permute-start | bytes 196616 | tf_op jit(solution)/shard_map/ppermute | solution.py:537
  37.7 1.3 %collective-permute-start.11 = (f32[64,256]{1,0:T(8,128)S(1)}, f32[64,256]{1,0:T(8,128)S(1)}, u32[]{:S(2)}, u32[]{:S(2)}) collective-permute-start(f32[64,256]{1,0:T(8,128)S(1)} %get-tuple-element.40), channel_id=1, source_target_pairs={{0,4},{4,0},{8,12},{12,8},{16,20},{20,16},{24,28},{28,24},{1,5},{5... | collective-permute-start | bytes 196616 | tf_op jit(solution)/shard_map/ppermute | solution.py:504

commit v8 on v7

--- a/solution.py
+++ b/solution.py
@@ -16,7 +16,6 @@
 DEPTH = 256
 VMEM_LIMIT = 28 * 1024 * 1024
 
-SMEM = pl.BlockSpec(memory_space=pltpu.SMEM)
 VMEM = pl.BlockSpec(memory_space=pltpu.VMEM)
 ANY = pl.BlockSpec(memory_space=pl.ANY)
 
@@ -31,7 +30,7 @@
     )
 
 
-def pack_kernel(bank_blocks, templates, available, moveout, mine, theirs, chosen, raw, usable, shifts, square, packed, sems):
+def pack_kernel(bank_blocks, templates, available, moveout, mine, theirs, owners, chosen, raw, usable, shifts, square, packed, sems):
     blocks, channels, events, tlen = templates.shape
     chips, _, group, _ = mine.shape
     half = channels // 2
@@ -49,6 +48,8 @@
     for copy in fetch[:3]:
         copy.wait()
     slots = [chosen[which] % blocks for which in range(2)]
+    row = lax.broadcasted_iota(jnp.int32, owners.shape, 0)
+    owners[...] = jnp.where(row == 0, chosen[0] // blocks, chosen[1] // blocks)
     flags = jnp.where(usable[...] > 0, shifts[...] + 1, 0).astype(jnp.float32)
     turned = []
     for which in range(2):
@@ -87,9 +88,10 @@
     ]
     return pl.pallas_call(
         pack_kernel,
-        out_shape=[jax.ShapeDtypeStruct(shape, jnp.bfloat16)] * 2,
+        out_shape=[jax.ShapeDtypeStruct(shape, jnp.bfloat16)] * 2
+        + [jax.ShapeDtypeStruct((8, LANES), jnp.int32)],
         in_specs=[ANY] * 4,
-        out_specs=[VMEM] * 2,
+        out_specs=[VMEM] * 3,
         scratch_shapes=[
             pltpu.SMEM(bank_blocks.shape, jnp.int32),
             pltpu.VMEM(templates.shape, jnp.bfloat16),
@@ -105,12 +107,12 @@
     )(*held)
 
 
-def merge_kernel(blocks, bank_blocks, mine, other, *outs):
+def merge_kernel(owners, mine, other, *outs):
     chips = len(outs)
     me = lax.axis_index("tm")
     for step, out in enumerate(outs):
         dest = jnp.bitwise_xor(me // 2, step)
-        owner = jnp.where(dest < chips // 2, bank_blocks[0], bank_blocks[1]) // blocks
+        owner = jnp.where(dest < chips // 2, owners[0, 0], owners[1, 0])
         here = owner % 2 == me % 2
 
         @pl.when(here)
@@ -122,30 +124,17 @@
             out[...] = other[dest]
 
 
-def merge(blocks, bank_blocks, mine, other):
+def merge(owners, mine, other):
     chips = mine.shape[0]
     return pl.pallas_call(
-        functools.partial(merge_kernel, blocks),
+        merge_kernel,
         out_shape=[jax.ShapeDtypeStruct(mine.shape[1:], mine.dtype)] * chips,
-        in_specs=[SMEM, VMEM, VMEM],
+        in_specs=[VMEM] * 3,
         out_specs=[VMEM] * chips,
         compiler_params=params(),
-        cost_estimate=cost(1),
+        cost_estimate=cost(0.3),
         name="merge",
-    )(bank_blocks, mine, other)
-
-
-def left(values, count):
-    return pltpu.roll(values, values.shape[1] - count, 1)
-
-
-def window_sums(values):
-    sums = {1: values}
-    width = 1
-    while width < 64:
-        sums[2 * width] = sums[width] + left(sums[width], width)
-        width *= 2
-    return sums[64] + left(sums[32], 64) + left(sums[4], 96)
+    )(owners, mine, other)
 
 
 def lagged(row, ahead):
@@ -154,60 +143,63 @@
 
 
 def pick(arrays, index):
-    value = arrays[0][...]
-    for number, array in enumerate(arrays[1:], 1):
-        value = jnp.where(index == number, array[...], value)
+    entries = [array.at[place] for array in arrays for place in range(array.shape[0])]
+    value = entries[0][...]
+    for number, entry in enumerate(entries[1:], 1):
+        value = jnp.where(index == number, entry[...], value)
     return value
 
 
-def choose_kernel(near, *refs):
+def choose_kernel(*refs):
     waves, out = refs[:-1], refs[-1]
+    near = out.shape[0]
     me = lax.axis_index("tm")
     for step in range(near):
         out[step] = pick(waves, jnp.bitwise_xor(me // 2, near * (1 - me % 2) + step))
 
 
-def choose_waves(waves):
-    near = len(waves) // 2
-    return pl.pallas_call(
-        functools.partial(choose_kernel, near),
-        out_shape=jax.ShapeDtypeStruct((near,) + waves[0].shape, waves[0].dtype),
+def choose_waves(near, waves):
+    return pl.pallas_call(
+        choose_kernel,
+        out_shape=jax.ShapeDtypeStruct((near,) + waves[0].shape[1:], waves[0].dtype),
         in_specs=[VMEM] * len(waves),
         out_specs=VMEM,
         compiler_params=params(),
-        cost_estimate=cost(0.3),
+        cost_estimate=cost(0.05),
         name="choose_waves",
     )(*waves)
 
 
-def own_kernel(blocks, bank_blocks, *refs):
+def own_kernel(owners, *refs):
     pieces, out = refs[:-1], refs[-1]
     chip = lax.axis_index("tm") // 2
-    first = chip < len(pieces) // 2
-    owner = jnp.where(first, bank_blocks[0], bank_blocks[1]) // blocks
-    out[...] = pick(pieces, jnp.bitwise_xor(owner // 2, chip))
-
-
-def choose_piece(blocks, bank_blocks, pieces):
-    return pl.pallas_call(
-        functools.partial(own_kernel, blocks),
+    owner = jnp.where(chip < len(pieces) // 2, owners[0, 0], owners[1, 0])
+    source = jnp.bitwise_xor(owner // 2, chip)
+    value = pieces[0][...]
+    for number, piece in enumerate(pieces[1:], 1):
+        value = jnp.where(source == number, piece[...], value)
+    out[...] = value
+
+
+def choose_piece(owners, pieces):
+    return pl.pallas_call(
+        own_kernel,
         out_shape=jax.ShapeDtypeStruct(pieces[0].shape, pieces[0].dtype),
-        in_specs=[SMEM] + [VMEM] * len(pieces),
+        in_specs=[VMEM] * (1 + len(pieces)),
         out_specs=VMEM,
         compiler_params=params(),
         cost_estimate=cost(0.3),
         name="choose_piece",
-    )(bank_blocks, *pieces)
-
-
-def waves_kernel(channels, tlen, swapped, *rest):
+    )(owners, *pieces)
+
+
+def waves_kernel(channels, tlen, unroll, swapped, *rest):
     local = rest[:-4]
     left_a, left_r, padded, inverse = rest[-4:]
-    chips = len(local)
-    samples = local[0].shape[1]
-    near = chips // 2
+    near, _, samples = swapped.shape
+    chips = 2 * near
     length = chips * samples
-    steps = length // STRIDE
+    count = padded.shape[1] // LANES
     me = lax.axis_index("tm")
     chip, core = me // 2, me % 2
     padded[...] = jnp.zeros_like(padded)
@@ -218,44 +210,57 @@
     rim = pick(local, jnp.bitwise_xor(chip, near))[:, 0 : padded.shape[1] - length]
     padded[0:channels, length:] = jnp.where(core == 0, rim.astype(jnp.float32), 0.0)
 
-    @pl.loop(0, 4)
-    def _(part):
-        rows = pl.ds(pl.multiple_of(part * 8, 8), 8)
-        values = padded[rows, :]
-        first_sum = window_sums(values)
-        second_sum = window_sums(values * values)
-        mean = first_sum / tlen
-        inverse[rows, :] = lax.rsqrt(second_sum / tlen - mean * mean + EPSILON)
-
-    @pl.loop(0, channels)
-    def _(channel):
-        row = padded[pl.ds(channel, 1), :]
-        scale = inverse[pl.ds(channel, 1), :]
+    rows = 32 * count
+    values = [padded[:, LANES * tile : LANES * (tile + 1)] for tile in range(count)]
+    values = jnp.concatenate(values + [jnp.zeros((32, LANES), jnp.float32)], axis=0)
+    square = values * values
+    high = square.astype(jnp.bfloat16)
+    low = (square - high.astype(jnp.float32)).astype(jnp.bfloat16)
+    values = values.astype(jnp.bfloat16)
+    lag = lax.broadcasted_iota(jnp.int32, (2 * LANES, LANES), 0)
+    lag = lag - lax.broadcasted_iota(jnp.int32, (2 * LANES, LANES), 1)
+    band = jnp.where(jnp.logical_and(lag >= 0, lag < tlen), 1.0, 0.0).astype(jnp.bfloat16)
+
+    def windows(array):
+        both = jnp.concatenate([array[0:rows], array[32 : rows + 32]], axis=1)
+        return jnp.dot(both, band, preferred_element_type=jnp.float32)
+
+    mean = windows(values) / tlen
+    scale = lax.rsqrt((windows(high) + windows(low)) / tlen - mean * mean + EPSILON)
+    for tile in range(count):
+        inverse[:, LANES * tile : LANES * (tile + 1)] = scale[32 * tile : 32 * (tile + 1)]
+
+    def interleaved(row, tiles):
         even, odd = lagged(row, 0), lagged(row, STRIDE)
-        even_scale, odd_scale = lagged(scale, 0), lagged(scale, STRIDE)
-        columns = ([], [], [])
-        for step in range(steps):
-            start = STRIDE * (step - step % 2)
-            values = odd if step % 2 else even
-            columns[0].append(values[:, start : start + LANES])
-            columns[1].append(values[:, start + LANES : start + 2 * LANES])
-            values = odd_scale if step % 2 else even_scale
-            columns[2].append(values[:, start : start + LANES])
-        left_a[channel, :, 0:LANES] = jnp.concatenate(columns[0], axis=0).astype(jnp.bfloat16)
-        left_a[channel, :, LANES:] = jnp.concatenate(columns[1], axis=0).astype(jnp.bfloat16)
-        value = jnp.concatenate(columns[2], axis=0)
-        high = value.astype(jnp.bfloat16)
-        left_r[channel, :, 0:LANES] = high
-        left_r[channel, :, LANES:] = (value - high.astype(jnp.float32)).astype(jnp.bfloat16)
+        parts = []
+        for tile in range(tiles):
+            lanes = slice(LANES * tile, LANES * (tile + 1))
+            parts += [even[:, lanes], odd[:, lanes]]
+        return jnp.concatenate(parts, axis=0)
+
+    @pl.loop(0, channels // unroll)
+    def _(step):
+        for item in range(unroll):
+            channel = step * unroll + item
+            value = interleaved(padded[pl.ds(channel, 1), :], length // LANES + 1)
+            left_a[channel] = value.astype(jnp.bfloat16)
+            value = interleaved(inverse[pl.ds(channel, 1), :], length // LANES)
+            high = value.astype(jnp.bfloat16)
+            left_r[channel, :, 0:LANES] = high
+            left_r[channel, :, LANES:] = (value - high.astype(jnp.float32)).astype(jnp.bfloat16)
 
 
 def prepare_waves(tlen, swapped, local):
-    channels, samples = local[0].shape
-    length = len(local) * samples
-    out = jax.ShapeDtypeStruct((channels, length // OFFSETS, DEPTH), jnp.bfloat16)
-    return pl.pallas_call(
-        functools.partial(waves_kernel, channels, tlen),
-        out_shape=[out, out],
+    near, channels, samples = swapped.shape
+    length = 2 * near * samples
+    rows = length // OFFSETS
+    unroll = max(step for step in (1, 2, 3) if channels % step == 0)
+    return pl.pallas_call(
+        functools.partial(waves_kernel, channels, tlen, unroll),
+        out_shape=[
+            jax.ShapeDtypeStruct((channels, rows + 16, LANES), jnp.bfloat16),
+            jax.ShapeDtypeStruct((channels, rows, 2 * LANES), jnp.bfloat16),
+        ],
         in_specs=[VMEM] * (1 + len(local)),
         out_specs=[VMEM, VMEM],
         scratch_shapes=[
@@ -274,7 +279,7 @@
         before, outs = outs[0], outs[1:]
     bank, expand, weight_a, weight_r, total = rest[-5:]
     core = lax.axis_index("tm") % 2
-    channels = left_a.shape[0]
+    channels, rows, _ = left_r.shape
     half = channels // 2
     base = half * jnp.where(core == side, 0, 1)
     slots = LANES // group
@@ -314,8 +319,8 @@
         for quarter in range(4):
             source, lanes = divmod(4 * extra + quarter, slots)
             values = turned[source][96:128]
-            rows = lag[96:128]
-            inside = jnp.logical_and(rows >= tlen, rows < tlen + QUARTER)
+            sample = lag[96:128]
+            inside = jnp.logical_and(sample >= tlen, sample < tlen + QUARTER)
             values = jnp.where(inside, values, 0.0)
             values = pltpu.roll(values, (slot - lanes) * group % LANES, 1)
             start = QUARTER * quarter - (tlen - 96)
@@ -381,7 +386,10 @@
     def apply(number, count):
         for slot in range(count):
             item = number * slots + slot
-            corr = jnp.dot(left_a[base + item], weight_a[item], preferred_element_type=jnp.float32)
+            both = [left_a[base + item, 0:rows, :], left_a[base + item, 16 : rows + 16, :]]
+            corr = jnp.dot(
+                jnp.concatenate(both, axis=1), weight_a[item], preferred_element_type=jnp.float32
+            )
             factor = jnp.dot(
                 left_r[base + item], weight_r[item], preferred_element_type=jnp.float32
             )
@@ -410,7 +418,7 @@
 
 
 def correlate(side, tlen, group, count, piece, left_a, left_r, *before):
-    channels, rows, _ = left_a.shape
+    channels, rows, _ = left_r.shape
     width = OFFSETS * group
     half = channels // 2
     if side:
@@ -506,8 +514,10 @@
     def across(array, step):
         return lax.ppermute(array, "tm", [(i, i ^ (2 * step)) for i in range(count_tm)])
 
-    local = [waveforms] + [across(waveforms, step) for step in range(1, chips)]
-    mine, theirs = pack(
+    local = [waveforms[None]]
+    for bit in range(chips.bit_length() - 1):
+        local.append(across(jnp.concatenate(local), 1 << bit))
+    mine, theirs, owners = pack(
         chips,
         group,
         bank_blocks,
@@ -516,14 +526,14 @@
         jnp.transpose(moveout, (2, 0, 1)),
     )
     other = swap(theirs)
-    merged = merge(blocks, bank_blocks, mine, other)
+    merged = merge(owners, mine, other)
     pieces = [across(merged[step], step) for step in reversed(range(1, chips))]
     pieces = [merged[0]] + pieces[::-1]
-    left_a, left_r = prepare_waves(tlen, swap(choose_waves(local)), local)
+    left_a, left_r = prepare_waves(tlen, swap(choose_waves(near, local)), local)
 
     left_a, left_r, *pieces = lax.optimization_barrier((left_a, left_r, *pieces[::-1]))
     pieces = pieces[::-1]
-    first = choose_piece(blocks, bank_blocks, pieces)
+    first = choose_piece(owners, pieces)
     second = swap(first)
     total = correlate(0, tlen, group, near, first, left_a, left_r)
     parts = correlate(1, tlen, group, near, second, left_a, left_r, *total)

time: 40 us -> 41.2 us (1.030)
  waiting for transfers between devices: 7.62 us -> 12 us
  Pallas kernels: 16.7 us -> 12.5 us
  starting transfers between devices: 15.4 us -> 16.5 us
    ppermute x6 -> x5, waiting for transfers between devices: 0.02 us -> 4.38 us  [across(): lax.ppermute(array, 'tm', [(i, i ^ 2 * step) for i in range(count_tm)])]
    pallas_call x4, Pallas kernels: 7.5 us -> 3.19 us  [the longest x1 2.85 us: prepare_waves(): pl.pallas_call(functools.partial(waves_kernel, channels, tlen, unroll), o...]
    ppermute x4, starting transfers between devices: 2.93 us -> 3.83 us  [swap(): return lax.ppermute(array, 'tm', [(i, i ^ 1) for i in range(count_tm)])]
    ppermute x6 -> x5, starting transfers between devices: 7.31 us -> 7.3 us  [across(): lax.ppermute(array, 'tm', [(i, i ^ 2 * step) for i in range(count_tm)])]
  transfers between devices with their start and end apart: 12 -> 11, of which waited for: 4 -> 6; matrix products, arithmetic and copies ran while one was open for 0% -> 0% of each run, Pallas kernels for 25% -> 15%
where the time goes in v8:
time: 41.2 us; the launch traced here: 41.1 us
  starting transfers between devices  16.5 us (40%)
  Pallas kernels  12.5 us (30%)
  waiting for transfers between devices  12 us (29%)
    ppermute x5, starting transfers between devices, across(): lax.ppermute(array, 'tm', [(i, i ^ 2 * step) for i in range(count_tm)])  7.3 us
    pallas_call x2, Pallas kernels, correlate(): pl.pallas_call(functools.partial(main_kernel, side, tlen, group), out_sha...  5.93 us
    ppermute x2, waiting for transfers between devices, shards(): gathered.append(lax.ppermute(parts[step], ('tm', 'sta'), route))  5.47 us
    ppermute x2, starting transfers between devices, shards(): gathered.append(lax.ppermute(parts[step], ('tm', 'sta'), route))  5.34 us
    ppermute x5, waiting for transfers between devices, across(): lax.ppermute(array, 'tm', [(i, i ^ 2 * step) for i in range(count_tm)])  4.38 us
    ppermute x4, starting transfers between devices, swap(): return lax.ppermute(array, 'tm', [(i, i ^ 1) for i in range(count_tm)])  3.83 us
    pallas_call x1, Pallas kernels, prepare_waves(): pl.pallas_call(functools.partial(waves_kernel, channels, tlen, unroll), o...  2.85 us
    pallas_call x1, Pallas kernels, pack(): pl.pallas_call(pack_kernel, out_shape=[jax.ShapeDtypeStruct(shape, jnp.bf...  2.46 us
  transfers between devices with their start and end apart: 11, of which 6 were waited for; matrix products, arithmetic and copies ran while one was open for 0% of the time, Pallas kernels for 15%

profile of v8, /device:TPU:7, one launch (start us, length us, event | category | flops | bytes accessed | tf_op | source)
XLA Modules:
  0.0 41.1 jit_solution(15001421833619624650)
XLA Ops:
  0.0 0.0 copy-start
  0.0 2.5 %pack.1 = (bf16[4,12,32,128]{3,2,1,0:T(8,128)(2,1)S(1)}, bf16[4,12,32,128]{3,2,1,0:T(8,128)(2,1)S(1)}, s32[8,128]{1,0:T(8,128)S(1)}) custom-call(s32[2]{0:T(128)} %bank_blocks.1, bf16[2,30,64,100]{3,2,1,0:T(8,128)(2,1)} %bitcast.8, s32[30,2,64]{2,1,0:T(2,128)} %bitcast.9, s32[30,2,64]{2,1,0:T(2,128)} %bitcast.10), custom_call_target="tpu_custom_call" | custom-call | flops 2000000000 | bytes 2000000 | tf_op jit(solution)/shard_map/pack/pallas_call | solution.py:89
  2.5 0.7 %collective-permute-start.3 = (bf16[4,12,32,128]{3,2,1,0:T(8,128)(2,1)S(1)}, bf16[4,12,32,128]{3,2,1,0:T(8,128)(2,1)S(1)}, u32[]{:S(2)}, u32[]{:S(2)}) collective-permute-start(bf16[4,12,32,128]{3,2,1,0:T(8,128)(2,1)S(1)} %get-tuple-element.28), channel_id=1, source_target_pairs={{0,4},{4,0},{8,12},{12,8},{16,20},{20,16},{24,28},{28,24},{1,5},{5... | collective-permute-start | bytes 1179656 | tf_op jit(solution)/shard_map/ppermute | solution.py:512
  3.2 0.0 copy-done
  3.2 1.3 %collective-permute-start = (bf16[1,30,512]{2,1,0:T(8,128)(2,1)S(1)}, bf16[1,30,512]{2,1,0:T(8,128)(2,1)S(1)}, u32[]{:S(2)}, u32[]{:S(2)}) collective-permute-start(bf16[1,30,512]{2,1,0:T(8,128)(2,1)S(1)} %bitcast.4), channel_id=1, source_target_pairs={{0,8},{4,12},{8,0},{12,4},{16,24},{20,28},{24,16},{28,20},{1,9},{5... | collective-permute-start | bytes 92168 | tf_op jit(solution)/shard_map/ppermute | solution.py:515
  4.5 1.5 %collective-permute-done.refs_1_.rest_1_ = bf16[1,30,512]{2,1,0:T(8,128)(2,1)S(1)} collective-permute-done((bf16[1,30,512]{2,1,0:T(8,128)(2,1)S(1)}, bf16[1,30,512]{2,1,0:T(8,128)(2,1)S(1)}, u32[]{:S(2)}, u32[]{:S(2)}) %collective-permute-start) | collective-permute-done | bytes 30752 | tf_op jit(solution)/shard_map/ppermute | solution.py:515
  6.0 2.4 %collective-permute-start.1 = (bf16[2,30,512]{2,1,0:T(8,128)(2,1)S(1)}, bf16[2,30,512]{2,1,0:T(8,128)(2,1)S(1)}, u32[]{:S(2)}, u32[]{:S(2)}) collective-permute-start(bf16[2,30,512]{2,1,0:T(8,128)(2,1)S(1)} %pad_maximum_fusion), channel_id=1, source_target_pairs={{0,16},{4,20},{8,24},{12,28},{16,0},{20,4},{24,8},{28,12},{1,17},{... | collective-permute-start | bytes 184328 | tf_op jit(solution)/shard_map/ppermute | solution.py:515
  8.4 0.0 collective-permute-done.3.other
  8.4 0.2 merge.1
  8.6 1.1 %collective-permute-start.4 = (bf16[12,32,128]{2,1,0:T(8,128)(2,1)S(1)}, bf16[12,32,128]{2,1,0:T(8,128)(2,1)S(1)}, u32[]{:S(2)}, u32[]{:S(2)}) collective-permute-start(bf16[12,32,128]{2,1,0:T(8,128)(2,1)S(1)} %get-tuple-element.29), channel_id=1, source_target_pairs={{0,24},{4,28},{8,16},{12,20},{16,8},{20,12},{24,0},{28,4},{1,25},{... | collective-permute-start | bytes 294920 | tf_op jit(solution)/shard_map/ppermute | solution.py:515
  9.7 1.4 %collective-permute-start.5 = (bf16[12,32,128]{2,1,0:T(8,128)(2,1)S(1)}, bf16[12,32,128]{2,1,0:T(8,128)(2,1)S(1)}, u32[]{:S(2)}, u32[]{:S(2)}) collective-permute-start(bf16[12,32,128]{2,1,0:T(8,128)(2,1)S(1)} %get-tuple-element.30), channel_id=1, source_target_pairs={{0,16},{4,20},{8,24},{12,28},{16,0},{20,4},{24,8},{28,12},{1,17},{... | collective-permute-start | bytes 294920 | tf_op jit(solution)/shard_map/ppermute | solution.py:515
  11.2 1.1 %collective-permute-start.6 = (bf16[12,32,128]{2,1,0:T(8,128)(2,1)S(1)}, bf16[12,32,128]{2,1,0:T(8,128)(2,1)S(1)}, u32[]{:S(2)}, u32[]{:S(2)}) collective-permute-start(bf16[12,32,128]{2,1,0:T(8,128)(2,1)S(1)} %get-tuple-element.31), channel_id=1, source_target_pairs={{0,8},{4,12},{8,0},{12,4},{16,24},{20,28},{24,16},{28,20},{1,9},{5... | collective-permute-start | bytes 294920 | tf_op jit(solution)/shard_map/ppermute | solution.py:515
  12.2 0.0 collective-permute-done.1.refs_2_.rest_2_
  12.3 2.4 %collective-permute-start.2 = (bf16[2,30,512]{2,1,0:T(8,128)(2,1)S(1)}, bf16[2,30,512]{2,1,0:T(8,128)(2,1)S(1)}, u32[]{:S(2)}, u32[]{:S(2)}) collective-permute-start(bf16[2,30,512]{2,1,0:T(8,128)(2,1)S(1)} %choose_waves.1), channel_id=1, source_target_pairs={{0,4},{4,0},{8,12},{12,8},{16,20},{20,16},{24,28},{28,24},{1,5},{5... | collective-permute-start | bytes 184328 | tf_op jit(solution)/shard_map/ppermute | solution.py:512
  14.7 0.9 %collective-permute-done.2.swapped = bf16[2,30,512]{2,1,0:T(8,128)(2,1)S(1)} collective-permute-done((bf16[2,30,512]{2,1,0:T(8,128)(2,1)S(1)}, bf16[2,30,512]{2,1,0:T(8,128)(2,1)S(1)}, u32[]{:S(2)}, u32[]{:S(2)}) %collective-permute-start.2) | collective-permute-done | bytes 61472 | tf_op jit(solution)/shard_map/ppermute | solution.py:512
  15.6 2.9 %prepare_waves.1 = (bf16[30,272,128]{2,1,0:T(8,128)(2,1)S(1)}, bf16[30,256,256]{2,1,0:T(8,128)(2,1)S(1)}) custom-call(bf16[2,30,512]{2,1,0:T(8,128)(2,1)S(1)} %collective-permute-done.2.swapped, bf16[1,30,512]{2,1,0:T(8,128)(2,1)S(1)} %bitcast.7, bf16[1,30,512]{2,1,0:T(8,128)(2,1)S(1)} %collective-permute-done.refs_1_.rest_1_, ...), custom_call_target="tpu_custom_call" | custom-call | flops 50000000 | bytes 50000 | tf_op jit(solution)/shard_map/prepare_waves/pallas_call | solution.py:258
  18.4 0.0 collective-permute-done.4.refs_3_
  18.4 2.9 %collective-permute-done.5.refs_2_ = bf16[12,32,128]{2,1,0:T(8,128)(2,1)S(1)} collective-permute-done((bf16[12,32,128]{2,1,0:T(8,128)(2,1)S(1)}, bf16[12,32,128]{2,1,0:T(8,128)(2,1)S(1)}, u32[]{:S(2)}, u32[]{:S(2)}) %collective-permute-start.5) | collective-permute-done | bytes 98336 | tf_op jit(solution)/shard_map/ppermute | solution.py:515
  21.3 0.0 collective-permute-done.6.refs_1_
  21.3 0.1 choose_piece.1.piece
  21.4 0.6 %collective-permute-start.7 = (bf16[12,32,128]{2,1,0:T(8,128)(2,1)S(1)}, bf16[12,32,128]{2,1,0:T(8,128)(2,1)S(1)}, u32[]{:S(2)}, u32[]{:S(2)}) collective-permute-start(bf16[12,32,128]{2,1,0:T(8,128)(2,1)S(1)} %choose_piece.1.piece), channel_id=1, source_target_pairs={{0,4},{4,0},{8,12},{12,8},{16,20},{20,16},{24,28},{28,24},{1,5},{5... | collective-permute-start | bytes 294920 | tf_op jit(solution)/shard_map/ppermute | solution.py:512
  22.1 2.9 %correlate_first.1.rest_0_ = f32[256,256]{1,0:T(8,128)S(1)} custom-call(bf16[12,32,128]{2,1,0:T(8,128)(2,1)S(1)} %choose_piece.1.piece, bf16[30,272,128]{2,1,0:T(8,128)(2,1)S(1)} %get-tuple-element.37.left_a, bf16[30,256,256]{2,1,0:T(8,128)(2,1)S(1)} %get-tuple-element.38.left_r), custom_call_target="tpu_custom_call" | custom-call | flops 3000000000 | bytes 3000000 | tf_op jit(solution)/shard_map/correlate_first/pallas_call | solution.py:428
  25.0 0.0 collective-permute-done.7.piece
  25.0 3.0 %correlate_second.1 = (bf16[128,256]{1,0:T(8,128)(2,1)S(1)}, bf16[128,256]{1,0:T(8,128)(2,1)S(1)}) custom-call(bf16[12,32,128]{2,1,0:T(8,128)(2,1)S(1)} %collective-permute-done.7.piece, bf16[30,272,128]{2,1,0:T(8,128)(2,1)S(1)} %get-tuple-element.37.left_a, bf16[30,256,256]{2,1,0:T(8,128)(2,1)S(1)} %get-tuple-element.38.left_r, ...), custom_call_target="tpu_custom_call" | custom-call | flops 3000000000 | bytes 3000000 | tf_op jit(solution)/shard_map/correlate_second/pallas_call | solution.py:428
  28.0 5.3 %collective-permute-start.8 = (bf16[128,256]{1,0:T(8,128)(2,1)S(1)}, bf16[128,256]{1,0:T(8,128)(2,1)S(1)}, u32[]{:S(2)}, u32[]{:S(2)}) collective-permute-start(bf16[128,256]{1,0:T(8,128)(2,1)S(1)} %get-tuple-element.39), channel_id=1, source_target_pairs={{0,0},{1,8},{2,4},{3,12},{4,16},{5,24},{6,20},{7,28},{8,1},{9,9},{... | collective-permute-start | bytes 196616 | tf_op jit(solution)/shard_map/ppermute | solution.py:547
  33.3 0.1 collective-permute-start.9
  33.4 2.9 %collective-permute-done.8.refs_0_ = bf16[128,256]{1,0:T(8,128)(2,1)S(1)} collective-permute-done((bf16[128,256]{1,0:T(8,128)(2,1)S(1)}, bf16[128,256]{1,0:T(8,128)(2,1)S(1)}, u32[]{:S(2)}, u32[]{:S(2)}) %collective-permute-start.8) | collective-permute-done | bytes 65568 | tf_op jit(solution)/shard_map/ppermute | solution.py:547
  36.3 2.6 %collective-permute-done.9.refs_1_ = bf16[128,256]{1,0:T(8,128)(2,1)S(1)} collective-permute-done((bf16[128,256]{1,0:T(8,128)(2,1)S(1)}, bf16[128,256]{1,0:T(8,128)(2,1)S(1)}, u32[]{:S(2)}, u32[]{:S(2)}) %collective-permute-start.9) | collective-permute-done | bytes 65568 | tf_op jit(solution)/shard_map/ppermute | solution.py:547
  38.9 0.1 collective-permute-start.10
  38.9 1.2 %collective-permute-done.10.received = f32[64,256]{1,0:T(8,128)S(1)} collective-permute-done((f32[64,256]{1,0:T(8,128)S(1)}, f32[64,256]{1,0:T(8,128)S(1)}, u32[]{:S(2)}, u32[]{:S(2)}) %collective-permute-start.10) | collective-permute-done | bytes 65568 | tf_op jit(solution)/shard_map/ppermute | solution.py:512
  40.2 0.9 %finish.1 = f32[32,512]{1,0:T(8,128)} custom-call(f32[64,256]{1,0:T(8,128)S(1)} %get-tuple-element.41.ours, f32[64,256]{1,0:T(8,128)S(1)} %collective-permute-done.10.received), custom_call_target="tpu_custom_call" | custom-call | flops 1000000000 | bytes 1000000 | tf_op jit(solution)/shard_map/finish/pallas_call | solution.py:491
  (3 shorter events, 0.0 us)
Async XLA Ops:
  0.0 3.2 %copy-start = (bf16[30,512]{1,0:T(8,128)(2,1)S(1)}, bf16[30,512]{1,0:T(8,128)(2,1)}, u32[]{:S(2)}) copy-start(bf16[30,512]{1,0:T(8,128)(2,1)} %param.5) | copy-start | bytes 92164
  2.5 5.9 %collective-permute-start.3 = (bf16[4,12,32,128]{3,2,1,0:T(8,128)(2,1)S(1)}, bf16[4,12,32,128]{3,2,1,0:T(8,128)(2,1)S(1)}, u32[]{:S(2)}, u32[]{:S(2)}) collective-permute-start(bf16[4,12,32,128]{3,2,1,0:T(8,128)(2,1)S(1)} %get-tuple-element.28), channel_id=1, source_target_pairs={{0,4},{4,0},{8,12},{12,8},{16,20},{20,16},{24,28},{28,24},{1,5},{5... | collective-permute-start | bytes 1179656 | tf_op jit(solution)/shard_map/ppermute | solution.py:512
  3.2 2.8 %collective-permute-start = (bf16[1,30,512]{2,1,0:T(8,128)(2,1)S(1)}, bf16[1,30,512]{2,1,0:T(8,128)(2,1)S(1)}, u32[]{:S(2)}, u32[]{:S(2)}) collective-permute-start(bf16[1,30,512]{2,1,0:T(8,128)(2,1)S(1)} %bitcast.4), channel_id=1, source_target_pairs={{0,8},{4,12},{8,0},{12,4},{16,24},{20,28},{24,16},{28,20},{1,9},{5... | collective-permute-start | bytes 92168 | tf_op jit(solution)/shard_map/ppermute | solution.py:515
  6.0 6.2 %collective-permute-start.1 = (bf16[2,30,512]{2,1,0:T(8,128)(2,1)S(1)}, bf16[2,30,512]{2,1,0:T(8,128)(2,1)S(1)}, u32[]{:S(2)}, u32[]{:S(2)}) collective-permute-start(bf16[2,30,512]{2,1,0:T(8,128)(2,1)S(1)} %pad_maximum_fusion), channel_id=1, source_target_pairs={{0,16},{4,20},{8,24},{12,28},{16,0},{20,4},{24,8},{28,12},{1,17},{... | collective-permute-start | bytes 184328 | tf_op jit(solution)/shard_map/ppermute | solution.py:515
  8.6 9.8 %collective-permute-start.4 = (bf16[12,32,128]{2,1,0:T(8,128)(2,1)S(1)}, bf16[12,32,128]{2,1,0:T(8,128)(2,1)S(1)}, u32[]{:S(2)}, u32[]{:S(2)}) collective-permute-start(bf16[12,32,128]{2,1,0:T(8,128)(2,1)S(1)} %get-tuple-element.29), channel_id=1, source_target_pairs={{0,24},{4,28},{8,16},{12,20},{16,8},{20,12},{24,0},{28,4},{1,25},{... | collective-permute-start | bytes 294920 | tf_op jit(solution)/shard_map/ppermute | solution.py:515
  9.7 11.6 %collective-permute-start.5 = (bf16[12,32,128]{2,1,0:T(8,128)(2,1)S(1)}, bf16[12,32,128]{2,1,0:T(8,128)(2,1)S(1)}, u32[]{:S(2)}, u32[]{:S(2)}) collective-permute-start(bf16[12,32,128]{2,1,0:T(8,128)(2,1)S(1)} %get-tuple-element.30), channel_id=1, source_target_pairs={{0,16},{4,20},{8,24},{12,28},{16,0},{20,4},{24,8},{28,12},{1,17},{... | collective-permute-start | bytes 294920 | tf_op jit(solution)/shard_map/ppermute | solution.py:515
  11.2 10.2 %collective-permute-start.6 = (bf16[12,32,128]{2,1,0:T(8,128)(2,1)S(1)}, bf16[12,32,128]{2,1,0:T(8,128)(2,1)S(1)}, u32[]{:S(2)}, u32[]{:S(2)}) collective-permute-start(bf16[12,32,128]{2,1,0:T(8,128)(2,1)S(1)} %get-tuple-element.31), channel_id=1, source_target_pairs={{0,8},{4,12},{8,0},{12,4},{16,24},{20,28},{24,16},{28,20},{1,9},{5... | collective-permute-start | bytes 294920 | tf_op jit(solution)/shard_map/ppermute | solution.py:515
  12.3 3.3 %collective-permute-start.2 = (bf16[2,30,512]{2,1,0:T(8,128)(2,1)S(1)}, bf16[2,30,512]{2,1,0:T(8,128)(2,1)S(1)}, u32[]{:S(2)}, u32[]{:S(2)}) collective-permute-start(bf16[2,30,512]{2,1,0:T(8,128)(2,1)S(1)} %choose_waves.1), channel_id=1, source_target_pairs={{0,4},{4,0},{8,12},{12,8},{16,20},{20,16},{24,28},{28,24},{1,5},{5... | collective-permute-start | bytes 184328 | tf_op jit(solution)/shard_map/ppermute | solution.py:512
  21.4 3.6 %collective-permute-start.7 = (bf16[12,32,128]{2,1,0:T(8,128)(2,1)S(1)}, bf16[12,32,128]{2,1,0:T(8,128)(2,1)S(1)}, u32[]{:S(2)}, u32[]{:S(2)}) collective-permute-start(bf16[12,32,128]{2,1,0:T(8,128)(2,1)S(1)} %choose_piece.1.piece), channel_id=1, source_target_pairs={{0,4},{4,0},{8,12},{12,8},{16,20},{20,16},{24,28},{28,24},{1,5},{5... | collective-permute-start | bytes 294920 | tf_op jit(solution)/shard_map/ppermute | solution.py:512
  28.0 8.3 %collective-permute-start.8 = (bf16[128,256]{1,0:T(8,128)(2,1)S(1)}, bf16[128,256]{1,0:T(8,128)(2,1)S(1)}, u32[]{:S(2)}, u32[]{:S(2)}) collective-permute-start(bf16[128,256]{1,0:T(8,128)(2,1)S(1)} %get-tuple-element.39), channel_id=1, source_target_pairs={{0,0},{1,8},{2,4},{3,12},{4,16},{5,24},{6,20},{7,28},{8,1},{9,9},{... | collective-permute-start | bytes 196616 | tf_op jit(solution)/shard_map/ppermute | solution.py:547
  33.3 5.5 %collective-permute-start.9 = (bf16[128,256]{1,0:T(8,128)(2,1)S(1)}, bf16[128,256]{1,0:T(8,128)(2,1)S(1)}, u32[]{:S(2)}, u32[]{:S(2)}) collective-permute-start(bf16[128,256]{1,0:T(8,128)(2,1)S(1)} %get-tuple-element.40), channel_id=1, source_target_pairs={{0,8},{1,0},{2,12},{3,4},{4,24},{5,16},{6,28},{7,20},{8,9},{9,1},{... | collective-permute-start | bytes 196616 | tf_op jit(solution)/shard_map/ppermute | solution.py:547
  38.9 1.3 %collective-permute-start.10 = (f32[64,256]{1,0:T(8,128)S(1)}, f32[64,256]{1,0:T(8,128)S(1)}, u32[]{:S(2)}, u32[]{:S(2)}) collective-permute-start(f32[64,256]{1,0:T(8,128)S(1)} %get-tuple-element.42), channel_id=1, source_target_pairs={{0,4},{4,0},{8,12},{12,8},{16,20},{20,16},{24,28},{28,24},{1,5},{5... | collective-permute-start | bytes 196616 | tf_op jit(solution)/shard_map/ppermute | solution.py:512

commit v9 on v8

--- a/solution.py
+++ b/solution.py
@@ -398,8 +398,7 @@
     total[...] = before[...] if side else jnp.zeros_like(total)
     build(0)
 
-    @pl.loop(1, banks)
-    def _(number):
+    for number in range(1, banks):
         apply(number - 1, slots)
         build(number)
 
@@ -515,8 +514,7 @@
         return lax.ppermute(array, "tm", [(i, i ^ (2 * step)) for i in range(count_tm)])
 
     local = [waveforms[None]]
-    for bit in range(chips.bit_length() - 1):
-        local.append(across(jnp.concatenate(local), 1 << bit))
+    local += [across(local[0], step) for step in range(1, chips)]
     mine, theirs, owners = pack(
         chips,
         group,

time: 41.2 us -> 37.6 us (0.913); the launches traced: 41.1 us -> 37.1 us
  waiting for transfers between devices: 12 us -> 10.1 us
  starting transfers between devices: 16.5 us -> 15.2 us
  Pallas kernels: 12.5 us -> 11.7 us
    ppermute x5 -> x6, waiting for transfers between devices: 4.38 us -> 2.56 us  [across(): lax.ppermute(array, 'tm', [(i, i ^ 2 * step) for i in range(count_tm)])]
    ppermute x2, starting transfers between devices: 5.34 us -> 3.65 us  [shards(): gathered.append(lax.ppermute(parts[step], ('tm', 'sta'), route))]
    pallas_call x2, Pallas kernels: 5.93 us -> 5.1 us  [correlate(): pl.pallas_call(functools.partial(main_kernel, side, tlen, group), out_sha...]
    ppermute x4, starting transfers between devices: 3.83 us -> 4.27 us  [swap(): return lax.ppermute(array, 'tm', [(i, i ^ 1) for i in range(count_tm)])]
    ppermute x5 -> x6, starting transfers between devices: 7.3 us -> 7.31 us  [across(): lax.ppermute(array, 'tm', [(i, i ^ 2 * step) for i in range(count_tm)])]
  transfers between devices with their start and end apart: 11 -> 12, of which waited for: 6 -> 5; matrix products, arithmetic and copies ran while one was open for 0% -> 0% of each run, Pallas kernels for 15% -> 15%
where the time goes in v9:
time: 37.6 us; the launch traced here: 37.1 us
  starting transfers between devices  15.2 us (40%)
  Pallas kernels  11.7 us (31%)
  waiting for transfers between devices  10.1 us (27%)
    ppermute x6, starting transfers between devices, across(): lax.ppermute(array, 'tm', [(i, i ^ 2 * step) for i in range(count_tm)])  7.31 us
    ppermute x2, waiting for transfers between devices, shards(): gathered.append(lax.ppermute(parts[step], ('tm', 'sta'), route))  5.71 us
    pallas_call x2, Pallas kernels, correlate(): pl.pallas_call(functools.partial(main_kernel, side, tlen, group), out_sha...  5.1 us
    ppermute x4, starting transfers between devices, swap(): return lax.ppermute(array, 'tm', [(i, i ^ 1) for i in range(count_tm)])  4.27 us
    ppermute x2, starting transfers between devices, shards(): gathered.append(lax.ppermute(parts[step], ('tm', 'sta'), route))  3.65 us
    pallas_call x1, Pallas kernels, prepare_waves(): pl.pallas_call(functools.partial(waves_kernel, channels, tlen, unroll), o...  2.85 us
    ppermute x6, waiting for transfers between devices, across(): lax.ppermute(array, 'tm', [(i, i ^ 2 * step) for i in range(count_tm)])  2.56 us
    pallas_call x1, Pallas kernels, pack(): pl.pallas_call(pack_kernel, out_shape=[jax.ShapeDtypeStruct(shape, jnp.bf...  2.46 us
  transfers between devices with their start and end apart: 12, of which 5 were waited for; matrix products, arithmetic and copies ran while one was open for 0% of the time, Pallas kernels for 15%

profile of v9, /device:TPU:7, one launch (start us, length us, event | category | flops | bytes accessed | tf_op | source)
XLA Modules:
  0.0 37.1 jit_solution(3860081849445185691)
XLA Ops:
  0.0 0.0 copy-start
  0.0 2.5 %pack.1 = (bf16[4,12,32,128]{3,2,1,0:T(8,128)(2,1)S(1)}, bf16[4,12,32,128]{3,2,1,0:T(8,128)(2,1)S(1)}, s32[8,128]{1,0:T(8,128)S(1)}) custom-call(s32[2]{0:T(128)} %bank_blocks.1, bf16[2,30,64,100]{3,2,1,0:T(8,128)(2,1)} %bitcast.9, s32[30,2,64]{2,1,0:T(2,128)} %bitcast.10, s32[30,2,64]{2,1,0:T(2,128)} %bitcast.11), custom_call_target="tpu_custom_call" | custom-call | flops 2000000000 | bytes 2000000 | tf_op jit(solution)/shard_map/pack/pallas_call | solution.py:89
  2.5 0.7 %collective-permute-start.4 = (bf16[4,12,32,128]{3,2,1,0:T(8,128)(2,1)S(1)}, bf16[4,12,32,128]{3,2,1,0:T(8,128)(2,1)S(1)}, u32[]{:S(2)}, u32[]{:S(2)}) collective-permute-start(bf16[4,12,32,128]{3,2,1,0:T(8,128)(2,1)S(1)} %get-tuple-element.28), channel_id=1, source_target_pairs={{0,4},{4,0},{8,12},{12,8},{16,20},{20,16},{24,28},{28,24},{1,5},{5... | collective-permute-start | bytes 1179656 | tf_op jit(solution)/shard_map/ppermute | solution.py:511
  3.2 0.0 copy-done
  3.2 3.3 %collective-permute-start.2 = (bf16[1,30,512]{2,1,0:T(8,128)(2,1)S(1)}, bf16[1,30,512]{2,1,0:T(8,128)(2,1)S(1)}, u32[]{:S(2)}, u32[]{:S(2)}) collective-permute-start(bf16[1,30,512]{2,1,0:T(8,128)(2,1)S(1)} %bitcast.4), channel_id=1, source_target_pairs={{0,24},{4,28},{8,16},{12,20},{16,8},{20,12},{24,0},{28,4},{1,25},{... | collective-permute-start | bytes 92168 | tf_op jit(solution)/shard_map/ppermute | solution.py:514
  6.5 0.0 collective-permute-start.1
  6.6 0.3 collective-permute-start
  6.8 0.0 collective-permute-done.4.other
  6.8 0.2 merge.1
  7.1 3.3 %collective-permute-start.5 = (bf16[12,32,128]{2,1,0:T(8,128)(2,1)S(1)}, bf16[12,32,128]{2,1,0:T(8,128)(2,1)S(1)}, u32[]{:S(2)}, u32[]{:S(2)}) collective-permute-start(bf16[12,32,128]{2,1,0:T(8,128)(2,1)S(1)} %get-tuple-element.29), channel_id=1, source_target_pairs={{0,24},{4,28},{8,16},{12,20},{16,8},{20,12},{24,0},{28,4},{1,25},{... | collective-permute-start | bytes 294920 | tf_op jit(solution)/shard_map/ppermute | solution.py:514
  10.4 0.0 collective-permute-start.6
  10.4 0.0 collective-permute-done.2.refs_3_.rest_3_
  10.4 0.4 collective-permute-start.7
  10.8 0.0 collective-permute-done.1.refs_2_.rest_2_
  10.8 0.0 collective-permute-done.refs_1_.rest_1_
  10.8 1.7 %collective-permute-start.3 = (bf16[2,30,512]{2,1,0:T(8,128)(2,1)S(1)}, bf16[2,30,512]{2,1,0:T(8,128)(2,1)S(1)}, u32[]{:S(2)}, u32[]{:S(2)}) collective-permute-start(bf16[2,30,512]{2,1,0:T(8,128)(2,1)S(1)} %choose_waves.1), channel_id=1, source_target_pairs={{0,4},{4,0},{8,12},{12,8},{16,20},{20,16},{24,28},{28,24},{1,5},{5... | collective-permute-start | bytes 184328 | tf_op jit(solution)/shard_map/ppermute | solution.py:511
  12.5 0.9 %collective-permute-done.3.swapped = bf16[2,30,512]{2,1,0:T(8,128)(2,1)S(1)} collective-permute-done((bf16[2,30,512]{2,1,0:T(8,128)(2,1)S(1)}, bf16[2,30,512]{2,1,0:T(8,128)(2,1)S(1)}, u32[]{:S(2)}, u32[]{:S(2)}) %collective-permute-start.3) | collective-permute-done | bytes 61472 | tf_op jit(solution)/shard_map/ppermute | solution.py:511
  13.4 2.9 %prepare_waves.1 = (bf16[30,272,128]{2,1,0:T(8,128)(2,1)S(1)}, bf16[30,256,256]{2,1,0:T(8,128)(2,1)S(1)}) custom-call(bf16[2,30,512]{2,1,0:T(8,128)(2,1)S(1)} %collective-permute-done.3.swapped, bf16[1,30,512]{2,1,0:T(8,128)(2,1)S(1)} %bitcast.8, bf16[1,30,512]{2,1,0:T(8,128)(2,1)S(1)} %collective-permute-done.refs_1_.rest_1_, ...), custom_call_target="tpu_custom_call" | custom-call | flops 50000000 | bytes 50000 | tf_op jit(solution)/shard_map/prepare_waves/pallas_call | solution.py:258
  16.2 0.0 collective-permute-done.5.refs_3_
  16.3 2.5 %collective-permute-done.6.refs_2_ = bf16[12,32,128]{2,1,0:T(8,128)(2,1)S(1)} collective-permute-done((bf16[12,32,128]{2,1,0:T(8,128)(2,1)S(1)}, bf16[12,32,128]{2,1,0:T(8,128)(2,1)S(1)}, u32[]{:S(2)}, u32[]{:S(2)}) %collective-permute-start.6) | collective-permute-done | bytes 98336 | tf_op jit(solution)/shard_map/ppermute | solution.py:514
  18.8 0.0 collective-permute-done.7.refs_1_
  18.8 0.1 choose_piece.1.piece
  18.9 1.2 %collective-permute-start.8 = (bf16[12,32,128]{2,1,0:T(8,128)(2,1)S(1)}, bf16[12,32,128]{2,1,0:T(8,128)(2,1)S(1)}, u32[]{:S(2)}, u32[]{:S(2)}) collective-permute-start(bf16[12,32,128]{2,1,0:T(8,128)(2,1)S(1)} %choose_piece.1.piece), channel_id=1, source_target_pairs={{0,4},{4,0},{8,12},{12,8},{16,20},{20,16},{24,28},{28,24},{1,5},{5... | collective-permute-start | bytes 294920 | tf_op jit(solution)/shard_map/ppermute | solution.py:511
  20.1 2.5 %correlate_first.1.rest_0_ = f32[256,256]{1,0:T(8,128)S(1)} custom-call(bf16[12,32,128]{2,1,0:T(8,128)(2,1)S(1)} %choose_piece.1.piece, bf16[30,272,128]{2,1,0:T(8,128)(2,1)S(1)} %get-tuple-element.37.left_a, bf16[30,256,256]{2,1,0:T(8,128)(2,1)S(1)} %get-tuple-element.38.left_r), custom_call_target="tpu_custom_call" | custom-call | flops 3000000000 | bytes 3000000 | tf_op jit(solution)/shard_map/correlate_first/pallas_call | solution.py:427
  22.6 0.0 collective-permute-done.8.piece
  22.6 2.6 %correlate_second.1 = (bf16[128,256]{1,0:T(8,128)(2,1)S(1)}, bf16[128,256]{1,0:T(8,128)(2,1)S(1)}) custom-call(bf16[12,32,128]{2,1,0:T(8,128)(2,1)S(1)} %collective-permute-done.8.piece, bf16[30,272,128]{2,1,0:T(8,128)(2,1)S(1)} %get-tuple-element.37.left_a, bf16[30,256,256]{2,1,0:T(8,128)(2,1)S(1)} %get-tuple-element.38.left_r, ...), custom_call_target="tpu_custom_call" | custom-call | flops 3000000000 | bytes 3000000 | tf_op jit(solution)/shard_map/correlate_second/pallas_call | solution.py:427
  25.2 3.6 %collective-permute-start.9 = (bf16[128,256]{1,0:T(8,128)(2,1)S(1)}, bf16[128,256]{1,0:T(8,128)(2,1)S(1)}, u32[]{:S(2)}, u32[]{:S(2)}) collective-permute-start(bf16[128,256]{1,0:T(8,128)(2,1)S(1)} %get-tuple-element.39), channel_id=1, source_target_pairs={{0,0},{1,8},{2,4},{3,12},{4,16},{5,24},{6,20},{7,28},{8,1},{9,9},{... | collective-permute-start | bytes 196616 | tf_op jit(solution)/shard_map/ppermute | solution.py:545
  28.8 0.1 collective-permute-start.10
  28.9 4.9 %collective-permute-done.9.refs_0_ = bf16[128,256]{1,0:T(8,128)(2,1)S(1)} collective-permute-done((bf16[128,256]{1,0:T(8,128)(2,1)S(1)}, bf16[128,256]{1,0:T(8,128)(2,1)S(1)}, u32[]{:S(2)}, u32[]{:S(2)}) %collective-permute-start.9) | collective-permute-done | bytes 65568 | tf_op jit(solution)/shard_map/ppermute | solution.py:545
  33.8 0.8 %collective-permute-done.10.refs_1_ = bf16[128,256]{1,0:T(8,128)(2,1)S(1)} collective-permute-done((bf16[128,256]{1,0:T(8,128)(2,1)S(1)}, bf16[128,256]{1,0:T(8,128)(2,1)S(1)}, u32[]{:S(2)}, u32[]{:S(2)}) %collective-permute-start.10) | collective-permute-done | bytes 65568 | tf_op jit(solution)/shard_map/ppermute | solution.py:545
  34.6 0.7 %collective-permute-start.11 = (f32[64,256]{1,0:T(8,128)S(1)}, f32[64,256]{1,0:T(8,128)S(1)}, u32[]{:S(2)}, u32[]{:S(2)}) collective-permute-start(f32[64,256]{1,0:T(8,128)S(1)} %get-tuple-element.42), channel_id=1, source_target_pairs={{0,4},{4,0},{8,12},{12,8},{16,20},{20,16},{24,28},{28,24},{1,5},{5... | collective-permute-start | bytes 196616 | tf_op jit(solution)/shard_map/ppermute | solution.py:511
  35.3 0.9 %collective-permute-done.11.received = f32[64,256]{1,0:T(8,128)S(1)} collective-permute-done((f32[64,256]{1,0:T(8,128)S(1)}, f32[64,256]{1,0:T(8,128)S(1)}, u32[]{:S(2)}, u32[]{:S(2)}) %collective-permute-start.11) | collective-permute-done | bytes 65568 | tf_op jit(solution)/shard_map/ppermute | solution.py:511
  36.2 0.9 %finish.1 = f32[32,512]{1,0:T(8,128)} custom-call(f32[64,256]{1,0:T(8,128)S(1)} %get-tuple-element.41.ours, f32[64,256]{1,0:T(8,128)S(1)} %collective-permute-done.11.received), custom_call_target="tpu_custom_call" | custom-call | flops 1000000000 | bytes 1000000 | tf_op jit(solution)/shard_map/finish/pallas_call | solution.py:490
  (2 shorter events, 0.0 us)
Async XLA Ops:
  0.0 3.2 %copy-start = (bf16[30,512]{1,0:T(8,128)(2,1)S(1)}, bf16[30,512]{1,0:T(8,128)(2,1)}, u32[]{:S(2)}) copy-start(bf16[30,512]{1,0:T(8,128)(2,1)} %param.5) | copy-start | bytes 92164
  2.5 4.4 %collective-permute-start.4 = (bf16[4,12,32,128]{3,2,1,0:T(8,128)(2,1)S(1)}, bf16[4,12,32,128]{3,2,1,0:T(8,128)(2,1)S(1)}, u32[]{:S(2)}, u32[]{:S(2)}) collective-permute-start(bf16[4,12,32,128]{3,2,1,0:T(8,128)(2,1)S(1)} %get-tuple-element.28), channel_id=1, source_target_pairs={{0,4},{4,0},{8,12},{12,8},{16,20},{20,16},{24,28},{28,24},{1,5},{5... | collective-permute-start | bytes 1179656 | tf_op jit(solution)/shard_map/ppermute | solution.py:511
  3.2 7.2 %collective-permute-start.2 = (bf16[1,30,512]{2,1,0:T(8,128)(2,1)S(1)}, bf16[1,30,512]{2,1,0:T(8,128)(2,1)S(1)}, u32[]{:S(2)}, u32[]{:S(2)}) collective-permute-start(bf16[1,30,512]{2,1,0:T(8,128)(2,1)S(1)} %bitcast.4), channel_id=1, source_target_pairs={{0,24},{4,28},{8,16},{12,20},{16,8},{20,12},{24,0},{28,4},{1,25},{... | collective-permute-start | bytes 92168 | tf_op jit(solution)/shard_map/ppermute | solution.py:514
  6.5 4.2 %collective-permute-start.1 = (bf16[1,30,512]{2,1,0:T(8,128)(2,1)S(1)}, bf16[1,30,512]{2,1,0:T(8,128)(2,1)S(1)}, u32[]{:S(2)}, u32[]{:S(2)}) collective-permute-start(bf16[1,30,512]{2,1,0:T(8,128)(2,1)S(1)} %bitcast.5), channel_id=1, source_target_pairs={{0,16},{4,20},{8,24},{12,28},{16,0},{20,4},{24,8},{28,12},{1,17},{... | collective-permute-start | bytes 92168 | tf_op jit(solution)/shard_map/ppermute | solution.py:514
  6.6 4.2 %collective-permute-start = (bf16[1,30,512]{2,1,0:T(8,128)(2,1)S(1)}, bf16[1,30,512]{2,1,0:T(8,128)(2,1)S(1)}, u32[]{:S(2)}, u32[]{:S(2)}) collective-permute-start(bf16[1,30,512]{2,1,0:T(8,128)(2,1)S(1)} %bitcast.6), channel_id=1, source_target_pairs={{0,8},{4,12},{8,0},{12,4},{16,24},{20,28},{24,16},{28,20},{1,9},{5... | collective-permute-start | bytes 92168 | tf_op jit(solution)/shard_map/ppermute | solution.py:514
  7.1 9.2 %collective-permute-start.5 = (bf16[12,32,128]{2,1,0:T(8,128)(2,1)S(1)}, bf16[12,32,128]{2,1,0:T(8,128)(2,1)S(1)}, u32[]{:S(2)}, u32[]{:S(2)}) collective-permute-start(bf16[12,32,128]{2,1,0:T(8,128)(2,1)S(1)} %get-tuple-element.29), channel_id=1, source_target_pairs={{0,24},{4,28},{8,16},{12,20},{16,8},{20,12},{24,0},{28,4},{1,25},{... | collective-permute-start | bytes 294920 | tf_op jit(solution)/shard_map/ppermute | solution.py:514
  10.4 8.4 %collective-permute-start.6 = (bf16[12,32,128]{2,1,0:T(8,128)(2,1)S(1)}, bf16[12,32,128]{2,1,0:T(8,128)(2,1)S(1)}, u32[]{:S(2)}, u32[]{:S(2)}) collective-permute-start(bf16[12,32,128]{2,1,0:T(8,128)(2,1)S(1)} %get-tuple-element.30), channel_id=1, source_target_pairs={{0,16},{4,20},{8,24},{12,28},{16,0},{20,4},{24,8},{28,12},{1,17},{... | collective-permute-start | bytes 294920 | tf_op jit(solution)/shard_map/ppermute | solution.py:514
  10.4 8.4 %collective-permute-start.7 = (bf16[12,32,128]{2,1,0:T(8,128)(2,1)S(1)}, bf16[12,32,128]{2,1,0:T(8,128)(2,1)S(1)}, u32[]{:S(2)}, u32[]{:S(2)}) collective-permute-start(bf16[12,32,128]{2,1,0:T(8,128)(2,1)S(1)} %get-tuple-element.31), channel_id=1, source_target_pairs={{0,8},{4,12},{8,0},{12,4},{16,24},{20,28},{24,16},{28,20},{1,9},{5... | collective-permute-start | bytes 294920 | tf_op jit(solution)/shard_map/ppermute | solution.py:514
  10.8 2.6 %collective-permute-start.3 = (bf16[2,30,512]{2,1,0:T(8,128)(2,1)S(1)}, bf16[2,30,512]{2,1,0:T(8,128)(2,1)S(1)}, u32[]{:S(2)}, u32[]{:S(2)}) collective-permute-start(bf16[2,30,512]{2,1,0:T(8,128)(2,1)S(1)} %choose_waves.1), channel_id=1, source_target_pairs={{0,4},{4,0},{8,12},{12,8},{16,20},{20,16},{24,28},{28,24},{1,5},{5... | collective-permute-start | bytes 184328 | tf_op jit(solution)/shard_map/ppermute | solution.py:511
  18.9 3.7 %collective-permute-start.8 = (bf16[12,32,128]{2,1,0:T(8,128)(2,1)S(1)}, bf16[12,32,128]{2,1,0:T(8,128)(2,1)S(1)}, u32[]{:S(2)}, u32[]{:S(2)}) collective-permute-start(bf16[12,32,128]{2,1,0:T(8,128)(2,1)S(1)} %choose_piece.1.piece), channel_id=1, source_target_pairs={{0,4},{4,0},{8,12},{12,8},{16,20},{20,16},{24,28},{28,24},{1,5},{5... | collective-permute-start | bytes 294920 | tf_op jit(solution)/shard_map/ppermute | solution.py:511
  25.2 8.6 %collective-permute-start.9 = (bf16[128,256]{1,0:T(8,128)(2,1)S(1)}, bf16[128,256]{1,0:T(8,128)(2,1)S(1)}, u32[]{:S(2)}, u32[]{:S(2)}) collective-permute-start(bf16[128,256]{1,0:T(8,128)(2,1)S(1)} %get-tuple-element.39), channel_id=1, source_target_pairs={{0,0},{1,8},{2,4},{3,12},{4,16},{5,24},{6,20},{7,28},{8,1},{9,9},{... | collective-permute-start | bytes 196616 | tf_op jit(solution)/shard_map/ppermute | solution.py:545
  28.8 5.8 %collective-permute-start.10 = (bf16[128,256]{1,0:T(8,128)(2,1)S(1)}, bf16[128,256]{1,0:T(8,128)(2,1)S(1)}, u32[]{:S(2)}, u32[]{:S(2)}) collective-permute-start(bf16[128,256]{1,0:T(8,128)(2,1)S(1)} %get-tuple-element.40), channel_id=1, source_target_pairs={{0,8},{1,0},{2,12},{3,4},{4,24},{5,16},{6,28},{7,20},{8,9},{9,1},{... | collective-permute-start | bytes 196616 | tf_op jit(solution)/shard_map/ppermute | solution.py:545
  34.6 1.6 %collective-permute-start.11 = (f32[64,256]{1,0:T(8,128)S(1)}, f32[64,256]{1,0:T(8,128)S(1)}, u32[]{:S(2)}, u32[]{:S(2)}) collective-permute-start(f32[64,256]{1,0:T(8,128)S(1)} %get-tuple-element.42), channel_id=1, source_target_pairs={{0,4},{4,0},{8,12},{12,8},{16,20},{20,16},{24,28},{28,24},{1,5},{5... | collective-permute-start | bytes 196616 | tf_op jit(solution)/shard_map/ppermute | solution.py:511

commit v10 on v9

--- a/solution.py
+++ b/solution.py
@@ -30,7 +30,7 @@
     )
 
 
-def pack_kernel(bank_blocks, templates, available, moveout, mine, theirs, owners, chosen, raw, usable, shifts, square, packed, sems):
+def pack_kernel(bank_blocks, templates, available, moveout, mine, theirs, owners, chosen, raw, usable, shifts, square, sems):
     blocks, channels, events, tlen = templates.shape
     chips, _, group, _ = mine.shape
     half = channels // 2
@@ -43,7 +43,8 @@
     ]
     for copy in fetch:
         copy.start()
-    packed[...] = jnp.zeros_like(packed)
+    mine[...] = jnp.zeros_like(mine)
+    theirs[...] = jnp.zeros_like(theirs)
     square[...] = jnp.zeros_like(square)
     for copy in fetch[:3]:
         copy.wait()
@@ -51,33 +52,34 @@
     row = lax.broadcasted_iota(jnp.int32, owners.shape, 0)
     owners[...] = jnp.where(row == 0, chosen[0] // blocks, chosen[1] // blocks)
     flags = jnp.where(usable[...] > 0, shifts[...] + 1, 0).astype(jnp.float32)
-    turned = []
+    codes = []
     for which in range(2):
         code = flags[:, 0, :]
         for block in range(1, blocks):
             code = jnp.where(slots[which] == block, flags[:, block, :], code)
         square[0:channels, 0:events] = code
-        turned.append(square[...].T.astype(jnp.bfloat16))
+        turned = square[...].T
+        later = pltpu.roll(turned, LANES - half, 1)
+        codes.append([jnp.where(me == core, turned, later) for core in range(2)])
     fetch[3].wait()
     for which in range(2):
-        for core in range(2):
+        for side, out in enumerate((mine, theirs)):
+            first = half * jnp.where(me == side, 0, 1)
+            code = codes[which][side].astype(jnp.bfloat16)
             for tile in range(TILES):
-                channel = half * core + tile
-                extra = half * core + TILES + tile // 4
+                extra = TILES + tile // 4
                 start = QUARTER * (tile % 4)
                 for index in range(events // group):
                     chip = which * (events // group) + index
                     rows = slice(index * group, (index + 1) * group)
-                    packed[core, chip, tile, :, 0:tlen] = raw[slots[which], channel, rows, :]
-                    packed[core, chip, tile, :, tlen : tlen + QUARTER] = raw[
-                        slots[which], extra, rows, start : start + QUARTER
+                    out[chip, tile, :, 0:tlen] = raw[slots[which], first + tile, rows, :]
+                    out[chip, tile, :, tlen : tlen + QUARTER] = raw[
+                        slots[which], first + extra, rows, start : start + QUARTER
                     ]
-                    packed[core, chip, tile, :, 125:126] = turned[which][rows, channel : channel + 1]
+                    out[chip, tile, :, 125:126] = code[rows, tile : tile + 1]
                     if tile < half - TILES:
-                        beyond = channel + TILES
-                        packed[core, chip, tile, :, 126:127] = turned[which][rows, beyond : beyond + 1]
-    mine[...] = packed[me]
-    theirs[...] = packed[1 - me]
+                        beyond = TILES + tile
+                        out[chip, tile, :, 126:127] = code[rows, beyond : beyond + 1]
 
 
 def pack(chips, group, bank_blocks, templates, available, moveout):
@@ -98,7 +100,6 @@
             pltpu.VMEM(available.shape, jnp.int32),
             pltpu.VMEM(moveout.shape, jnp.int32),
             pltpu.VMEM((LANES, LANES), jnp.float32),
-            pltpu.VMEM((2,) + shape, jnp.bfloat16),
             pltpu.SemaphoreType.DMA((4,)),
         ],
         compiler_params=params(),

time: 37.6 us -> 37.4 us (level)
  no operation moved by 1% of the time
where the time goes in v10:
time: 37.4 us; the launch traced here: 36.8 us
  starting transfers between devices  15.2 us (41%)
  Pallas kernels  11.4 us (30%)
  waiting for transfers between devices  10.1 us (27%)
    ppermute x6, starting transfers between devices, across(): lax.ppermute(array, 'tm', [(i, i ^ 2 * step) for i in range(count_tm)])  7.31 us
    ppermute x2, waiting for transfers between devices, shards(): gathered.append(lax.ppermute(parts[step], ('tm', 'sta'), route))  5.71 us
    pallas_call x2, Pallas kernels, correlate(): pl.pallas_call(functools.partial(main_kernel, side, tlen, group), out_sha...  5.1 us
    ppermute x4, starting transfers between devices, swap(): return lax.ppermute(array, 'tm', [(i, i ^ 1) for i in range(count_tm)])  4.27 us
    ppermute x2, starting transfers between devices, shards(): gathered.append(lax.ppermute(parts[step], ('tm', 'sta'), route))  3.64 us
    pallas_call x1, Pallas kernels, prepare_waves(): pl.pallas_call(functools.partial(waves_kernel, channels, tlen, unroll), o...  2.85 us
    ppermute x6, waiting for transfers between devices, across(): lax.ppermute(array, 'tm', [(i, i ^ 2 * step) for i in range(count_tm)])  2.56 us
    pallas_call x1, Pallas kernels, pack(): pl.pallas_call(pack_kernel, out_shape=[jax.ShapeDtypeStruct(shape, jnp.bf...  2.23 us
  transfers between devices with their start and end apart: 12, of which 5 were waited for; matrix products, arithmetic and copies ran while one was open for 0% of the time, Pallas kernels for 15%

profile of v10, /device:TPU:7, one launch (start us, length us, event | category | flops | bytes accessed | tf_op | source)
XLA Modules:
  0.0 36.8 jit_solution(14687039280384263386)
XLA Ops:
  0.0 0.0 copy-start
  0.0 2.2 %pack.1 = (bf16[4,12,32,128]{3,2,1,0:T(8,128)(2,1)S(1)}, bf16[4,12,32,128]{3,2,1,0:T(8,128)(2,1)S(1)}, s32[8,128]{1,0:T(8,128)S(1)}) custom-call(s32[2]{0:T(128)} %bank_blocks.1, bf16[2,30,64,100]{3,2,1,0:T(8,128)(2,1)} %bitcast.9, s32[30,2,64]{2,1,0:T(2,128)} %bitcast.10, s32[30,2,64]{2,1,0:T(2,128)} %bitcast.11), custom_call_target="tpu_custom_call" | custom-call | flops 2000000000 | bytes 2000000 | tf_op jit(solution)/shard_map/pack/pallas_call | solution.py:91
  2.2 0.7 %collective-permute-start.4 = (bf16[4,12,32,128]{3,2,1,0:T(8,128)(2,1)S(1)}, bf16[4,12,32,128]{3,2,1,0:T(8,128)(2,1)S(1)}, u32[]{:S(2)}, u32[]{:S(2)}) collective-permute-start(bf16[4,12,32,128]{3,2,1,0:T(8,128)(2,1)S(1)} %get-tuple-element.28), channel_id=1, source_target_pairs={{0,4},{4,0},{8,12},{12,8},{16,20},{20,16},{24,28},{28,24},{1,5},{5... | collective-permute-start | bytes 1179656 | tf_op jit(solution)/shard_map/ppermute | solution.py:512
  3.0 0.0 copy-done
  3.0 3.3 %collective-permute-start.2 = (bf16[1,30,512]{2,1,0:T(8,128)(2,1)S(1)}, bf16[1,30,512]{2,1,0:T(8,128)(2,1)S(1)}, u32[]{:S(2)}, u32[]{:S(2)}) collective-permute-start(bf16[1,30,512]{2,1,0:T(8,128)(2,1)S(1)} %bitcast.4), channel_id=1, source_target_pairs={{0,24},{4,28},{8,16},{12,20},{16,8},{20,12},{24,0},{28,4},{1,25},{... | collective-permute-start | bytes 92168 | tf_op jit(solution)/shard_map/ppermute | solution.py:515
  6.3 0.0 collective-permute-start.1
  6.3 0.3 collective-permute-start
  6.6 0.0 collective-permute-done.4.other
  6.6 0.2 merge.1
  6.8 3.3 %collective-permute-start.5 = (bf16[12,32,128]{2,1,0:T(8,128)(2,1)S(1)}, bf16[12,32,128]{2,1,0:T(8,128)(2,1)S(1)}, u32[]{:S(2)}, u32[]{:S(2)}) collective-permute-start(bf16[12,32,128]{2,1,0:T(8,128)(2,1)S(1)} %get-tuple-element.29), channel_id=1, source_target_pairs={{0,24},{4,28},{8,16},{12,20},{16,8},{20,12},{24,0},{28,4},{1,25},{... | collective-permute-start | bytes 294920 | tf_op jit(solution)/shard_map/ppermute | solution.py:515
  10.2 0.0 collective-permute-start.6
  10.2 0.0 collective-permute-done.2.refs_3_.rest_3_
  10.2 0.4 collective-permute-start.7
  10.5 0.0 collective-permute-done.1.refs_2_.rest_2_
  10.5 0.0 collective-permute-done.refs_1_.rest_1_
  10.6 1.7 %collective-permute-start.3 = (bf16[2,30,512]{2,1,0:T(8,128)(2,1)S(1)}, bf16[2,30,512]{2,1,0:T(8,128)(2,1)S(1)}, u32[]{:S(2)}, u32[]{:S(2)}) collective-permute-start(bf16[2,30,512]{2,1,0:T(8,128)(2,1)S(1)} %choose_waves.1), channel_id=1, source_target_pairs={{0,4},{4,0},{8,12},{12,8},{16,20},{20,16},{24,28},{28,24},{1,5},{5... | collective-permute-start | bytes 184328 | tf_op jit(solution)/shard_map/ppermute | solution.py:512
  12.2 0.9 %collective-permute-done.3.swapped = bf16[2,30,512]{2,1,0:T(8,128)(2,1)S(1)} collective-permute-done((bf16[2,30,512]{2,1,0:T(8,128)(2,1)S(1)}, bf16[2,30,512]{2,1,0:T(8,128)(2,1)S(1)}, u32[]{:S(2)}, u32[]{:S(2)}) %collective-permute-start.3) | collective-permute-done | bytes 61472 | tf_op jit(solution)/shard_map/ppermute | solution.py:512
  13.1 2.9 %prepare_waves.1 = (bf16[30,272,128]{2,1,0:T(8,128)(2,1)S(1)}, bf16[30,256,256]{2,1,0:T(8,128)(2,1)S(1)}) custom-call(bf16[2,30,512]{2,1,0:T(8,128)(2,1)S(1)} %collective-permute-done.3.swapped, bf16[1,30,512]{2,1,0:T(8,128)(2,1)S(1)} %bitcast.8, bf16[1,30,512]{2,1,0:T(8,128)(2,1)S(1)} %collective-permute-done.refs_1_.rest_1_, ...), custom_call_target="tpu_custom_call" | custom-call | flops 50000000 | bytes 50000 | tf_op jit(solution)/shard_map/prepare_waves/pallas_call | solution.py:259
  16.0 0.0 collective-permute-done.5.refs_3_
  16.0 2.5 %collective-permute-done.6.refs_2_ = bf16[12,32,128]{2,1,0:T(8,128)(2,1)S(1)} collective-permute-done((bf16[12,32,128]{2,1,0:T(8,128)(2,1)S(1)}, bf16[12,32,128]{2,1,0:T(8,128)(2,1)S(1)}, u32[]{:S(2)}, u32[]{:S(2)}) %collective-permute-start.6) | collective-permute-done | bytes 98336 | tf_op jit(solution)/shard_map/ppermute | solution.py:515
  18.6 0.0 collective-permute-done.7.refs_1_
  18.6 0.1 choose_piece.1.piece
  18.7 1.2 %collective-permute-start.8 = (bf16[12,32,128]{2,1,0:T(8,128)(2,1)S(1)}, bf16[12,32,128]{2,1,0:T(8,128)(2,1)S(1)}, u32[]{:S(2)}, u32[]{:S(2)}) collective-permute-start(bf16[12,32,128]{2,1,0:T(8,128)(2,1)S(1)} %choose_piece.1.piece), channel_id=1, source_target_pairs={{0,4},{4,0},{8,12},{12,8},{16,20},{20,16},{24,28},{28,24},{1,5},{5... | collective-permute-start | bytes 294920 | tf_op jit(solution)/shard_map/ppermute | solution.py:512
  19.8 2.5 %correlate_first.1.rest_0_ = f32[256,256]{1,0:T(8,128)S(1)} custom-call(bf16[12,32,128]{2,1,0:T(8,128)(2,1)S(1)} %choose_piece.1.piece, bf16[30,272,128]{2,1,0:T(8,128)(2,1)S(1)} %get-tuple-element.37.left_a, bf16[30,256,256]{2,1,0:T(8,128)(2,1)S(1)} %get-tuple-element.38.left_r), custom_call_target="tpu_custom_call" | custom-call | flops 3000000000 | bytes 3000000 | tf_op jit(solution)/shard_map/correlate_first/pallas_call | solution.py:428
  22.4 0.0 collective-permute-done.8.piece
  22.4 2.6 %correlate_second.1 = (bf16[128,256]{1,0:T(8,128)(2,1)S(1)}, bf16[128,256]{1,0:T(8,128)(2,1)S(1)}) custom-call(bf16[12,32,128]{2,1,0:T(8,128)(2,1)S(1)} %collective-permute-done.8.piece, bf16[30,272,128]{2,1,0:T(8,128)(2,1)S(1)} %get-tuple-element.37.left_a, bf16[30,256,256]{2,1,0:T(8,128)(2,1)S(1)} %get-tuple-element.38.left_r, ...), custom_call_target="tpu_custom_call" | custom-call | flops 3000000000 | bytes 3000000 | tf_op jit(solution)/shard_map/correlate_second/pallas_call | solution.py:428
  25.0 3.6 %collective-permute-start.9 = (bf16[128,256]{1,0:T(8,128)(2,1)S(1)}, bf16[128,256]{1,0:T(8,128)(2,1)S(1)}, u32[]{:S(2)}, u32[]{:S(2)}) collective-permute-start(bf16[128,256]{1,0:T(8,128)(2,1)S(1)} %get-tuple-element.39), channel_id=1, source_target_pairs={{0,0},{1,8},{2,4},{3,12},{4,16},{5,24},{6,20},{7,28},{8,1},{9,9},{... | collective-permute-start | bytes 196616 | tf_op jit(solution)/shard_map/ppermute | solution.py:546
  28.5 0.1 collective-permute-start.10
  28.6 4.9 %collective-permute-done.9.refs_0_ = bf16[128,256]{1,0:T(8,128)(2,1)S(1)} collective-permute-done((bf16[128,256]{1,0:T(8,128)(2,1)S(1)}, bf16[128,256]{1,0:T(8,128)(2,1)S(1)}, u32[]{:S(2)}, u32[]{:S(2)}) %collective-permute-start.9) | collective-permute-done | bytes 65568 | tf_op jit(solution)/shard_map/ppermute | solution.py:546
  33.5 0.8 %collective-permute-done.10.refs_1_ = bf16[128,256]{1,0:T(8,128)(2,1)S(1)} collective-permute-done((bf16[128,256]{1,0:T(8,128)(2,1)S(1)}, bf16[128,256]{1,0:T(8,128)(2,1)S(1)}, u32[]{:S(2)}, u32[]{:S(2)}) %collective-permute-start.10) | collective-permute-done | bytes 65568 | tf_op jit(solution)/shard_map/ppermute | solution.py:546
  34.4 0.7 %collective-permute-start.11 = (f32[64,256]{1,0:T(8,128)S(1)}, f32[64,256]{1,0:T(8,128)S(1)}, u32[]{:S(2)}, u32[]{:S(2)}) collective-permute-start(f32[64,256]{1,0:T(8,128)S(1)} %get-tuple-element.42), channel_id=1, source_target_pairs={{0,4},{4,0},{8,12},{12,8},{16,20},{20,16},{24,28},{28,24},{1,5},{5... | collective-permute-start | bytes 196616 | tf_op jit(solution)/shard_map/ppermute | solution.py:512
  35.0 0.9 %collective-permute-done.11.received = f32[64,256]{1,0:T(8,128)S(1)} collective-permute-done((f32[64,256]{1,0:T(8,128)S(1)}, f32[64,256]{1,0:T(8,128)S(1)}, u32[]{:S(2)}, u32[]{:S(2)}) %collective-permute-start.11) | collective-permute-done | bytes 65568 | tf_op jit(solution)/shard_map/ppermute | solution.py:512
  35.9 0.9 %finish.1 = f32[32,512]{1,0:T(8,128)} custom-call(f32[64,256]{1,0:T(8,128)S(1)} %get-tuple-element.41.ours, f32[64,256]{1,0:T(8,128)S(1)} %collective-permute-done.11.received), custom_call_target="tpu_custom_call" | custom-call | flops 1000000000 | bytes 1000000 | tf_op jit(solution)/shard_map/finish/pallas_call | solution.py:491
  (2 shorter events, 0.0 us)
Async XLA Ops:
  0.0 3.0 %copy-start = (bf16[30,512]{1,0:T(8,128)(2,1)S(1)}, bf16[30,512]{1,0:T(8,128)(2,1)}, u32[]{:S(2)}) copy-start(bf16[30,512]{1,0:T(8,128)(2,1)} %param.5) | copy-start | bytes 92164
  2.2 4.4 %collective-permute-start.4 = (bf16[4,12,32,128]{3,2,1,0:T(8,128)(2,1)S(1)}, bf16[4,12,32,128]{3,2,1,0:T(8,128)(2,1)S(1)}, u32[]{:S(2)}, u32[]{:S(2)}) collective-permute-start(bf16[4,12,32,128]{3,2,1,0:T(8,128)(2,1)S(1)} %get-tuple-element.28), channel_id=1, source_target_pairs={{0,4},{4,0},{8,12},{12,8},{16,20},{20,16},{24,28},{28,24},{1,5},{5... | collective-permute-start | bytes 1179656 | tf_op jit(solution)/shard_map/ppermute | solution.py:512
  3.0 7.2 %collective-permute-start.2 = (bf16[1,30,512]{2,1,0:T(8,128)(2,1)S(1)}, bf16[1,30,512]{2,1,0:T(8,128)(2,1)S(1)}, u32[]{:S(2)}, u32[]{:S(2)}) collective-permute-start(bf16[1,30,512]{2,1,0:T(8,128)(2,1)S(1)} %bitcast.4), channel_id=1, source_target_pairs={{0,24},{4,28},{8,16},{12,20},{16,8},{20,12},{24,0},{28,4},{1,25},{... | collective-permute-start | bytes 92168 | tf_op jit(solution)/shard_map/ppermute | solution.py:515
  6.3 4.2 %collective-permute-start.1 = (bf16[1,30,512]{2,1,0:T(8,128)(2,1)S(1)}, bf16[1,30,512]{2,1,0:T(8,128)(2,1)S(1)}, u32[]{:S(2)}, u32[]{:S(2)}) collective-permute-start(bf16[1,30,512]{2,1,0:T(8,128)(2,1)S(1)} %bitcast.5), channel_id=1, source_target_pairs={{0,16},{4,20},{8,24},{12,28},{16,0},{20,4},{24,8},{28,12},{1,17},{... | collective-permute-start | bytes 92168 | tf_op jit(solution)/shard_map/ppermute | solution.py:515
  6.3 4.2 %collective-permute-start = (bf16[1,30,512]{2,1,0:T(8,128)(2,1)S(1)}, bf16[1,30,512]{2,1,0:T(8,128)(2,1)S(1)}, u32[]{:S(2)}, u32[]{:S(2)}) collective-permute-start(bf16[1,30,512]{2,1,0:T(8,128)(2,1)S(1)} %bitcast.6), channel_id=1, source_target_pairs={{0,8},{4,12},{8,0},{12,4},{16,24},{20,28},{24,16},{28,20},{1,9},{5... | collective-permute-start | bytes 92168 | tf_op jit(solution)/shard_map/ppermute | solution.py:515
  6.8 9.2 %collective-permute-start.5 = (bf16[12,32,128]{2,1,0:T(8,128)(2,1)S(1)}, bf16[12,32,128]{2,1,0:T(8,128)(2,1)S(1)}, u32[]{:S(2)}, u32[]{:S(2)}) collective-permute-start(bf16[12,32,128]{2,1,0:T(8,128)(2,1)S(1)} %get-tuple-element.29), channel_id=1, source_target_pairs={{0,24},{4,28},{8,16},{12,20},{16,8},{20,12},{24,0},{28,4},{1,25},{... | collective-permute-start | bytes 294920 | tf_op jit(solution)/shard_map/ppermute | solution.py:515
  10.2 8.4 %collective-permute-start.6 = (bf16[12,32,128]{2,1,0:T(8,128)(2,1)S(1)}, bf16[12,32,128]{2,1,0:T(8,128)(2,1)S(1)}, u32[]{:S(2)}, u32[]{:S(2)}) collective-permute-start(bf16[12,32,128]{2,1,0:T(8,128)(2,1)S(1)} %get-tuple-element.30), channel_id=1, source_target_pairs={{0,16},{4,20},{8,24},{12,28},{16,0},{20,4},{24,8},{28,12},{1,17},{... | collective-permute-start | bytes 294920 | tf_op jit(solution)/shard_map/ppermute | solution.py:515
  10.2 8.4 %collective-permute-start.7 = (bf16[12,32,128]{2,1,0:T(8,128)(2,1)S(1)}, bf16[12,32,128]{2,1,0:T(8,128)(2,1)S(1)}, u32[]{:S(2)}, u32[]{:S(2)}) collective-permute-start(bf16[12,32,128]{2,1,0:T(8,128)(2,1)S(1)} %get-tuple-element.31), channel_id=1, source_target_pairs={{0,8},{4,12},{8,0},{12,4},{16,24},{20,28},{24,16},{28,20},{1,9},{5... | collective-permute-start | bytes 294920 | tf_op jit(solution)/shard_map/ppermute | solution.py:515
  10.6 2.6 %collective-permute-start.3 = (bf16[2,30,512]{2,1,0:T(8,128)(2,1)S(1)}, bf16[2,30,512]{2,1,0:T(8,128)(2,1)S(1)}, u32[]{:S(2)}, u32[]{:S(2)}) collective-permute-start(bf16[2,30,512]{2,1,0:T(8,128)(2,1)S(1)} %choose_waves.1), channel_id=1, source_target_pairs={{0,4},{4,0},{8,12},{12,8},{16,20},{20,16},{24,28},{28,24},{1,5},{5... | collective-permute-start | bytes 184328 | tf_op jit(solution)/shard_map/ppermute | solution.py:512
  18.7 3.7 %collective-permute-start.8 = (bf16[12,32,128]{2,1,0:T(8,128)(2,1)S(1)}, bf16[12,32,128]{2,1,0:T(8,128)(2,1)S(1)}, u32[]{:S(2)}, u32[]{:S(2)}) collective-permute-start(bf16[12,32,128]{2,1,0:T(8,128)(2,1)S(1)} %choose_piece.1.piece), channel_id=1, source_target_pairs={{0,4},{4,0},{8,12},{12,8},{16,20},{20,16},{24,28},{28,24},{1,5},{5... | collective-permute-start | bytes 294920 | tf_op jit(solution)/shard_map/ppermute | solution.py:512
  25.0 8.6 %collective-permute-start.9 = (bf16[128,256]{1,0:T(8,128)(2,1)S(1)}, bf16[128,256]{1,0:T(8,128)(2,1)S(1)}, u32[]{:S(2)}, u32[]{:S(2)}) collective-permute-start(bf16[128,256]{1,0:T(8,128)(2,1)S(1)} %get-tuple-element.39), channel_id=1, source_target_pairs={{0,0},{1,8},{2,4},{3,12},{4,16},{5,24},{6,20},{7,28},{8,1},{9,9},{... | collective-permute-start | bytes 196616 | tf_op jit(solution)/shard_map/ppermute | solution.py:546
  28.5 5.8 %collective-permute-start.10 = (bf16[128,256]{1,0:T(8,128)(2,1)S(1)}, bf16[128,256]{1,0:T(8,128)(2,1)S(1)}, u32[]{:S(2)}, u32[]{:S(2)}) collective-permute-start(bf16[128,256]{1,0:T(8,128)(2,1)S(1)} %get-tuple-element.40), channel_id=1, source_target_pairs={{0,8},{1,0},{2,12},{3,4},{4,24},{5,16},{6,28},{7,20},{8,9},{9,1},{... | collective-permute-start | bytes 196616 | tf_op jit(solution)/shard_map/ppermute | solution.py:546
  34.4 1.6 %collective-permute-start.11 = (f32[64,256]{1,0:T(8,128)S(1)}, f32[64,256]{1,0:T(8,128)S(1)}, u32[]{:S(2)}, u32[]{:S(2)}) collective-permute-start(f32[64,256]{1,0:T(8,128)S(1)} %get-tuple-element.42), channel_id=1, source_target_pairs={{0,4},{4,0},{8,12},{12,8},{16,20},{20,16},{24,28},{28,24},{1,5},{5... | collective-permute-start | bytes 196616 | tf_op jit(solution)/shard_map/ppermute | solution.py:512

commit v11 on v10

--- a/solution.py
+++ b/solution.py
@@ -143,32 +143,61 @@
     return pltpu.roll(copies, row.shape[1] - 7 - ahead, 1, stride=1, stride_axis=0)
 
 
-def pick(arrays, index):
-    entries = [array.at[place] for array in arrays for place in range(array.shape[0])]
-    value = entries[0][...]
-    for number, entry in enumerate(entries[1:], 1):
-        value = jnp.where(index == number, entry[...], value)
+def segment(me, other, parity, pair, beside, far, default):
+    chip, core = me // 2, me % 2
+    chips = 2 * len(far) + 2
+    step = jnp.bitwise_xor(chip, other)
+    value = default[...]
+    value = jnp.where(jnp.logical_and(step == 1, core == parity), beside[...], value)
+    value = jnp.where(step == 0, pair[parity], value)
+    for number, array in enumerate(far):
+        value = jnp.where(step == chips - 1 - 2 * number - core, array[parity], value)
     return value
 
 
-def choose_kernel(*refs):
-    waves, out = refs[:-1], refs[-1]
-    near = out.shape[0]
+def pair_kernel(own, partner, out):
+    core = lax.axis_index("tm") % 2
+    out[core] = own[...]
+    out[1 - core] = partner[...]
+
+
+def pair_waves(own, partner):
+    return pl.pallas_call(
+        pair_kernel,
+        out_shape=jax.ShapeDtypeStruct((2,) + own.shape, own.dtype),
+        in_specs=[VMEM] * 2,
+        out_specs=VMEM,
+        compiler_params=params(),
+        cost_estimate=cost(0.05),
+        name="pair_waves",
+    )(own, partner)
+
+
+def choose_kernel(pair, beside, *rest):
+    far, out = rest[:-1], rest[-1]
+    near = out.shape[0] - 1
     me = lax.axis_index("tm")
-    for step in range(near):
-        out[step] = pick(waves, jnp.bitwise_xor(me // 2, near * (1 - me % 2) + step))
-
-
-def choose_waves(near, waves):
+    chip, core = me // 2, me % 2
+    for entry in range(near):
+        number, parity = divmod(entry, 2)
+        step = jnp.bitwise_xor(chip, near * (1 - core) + 2 * number) // 2
+        value = beside[...]
+        for place, array in enumerate(far):
+            value = jnp.where(step == near - 1 - place, array[parity], value)
+        out[entry] = value
+    out[near] = segment(me, near, 0, pair, beside, far, beside)
+
+
+def choose_waves(pair, beside, far):
     return pl.pallas_call(
         choose_kernel,
-        out_shape=jax.ShapeDtypeStruct((near,) + waves[0].shape[1:], waves[0].dtype),
-        in_specs=[VMEM] * len(waves),
+        out_shape=jax.ShapeDtypeStruct((len(far) + 2,) + beside.shape, beside.dtype),
+        in_specs=[VMEM] * (2 + len(far)),
         out_specs=VMEM,
         compiler_params=params(),
         cost_estimate=cost(0.05),
         name="choose_waves",
-    )(*waves)
+    )(pair, beside, *far)
 
 
 def own_kernel(owners, *refs):
@@ -194,22 +223,24 @@
     )(owners, *pieces)
 
 
-def waves_kernel(channels, tlen, unroll, swapped, *rest):
-    local = rest[:-4]
+def waves_kernel(channels, tlen, unroll, swapped, pair, beside, *rest):
+    far = rest[:-4]
     left_a, left_r, padded, inverse = rest[-4:]
-    near, _, samples = swapped.shape
-    chips = 2 * near
-    length = chips * samples
+    samples = beside.shape[1]
+    near = swapped.shape[0] - 1
+    length = 2 * near * samples
     count = padded.shape[1] // LANES
     me = lax.axis_index("tm")
-    chip, core = me // 2, me % 2
+    core = me % 2
     padded[...] = jnp.zeros_like(padded)
-    for index in range(chips):
-        wave = pick(local, jnp.bitwise_xor(chip, near * core + index // 2))
-        wave = jnp.where(core == index % 2, wave, swapped[index // 2])
+    for index in range(2 * near):
+        entry, parity = divmod(index, 2)
+        given = swapped.at[2 * (entry // 2) + parity]
+        wave = segment(me, near * core + entry, parity, pair, beside, far, given)
         padded[0:channels, samples * index : samples * (index + 1)] = wave.astype(jnp.float32)
-    rim = pick(local, jnp.bitwise_xor(chip, near))[:, 0 : padded.shape[1] - length]
-    padded[0:channels, length:] = jnp.where(core == 0, rim.astype(jnp.float32), 0.0)
+    rim = segment(me, near * core + near, 0, pair, beside, far, swapped.at[near])
+    rim = rim[:, 0 : padded.shape[1] - length].astype(jnp.float32)
+    padded[0:channels, length:] = jnp.where(core == 0, rim, 0.0)
 
     rows = 32 * count
     values = [padded[:, LANES * tile : LANES * (tile + 1)] for tile in range(count)]
@@ -251,9 +282,9 @@
             left_r[channel, :, LANES:] = (value - high.astype(jnp.float32)).astype(jnp.bfloat16)
 
 
-def prepare_waves(tlen, swapped, local):
-    near, channels, samples = swapped.shape
-    length = 2 * near * samples
+def prepare_waves(tlen, swapped, pair, beside, far):
+    channels, samples = beside.shape
+    length = 2 * (swapped.shape[0] - 1) * samples
     rows = length // OFFSETS
     unroll = max(step for step in (1, 2, 3) if channels % step == 0)
     return pl.pallas_call(
@@ -262,7 +293,7 @@
             jax.ShapeDtypeStruct((channels, rows + 16, LANES), jnp.bfloat16),
             jax.ShapeDtypeStruct((channels, rows, 2 * LANES), jnp.bfloat16),
         ],
-        in_specs=[VMEM] * (1 + len(local)),
+        in_specs=[VMEM] * (3 + len(far)),
         out_specs=[VMEM, VMEM],
         scratch_shapes=[
             pltpu.VMEM((32, length + 2 * LANES), jnp.float32),
@@ -271,7 +302,7 @@
         compiler_params=params(),
         cost_estimate=cost(0.05),
         name="prepare_waves",
-    )(swapped, *local)
+    )(swapped, pair, beside, *far)
 
 
 def main_kernel(side, tlen, group, piece, left_a, left_r, *rest):
@@ -514,8 +545,7 @@
     def across(array, step):
         return lax.ppermute(array, "tm", [(i, i ^ (2 * step)) for i in range(count_tm)])
 
-    local = [waveforms[None]]
-    local += [across(local[0], step) for step in range(1, chips)]
+    partner = swap(waveforms)
     mine, theirs, owners = pack(
         chips,
         group,
@@ -524,11 +554,20 @@
         jnp.transpose(available, (2, 0, 1)),
         jnp.transpose(moveout, (2, 0, 1)),
     )
+    theirs, partner = lax.optimization_barrier((theirs, partner))
     other = swap(theirs)
-    merged = merge(owners, mine, other)
+    pair = pair_waves(waveforms, partner)
+    far = []
+    for number in range(near - 1):
+        steps = (chips - 1 - 2 * number, chips - 2 - 2 * number)
+        route = [(2 * z + c, 2 * (z ^ steps[c]) + c) for z in range(chips) for c in range(2)]
+        far.append(lax.ppermute(pair, "tm", route))
+    beside = across(waveforms, 1)
+    merged = list(merge(owners, mine, other))
     pieces = [across(merged[step], step) for step in reversed(range(1, chips))]
     pieces = [merged[0]] + pieces[::-1]
-    left_a, left_r = prepare_waves(tlen, swap(choose_waves(near, local)), local)
+    swapped = swap(choose_waves(pair, beside, far))
+    left_a, left_r = prepare_waves(tlen, swapped, pair, beside, far)
 
     left_a, left_r, *pieces = lax.optimization_barrier((left_a, left_r, *pieces[::-1]))
     pieces = pieces[::-1]

time: 37.4 us -> 36.8 us (0.984)
  waiting for transfers between devices: 10.1 us -> 9.19 us
  starting transfers between devices: 15.2 us -> 15.7 us
    ppermute x6 -> x4, starting transfers between devices: 7.31 us -> 4.91 us  [across(): lax.ppermute(array, 'tm', [(i, i ^ 2 * step) for i in range(count_tm)])]
    ppermute x0 -> x1, starting transfers between devices: none -> 2.37 us  [shards(): far.append(lax.ppermute(pair, 'tm', route))]
    ppermute x6 -> x4, waiting for transfers between devices: 2.56 us -> 1.74 us  [across(): lax.ppermute(array, 'tm', [(i, i ^ 2 * step) for i in range(count_tm)])]
    ppermute x2, starting transfers between devices: 3.64 us -> 4.15 us  [shards(): gathered.append(lax.ppermute(parts[step], ('tm', 'sta'), route))]
    ppermute x4 -> x5, waiting for transfers between devices: 1.81 us -> 1.97 us  [swap(): return lax.ppermute(array, 'tm', [(i, i ^ 1) for i in range(count_tm)])]
    ppermute x4 -> x5, starting transfers between devices: 4.27 us -> 4.25 us  [swap(): return lax.ppermute(array, 'tm', [(i, i ^ 1) for i in range(count_tm)])]
  transfers between devices with their start and end apart: 12 -> 12, of which waited for: 5 -> 5; matrix products, arithmetic and copies ran while one was open for 0% -> 0% of each run, Pallas kernels for 15% -> 22%
where the time goes in v11:
time: 36.8 us; the launch traced here: 36.4 us
  starting transfers between devices  15.7 us (43%)
  Pallas kernels  11.4 us (31%)
  waiting for transfers between devices  9.19 us (25%)
    ppermute x2, waiting for transfers between devices, shards(): gathered.append(lax.ppermute(parts[step], ('tm', 'sta'), route))  5.47 us
    pallas_call x2, Pallas kernels, correlate(): pl.pallas_call(functools.partial(main_kernel, side, tlen, group), out_sha...  5.09 us
    ppermute x4, starting transfers between devices, across(): lax.ppermute(array, 'tm', [(i, i ^ 2 * step) for i in range(count_tm)])  4.91 us
    ppermute x5, starting transfers between devices, swap(): return lax.ppermute(array, 'tm', [(i, i ^ 1) for i in range(count_tm)])  4.25 us
    ppermute x2, starting transfers between devices, shards(): gathered.append(lax.ppermute(parts[step], ('tm', 'sta'), route))  4.15 us
    pallas_call x1, Pallas kernels, prepare_waves(): pl.pallas_call(functools.partial(waves_kernel, channels, tlen, unroll), o...  2.85 us
    ppermute x1, starting transfers between devices, shards(): far.append(lax.ppermute(pair, 'tm', route))  2.37 us
    pallas_call x1, Pallas kernels, pack(): pl.pallas_call(pack_kernel, out_shape=[jax.ShapeDtypeStruct(shape, jnp.bf...  2.22 us
  transfers between devices with their start and end apart: 12, of which 5 were waited for; matrix products, arithmetic and copies ran while one was open for 0% of the time, Pallas kernels for 22%

profile of v11, /device:TPU:7, one launch (start us, length us, event | category | flops | bytes accessed | tf_op | source)
XLA Modules:
  0.0 36.4 jit_solution(6486779473765426893)
XLA Ops:
  0.0 0.0 copy-start
  0.0 0.7 %collective-permute-start = (bf16[30,512]{1,0:T(8,128)(2,1)}, bf16[30,512]{1,0:T(8,128)(2,1)S(1)}, u32[]{:S(2)}, u32[]{:S(2)}) collective-permute-start(bf16[30,512]{1,0:T(8,128)(2,1)} %own.1), channel_id=1, source_target_pairs={{0,4},{4,0},{8,12},{12,8},{16,20},{20,16},{24,28},{28,24},{1,5},{5... | collective-permute-start | bytes 92168 | tf_op jit(solution)/shard_map/ppermute | solution.py:543
  0.7 2.2 %pack.1 = (bf16[4,12,32,128]{3,2,1,0:T(8,128)(2,1)S(1)}, bf16[4,12,32,128]{3,2,1,0:T(8,128)(2,1)S(1)}, s32[8,128]{1,0:T(8,128)S(1)}) custom-call(s32[2]{0:T(128)} %bank_blocks.1, bf16[2,30,64,100]{3,2,1,0:T(8,128)(2,1)} %bitcast.3, s32[30,2,64]{2,1,0:T(2,128)} %bitcast.4, s32[30,2,64]{2,1,0:T(2,128)} %bitcast.5), custom_call_target="tpu_custom_call" | custom-call | flops 2000000000 | bytes 2000000 | tf_op jit(solution)/shard_map/pack/pallas_call | solution.py:91
  2.9 0.0 collective-permute-done.partner
  2.9 0.1 collective-permute-start.4
  3.0 0.0 copy-done
  3.0 2.4 %collective-permute-start.2 = (bf16[2,30,512]{2,1,0:T(8,128)(2,1)S(1)}, bf16[2,30,512]{2,1,0:T(8,128)(2,1)S(1)}, u32[]{:S(2)}, u32[]{:S(2)}) collective-permute-start(bf16[2,30,512]{2,1,0:T(8,128)(2,1)S(1)} %pair_waves.1.pair), channel_id=1, source_target_pairs={{0,24},{4,20},{8,16},{12,28},{16,8},{20,4},{24,0},{28,12},{1,25},{... | collective-permute-start | bytes 184328 | tf_op jit(solution)/shard_map/ppermute | solution.py:564
  5.4 1.3 %collective-permute-start.1 = (bf16[30,512]{1,0:T(8,128)(2,1)S(1)}, bf16[30,512]{1,0:T(8,128)(2,1)S(1)}, u32[]{:S(2)}, u32[]{:S(2)}) collective-permute-start(bf16[30,512]{1,0:T(8,128)(2,1)S(1)} %copy-done), channel_id=1, source_target_pairs={{0,8},{4,12},{8,0},{12,4},{16,24},{20,28},{24,16},{28,20},{1,9},{5... | collective-permute-start | bytes 92168 | tf_op jit(solution)/shard_map/ppermute | solution.py:546
  6.7 0.0 collective-permute-done.4.other
  6.7 0.2 merge.1
  6.9 1.4 %collective-permute-start.5 = (bf16[12,32,128]{2,1,0:T(8,128)(2,1)S(1)}, bf16[12,32,128]{2,1,0:T(8,128)(2,1)S(1)}, u32[]{:S(2)}, u32[]{:S(2)}) collective-permute-start(bf16[12,32,128]{2,1,0:T(8,128)(2,1)S(1)} %get-tuple-element.33), channel_id=1, source_target_pairs={{0,24},{4,28},{8,16},{12,20},{16,8},{20,12},{24,0},{28,4},{1,25},{... | collective-permute-start | bytes 294920 | tf_op jit(solution)/shard_map/ppermute | solution.py:546
  8.3 0.0 collective-permute-start.6
  8.4 2.2 %collective-permute-start.7 = (bf16[12,32,128]{2,1,0:T(8,128)(2,1)S(1)}, bf16[12,32,128]{2,1,0:T(8,128)(2,1)S(1)}, u32[]{:S(2)}, u32[]{:S(2)}) collective-permute-start(bf16[12,32,128]{2,1,0:T(8,128)(2,1)S(1)} %get-tuple-element.35), channel_id=1, source_target_pairs={{0,8},{4,12},{8,0},{12,4},{16,24},{20,28},{24,16},{28,20},{1,9},{5... | collective-permute-start | bytes 294920 | tf_op jit(solution)/shard_map/ppermute | solution.py:546
  10.5 0.0 collective-permute-done.1.beside
  10.6 0.0 collective-permute-done.2.rest_0_
  10.6 1.4 %collective-permute-start.3 = (bf16[3,30,512]{2,1,0:T(8,128)(2,1)S(1)}, bf16[3,30,512]{2,1,0:T(8,128)(2,1)S(1)}, u32[]{:S(2)}, u32[]{:S(2)}) collective-permute-start(bf16[3,30,512]{2,1,0:T(8,128)(2,1)S(1)} %choose_waves.1), channel_id=1, source_target_pairs={{0,4},{4,0},{8,12},{12,8},{16,20},{20,16},{24,28},{28,24},{1,5},{5... | collective-permute-start | bytes 276488 | tf_op jit(solution)/shard_map/ppermute | solution.py:543
  12.0 0.9 %collective-permute-done.3.swapped = bf16[3,30,512]{2,1,0:T(8,128)(2,1)S(1)} collective-permute-done((bf16[3,30,512]{2,1,0:T(8,128)(2,1)S(1)}, bf16[3,30,512]{2,1,0:T(8,128)(2,1)S(1)}, u32[]{:S(2)}, u32[]{:S(2)}) %collective-permute-start.3) | collective-permute-done | bytes 92192 | tf_op jit(solution)/shard_map/ppermute | solution.py:543
  12.9 2.9 %prepare_waves.1 = (bf16[30,272,128]{2,1,0:T(8,128)(2,1)S(1)}, bf16[30,256,256]{2,1,0:T(8,128)(2,1)S(1)}) custom-call(bf16[3,30,512]{2,1,0:T(8,128)(2,1)S(1)} %collective-permute-done.3.swapped, bf16[2,30,512]{2,1,0:T(8,128)(2,1)S(1)} %pair_waves.1.pair, bf16[30,512]{1,0:T(8,128)(2,1)S(1)} %collective-permute-done.1.beside, ...), custom_call_target="tpu_custom_call" | custom-call | flops 50000000 | bytes 50000 | tf_op jit(solution)/shard_map/prepare_waves/pallas_call | solution.py:290
  15.8 0.0 collective-permute-done.5.refs_3_
  15.8 1.7 %collective-permute-done.6.refs_2_ = bf16[12,32,128]{2,1,0:T(8,128)(2,1)S(1)} collective-permute-done((bf16[12,32,128]{2,1,0:T(8,128)(2,1)S(1)}, bf16[12,32,128]{2,1,0:T(8,128)(2,1)S(1)}, u32[]{:S(2)}, u32[]{:S(2)}) %collective-permute-start.6) | collective-permute-done | bytes 98336 | tf_op jit(solution)/shard_map/ppermute | solution.py:546
  17.5 0.0 collective-permute-done.7.refs_1_
  17.5 0.1 choose_piece.1.piece
  17.6 1.8 %collective-permute-start.8 = (bf16[12,32,128]{2,1,0:T(8,128)(2,1)S(1)}, bf16[12,32,128]{2,1,0:T(8,128)(2,1)S(1)}, u32[]{:S(2)}, u32[]{:S(2)}) collective-permute-start(bf16[12,32,128]{2,1,0:T(8,128)(2,1)S(1)} %choose_piece.1.piece), channel_id=1, source_target_pairs={{0,4},{4,0},{8,12},{12,8},{16,20},{20,16},{24,28},{28,24},{1,5},{5... | collective-permute-start | bytes 294920 | tf_op jit(solution)/shard_map/ppermute | solution.py:543
  19.4 2.5 %correlate_first.1.rest_0_ = f32[256,256]{1,0:T(8,128)S(1)} custom-call(bf16[12,32,128]{2,1,0:T(8,128)(2,1)S(1)} %choose_piece.1.piece, bf16[30,272,128]{2,1,0:T(8,128)(2,1)S(1)} %get-tuple-element.41.left_a, bf16[30,256,256]{2,1,0:T(8,128)(2,1)S(1)} %get-tuple-element.42.left_r), custom_call_target="tpu_custom_call" | custom-call | flops 3000000000 | bytes 3000000 | tf_op jit(solution)/shard_map/correlate_first/pallas_call | solution.py:459
  22.0 0.0 collective-permute-done.8.piece
  22.0 2.6 %correlate_second.1 = (bf16[128,256]{1,0:T(8,128)(2,1)S(1)}, bf16[128,256]{1,0:T(8,128)(2,1)S(1)}) custom-call(bf16[12,32,128]{2,1,0:T(8,128)(2,1)S(1)} %collective-permute-done.8.piece, bf16[30,272,128]{2,1,0:T(8,128)(2,1)S(1)} %get-tuple-element.41.left_a, bf16[30,256,256]{2,1,0:T(8,128)(2,1)S(1)} %get-tuple-element.42.left_r, ...), custom_call_target="tpu_custom_call" | custom-call | flops 3000000000 | bytes 3000000 | tf_op jit(solution)/shard_map/correlate_second/pallas_call | solution.py:459
  24.6 4.1 %collective-permute-start.9 = (bf16[128,256]{1,0:T(8,128)(2,1)S(1)}, bf16[128,256]{1,0:T(8,128)(2,1)S(1)}, u32[]{:S(2)}, u32[]{:S(2)}) collective-permute-start(bf16[128,256]{1,0:T(8,128)(2,1)S(1)} %get-tuple-element.43), channel_id=1, source_target_pairs={{0,0},{1,8},{2,4},{3,12},{4,16},{5,24},{6,20},{7,28},{8,1},{9,9},{... | collective-permute-start | bytes 196616 | tf_op jit(solution)/shard_map/ppermute | solution.py:585
  28.6 0.1 collective-permute-start.10
  28.7 4.4 %collective-permute-done.9.refs_0_ = bf16[128,256]{1,0:T(8,128)(2,1)S(1)} collective-permute-done((bf16[128,256]{1,0:T(8,128)(2,1)S(1)}, bf16[128,256]{1,0:T(8,128)(2,1)S(1)}, u32[]{:S(2)}, u32[]{:S(2)}) %collective-permute-start.9) | collective-permute-done | bytes 65568 | tf_op jit(solution)/shard_map/ppermute | solution.py:585
  33.1 1.1 %collective-permute-done.10.refs_1_ = bf16[128,256]{1,0:T(8,128)(2,1)S(1)} collective-permute-done((bf16[128,256]{1,0:T(8,128)(2,1)S(1)}, bf16[128,256]{1,0:T(8,128)(2,1)S(1)}, u32[]{:S(2)}, u32[]{:S(2)}) %collective-permute-start.10) | collective-permute-done | bytes 65568 | tf_op jit(solution)/shard_map/ppermute | solution.py:585
  34.2 0.3 collective-permute-start.11
  34.5 1.0 %collective-permute-done.11.received = f32[64,256]{1,0:T(8,128)S(1)} collective-permute-done((f32[64,256]{1,0:T(8,128)S(1)}, f32[64,256]{1,0:T(8,128)S(1)}, u32[]{:S(2)}, u32[]{:S(2)}) %collective-permute-start.11) | collective-permute-done | bytes 65568 | tf_op jit(solution)/shard_map/ppermute | solution.py:543
  35.5 0.9 %finish.1 = f32[32,512]{1,0:T(8,128)} custom-call(f32[64,256]{1,0:T(8,128)S(1)} %get-tuple-element.45.ours, f32[64,256]{1,0:T(8,128)S(1)} %collective-permute-done.11.received), custom_call_target="tpu_custom_call" | custom-call | flops 1000000000 | bytes 1000000 | tf_op jit(solution)/shard_map/finish/pallas_call | solution.py:522
  (3 shorter events, 0.1 us)
Async XLA Ops:
  0.0 3.0 %copy-start = (bf16[30,512]{1,0:T(8,128)(2,1)S(1)}, bf16[30,512]{1,0:T(8,128)(2,1)}, u32[]{:S(2)}) copy-start(bf16[30,512]{1,0:T(8,128)(2,1)} %own.1) | copy-start | bytes 92164
  0.0 2.9 %collective-permute-start = (bf16[30,512]{1,0:T(8,128)(2,1)}, bf16[30,512]{1,0:T(8,128)(2,1)S(1)}, u32[]{:S(2)}, u32[]{:S(2)}) collective-permute-start(bf16[30,512]{1,0:T(8,128)(2,1)} %own.1), channel_id=1, source_target_pairs={{0,4},{4,0},{8,12},{12,8},{16,20},{20,16},{24,28},{28,24},{1,5},{5... | collective-permute-start | bytes 92168 | tf_op jit(solution)/shard_map/ppermute | solution.py:543
  2.9 3.8 %collective-permute-start.4 = (bf16[4,12,32,128]{3,2,1,0:T(8,128)(2,1)S(1)}, bf16[4,12,32,128]{3,2,1,0:T(8,128)(2,1)S(1)}, u32[]{:S(2)}, u32[]{:S(2)}) collective-permute-start(bf16[4,12,32,128]{3,2,1,0:T(8,128)(2,1)S(1)} %get-tuple-element.32), channel_id=1, source_target_pairs={{0,4},{4,0},{8,12},{12,8},{16,20},{20,16},{24,28},{28,24},{1,5},{5... | collective-permute-start | bytes 1179656 | tf_op jit(solution)/shard_map/ppermute | solution.py:543
  3.0 7.5 %collective-permute-start.2 = (bf16[2,30,512]{2,1,0:T(8,128)(2,1)S(1)}, bf16[2,30,512]{2,1,0:T(8,128)(2,1)S(1)}, u32[]{:S(2)}, u32[]{:S(2)}) collective-permute-start(bf16[2,30,512]{2,1,0:T(8,128)(2,1)S(1)} %pair_waves.1.pair), channel_id=1, source_target_pairs={{0,24},{4,20},{8,16},{12,28},{16,8},{20,4},{24,0},{28,12},{1,25},{... | collective-permute-start | bytes 184328 | tf_op jit(solution)/shard_map/ppermute | solution.py:564
  5.4 5.1 %collective-permute-start.1 = (bf16[30,512]{1,0:T(8,128)(2,1)S(1)}, bf16[30,512]{1,0:T(8,128)(2,1)S(1)}, u32[]{:S(2)}, u32[]{:S(2)}) collective-permute-start(bf16[30,512]{1,0:T(8,128)(2,1)S(1)} %copy-done), channel_id=1, source_target_pairs={{0,8},{4,12},{8,0},{12,4},{16,24},{20,28},{24,16},{28,20},{1,9},{5... | collective-permute-start | bytes 92168 | tf_op jit(solution)/shard_map/ppermute | solution.py:546
  6.9 8.8 %collective-permute-start.5 = (bf16[12,32,128]{2,1,0:T(8,128)(2,1)S(1)}, bf16[12,32,128]{2,1,0:T(8,128)(2,1)S(1)}, u32[]{:S(2)}, u32[]{:S(2)}) collective-permute-start(bf16[12,32,128]{2,1,0:T(8,128)(2,1)S(1)} %get-tuple-element.33), channel_id=1, source_target_pairs={{0,24},{4,28},{8,16},{12,20},{16,8},{20,12},{24,0},{28,4},{1,25},{... | collective-permute-start | bytes 294920 | tf_op jit(solution)/shard_map/ppermute | solution.py:546
  8.3 9.2 %collective-permute-start.6 = (bf16[12,32,128]{2,1,0:T(8,128)(2,1)S(1)}, bf16[12,32,128]{2,1,0:T(8,128)(2,1)S(1)}, u32[]{:S(2)}, u32[]{:S(2)}) collective-permute-start(bf16[12,32,128]{2,1,0:T(8,128)(2,1)S(1)} %get-tuple-element.34), channel_id=1, source_target_pairs={{0,16},{4,20},{8,24},{12,28},{16,0},{20,4},{24,8},{28,12},{1,17},{... | collective-permute-start | bytes 294920 | tf_op jit(solution)/shard_map/ppermute | solution.py:546
  8.4 9.2 %collective-permute-start.7 = (bf16[12,32,128]{2,1,0:T(8,128)(2,1)S(1)}, bf16[12,32,128]{2,1,0:T(8,128)(2,1)S(1)}, u32[]{:S(2)}, u32[]{:S(2)}) collective-permute-start(bf16[12,32,128]{2,1,0:T(8,128)(2,1)S(1)} %get-tuple-element.35), channel_id=1, source_target_pairs={{0,8},{4,12},{8,0},{12,4},{16,24},{20,28},{24,16},{28,20},{1,9},{5... | collective-permute-start | bytes 294920 | tf_op jit(solution)/shard_map/ppermute | solution.py:546
  10.6 2.3 %collective-permute-start.3 = (bf16[3,30,512]{2,1,0:T(8,128)(2,1)S(1)}, bf16[3,30,512]{2,1,0:T(8,128)(2,1)S(1)}, u32[]{:S(2)}, u32[]{:S(2)}) collective-permute-start(bf16[3,30,512]{2,1,0:T(8,128)(2,1)S(1)} %choose_waves.1), channel_id=1, source_target_pairs={{0,4},{4,0},{8,12},{12,8},{16,20},{20,16},{24,28},{28,24},{1,5},{5... | collective-permute-start | bytes 276488 | tf_op jit(solution)/shard_map/ppermute | solution.py:543
  17.6 4.3 %collective-permute-start.8 = (bf16[12,32,128]{2,1,0:T(8,128)(2,1)S(1)}, bf16[12,32,128]{2,1,0:T(8,128)(2,1)S(1)}, u32[]{:S(2)}, u32[]{:S(2)}) collective-permute-start(bf16[12,32,128]{2,1,0:T(8,128)(2,1)S(1)} %choose_piece.1.piece), channel_id=1, source_target_pairs={{0,4},{4,0},{8,12},{12,8},{16,20},{20,16},{24,28},{28,24},{1,5},{5... | collective-permute-start | bytes 294920 | tf_op jit(solution)/shard_map/ppermute | solution.py:543
  24.6 8.6 %collective-permute-start.9 = (bf16[128,256]{1,0:T(8,128)(2,1)S(1)}, bf16[128,256]{1,0:T(8,128)(2,1)S(1)}, u32[]{:S(2)}, u32[]{:S(2)}) collective-permute-start(bf16[128,256]{1,0:T(8,128)(2,1)S(1)} %get-tuple-element.43), channel_id=1, source_target_pairs={{0,0},{1,8},{2,4},{3,12},{4,16},{5,24},{6,20},{7,28},{8,1},{9,9},{... | collective-permute-start | bytes 196616 | tf_op jit(solution)/shard_map/ppermute | solution.py:585
  28.6 5.5 %collective-permute-start.10 = (bf16[128,256]{1,0:T(8,128)(2,1)S(1)}, bf16[128,256]{1,0:T(8,128)(2,1)S(1)}, u32[]{:S(2)}, u32[]{:S(2)}) collective-permute-start(bf16[128,256]{1,0:T(8,128)(2,1)S(1)} %get-tuple-element.44), channel_id=1, source_target_pairs={{0,8},{1,0},{2,12},{3,4},{4,24},{5,16},{6,28},{7,20},{8,9},{9,1},{... | collective-permute-start | bytes 196616 | tf_op jit(solution)/shard_map/ppermute | solution.py:585
  34.2 1.3 %collective-permute-start.11 = (f32[64,256]{1,0:T(8,128)S(1)}, f32[64,256]{1,0:T(8,128)S(1)}, u32[]{:S(2)}, u32[]{:S(2)}) collective-permute-start(f32[64,256]{1,0:T(8,128)S(1)} %get-tuple-element.46), channel_id=1, source_target_pairs={{0,4},{4,0},{8,12},{12,8},{16,20},{20,16},{24,28},{28,24},{1,5},{5... | collective-permute-start | bytes 196616 | tf_op jit(solution)/shard_map/ppermute | solution.py:543

commit v12 on v11

--- a/solution.py
+++ b/solution.py
@@ -35,6 +35,7 @@
     chips, _, group, _ = mine.shape
     half = channels // 2
     me = lax.axis_index("tm") % 2
+    station = lax.axis_index("sta")
     fetch = [
         pltpu.make_async_copy(source, target, sems.at[index])
         for index, (source, target) in enumerate(
@@ -70,7 +71,7 @@
                 extra = TILES + tile // 4
                 start = QUARTER * (tile % 4)
                 for index in range(events // group):
-                    chip = which * (events // group) + index
+                    chip = jnp.bitwise_xor(station, which * (events // group) + index)
                     rows = slice(index * group, (index + 1) * group)
                     out[chip, tile, :, 0:tlen] = raw[slots[which], first + tile, rows, :]
                     out[chip, tile, :, tlen : tlen + QUARTER] = raw[
@@ -111,9 +112,11 @@
 def merge_kernel(owners, mine, other, *outs):
     chips = len(outs)
     me = lax.axis_index("tm")
+    station = lax.axis_index("sta")
     for step, out in enumerate(outs):
         dest = jnp.bitwise_xor(me // 2, step)
-        owner = jnp.where(dest < chips // 2, owners[0, 0], owners[1, 0])
+        first = jnp.bitwise_xor(dest, station) < chips // 2
+        owner = jnp.where(first, owners[0, 0], owners[1, 0])
         here = owner % 2 == me % 2
 
         @pl.when(here)
@@ -203,7 +206,8 @@
 def own_kernel(owners, *refs):
     pieces, out = refs[:-1], refs[-1]
     chip = lax.axis_index("tm") // 2
-    owner = jnp.where(chip < len(pieces) // 2, owners[0, 0], owners[1, 0])
+    first = jnp.bitwise_xor(chip, lax.axis_index("sta")) < len(pieces) // 2
+    owner = jnp.where(first, owners[0, 0], owners[1, 0])
     source = jnp.bitwise_xor(owner // 2, chip)
     value = pieces[0][...]
     for number, piece in enumerate(pieces[1:], 1):
@@ -581,7 +585,8 @@
         for d in range(count_tm):
             for s in range(count_sta):
                 dest = near * (d % 2) + (s % near ^ step)
-                route.append((d * count_sta + s, (2 * dest + s // near) * count_sta + d // 2))
+                sta = d // 2 ^ s
+                route.append((d * count_sta + s, (2 * dest + s // near) * count_sta + sta))
         gathered.append(lax.ppermute(parts[step], ("tm", "sta"), route))
     ours, send = add(gathered)
     return finish(group, samples, ours, swap(send))

time: 36.8 us -> 39 us (1.060)
  the two profiles are of different devices: /device:TPU:7 before, /device:TPU:5 now
where the time goes in v12:
time: 39 us; the launch traced here: 38.9 us
  starting transfers between devices  21.4 us (55%)
  Pallas kernels  11.4 us (29%)
  waiting for transfers between devices  5.88 us (15%)
    ppermute x5, starting transfers between devices, swap(): return lax.ppermute(array, 'tm', [(i, i ^ 1) for i in range(count_tm)])  8.03 us
    ppermute x2, starting transfers between devices, shards(): gathered.append(lax.ppermute(parts[step], ('tm', 'sta'), route))  6.1 us
    pallas_call x2, Pallas kernels, correlate(): pl.pallas_call(functools.partial(main_kernel, side, tlen, group), out_sha...  5.08 us
    ppermute x4, starting transfers between devices, across(): lax.ppermute(array, 'tm', [(i, i ^ 2 * step) for i in range(count_tm)])  4.91 us
    pallas_call x1, Pallas kernels, prepare_waves(): pl.pallas_call(functools.partial(waves_kernel, channels, tlen, unroll), o...  2.85 us
    ppermute x1, starting transfers between devices, shards(): far.append(lax.ppermute(pair, 'tm', route))  2.37 us
    ppermute x2, waiting for transfers between devices, shards(): gathered.append(lax.ppermute(parts[step], ('tm', 'sta'), route))  2.29 us
    pallas_call x1, Pallas kernels, pack(): pl.pallas_call(pack_kernel, out_shape=[jax.ShapeDtypeStruct(shape, jnp.bf...  2.22 us
  transfers between devices with their start and end apart: 12, of which 4 were waited for; matrix products, arithmetic and copies ran while one was open for 0% of the time, Pallas kernels for 20%

profile of v12, /device:TPU:5, one launch (start us, length us, event | category | flops | bytes accessed | tf_op | source)
XLA Modules:
  0.0 38.9 jit_solution(1862394971828406776)
XLA Ops:
  0.0 0.0 copy-start
  0.0 0.7 %collective-permute-start = (bf16[30,512]{1,0:T(8,128)(2,1)}, bf16[30,512]{1,0:T(8,128)(2,1)S(1)}, u32[]{:S(2)}, u32[]{:S(2)}) collective-permute-start(bf16[30,512]{1,0:T(8,128)(2,1)} %own.1), channel_id=1, source_target_pairs={{0,4},{4,0},{8,12},{12,8},{16,20},{20,16},{24,28},{28,24},{1,5},{5... | collective-permute-start | bytes 92168 | tf_op jit(solution)/shard_map/ppermute | solution.py:547
  0.7 2.2 %pack.1 = (bf16[4,12,32,128]{3,2,1,0:T(8,128)(2,1)S(1)}, bf16[4,12,32,128]{3,2,1,0:T(8,128)(2,1)S(1)}, s32[8,128]{1,0:T(8,128)S(1)}) custom-call(s32[2]{0:T(128)} %bank_blocks.1, bf16[2,30,64,100]{3,2,1,0:T(8,128)(2,1)} %bitcast.3, s32[30,2,64]{2,1,0:T(2,128)} %bitcast.4, s32[30,2,64]{2,1,0:T(2,128)} %bitcast.5), custom_call_target="tpu_custom_call" | custom-call | flops 2000000000 | bytes 2000000 | tf_op jit(solution)/shard_map/pack/pallas_call | solution.py:92
  2.9 0.0 collective-permute-done.partner
  2.9 0.1 collective-permute-start.4
  3.0 0.0 copy-done
  3.0 2.4 %collective-permute-start.2 = (bf16[2,30,512]{2,1,0:T(8,128)(2,1)S(1)}, bf16[2,30,512]{2,1,0:T(8,128)(2,1)S(1)}, u32[]{:S(2)}, u32[]{:S(2)}) collective-permute-start(bf16[2,30,512]{2,1,0:T(8,128)(2,1)S(1)} %pair_waves.1.pair), channel_id=1, source_target_pairs={{0,24},{4,20},{8,16},{12,28},{16,8},{20,4},{24,0},{28,12},{1,25},{... | collective-permute-start | bytes 184328 | tf_op jit(solution)/shard_map/ppermute | solution.py:568
  5.4 1.3 %collective-permute-start.1 = (bf16[30,512]{1,0:T(8,128)(2,1)S(1)}, bf16[30,512]{1,0:T(8,128)(2,1)S(1)}, u32[]{:S(2)}, u32[]{:S(2)}) collective-permute-start(bf16[30,512]{1,0:T(8,128)(2,1)S(1)} %copy-done), channel_id=1, source_target_pairs={{0,8},{4,12},{8,0},{12,4},{16,24},{20,28},{24,16},{28,20},{1,9},{5... | collective-permute-start | bytes 92168 | tf_op jit(solution)/shard_map/ppermute | solution.py:550
  6.7 0.0 collective-permute-done.4.other
  6.7 0.2 merge.1
  6.9 1.4 %collective-permute-start.5 = (bf16[12,32,128]{2,1,0:T(8,128)(2,1)S(1)}, bf16[12,32,128]{2,1,0:T(8,128)(2,1)S(1)}, u32[]{:S(2)}, u32[]{:S(2)}) collective-permute-start(bf16[12,32,128]{2,1,0:T(8,128)(2,1)S(1)} %get-tuple-element.33), channel_id=1, source_target_pairs={{0,24},{4,28},{8,16},{12,20},{16,8},{20,12},{24,0},{28,4},{1,25},{... | collective-permute-start | bytes 294920 | tf_op jit(solution)/shard_map/ppermute | solution.py:550
  8.3 0.0 collective-permute-start.6
  8.4 2.2 %collective-permute-start.7 = (bf16[12,32,128]{2,1,0:T(8,128)(2,1)S(1)}, bf16[12,32,128]{2,1,0:T(8,128)(2,1)S(1)}, u32[]{:S(2)}, u32[]{:S(2)}) collective-permute-start(bf16[12,32,128]{2,1,0:T(8,128)(2,1)S(1)} %get-tuple-element.35), channel_id=1, source_target_pairs={{0,8},{4,12},{8,0},{12,4},{16,24},{20,28},{24,16},{28,20},{1,9},{5... | collective-permute-start | bytes 294920 | tf_op jit(solution)/shard_map/ppermute | solution.py:550
  10.5 0.0 collective-permute-done.1.beside
  10.6 0.0 collective-permute-done.2.rest_0_
  10.6 1.4 %collective-permute-start.3 = (bf16[3,30,512]{2,1,0:T(8,128)(2,1)S(1)}, bf16[3,30,512]{2,1,0:T(8,128)(2,1)S(1)}, u32[]{:S(2)}, u32[]{:S(2)}) collective-permute-start(bf16[3,30,512]{2,1,0:T(8,128)(2,1)S(1)} %choose_waves.1), channel_id=1, source_target_pairs={{0,4},{4,0},{8,12},{12,8},{16,20},{20,16},{24,28},{28,24},{1,5},{5... | collective-permute-start | bytes 276488 | tf_op jit(solution)/shard_map/ppermute | solution.py:547
  12.0 0.9 %collective-permute-done.3.swapped = bf16[3,30,512]{2,1,0:T(8,128)(2,1)S(1)} collective-permute-done((bf16[3,30,512]{2,1,0:T(8,128)(2,1)S(1)}, bf16[3,30,512]{2,1,0:T(8,128)(2,1)S(1)}, u32[]{:S(2)}, u32[]{:S(2)}) %collective-permute-start.3) | collective-permute-done | bytes 92192 | tf_op jit(solution)/shard_map/ppermute | solution.py:547
  12.9 2.9 %prepare_waves.1 = (bf16[30,272,128]{2,1,0:T(8,128)(2,1)S(1)}, bf16[30,256,256]{2,1,0:T(8,128)(2,1)S(1)}) custom-call(bf16[3,30,512]{2,1,0:T(8,128)(2,1)S(1)} %collective-permute-done.3.swapped, bf16[2,30,512]{2,1,0:T(8,128)(2,1)S(1)} %pair_waves.1.pair, bf16[30,512]{1,0:T(8,128)(2,1)S(1)} %collective-permute-done.1.beside, ...), custom_call_target="tpu_custom_call" | custom-call | flops 50000000 | bytes 50000 | tf_op jit(solution)/shard_map/prepare_waves/pallas_call | solution.py:294
  15.8 0.0 collective-permute-done.5.refs_3_
  15.8 1.7 %collective-permute-done.6.refs_2_ = bf16[12,32,128]{2,1,0:T(8,128)(2,1)S(1)} collective-permute-done((bf16[12,32,128]{2,1,0:T(8,128)(2,1)S(1)}, bf16[12,32,128]{2,1,0:T(8,128)(2,1)S(1)}, u32[]{:S(2)}, u32[]{:S(2)}) %collective-permute-start.6) | collective-permute-done | bytes 98336 | tf_op jit(solution)/shard_map/ppermute | solution.py:550
  17.5 0.0 collective-permute-done.7.refs_1_
  17.5 0.1 choose_piece.1.piece
  17.6 1.8 %collective-permute-start.8 = (bf16[12,32,128]{2,1,0:T(8,128)(2,1)S(1)}, bf16[12,32,128]{2,1,0:T(8,128)(2,1)S(1)}, u32[]{:S(2)}, u32[]{:S(2)}) collective-permute-start(bf16[12,32,128]{2,1,0:T(8,128)(2,1)S(1)} %choose_piece.1.piece), channel_id=1, source_target_pairs={{0,4},{4,0},{8,12},{12,8},{16,20},{20,16},{24,28},{28,24},{1,5},{5... | collective-permute-start | bytes 294920 | tf_op jit(solution)/shard_map/ppermute | solution.py:547
  19.4 2.5 %correlate_first.1.rest_0_ = f32[256,256]{1,0:T(8,128)S(1)} custom-call(bf16[12,32,128]{2,1,0:T(8,128)(2,1)S(1)} %choose_piece.1.piece, bf16[30,272,128]{2,1,0:T(8,128)(2,1)S(1)} %get-tuple-element.41.left_a, bf16[30,256,256]{2,1,0:T(8,128)(2,1)S(1)} %get-tuple-element.42.left_r), custom_call_target="tpu_custom_call" | custom-call | flops 3000000000 | bytes 3000000 | tf_op jit(solution)/shard_map/correlate_first/pallas_call | solution.py:463
  22.0 0.0 collective-permute-done.8.piece
  22.0 2.6 %correlate_second.1 = (bf16[128,256]{1,0:T(8,128)(2,1)S(1)}, bf16[128,256]{1,0:T(8,128)(2,1)S(1)}) custom-call(bf16[12,32,128]{2,1,0:T(8,128)(2,1)S(1)} %collective-permute-done.8.piece, bf16[30,272,128]{2,1,0:T(8,128)(2,1)S(1)} %get-tuple-element.41.left_a, bf16[30,256,256]{2,1,0:T(8,128)(2,1)S(1)} %get-tuple-element.42.left_r, ...), custom_call_target="tpu_custom_call" | custom-call | flops 3000000000 | bytes 3000000 | tf_op jit(solution)/shard_map/correlate_second/pallas_call | solution.py:463
  24.5 1.9 %collective-permute-start.9 = (bf16[128,256]{1,0:T(8,128)(2,1)S(1)}, bf16[128,256]{1,0:T(8,128)(2,1)S(1)}, u32[]{:S(2)}, u32[]{:S(2)}) collective-permute-start(bf16[128,256]{1,0:T(8,128)(2,1)S(1)} %get-tuple-element.43), channel_id=1, source_target_pairs={{0,0},{1,9},{2,6},{3,15},{4,16},{5,25},{6,22},{7,31},{8,1},{9,8},{... | collective-permute-start | bytes 196616 | tf_op jit(solution)/shard_map/ppermute | solution.py:590
  26.5 4.2 %collective-permute-start.10 = (bf16[128,256]{1,0:T(8,128)(2,1)S(1)}, bf16[128,256]{1,0:T(8,128)(2,1)S(1)}, u32[]{:S(2)}, u32[]{:S(2)}) collective-permute-start(bf16[128,256]{1,0:T(8,128)(2,1)S(1)} %get-tuple-element.44), channel_id=1, source_target_pairs={{0,8},{1,1},{2,14},{3,7},{4,24},{5,17},{6,30},{7,23},{8,9},{9,0},{... | collective-permute-start | bytes 196616 | tf_op jit(solution)/shard_map/ppermute | solution.py:590
  30.7 0.0 collective-permute-done.9.refs_0_
  30.7 2.3 %collective-permute-done.10.refs_1_ = bf16[128,256]{1,0:T(8,128)(2,1)S(1)} collective-permute-done((bf16[128,256]{1,0:T(8,128)(2,1)S(1)}, bf16[128,256]{1,0:T(8,128)(2,1)S(1)}, u32[]{:S(2)}, u32[]{:S(2)}) %collective-permute-start.10) | collective-permute-done | bytes 65568 | tf_op jit(solution)/shard_map/ppermute | solution.py:590
  33.0 4.1 %collective-permute-start.11 = (f32[64,256]{1,0:T(8,128)S(1)}, f32[64,256]{1,0:T(8,128)S(1)}, u32[]{:S(2)}, u32[]{:S(2)}) collective-permute-start(f32[64,256]{1,0:T(8,128)S(1)} %get-tuple-element.46), channel_id=1, source_target_pairs={{0,4},{4,0},{8,12},{12,8},{16,20},{20,16},{24,28},{28,24},{1,5},{5... | collective-permute-start | bytes 196616 | tf_op jit(solution)/shard_map/ppermute | solution.py:547
  37.1 0.9 %collective-permute-done.11.received = f32[64,256]{1,0:T(8,128)S(1)} collective-permute-done((f32[64,256]{1,0:T(8,128)S(1)}, f32[64,256]{1,0:T(8,128)S(1)}, u32[]{:S(2)}, u32[]{:S(2)}) %collective-permute-start.11) | collective-permute-done | bytes 65568 | tf_op jit(solution)/shard_map/ppermute | solution.py:547
  38.0 0.9 %finish.1 = f32[32,512]{1,0:T(8,128)} custom-call(f32[64,256]{1,0:T(8,128)S(1)} %get-tuple-element.45.ours, f32[64,256]{1,0:T(8,128)S(1)} %collective-permute-done.11.received), custom_call_target="tpu_custom_call" | custom-call | flops 1000000000 | bytes 1000000 | tf_op jit(solution)/shard_map/finish/pallas_call | solution.py:526
  (3 shorter events, 0.1 us)
Async XLA Ops:
  0.0 3.0 %copy-start = (bf16[30,512]{1,0:T(8,128)(2,1)S(1)}, bf16[30,512]{1,0:T(8,128)(2,1)}, u32[]{:S(2)}) copy-start(bf16[30,512]{1,0:T(8,128)(2,1)} %own.1) | copy-start | bytes 92164
  0.0 2.9 %collective-permute-start = (bf16[30,512]{1,0:T(8,128)(2,1)}, bf16[30,512]{1,0:T(8,128)(2,1)S(1)}, u32[]{:S(2)}, u32[]{:S(2)}) collective-permute-start(bf16[30,512]{1,0:T(8,128)(2,1)} %own.1), channel_id=1, source_target_pairs={{0,4},{4,0},{8,12},{12,8},{16,20},{20,16},{24,28},{28,24},{1,5},{5... | collective-permute-start | bytes 92168 | tf_op jit(solution)/shard_map/ppermute | solution.py:547
  2.9 3.8 %collective-permute-start.4 = (bf16[4,12,32,128]{3,2,1,0:T(8,128)(2,1)S(1)}, bf16[4,12,32,128]{3,2,1,0:T(8,128)(2,1)S(1)}, u32[]{:S(2)}, u32[]{:S(2)}) collective-permute-start(bf16[4,12,32,128]{3,2,1,0:T(8,128)(2,1)S(1)} %get-tuple-element.32), channel_id=1, source_target_pairs={{0,4},{4,0},{8,12},{12,8},{16,20},{20,16},{24,28},{28,24},{1,5},{5... | collective-permute-start | bytes 1179656 | tf_op jit(solution)/shard_map/ppermute | solution.py:547
  3.0 7.5 %collective-permute-start.2 = (bf16[2,30,512]{2,1,0:T(8,128)(2,1)S(1)}, bf16[2,30,512]{2,1,0:T(8,128)(2,1)S(1)}, u32[]{:S(2)}, u32[]{:S(2)}) collective-permute-start(bf16[2,30,512]{2,1,0:T(8,128)(2,1)S(1)} %pair_waves.1.pair), channel_id=1, source_target_pairs={{0,24},{4,20},{8,16},{12,28},{16,8},{20,4},{24,0},{28,12},{1,25},{... | collective-permute-start | bytes 184328 | tf_op jit(solution)/shard_map/ppermute | solution.py:568
  5.4 5.1 %collective-permute-start.1 = (bf16[30,512]{1,0:T(8,128)(2,1)S(1)}, bf16[30,512]{1,0:T(8,128)(2,1)S(1)}, u32[]{:S(2)}, u32[]{:S(2)}) collective-permute-start(bf16[30,512]{1,0:T(8,128)(2,1)S(1)} %copy-done), channel_id=1, source_target_pairs={{0,8},{4,12},{8,0},{12,4},{16,24},{20,28},{24,16},{28,20},{1,9},{5... | collective-permute-start | bytes 92168 | tf_op jit(solution)/shard_map/ppermute | solution.py:550
  6.9 8.8 %collective-permute-start.5 = (bf16[12,32,128]{2,1,0:T(8,128)(2,1)S(1)}, bf16[12,32,128]{2,1,0:T(8,128)(2,1)S(1)}, u32[]{:S(2)}, u32[]{:S(2)}) collective-permute-start(bf16[12,32,128]{2,1,0:T(8,128)(2,1)S(1)} %get-tuple-element.33), channel_id=1, source_target_pairs={{0,24},{4,28},{8,16},{12,20},{16,8},{20,12},{24,0},{28,4},{1,25},{... | collective-permute-start | bytes 294920 | tf_op jit(solution)/shard_map/ppermute | solution.py:550
  8.3 9.2 %collective-permute-start.6 = (bf16[12,32,128]{2,1,0:T(8,128)(2,1)S(1)}, bf16[12,32,128]{2,1,0:T(8,128)(2,1)S(1)}, u32[]{:S(2)}, u32[]{:S(2)}) collective-permute-start(bf16[12,32,128]{2,1,0:T(8,128)(2,1)S(1)} %get-tuple-element.34), channel_id=1, source_target_pairs={{0,16},{4,20},{8,24},{12,28},{16,0},{20,4},{24,8},{28,12},{1,17},{... | collective-permute-start | bytes 294920 | tf_op jit(solution)/shard_map/ppermute | solution.py:550
  8.4 9.2 %collective-permute-start.7 = (bf16[12,32,128]{2,1,0:T(8,128)(2,1)S(1)}, bf16[12,32,128]{2,1,0:T(8,128)(2,1)S(1)}, u32[]{:S(2)}, u32[]{:S(2)}) collective-permute-start(bf16[12,32,128]{2,1,0:T(8,128)(2,1)S(1)} %get-tuple-element.35), channel_id=1, source_target_pairs={{0,8},{4,12},{8,0},{12,4},{16,24},{20,28},{24,16},{28,20},{1,9},{5... | collective-permute-start | bytes 294920 | tf_op jit(solution)/shard_map/ppermute | solution.py:550
  10.6 2.3 %collective-permute-start.3 = (bf16[3,30,512]{2,1,0:T(8,128)(2,1)S(1)}, bf16[3,30,512]{2,1,0:T(8,128)(2,1)S(1)}, u32[]{:S(2)}, u32[]{:S(2)}) collective-permute-start(bf16[3,30,512]{2,1,0:T(8,128)(2,1)S(1)} %choose_waves.1), channel_id=1, source_target_pairs={{0,4},{4,0},{8,12},{12,8},{16,20},{20,16},{24,28},{28,24},{1,5},{5... | collective-permute-start | bytes 276488 | tf_op jit(solution)/shard_map/ppermute | solution.py:547
  17.6 4.3 %collective-permute-start.8 = (bf16[12,32,128]{2,1,0:T(8,128)(2,1)S(1)}, bf16[12,32,128]{2,1,0:T(8,128)(2,1)S(1)}, u32[]{:S(2)}, u32[]{:S(2)}) collective-permute-start(bf16[12,32,128]{2,1,0:T(8,128)(2,1)S(1)} %choose_piece.1.piece), channel_id=1, source_target_pairs={{0,4},{4,0},{8,12},{12,8},{16,20},{20,16},{24,28},{28,24},{1,5},{5... | collective-permute-start | bytes 294920 | tf_op jit(solution)/shard_map/ppermute | solution.py:547
  24.5 6.1 %collective-permute-start.9 = (bf16[128,256]{1,0:T(8,128)(2,1)S(1)}, bf16[128,256]{1,0:T(8,128)(2,1)S(1)}, u32[]{:S(2)}, u32[]{:S(2)}) collective-permute-start(bf16[128,256]{1,0:T(8,128)(2,1)S(1)} %get-tuple-element.43), channel_id=1, source_target_pairs={{0,0},{1,9},{2,6},{3,15},{4,16},{5,25},{6,22},{7,31},{8,1},{9,8},{... | collective-permute-start | bytes 196616 | tf_op jit(solution)/shard_map/ppermute | solution.py:590
  26.5 6.5 %collective-permute-start.10 = (bf16[128,256]{1,0:T(8,128)(2,1)S(1)}, bf16[128,256]{1,0:T(8,128)(2,1)S(1)}, u32[]{:S(2)}, u32[]{:S(2)}) collective-permute-start(bf16[128,256]{1,0:T(8,128)(2,1)S(1)} %get-tuple-element.44), channel_id=1, source_target_pairs={{0,8},{1,1},{2,14},{3,7},{4,24},{5,17},{6,30},{7,23},{8,9},{9,0},{... | collective-permute-start | bytes 196616 | tf_op jit(solution)/shard_map/ppermute | solution.py:590
  33.0 5.0 %collective-permute-start.11 = (f32[64,256]{1,0:T(8,128)S(1)}, f32[64,256]{1,0:T(8,128)S(1)}, u32[]{:S(2)}, u32[]{:S(2)}) collective-permute-start(f32[64,256]{1,0:T(8,128)S(1)} %get-tuple-element.46), channel_id=1, source_target_pairs={{0,4},{4,0},{8,12},{12,8},{16,20},{20,16},{24,28},{28,24},{1,5},{5... | collective-permute-start | bytes 196616 | tf_op jit(solution)/shard_map/ppermute | solution.py:547

commit v13 on v11

--- a/solution.py
+++ b/solution.py
@@ -108,34 +108,85 @@
     )(*held)
 
 
+def owner_chip(owners, dest, chips):
+    return jnp.where(dest < chips // 2, owners[0, 0], owners[1, 0]) // 2
+
+
 def merge_kernel(owners, mine, other, *outs):
-    chips = len(outs)
+    chips = mine.shape[0]
+    size = TILES // 2
     me = lax.axis_index("tm")
-    for step, out in enumerate(outs):
+    for step in range(chips):
         dest = jnp.bitwise_xor(me // 2, step)
         owner = jnp.where(dest < chips // 2, owners[0, 0], owners[1, 0])
-        here = owner % 2 == me % 2
-
-        @pl.when(here)
-        def _():
-            out[...] = mine[dest]
-
-        @pl.when(jnp.logical_not(here))
-        def _():
-            out[...] = other[dest]
+        for source, taken in ((mine, owner % 2 == me % 2), (other, owner % 2 != me % 2)):
+
+            @pl.when(taken)
+            def _():
+                for part in range(2):
+                    tiles = slice(size * part, size * (part + 1))
+                    outs[2 * part + step % 2][step // 2] = source[dest, tiles]
 
 
 def merge(owners, mine, other):
-    chips = mine.shape[0]
+    chips, _, group, _ = mine.shape
+    out = jax.ShapeDtypeStruct((chips // 2, TILES // 2, group, LANES), mine.dtype)
     return pl.pallas_call(
         merge_kernel,
-        out_shape=[jax.ShapeDtypeStruct(mine.shape[1:], mine.dtype)] * chips,
+        out_shape=[out] * 4,
         in_specs=[VMEM] * 3,
-        out_specs=[VMEM] * chips,
+        out_specs=[VMEM] * 4,
         compiler_params=params(),
         cost_estimate=cost(0.3),
         name="merge",
     )(owners, mine, other)
+
+
+def halve_kernel(bit, chips, owners, keep, received, *outs):
+    chip = lax.axis_index("tm") // 2
+    for entry in range(keep.shape[0]):
+        dest = jnp.bitwise_xor(chip, 2 * bit * entry)
+        owner = owner_chip(owners, dest, chips)
+        there = jnp.bitwise_and(jnp.bitwise_xor(owner, chip), bit) > 0
+        outs[entry % 2][entry // 2] = jnp.where(there, received[entry], keep[entry])
+
+
+def halve(bit, chips, owners, keep, received):
+    count = keep.shape[0] // 2
+    out = jax.ShapeDtypeStruct((count,) + keep.shape[1:], keep.dtype)
+    return pl.pallas_call(
+        functools.partial(halve_kernel, bit, chips),
+        out_shape=[out] * 2,
+        in_specs=[VMEM] * 3,
+        out_specs=[VMEM] * 2,
+        compiler_params=params(),
+        cost_estimate=cost(0.05),
+        name="halve",
+    )(owners, keep, received)
+
+
+def own_kernel(chips, owners, *refs):
+    parts, out = refs[:-1], refs[-1]
+    chip = lax.axis_index("tm") // 2
+    owner = owner_chip(owners, chip, chips)
+    there = jnp.bitwise_and(jnp.bitwise_xor(owner, chip), chips // 2) > 0
+    size = parts[0].shape[1]
+    for part in range(2):
+        keep, received = parts[2 * part : 2 * part + 2]
+        out[size * part : size * (part + 1)] = jnp.where(there, received[0], keep[0])
+
+
+def choose_piece(chips, owners, parts):
+    _, size, group, lanes = parts[0].shape
+    return pl.pallas_call(
+        functools.partial(own_kernel, chips),
+        out_shape=jax.ShapeDtypeStruct((2 * size, group, lanes), parts[0].dtype),
+        in_specs=[VMEM] * 5,
+        out_specs=VMEM,
+        compiler_params=params(),
+        cost_estimate=cost(0.3),
+        name="choose_piece",
+    )(owners, *parts)
 
 
 def lagged(row, ahead):
@@ -198,29 +249,6 @@
         cost_estimate=cost(0.05),
         name="choose_waves",
     )(pair, beside, *far)
-
-
-def own_kernel(owners, *refs):
-    pieces, out = refs[:-1], refs[-1]
-    chip = lax.axis_index("tm") // 2
-    owner = jnp.where(chip < len(pieces) // 2, owners[0, 0], owners[1, 0])
-    source = jnp.bitwise_xor(owner // 2, chip)
-    value = pieces[0][...]
-    for number, piece in enumerate(pieces[1:], 1):
-        value = jnp.where(source == number, piece[...], value)
-    out[...] = value
-
-
-def choose_piece(owners, pieces):
-    return pl.pallas_call(
-        own_kernel,
-        out_shape=jax.ShapeDtypeStruct(pieces[0].shape, pieces[0].dtype),
-        in_specs=[VMEM] * (1 + len(pieces)),
-        out_specs=VMEM,
-        compiler_params=params(),
-        cost_estimate=cost(0.3),
-        name="choose_piece",
-    )(owners, *pieces)
 
 
 def waves_kernel(channels, tlen, unroll, swapped, pair, beside, *rest):
@@ -563,15 +591,18 @@
         route = [(2 * z + c, 2 * (z ^ steps[c]) + c) for z in range(chips) for c in range(2)]
         far.append(lax.ppermute(pair, "tm", route))
     beside = across(waveforms, 1)
-    merged = list(merge(owners, mine, other))
-    pieces = [across(merged[step], step) for step in reversed(range(1, chips))]
-    pieces = [merged[0]] + pieces[::-1]
+    kept_0, sent_0, kept_1, sent_1 = merge(owners, mine, other)
+    parts = [(kept_0, sent_0), (kept_1, sent_1)]
+    bit = 1
+    while 2 * bit < chips:
+        parts = [halve(bit, chips, owners, kept, across(sent, bit)) for kept, sent in parts]
+        bit *= 2
+    pieces = [piece for kept, sent in parts for piece in (kept, across(sent, bit))]
     swapped = swap(choose_waves(pair, beside, far))
     left_a, left_r = prepare_waves(tlen, swapped, pair, beside, far)
 
-    left_a, left_r, *pieces = lax.optimization_barrier((left_a, left_r, *pieces[::-1]))
-    pieces = pieces[::-1]
-    first = choose_piece(owners, pieces)
+    left_a, left_r, *pieces = lax.optimization_barrier((left_a, left_r, *pieces))
+    first = choose_piece(chips, owners, pieces)
     second = swap(first)
     total = correlate(0, tlen, group, near, first, left_a, left_r)
     parts = correlate(1, tlen, group, near, second, left_a, left_r, *total)

time: 36.8 us -> 40 us (1.087)
  waiting for transfers between devices: 9.19 us -> 11.7 us
  starting transfers between devices: 15.7 us -> 16.5 us
    ppermute x4 -> x5, waiting for transfers between devices: 1.74 us -> 5.3 us  [across(): lax.ppermute(array, 'tm', [(i, i ^ 2 * step) for i in range(count_tm)])]
    ppermute x5, waiting for transfers between devices: 1.97 us -> 0.91 us  [swap(): return lax.ppermute(array, 'tm', [(i, i ^ 1) for i in range(count_tm)])]
    ppermute x2, starting transfers between devices: 4.15 us -> 5.03 us  [shards(): gathered.append(lax.ppermute(parts[step], ('tm', 'sta'), route))]
    ppermute x5, starting transfers between devices: 4.25 us -> 3.78 us  [swap(): return lax.ppermute(array, 'tm', [(i, i ^ 1) for i in range(count_tm)])]
    ppermute x4 -> x5, starting transfers between devices: 4.91 us -> 5.32 us  [across(): lax.ppermute(array, 'tm', [(i, i ^ 2 * step) for i in range(count_tm)])]
  transfers between devices with their start and end apart: 12 -> 13, of which waited for: 5 -> 5; matrix products, arithmetic and copies ran while one was open for 0% -> 0% of each run, Pallas kernels for 22% -> 20%
where the time goes in v13:
time: 40 us; the launch traced here: 39.9 us
  starting transfers between devices  16.5 us (41%)
  waiting for transfers between devices  11.7 us (29%)
  Pallas kernels  11.5 us (29%)
    ppermute x2, waiting for transfers between devices, shards(): gathered.append(lax.ppermute(parts[step], ('tm', 'sta'), route))  5.47 us
    ppermute x5, starting transfers between devices, across(): lax.ppermute(array, 'tm', [(i, i ^ 2 * step) for i in range(count_tm)])  5.32 us
    ppermute x5, waiting for transfers between devices, across(): lax.ppermute(array, 'tm', [(i, i ^ 2 * step) for i in range(count_tm)])  5.3 us
    pallas_call x2, Pallas kernels, correlate(): pl.pallas_call(functools.partial(main_kernel, side, tlen, group), out_sha...  5.09 us
    ppermute x2, starting transfers between devices, shards(): gathered.append(lax.ppermute(parts[step], ('tm', 'sta'), route))  5.03 us
    ppermute x5, starting transfers between devices, swap(): return lax.ppermute(array, 'tm', [(i, i ^ 1) for i in range(count_tm)])  3.78 us
    pallas_call x1, Pallas kernels, prepare_waves(): pl.pallas_call(functools.partial(waves_kernel, channels, tlen, unroll), o...  2.86 us
    ppermute x1, starting transfers between devices, shards(): far.append(lax.ppermute(pair, 'tm', route))  2.37 us
  transfers between devices with their start and end apart: 13, of which 5 were waited for; matrix products, arithmetic and copies ran while one was open for 0% of the time, Pallas kernels for 20%

profile of v13, /device:TPU:7, one launch (start us, length us, event | category | flops | bytes accessed | tf_op | source)
XLA Modules:
  0.0 39.9 jit_solution(7637762501308974401)
XLA Ops:
  0.0 0.0 copy-start
  0.0 0.7 %collective-permute-start = (bf16[30,512]{1,0:T(8,128)(2,1)}, bf16[30,512]{1,0:T(8,128)(2,1)S(1)}, u32[]{:S(2)}, u32[]{:S(2)}) collective-permute-start(bf16[30,512]{1,0:T(8,128)(2,1)} %own.1), channel_id=1, source_target_pairs={{0,4},{4,0},{8,12},{12,8},{16,20},{20,16},{24,28},{28,24},{1,5},{5... | collective-permute-start | bytes 92168 | tf_op jit(solution)/shard_map/ppermute | solution.py:571
  0.7 2.2 %pack.1 = (bf16[4,12,32,128]{3,2,1,0:T(8,128)(2,1)S(1)}, bf16[4,12,32,128]{3,2,1,0:T(8,128)(2,1)S(1)}, s32[8,128]{1,0:T(8,128)S(1)}) custom-call(s32[2]{0:T(128)} %bank_blocks.1, bf16[2,30,64,100]{3,2,1,0:T(8,128)(2,1)} %bitcast.3, s32[30,2,64]{2,1,0:T(2,128)} %bitcast.4, s32[30,2,64]{2,1,0:T(2,128)} %bitcast.5), custom_call_target="tpu_custom_call" | custom-call | flops 2000000000 | bytes 2000000 | tf_op jit(solution)/shard_map/pack/pallas_call | solution.py:91
  2.9 0.0 collective-permute-done.partner
  2.9 0.1 collective-permute-start.4
  3.0 0.0 copy-done
  3.0 2.4 %collective-permute-start.2 = (bf16[2,30,512]{2,1,0:T(8,128)(2,1)S(1)}, bf16[2,30,512]{2,1,0:T(8,128)(2,1)S(1)}, u32[]{:S(2)}, u32[]{:S(2)}) collective-permute-start(bf16[2,30,512]{2,1,0:T(8,128)(2,1)S(1)} %pair_waves.1.pair), channel_id=1, source_target_pairs={{0,24},{4,20},{8,16},{12,28},{16,8},{20,4},{24,0},{28,12},{1,25},{... | collective-permute-start | bytes 184328 | tf_op jit(solution)/shard_map/ppermute | solution.py:592
  5.4 0.0 collective-permute-done.4.other
  5.4 0.2 merge.1
  5.6 1.4 %collective-permute-start.5 = (bf16[2,6,32,128]{3,2,1,0:T(8,128)(2,1)S(1)}, bf16[2,6,32,128]{3,2,1,0:T(8,128)(2,1)S(1)}, u32[]{:S(2)}, u32[]{:S(2)}) collective-permute-start(bf16[2,6,32,128]{3,2,1,0:T(8,128)(2,1)S(1)} %get-tuple-element.38), channel_id=1, source_target_pairs={{0,8},{4,12},{8,0},{12,4},{16,24},{20,28},{24,16},{28,20},{1,9},{5... | collective-permute-start | bytes 294920 | tf_op jit(solution)/shard_map/ppermute | solution.py:574
  7.0 0.2 collective-permute-start.7
  7.2 1.3 %collective-permute-start.1 = (bf16[30,512]{1,0:T(8,128)(2,1)S(1)}, bf16[30,512]{1,0:T(8,128)(2,1)S(1)}, u32[]{:S(2)}, u32[]{:S(2)}) collective-permute-start(bf16[30,512]{1,0:T(8,128)(2,1)S(1)} %copy-done), channel_id=1, source_target_pairs={{0,8},{4,12},{8,0},{12,4},{16,24},{20,28},{24,16},{28,20},{1,9},{5... | collective-permute-start | bytes 92168 | tf_op jit(solution)/shard_map/ppermute | solution.py:574
  8.5 4.0 %collective-permute-done.1.beside = bf16[30,512]{1,0:T(8,128)(2,1)S(1)} collective-permute-done((bf16[30,512]{1,0:T(8,128)(2,1)S(1)}, bf16[30,512]{1,0:T(8,128)(2,1)S(1)}, u32[]{:S(2)}, u32[]{:S(2)}) %collective-permute-start.1) | collective-permute-done | bytes 30752 | tf_op jit(solution)/shard_map/ppermute | solution.py:574
  12.4 0.0 collective-permute-done.2.rest_0_
  12.5 2.1 %collective-permute-start.3 = (bf16[3,30,512]{2,1,0:T(8,128)(2,1)S(1)}, bf16[3,30,512]{2,1,0:T(8,128)(2,1)S(1)}, u32[]{:S(2)}, u32[]{:S(2)}) collective-permute-start(bf16[3,30,512]{2,1,0:T(8,128)(2,1)S(1)} %choose_waves.1), channel_id=1, source_target_pairs={{0,4},{4,0},{8,12},{12,8},{16,20},{20,16},{24,28},{28,24},{1,5},{5... | collective-permute-start | bytes 276488 | tf_op jit(solution)/shard_map/ppermute | solution.py:571
  14.5 0.0 collective-permute-done.5.received
  14.5 0.1 halve.2
  14.6 1.3 %collective-permute-start.6 = (bf16[1,6,32,128]{3,2,1,0:T(8,128)(2,1)S(1)}, bf16[1,6,32,128]{3,2,1,0:T(8,128)(2,1)S(1)}, u32[]{:S(2)}, u32[]{:S(2)}) collective-permute-start(bf16[1,6,32,128]{3,2,1,0:T(8,128)(2,1)S(1)} %get-tuple-element.40), channel_id=1, source_target_pairs={{0,16},{4,20},{8,24},{12,28},{16,0},{20,4},{24,8},{28,12},{1,17},{... | collective-permute-start | bytes 147464 | tf_op jit(solution)/shard_map/ppermute | solution.py:574
  15.9 0.0 collective-permute-done.7.received
  15.9 0.1 halve.3
  15.9 1.2 %collective-permute-start.8 = (bf16[1,6,32,128]{3,2,1,0:T(8,128)(2,1)S(1)}, bf16[1,6,32,128]{3,2,1,0:T(8,128)(2,1)S(1)}, u32[]{:S(2)}, u32[]{:S(2)}) collective-permute-start(bf16[1,6,32,128]{3,2,1,0:T(8,128)(2,1)S(1)} %get-tuple-element.44), channel_id=1, source_target_pairs={{0,16},{4,20},{8,24},{12,28},{16,0},{20,4},{24,8},{28,12},{1,17},{... | collective-permute-start | bytes 147464 | tf_op jit(solution)/shard_map/ppermute | solution.py:574
  17.2 0.0 collective-permute-done.3.swapped
  17.2 2.9 %prepare_waves.1 = (bf16[30,272,128]{2,1,0:T(8,128)(2,1)S(1)}, bf16[30,256,256]{2,1,0:T(8,128)(2,1)S(1)}) custom-call(bf16[3,30,512]{2,1,0:T(8,128)(2,1)S(1)} %collective-permute-done.3.swapped, bf16[2,30,512]{2,1,0:T(8,128)(2,1)S(1)} %pair_waves.1.pair, bf16[30,512]{1,0:T(8,128)(2,1)S(1)} %collective-permute-done.1.beside, ...), custom_call_target="tpu_custom_call" | custom-call | flops 50000000 | bytes 50000 | tf_op jit(solution)/shard_map/prepare_waves/pallas_call | solution.py:318
  20.0 0.0 collective-permute-done.6.refs_1_
  20.1 1.3 %collective-permute-done.8.refs_3_ = bf16[1,6,32,128]{3,2,1,0:T(8,128)(2,1)S(1)} collective-permute-done((bf16[1,6,32,128]{3,2,1,0:T(8,128)(2,1)S(1)}, bf16[1,6,32,128]{3,2,1,0:T(8,128)(2,1)S(1)}, u32[]{:S(2)}, u32[]{:S(2)}) %collective-permute-start.8) | collective-permute-done | bytes 49184 | tf_op jit(solution)/shard_map/ppermute | solution.py:574
  21.4 0.1 choose_piece.1.piece
  21.4 0.5 %collective-permute-start.9 = (bf16[12,32,128]{2,1,0:T(8,128)(2,1)S(1)}, bf16[12,32,128]{2,1,0:T(8,128)(2,1)S(1)}, u32[]{:S(2)}, u32[]{:S(2)}) collective-permute-start(bf16[12,32,128]{2,1,0:T(8,128)(2,1)S(1)} %choose_piece.1.piece), channel_id=1, source_target_pairs={{0,4},{4,0},{8,12},{12,8},{16,20},{20,16},{24,28},{28,24},{1,5},{5... | collective-permute-start | bytes 294920 | tf_op jit(solution)/shard_map/ppermute | solution.py:571
  22.0 2.5 %correlate_first.1.rest_0_ = f32[256,256]{1,0:T(8,128)S(1)} custom-call(bf16[12,32,128]{2,1,0:T(8,128)(2,1)S(1)} %choose_piece.1.piece, bf16[30,272,128]{2,1,0:T(8,128)(2,1)S(1)} %get-tuple-element.49.left_a, bf16[30,256,256]{2,1,0:T(8,128)(2,1)S(1)} %get-tuple-element.50.left_r), custom_call_target="tpu_custom_call" | custom-call | flops 3000000000 | bytes 3000000 | tf_op jit(solution)/shard_map/correlate_first/pallas_call | solution.py:487
  24.5 0.0 collective-permute-done.9.piece
  24.5 2.6 %correlate_second.1 = (bf16[128,256]{1,0:T(8,128)(2,1)S(1)}, bf16[128,256]{1,0:T(8,128)(2,1)S(1)}) custom-call(bf16[12,32,128]{2,1,0:T(8,128)(2,1)S(1)} %collective-permute-done.9.piece, bf16[30,272,128]{2,1,0:T(8,128)(2,1)S(1)} %get-tuple-element.49.left_a, bf16[30,256,256]{2,1,0:T(8,128)(2,1)S(1)} %get-tuple-element.50.left_r, ...), custom_call_target="tpu_custom_call" | custom-call | flops 3000000000 | bytes 3000000 | tf_op jit(solution)/shard_map/correlate_second/pallas_call | solution.py:487
  27.1 5.0 %collective-permute-start.10 = (bf16[128,256]{1,0:T(8,128)(2,1)S(1)}, bf16[128,256]{1,0:T(8,128)(2,1)S(1)}, u32[]{:S(2)}, u32[]{:S(2)}) collective-permute-start(bf16[128,256]{1,0:T(8,128)(2,1)S(1)} %get-tuple-element.51), channel_id=1, source_target_pairs={{0,0},{1,8},{2,4},{3,12},{4,16},{5,24},{6,20},{7,28},{8,1},{9,9},{... | collective-permute-start | bytes 196616 | tf_op jit(solution)/shard_map/ppermute | solution.py:616
  32.0 0.1 collective-permute-start.11
  32.1 3.2 %collective-permute-done.10.refs_0_ = bf16[128,256]{1,0:T(8,128)(2,1)S(1)} collective-permute-done((bf16[128,256]{1,0:T(8,128)(2,1)S(1)}, bf16[128,256]{1,0:T(8,128)(2,1)S(1)}, u32[]{:S(2)}, u32[]{:S(2)}) %collective-permute-start.10) | collective-permute-done | bytes 65568 | tf_op jit(solution)/shard_map/ppermute | solution.py:616
  35.4 2.2 %collective-permute-done.11.refs_1_ = bf16[128,256]{1,0:T(8,128)(2,1)S(1)} collective-permute-done((bf16[128,256]{1,0:T(8,128)(2,1)S(1)}, bf16[128,256]{1,0:T(8,128)(2,1)S(1)}, u32[]{:S(2)}, u32[]{:S(2)}) %collective-permute-start.11) | collective-permute-done | bytes 65568 | tf_op jit(solution)/shard_map/ppermute | solution.py:616
  37.6 0.5 %collective-permute-start.12 = (f32[64,256]{1,0:T(8,128)S(1)}, f32[64,256]{1,0:T(8,128)S(1)}, u32[]{:S(2)}, u32[]{:S(2)}) collective-permute-start(f32[64,256]{1,0:T(8,128)S(1)} %get-tuple-element.54), channel_id=1, source_target_pairs={{0,4},{4,0},{8,12},{12,8},{16,20},{20,16},{24,28},{28,24},{1,5},{5... | collective-permute-start | bytes 196616 | tf_op jit(solution)/shard_map/ppermute | solution.py:571
  38.1 0.9 %collective-permute-done.12.received = f32[64,256]{1,0:T(8,128)S(1)} collective-permute-done((f32[64,256]{1,0:T(8,128)S(1)}, f32[64,256]{1,0:T(8,128)S(1)}, u32[]{:S(2)}, u32[]{:S(2)}) %collective-permute-start.12) | collective-permute-done | bytes 65568 | tf_op jit(solution)/shard_map/ppermute | solution.py:571
  39.0 0.9 %finish.1 = f32[32,512]{1,0:T(8,128)} custom-call(f32[64,256]{1,0:T(8,128)S(1)} %get-tuple-element.53.ours, f32[64,256]{1,0:T(8,128)S(1)} %collective-permute-done.12.received), custom_call_target="tpu_custom_call" | custom-call | flops 1000000000 | bytes 1000000 | tf_op jit(solution)/shard_map/finish/pallas_call | solution.py:550
  (3 shorter events, 0.1 us)
Async XLA Ops:
  0.0 3.0 %copy-start = (bf16[30,512]{1,0:T(8,128)(2,1)S(1)}, bf16[30,512]{1,0:T(8,128)(2,1)}, u32[]{:S(2)}) copy-start(bf16[30,512]{1,0:T(8,128)(2,1)} %own.1) | copy-start | bytes 92164
  0.0 2.9 %collective-permute-start = (bf16[30,512]{1,0:T(8,128)(2,1)}, bf16[30,512]{1,0:T(8,128)(2,1)S(1)}, u32[]{:S(2)}, u32[]{:S(2)}) collective-permute-start(bf16[30,512]{1,0:T(8,128)(2,1)} %own.1), channel_id=1, source_target_pairs={{0,4},{4,0},{8,12},{12,8},{16,20},{20,16},{24,28},{28,24},{1,5},{5... | collective-permute-start | bytes 92168 | tf_op jit(solution)/shard_map/ppermute | solution.py:571
  2.9 2.5 %collective-permute-start.4 = (bf16[4,12,32,128]{3,2,1,0:T(8,128)(2,1)S(1)}, bf16[4,12,32,128]{3,2,1,0:T(8,128)(2,1)S(1)}, u32[]{:S(2)}, u32[]{:S(2)}) collective-permute-start(bf16[4,12,32,128]{3,2,1,0:T(8,128)(2,1)S(1)} %get-tuple-element.36), channel_id=1, source_target_pairs={{0,4},{4,0},{8,12},{12,8},{16,20},{20,16},{24,28},{28,24},{1,5},{5... | collective-permute-start | bytes 1179656 | tf_op jit(solution)/shard_map/ppermute | solution.py:571
  3.0 9.4 %collective-permute-start.2 = (bf16[2,30,512]{2,1,0:T(8,128)(2,1)S(1)}, bf16[2,30,512]{2,1,0:T(8,128)(2,1)S(1)}, u32[]{:S(2)}, u32[]{:S(2)}) collective-permute-start(bf16[2,30,512]{2,1,0:T(8,128)(2,1)S(1)} %pair_waves.1.pair), channel_id=1, source_target_pairs={{0,24},{4,20},{8,16},{12,28},{16,8},{20,4},{24,0},{28,12},{1,25},{... | collective-permute-start | bytes 184328 | tf_op jit(solution)/shard_map/ppermute | solution.py:592
  5.6 8.9 %collective-permute-start.5 = (bf16[2,6,32,128]{3,2,1,0:T(8,128)(2,1)S(1)}, bf16[2,6,32,128]{3,2,1,0:T(8,128)(2,1)S(1)}, u32[]{:S(2)}, u32[]{:S(2)}) collective-permute-start(bf16[2,6,32,128]{3,2,1,0:T(8,128)(2,1)S(1)} %get-tuple-element.38), channel_id=1, source_target_pairs={{0,8},{4,12},{8,0},{12,4},{16,24},{20,28},{24,16},{28,20},{1,9},{5... | collective-permute-start | bytes 294920 | tf_op jit(solution)/shard_map/ppermute | solution.py:574
  7.0 8.9 %collective-permute-start.7 = (bf16[2,6,32,128]{3,2,1,0:T(8,128)(2,1)S(1)}, bf16[2,6,32,128]{3,2,1,0:T(8,128)(2,1)S(1)}, u32[]{:S(2)}, u32[]{:S(2)}) collective-permute-start(bf16[2,6,32,128]{3,2,1,0:T(8,128)(2,1)S(1)} %get-tuple-element.42), channel_id=1, source_target_pairs={{0,8},{4,12},{8,0},{12,4},{16,24},{20,28},{24,16},{28,20},{1,9},{5... | collective-permute-start | bytes 294920 | tf_op jit(solution)/shard_map/ppermute | solution.py:574
  7.2 5.3 %collective-permute-start.1 = (bf16[30,512]{1,0:T(8,128)(2,1)S(1)}, bf16[30,512]{1,0:T(8,128)(2,1)S(1)}, u32[]{:S(2)}, u32[]{:S(2)}) collective-permute-start(bf16[30,512]{1,0:T(8,128)(2,1)S(1)} %copy-done), channel_id=1, source_target_pairs={{0,8},{4,12},{8,0},{12,4},{16,24},{20,28},{24,16},{28,20},{1,9},{5... | collective-permute-start | bytes 92168 | tf_op jit(solution)/shard_map/ppermute | solution.py:574
  12.5 4.7 %collective-permute-start.3 = (bf16[3,30,512]{2,1,0:T(8,128)(2,1)S(1)}, bf16[3,30,512]{2,1,0:T(8,128)(2,1)S(1)}, u32[]{:S(2)}, u32[]{:S(2)}) collective-permute-start(bf16[3,30,512]{2,1,0:T(8,128)(2,1)S(1)} %choose_waves.1), channel_id=1, source_target_pairs={{0,4},{4,0},{8,12},{12,8},{16,20},{20,16},{24,28},{28,24},{1,5},{5... | collective-permute-start | bytes 276488 | tf_op jit(solution)/shard_map/ppermute | solution.py:571
  14.6 5.4 %collective-permute-start.6 = (bf16[1,6,32,128]{3,2,1,0:T(8,128)(2,1)S(1)}, bf16[1,6,32,128]{3,2,1,0:T(8,128)(2,1)S(1)}, u32[]{:S(2)}, u32[]{:S(2)}) collective-permute-start(bf16[1,6,32,128]{3,2,1,0:T(8,128)(2,1)S(1)} %get-tuple-element.40), channel_id=1, source_target_pairs={{0,16},{4,20},{8,24},{12,28},{16,0},{20,4},{24,8},{28,12},{1,17},{... | collective-permute-start | bytes 147464 | tf_op jit(solution)/shard_map/ppermute | solution.py:574
  15.9 5.4 %collective-permute-start.8 = (bf16[1,6,32,128]{3,2,1,0:T(8,128)(2,1)S(1)}, bf16[1,6,32,128]{3,2,1,0:T(8,128)(2,1)S(1)}, u32[]{:S(2)}, u32[]{:S(2)}) collective-permute-start(bf16[1,6,32,128]{3,2,1,0:T(8,128)(2,1)S(1)} %get-tuple-element.44), channel_id=1, source_target_pairs={{0,16},{4,20},{8,24},{12,28},{16,0},{20,4},{24,8},{28,12},{1,17},{... | collective-permute-start | bytes 147464 | tf_op jit(solution)/shard_map/ppermute | solution.py:574
  21.4 3.0 %collective-permute-start.9 = (bf16[12,32,128]{2,1,0:T(8,128)(2,1)S(1)}, bf16[12,32,128]{2,1,0:T(8,128)(2,1)S(1)}, u32[]{:S(2)}, u32[]{:S(2)}) collective-permute-start(bf16[12,32,128]{2,1,0:T(8,128)(2,1)S(1)} %choose_piece.1.piece), channel_id=1, source_target_pairs={{0,4},{4,0},{8,12},{12,8},{16,20},{20,16},{24,28},{28,24},{1,5},{5... | collective-permute-start | bytes 294920 | tf_op jit(solution)/shard_map/ppermute | solution.py:571
  27.1 8.3 %collective-permute-start.10 = (bf16[128,256]{1,0:T(8,128)(2,1)S(1)}, bf16[128,256]{1,0:T(8,128)(2,1)S(1)}, u32[]{:S(2)}, u32[]{:S(2)}) collective-permute-start(bf16[128,256]{1,0:T(8,128)(2,1)S(1)} %get-tuple-element.51), channel_id=1, source_target_pairs={{0,0},{1,8},{2,4},{3,12},{4,16},{5,24},{6,20},{7,28},{8,1},{9,9},{... | collective-permute-start | bytes 196616 | tf_op jit(solution)/shard_map/ppermute | solution.py:616
  32.0 5.5 %collective-permute-start.11 = (bf16[128,256]{1,0:T(8,128)(2,1)S(1)}, bf16[128,256]{1,0:T(8,128)(2,1)S(1)}, u32[]{:S(2)}, u32[]{:S(2)}) collective-permute-start(bf16[128,256]{1,0:T(8,128)(2,1)S(1)} %get-tuple-element.52), channel_id=1, source_target_pairs={{0,8},{1,0},{2,12},{3,4},{4,24},{5,16},{6,28},{7,20},{8,9},{9,1},{... | collective-permute-start | bytes 196616 | tf_op jit(solution)/shard_map/ppermute | solution.py:616
  37.6 1.4 %collective-permute-start.12 = (f32[64,256]{1,0:T(8,128)S(1)}, f32[64,256]{1,0:T(8,128)S(1)}, u32[]{:S(2)}, u32[]{:S(2)}) collective-permute-start(f32[64,256]{1,0:T(8,128)S(1)} %get-tuple-element.54), channel_id=1, source_target_pairs={{0,4},{4,0},{8,12},{12,8},{16,20},{20,16},{24,28},{28,24},{1,5},{5... | collective-permute-start | bytes 196616 | tf_op jit(solution)/shard_map/ppermute | solution.py:571

commit v14 on v11

--- a/solution.py
+++ b/solution.py
@@ -442,7 +442,7 @@
     rows_out = outs[0].shape[0]
     station = lax.axis_index("sta") % len(outs)
     for step, out in enumerate(outs):
-        part = jnp.bitwise_xor(station, step)
+        part = jnp.bitwise_xor(station, len(outs) - 1 - step)
         out[...] = total[pl.ds(pl.multiple_of(part * rows_out, rows_out), rows_out), :].astype(
             jnp.bfloat16
         )
@@ -500,22 +500,31 @@
     )(*parts)
 
 
-def finish_kernel(group, ours, received, out):
+def finish_kernel(group, ours, received, out, result, sems):
     samples = out.shape[1]
     rows = ours.shape[0]
     value = ours[...] + received[...]
     high = value.astype(jnp.bfloat16).astype(jnp.float32)
     both = jnp.concatenate([high, value - high], axis=0).T.astype(jnp.bfloat16)
-    row = lax.broadcasted_iota(jnp.int32, (2 * rows, samples), 0) % rows
-    lane = lax.broadcasted_iota(jnp.int32, (2 * rows, samples), 1)
-    place = jnp.logical_and(lane // STRIDE == row // 8, lane % 8 == 7 - row % 8)
-    place = jnp.where(place, 1.0, 0.0).astype(jnp.bfloat16)
-    wide = jnp.dot(both, place, preferred_element_type=jnp.float32)
-    lane = lax.broadcasted_iota(jnp.int32, (group, samples), 1) // 8 % OFFSETS
-    result = jnp.zeros((group, samples), jnp.float32)
-    for offset in range(OFFSETS):
-        result = jnp.where(lane == offset, wide[offset * group : (offset + 1) * group], result)
-    out[...] = result
+    half = samples // 2
+    copies = []
+    for number in range(2):
+        row = lax.broadcasted_iota(jnp.int32, (2 * rows, half), 0) % rows
+        lane = lax.broadcasted_iota(jnp.int32, (2 * rows, half), 1) + half * number
+        place = jnp.logical_and(lane // STRIDE == row // 8, lane % 8 == 7 - row % 8)
+        place = jnp.where(place, 1.0, 0.0).astype(jnp.bfloat16)
+        wide = jnp.dot(both, place, preferred_element_type=jnp.float32)
+        lane = lax.broadcasted_iota(jnp.int32, (group, half), 1) // 8 % OFFSETS
+        piece = jnp.zeros((group, half), jnp.float32)
+        for offset in range(OFFSETS):
+            piece = jnp.where(lane == offset, wide[offset * group : (offset + 1) * group], piece)
+        lanes = pl.ds(half * number, half)
+        result[:, lanes] = piece
+        copy = pltpu.make_async_copy(result.at[:, lanes], out.at[:, lanes], sems.at[number])
+        copy.start()
+        copies.append(copy)
+    for copy in copies:
+        copy.wait()
 
 
 def finish(group, samples, ours, received):
@@ -523,7 +532,11 @@
         functools.partial(finish_kernel, group),
         out_shape=jax.ShapeDtypeStruct((group, samples), jnp.float32),
         in_specs=[VMEM, VMEM],
-        out_specs=VMEM,
+        out_specs=ANY,
+        scratch_shapes=[
+            pltpu.VMEM((group, samples), jnp.float32),
+            pltpu.SemaphoreType.DMA((2,)),
+        ],
         compiler_params=params(),
         cost_estimate=cost(1),
         name="finish",
@@ -580,7 +593,7 @@
         route = []
         for d in range(count_tm):
             for s in range(count_sta):
-                dest = near * (d % 2) + (s % near ^ step)
+                dest = near * (d % 2) + (s % near ^ (near - 1 - step))
                 route.append((d * count_sta + s, (2 * dest + s // near) * count_sta + d // 2))
         gathered.append(lax.ppermute(parts[step], ("tm", "sta"), route))
     ours, send = add(gathered)

time: 36.8 us -> 37.2 us (1.011)
  starting transfers between devices: 15.7 us -> 19.7 us
  waiting for transfers between devices: 9.19 us -> 5.72 us
    ppermute x2, waiting for transfers between devices: 5.47 us -> 2.12 us  [shards(): gathered.append(lax.ppermute(parts[step], ('tm', 'sta'), route))]
    ppermute x2, starting transfers between devices: 4.15 us -> 6.24 us  [shards(): gathered.append(lax.ppermute(parts[step], ('tm', 'sta'), route))]
    ppermute x5, starting transfers between devices: 4.25 us -> 6.21 us  [swap(): return lax.ppermute(array, 'tm', [(i, i ^ 1) for i in range(count_tm)])]
  transfers between devices with their start and end apart: 12 -> 12, of which waited for: 5 -> 4; matrix products, arithmetic and copies ran while one was open for 0% -> 0% of each run, Pallas kernels for 22% -> 21%
where the time goes in v14:
time: 37.2 us; the launch traced here: 37 us
  starting transfers between devices  19.7 us (53%)
  Pallas kernels  11.4 us (31%)
  waiting for transfers between devices  5.72 us (15%)
    ppermute x2, starting transfers between devices, shards(): gathered.append(lax.ppermute(parts[step], ('tm', 'sta'), route))  6.24 us
    ppermute x5, starting transfers between devices, swap(): return lax.ppermute(array, 'tm', [(i, i ^ 1) for i in range(count_tm)])  6.21 us
    pallas_call x2, Pallas kernels, correlate(): pl.pallas_call(functools.partial(main_kernel, side, tlen, group), out_sha...  5.09 us
    ppermute x4, starting transfers between devices, across(): lax.ppermute(array, 'tm', [(i, i ^ 2 * step) for i in range(count_tm)])  4.91 us
    pallas_call x1, Pallas kernels, prepare_waves(): pl.pallas_call(functools.partial(waves_kernel, channels, tlen, unroll), o...  2.85 us
    ppermute x1, starting transfers between devices, shards(): far.append(lax.ppermute(pair, 'tm', route))  2.37 us
    pallas_call x1, Pallas kernels, pack(): pl.pallas_call(pack_kernel, out_shape=[jax.ShapeDtypeStruct(shape, jnp.bf...  2.22 us
    ppermute x2, waiting for transfers between devices, shards(): gathered.append(lax.ppermute(parts[step], ('tm', 'sta'), route))  2.12 us
  transfers between devices with their start and end apart: 12, of which 4 were waited for; matrix products, arithmetic and copies ran while one was open for 0% of the time, Pallas kernels for 21%

profile of v14, /device:TPU:7, one launch (start us, length us, event | category | flops | bytes accessed | tf_op | source)
XLA Modules:
  0.0 37.0 jit_solution(10717903476122843176)
XLA Ops:
  0.0 0.0 copy-start
  0.0 0.7 %collective-permute-start = (bf16[30,512]{1,0:T(8,128)(2,1)}, bf16[30,512]{1,0:T(8,128)(2,1)S(1)}, u32[]{:S(2)}, u32[]{:S(2)}) collective-permute-start(bf16[30,512]{1,0:T(8,128)(2,1)} %own.1), channel_id=1, source_target_pairs={{0,4},{4,0},{8,12},{12,8},{16,20},{20,16},{24,28},{28,24},{1,5},{5... | collective-permute-start | bytes 92168 | tf_op jit(solution)/shard_map/ppermute | solution.py:556
  0.7 2.2 %pack.1 = (bf16[4,12,32,128]{3,2,1,0:T(8,128)(2,1)S(1)}, bf16[4,12,32,128]{3,2,1,0:T(8,128)(2,1)S(1)}, s32[8,128]{1,0:T(8,128)S(1)}) custom-call(s32[2]{0:T(128)} %bank_blocks.1, bf16[2,30,64,100]{3,2,1,0:T(8,128)(2,1)} %bitcast.3, s32[30,2,64]{2,1,0:T(2,128)} %bitcast.4, s32[30,2,64]{2,1,0:T(2,128)} %bitcast.5), custom_call_target="tpu_custom_call" | custom-call | flops 2000000000 | bytes 2000000 | tf_op jit(solution)/shard_map/pack/pallas_call | solution.py:91
  2.9 0.0 collective-permute-done.partner
  2.9 0.1 collective-permute-start.4
  3.0 0.0 copy-done
  3.0 2.4 %collective-permute-start.2 = (bf16[2,30,512]{2,1,0:T(8,128)(2,1)S(1)}, bf16[2,30,512]{2,1,0:T(8,128)(2,1)S(1)}, u32[]{:S(2)}, u32[]{:S(2)}) collective-permute-start(bf16[2,30,512]{2,1,0:T(8,128)(2,1)S(1)} %pair_waves.1.pair), channel_id=1, source_target_pairs={{0,24},{4,20},{8,16},{12,28},{16,8},{20,4},{24,0},{28,12},{1,25},{... | collective-permute-start | bytes 184328 | tf_op jit(solution)/shard_map/ppermute | solution.py:577
  5.4 1.3 %collective-permute-start.1 = (bf16[30,512]{1,0:T(8,128)(2,1)S(1)}, bf16[30,512]{1,0:T(8,128)(2,1)S(1)}, u32[]{:S(2)}, u32[]{:S(2)}) collective-permute-start(bf16[30,512]{1,0:T(8,128)(2,1)S(1)} %copy-done), channel_id=1, source_target_pairs={{0,8},{4,12},{8,0},{12,4},{16,24},{20,28},{24,16},{28,20},{1,9},{5... | collective-permute-start | bytes 92168 | tf_op jit(solution)/shard_map/ppermute | solution.py:559
  6.7 0.0 collective-permute-done.4.other
  6.7 0.2 merge.1
  6.9 1.4 %collective-permute-start.5 = (bf16[12,32,128]{2,1,0:T(8,128)(2,1)S(1)}, bf16[12,32,128]{2,1,0:T(8,128)(2,1)S(1)}, u32[]{:S(2)}, u32[]{:S(2)}) collective-permute-start(bf16[12,32,128]{2,1,0:T(8,128)(2,1)S(1)} %get-tuple-element.33), channel_id=1, source_target_pairs={{0,24},{4,28},{8,16},{12,20},{16,8},{20,12},{24,0},{28,4},{1,25},{... | collective-permute-start | bytes 294920 | tf_op jit(solution)/shard_map/ppermute | solution.py:559
  8.3 0.0 collective-permute-start.6
  8.4 2.2 %collective-permute-start.7 = (bf16[12,32,128]{2,1,0:T(8,128)(2,1)S(1)}, bf16[12,32,128]{2,1,0:T(8,128)(2,1)S(1)}, u32[]{:S(2)}, u32[]{:S(2)}) collective-permute-start(bf16[12,32,128]{2,1,0:T(8,128)(2,1)S(1)} %get-tuple-element.35), channel_id=1, source_target_pairs={{0,8},{4,12},{8,0},{12,4},{16,24},{20,28},{24,16},{28,20},{1,9},{5... | collective-permute-start | bytes 294920 | tf_op jit(solution)/shard_map/ppermute | solution.py:559
  10.5 0.0 collective-permute-done.1.beside
  10.6 0.0 collective-permute-done.2.rest_0_
  10.6 1.4 %collective-permute-start.3 = (bf16[3,30,512]{2,1,0:T(8,128)(2,1)S(1)}, bf16[3,30,512]{2,1,0:T(8,128)(2,1)S(1)}, u32[]{:S(2)}, u32[]{:S(2)}) collective-permute-start(bf16[3,30,512]{2,1,0:T(8,128)(2,1)S(1)} %choose_waves.1), channel_id=1, source_target_pairs={{0,4},{4,0},{8,12},{12,8},{16,20},{20,16},{24,28},{28,24},{1,5},{5... | collective-permute-start | bytes 276488 | tf_op jit(solution)/shard_map/ppermute | solution.py:556
  12.0 0.9 %collective-permute-done.3.swapped = bf16[3,30,512]{2,1,0:T(8,128)(2,1)S(1)} collective-permute-done((bf16[3,30,512]{2,1,0:T(8,128)(2,1)S(1)}, bf16[3,30,512]{2,1,0:T(8,128)(2,1)S(1)}, u32[]{:S(2)}, u32[]{:S(2)}) %collective-permute-start.3) | collective-permute-done | bytes 92192 | tf_op jit(solution)/shard_map/ppermute | solution.py:556
  12.9 2.9 %prepare_waves.1 = (bf16[30,272,128]{2,1,0:T(8,128)(2,1)S(1)}, bf16[30,256,256]{2,1,0:T(8,128)(2,1)S(1)}) custom-call(bf16[3,30,512]{2,1,0:T(8,128)(2,1)S(1)} %collective-permute-done.3.swapped, bf16[2,30,512]{2,1,0:T(8,128)(2,1)S(1)} %pair_waves.1.pair, bf16[30,512]{1,0:T(8,128)(2,1)S(1)} %collective-permute-done.1.beside, ...), custom_call_target="tpu_custom_call" | custom-call | flops 50000000 | bytes 50000 | tf_op jit(solution)/shard_map/prepare_waves/pallas_call | solution.py:290
  15.8 0.0 collective-permute-done.5.refs_3_
  15.8 1.7 %collective-permute-done.6.refs_2_ = bf16[12,32,128]{2,1,0:T(8,128)(2,1)S(1)} collective-permute-done((bf16[12,32,128]{2,1,0:T(8,128)(2,1)S(1)}, bf16[12,32,128]{2,1,0:T(8,128)(2,1)S(1)}, u32[]{:S(2)}, u32[]{:S(2)}) %collective-permute-start.6) | collective-permute-done | bytes 98336 | tf_op jit(solution)/shard_map/ppermute | solution.py:559
  17.5 0.0 collective-permute-done.7.refs_1_
  17.5 0.1 choose_piece.1.piece
  17.6 1.8 %collective-permute-start.8 = (bf16[12,32,128]{2,1,0:T(8,128)(2,1)S(1)}, bf16[12,32,128]{2,1,0:T(8,128)(2,1)S(1)}, u32[]{:S(2)}, u32[]{:S(2)}) collective-permute-start(bf16[12,32,128]{2,1,0:T(8,128)(2,1)S(1)} %choose_piece.1.piece), channel_id=1, source_target_pairs={{0,4},{4,0},{8,12},{12,8},{16,20},{20,16},{24,28},{28,24},{1,5},{5... | collective-permute-start | bytes 294920 | tf_op jit(solution)/shard_map/ppermute | solution.py:556
  19.4 2.5 %correlate_first.1.rest_0_ = f32[256,256]{1,0:T(8,128)S(1)} custom-call(bf16[12,32,128]{2,1,0:T(8,128)(2,1)S(1)} %choose_piece.1.piece, bf16[30,272,128]{2,1,0:T(8,128)(2,1)S(1)} %get-tuple-element.41.left_a, bf16[30,256,256]{2,1,0:T(8,128)(2,1)S(1)} %get-tuple-element.42.left_r), custom_call_target="tpu_custom_call" | custom-call | flops 3000000000 | bytes 3000000 | tf_op jit(solution)/shard_map/correlate_first/pallas_call | solution.py:459
  22.0 0.0 collective-permute-done.8.piece
  22.0 2.6 %correlate_second.1 = (bf16[128,256]{1,0:T(8,128)(2,1)S(1)}, bf16[128,256]{1,0:T(8,128)(2,1)S(1)}) custom-call(bf16[12,32,128]{2,1,0:T(8,128)(2,1)S(1)} %collective-permute-done.8.piece, bf16[30,272,128]{2,1,0:T(8,128)(2,1)S(1)} %get-tuple-element.41.left_a, bf16[30,256,256]{2,1,0:T(8,128)(2,1)S(1)} %get-tuple-element.42.left_r, ...), custom_call_target="tpu_custom_call" | custom-call | flops 3000000000 | bytes 3000000 | tf_op jit(solution)/shard_map/correlate_second/pallas_call | solution.py:459
  24.6 0.1 collective-permute-start.9
  24.6 6.2 %collective-permute-start.10 = (bf16[128,256]{1,0:T(8,128)(2,1)S(1)}, bf16[128,256]{1,0:T(8,128)(2,1)S(1)}, u32[]{:S(2)}, u32[]{:S(2)}) collective-permute-start(bf16[128,256]{1,0:T(8,128)(2,1)S(1)} %get-tuple-element.44), channel_id=1, source_target_pairs={{0,0},{1,8},{2,4},{3,12},{4,16},{5,24},{6,20},{7,28},{8,1},{9,9},{... | collective-permute-start | bytes 196616 | tf_op jit(solution)/shard_map/ppermute | solution.py:598
  30.8 0.0 collective-permute-done.9.refs_0_
  30.8 2.1 %collective-permute-done.10.refs_1_ = bf16[128,256]{1,0:T(8,128)(2,1)S(1)} collective-permute-done((bf16[128,256]{1,0:T(8,128)(2,1)S(1)}, bf16[128,256]{1,0:T(8,128)(2,1)S(1)}, u32[]{:S(2)}, u32[]{:S(2)}) %collective-permute-start.10) | collective-permute-done | bytes 65568 | tf_op jit(solution)/shard_map/ppermute | solution.py:598
  33.0 2.3 %collective-permute-start.11 = (f32[64,256]{1,0:T(8,128)S(1)}, f32[64,256]{1,0:T(8,128)S(1)}, u32[]{:S(2)}, u32[]{:S(2)}) collective-permute-start(f32[64,256]{1,0:T(8,128)S(1)} %get-tuple-element.46), channel_id=1, source_target_pairs={{0,4},{4,0},{8,12},{12,8},{16,20},{20,16},{24,28},{28,24},{1,5},{5... | collective-permute-start | bytes 196616 | tf_op jit(solution)/shard_map/ppermute | solution.py:556
  35.2 0.9 %collective-permute-done.11.received = f32[64,256]{1,0:T(8,128)S(1)} collective-permute-done((f32[64,256]{1,0:T(8,128)S(1)}, f32[64,256]{1,0:T(8,128)S(1)}, u32[]{:S(2)}, u32[]{:S(2)}) %collective-permute-start.11) | collective-permute-done | bytes 65568 | tf_op jit(solution)/shard_map/ppermute | solution.py:556
  36.1 0.9 %finish.1 = f32[32,512]{1,0:T(8,128)} custom-call(f32[64,256]{1,0:T(8,128)S(1)} %get-tuple-element.45.ours, f32[64,256]{1,0:T(8,128)S(1)} %collective-permute-done.11.received), custom_call_target="tpu_custom_call" | custom-call | flops 1000000000 | bytes 1000000 | tf_op jit(solution)/shard_map/finish/pallas_call | solution.py:531
  (3 shorter events, 0.1 us)
Async XLA Ops:
  0.0 3.0 %copy-start = (bf16[30,512]{1,0:T(8,128)(2,1)S(1)}, bf16[30,512]{1,0:T(8,128)(2,1)}, u32[]{:S(2)}) copy-start(bf16[30,512]{1,0:T(8,128)(2,1)} %own.1) | copy-start | bytes 92164
  0.0 2.9 %collective-permute-start = (bf16[30,512]{1,0:T(8,128)(2,1)}, bf16[30,512]{1,0:T(8,128)(2,1)S(1)}, u32[]{:S(2)}, u32[]{:S(2)}) collective-permute-start(bf16[30,512]{1,0:T(8,128)(2,1)} %own.1), channel_id=1, source_target_pairs={{0,4},{4,0},{8,12},{12,8},{16,20},{20,16},{24,28},{28,24},{1,5},{5... | collective-permute-start | bytes 92168 | tf_op jit(solution)/shard_map/ppermute | solution.py:556
  2.9 3.8 %collective-permute-start.4 = (bf16[4,12,32,128]{3,2,1,0:T(8,128)(2,1)S(1)}, bf16[4,12,32,128]{3,2,1,0:T(8,128)(2,1)S(1)}, u32[]{:S(2)}, u32[]{:S(2)}) collective-permute-start(bf16[4,12,32,128]{3,2,1,0:T(8,128)(2,1)S(1)} %get-tuple-element.32), channel_id=1, source_target_pairs={{0,4},{4,0},{8,12},{12,8},{16,20},{20,16},{24,28},{28,24},{1,5},{5... | collective-permute-start | bytes 1179656 | tf_op jit(solution)/shard_map/ppermute | solution.py:556
  3.0 7.5 %collective-permute-start.2 = (bf16[2,30,512]{2,1,0:T(8,128)(2,1)S(1)}, bf16[2,30,512]{2,1,0:T(8,128)(2,1)S(1)}, u32[]{:S(2)}, u32[]{:S(2)}) collective-permute-start(bf16[2,30,512]{2,1,0:T(8,128)(2,1)S(1)} %pair_waves.1.pair), channel_id=1, source_target_pairs={{0,24},{4,20},{8,16},{12,28},{16,8},{20,4},{24,0},{28,12},{1,25},{... | collective-permute-start | bytes 184328 | tf_op jit(solution)/shard_map/ppermute | solution.py:577
  5.4 5.1 %collective-permute-start.1 = (bf16[30,512]{1,0:T(8,128)(2,1)S(1)}, bf16[30,512]{1,0:T(8,128)(2,1)S(1)}, u32[]{:S(2)}, u32[]{:S(2)}) collective-permute-start(bf16[30,512]{1,0:T(8,128)(2,1)S(1)} %copy-done), channel_id=1, source_target_pairs={{0,8},{4,12},{8,0},{12,4},{16,24},{20,28},{24,16},{28,20},{1,9},{5... | collective-permute-start | bytes 92168 | tf_op jit(solution)/shard_map/ppermute | solution.py:559
  6.9 8.8 %collective-permute-start.5 = (bf16[12,32,128]{2,1,0:T(8,128)(2,1)S(1)}, bf16[12,32,128]{2,1,0:T(8,128)(2,1)S(1)}, u32[]{:S(2)}, u32[]{:S(2)}) collective-permute-start(bf16[12,32,128]{2,1,0:T(8,128)(2,1)S(1)} %get-tuple-element.33), channel_id=1, source_target_pairs={{0,24},{4,28},{8,16},{12,20},{16,8},{20,12},{24,0},{28,4},{1,25},{... | collective-permute-start | bytes 294920 | tf_op jit(solution)/shard_map/ppermute | solution.py:559
  8.3 9.2 %collective-permute-start.6 = (bf16[12,32,128]{2,1,0:T(8,128)(2,1)S(1)}, bf16[12,32,128]{2,1,0:T(8,128)(2,1)S(1)}, u32[]{:S(2)}, u32[]{:S(2)}) collective-permute-start(bf16[12,32,128]{2,1,0:T(8,128)(2,1)S(1)} %get-tuple-element.34), channel_id=1, source_target_pairs={{0,16},{4,20},{8,24},{12,28},{16,0},{20,4},{24,8},{28,12},{1,17},{... | collective-permute-start | bytes 294920 | tf_op jit(solution)/shard_map/ppermute | solution.py:559
  8.4 9.2 %collective-permute-start.7 = (bf16[12,32,128]{2,1,0:T(8,128)(2,1)S(1)}, bf16[12,32,128]{2,1,0:T(8,128)(2,1)S(1)}, u32[]{:S(2)}, u32[]{:S(2)}) collective-permute-start(bf16[12,32,128]{2,1,0:T(8,128)(2,1)S(1)} %get-tuple-element.35), channel_id=1, source_target_pairs={{0,8},{4,12},{8,0},{12,4},{16,24},{20,28},{24,16},{28,20},{1,9},{5... | collective-permute-start | bytes 294920 | tf_op jit(solution)/shard_map/ppermute | solution.py:559
  10.6 2.3 %collective-permute-start.3 = (bf16[3,30,512]{2,1,0:T(8,128)(2,1)S(1)}, bf16[3,30,512]{2,1,0:T(8,128)(2,1)S(1)}, u32[]{:S(2)}, u32[]{:S(2)}) collective-permute-start(bf16[3,30,512]{2,1,0:T(8,128)(2,1)S(1)} %choose_waves.1), channel_id=1, source_target_pairs={{0,4},{4,0},{8,12},{12,8},{16,20},{20,16},{24,28},{28,24},{1,5},{5... | collective-permute-start | bytes 276488 | tf_op jit(solution)/shard_map/ppermute | solution.py:556
  17.6 4.3 %collective-permute-start.8 = (bf16[12,32,128]{2,1,0:T(8,128)(2,1)S(1)}, bf16[12,32,128]{2,1,0:T(8,128)(2,1)S(1)}, u32[]{:S(2)}, u32[]{:S(2)}) collective-permute-start(bf16[12,32,128]{2,1,0:T(8,128)(2,1)S(1)} %choose_piece.1.piece), channel_id=1, source_target_pairs={{0,4},{4,0},{8,12},{12,8},{16,20},{20,16},{24,28},{28,24},{1,5},{5... | collective-permute-start | bytes 294920 | tf_op jit(solution)/shard_map/ppermute | solution.py:556
  24.6 6.3 %collective-permute-start.9 = (bf16[128,256]{1,0:T(8,128)(2,1)S(1)}, bf16[128,256]{1,0:T(8,128)(2,1)S(1)}, u32[]{:S(2)}, u32[]{:S(2)}) collective-permute-start(bf16[128,256]{1,0:T(8,128)(2,1)S(1)} %get-tuple-element.43), channel_id=1, source_target_pairs={{0,8},{1,0},{2,12},{3,4},{4,24},{5,16},{6,28},{7,20},{8,9},{9,1},{... | collective-permute-start | bytes 196616 | tf_op jit(solution)/shard_map/ppermute | solution.py:598
  24.6 8.3 %collective-permute-start.10 = (bf16[128,256]{1,0:T(8,128)(2,1)S(1)}, bf16[128,256]{1,0:T(8,128)(2,1)S(1)}, u32[]{:S(2)}, u32[]{:S(2)}) collective-permute-start(bf16[128,256]{1,0:T(8,128)(2,1)S(1)} %get-tuple-element.44), channel_id=1, source_target_pairs={{0,0},{1,8},{2,4},{3,12},{4,16},{5,24},{6,20},{7,28},{8,1},{9,9},{... | collective-permute-start | bytes 196616 | tf_op jit(solution)/shard_map/ppermute | solution.py:598
  33.0 3.2 %collective-permute-start.11 = (f32[64,256]{1,0:T(8,128)S(1)}, f32[64,256]{1,0:T(8,128)S(1)}, u32[]{:S(2)}, u32[]{:S(2)}) collective-permute-start(f32[64,256]{1,0:T(8,128)S(1)} %get-tuple-element.46), channel_id=1, source_target_pairs={{0,4},{4,0},{8,12},{12,8},{16,20},{20,16},{24,28},{28,24},{1,5},{5... | collective-permute-start | bytes 196616 | tf_op jit(solution)/shard_map/ppermute | solution.py:556

commit v15 on v11

--- a/solution.py
+++ b/solution.py
@@ -38,9 +38,17 @@
     fetch = [
         pltpu.make_async_copy(source, target, sems.at[index])
         for index, (source, target) in enumerate(
-            ((bank_blocks, chosen), (available, usable), (moveout, shifts), (templates, raw))
+            ((bank_blocks, chosen), (available, usable), (moveout, shifts))
         )
     ]
+    for block in range(blocks):
+        for part in range(2):
+            place = (block, pl.ds(half * part, half))
+            fetch.append(
+                pltpu.make_async_copy(
+                    templates.at[place], raw.at[place], sems.at[3 + 2 * block + part]
+                )
+            )
     for copy in fetch:
         copy.start()
     mine[...] = jnp.zeros_like(mine)
@@ -61,7 +69,8 @@
         turned = square[...].T
         later = pltpu.roll(turned, LANES - half, 1)
         codes.append([jnp.where(me == core, turned, later) for core in range(2)])
-    fetch[3].wait()
+    for copy in fetch[3:]:
+        copy.wait()
     for which in range(2):
         for side, out in enumerate((mine, theirs)):
             first = half * jnp.where(me == side, 0, 1)
@@ -100,7 +109,7 @@
             pltpu.VMEM(available.shape, jnp.int32),
             pltpu.VMEM(moveout.shape, jnp.int32),
             pltpu.VMEM((LANES, LANES), jnp.float32),
-            pltpu.SemaphoreType.DMA((4,)),
+            pltpu.SemaphoreType.DMA((3 + 2 * templates.shape[0],)),
         ],
         compiler_params=params(),
         cost_estimate=cost(2),
@@ -257,8 +266,10 @@
         both = jnp.concatenate([array[0:rows], array[32 : rows + 32]], axis=1)
         return jnp.dot(both, band, preferred_element_type=jnp.float32)
 
-    mean = windows(values) / tlen
-    scale = lax.rsqrt((windows(high) + windows(low)) / tlen - mean * mean + EPSILON)
+    first_sum = windows(values)
+    second_sum = windows(high) + windows(low)
+    variance = (second_sum * tlen - first_sum * first_sum) * (1.0 / tlen**2)
+    scale = lax.rsqrt(variance + EPSILON)
     for tile in range(count):
         inverse[:, LANES * tile : LANES * (tile + 1)] = scale[32 * tile : 32 * (tile + 1)]
 
@@ -369,10 +380,10 @@
             heads[place] = heads[place] + jnp.where(mask, values[0:LANES], 0.0)
     for index, (values, code) in enumerate(zip(heads, codes)):
         code = jnp.where(slots * index + ahead < half, code, 0.0)
-        center = jnp.sum(values, axis=0, keepdims=True) / tlen
-        deviate = jnp.where(used, values - center, 0.0)
-        spread = jnp.sqrt(jnp.sum(deviate * deviate, axis=0, keepdims=True) / tlen + EPSILON)
-        unit = (deviate / (spread * tlen)).astype(jnp.bfloat16).astype(jnp.float32)
+        deviate = jnp.where(used, values * tlen - jnp.sum(values, axis=0, keepdims=True), 0.0)
+        square = jnp.sum(deviate * deviate, axis=0, keepdims=True) * (1.0 / tlen**3)
+        unit = deviate / (jnp.sqrt(square + EPSILON) * tlen**2)
+        unit = unit.astype(jnp.bfloat16).astype(jnp.float32)
         unit = jnp.where(code > 0, unit, 0.0)
         shift = code.astype(jnp.int32) - 1
         for bit in (1, 2, 4):

time: 36.8 us -> 36.9 us (level)
  no operation moved by 1% of the time
where the time goes in v15:
time: 36.9 us; the launch traced here: 36.5 us
  starting transfers between devices  15.7 us (43%)
  Pallas kernels  11.5 us (31%)
  waiting for transfers between devices  9.19 us (25%)
    ppermute x2, waiting for transfers between devices, shards(): gathered.append(lax.ppermute(parts[step], ('tm', 'sta'), route))  5.47 us
    pallas_call x2, Pallas kernels, correlate(): pl.pallas_call(functools.partial(main_kernel, side, tlen, group), out_sha...  5.06 us
    ppermute x4, starting transfers between devices, across(): lax.ppermute(array, 'tm', [(i, i ^ 2 * step) for i in range(count_tm)])  4.91 us
    ppermute x5, starting transfers between devices, swap(): return lax.ppermute(array, 'tm', [(i, i ^ 1) for i in range(count_tm)])  4.24 us
    ppermute x2, starting transfers between devices, shards(): gathered.append(lax.ppermute(parts[step], ('tm', 'sta'), route))  4.15 us
    pallas_call x1, Pallas kernels, prepare_waves(): pl.pallas_call(functools.partial(waves_kernel, channels, tlen, unroll), o...  2.86 us
    ppermute x1, starting transfers between devices, shards(): far.append(lax.ppermute(pair, 'tm', route))  2.37 us
    pallas_call x1, Pallas kernels, pack(): pl.pallas_call(pack_kernel, out_shape=[jax.ShapeDtypeStruct(shape, jnp.bf...  2.3 us
  transfers between devices with their start and end apart: 12, of which 5 were waited for; matrix products, arithmetic and copies ran while one was open for 0% of the time, Pallas kernels for 22%

profile of v15, /device:TPU:7, one launch (start us, length us, event | category | flops | bytes accessed | tf_op | source)
XLA Modules:
  0.0 36.5 jit_solution(8832154360187911053)
XLA Ops:
  0.0 0.0 copy-start
  0.0 0.7 %collective-permute-start = (bf16[30,512]{1,0:T(8,128)(2,1)}, bf16[30,512]{1,0:T(8,128)(2,1)S(1)}, u32[]{:S(2)}, u32[]{:S(2)}) collective-permute-start(bf16[30,512]{1,0:T(8,128)(2,1)} %own.1), channel_id=1, source_target_pairs={{0,4},{4,0},{8,12},{12,8},{16,20},{20,16},{24,28},{28,24},{1,5},{5... | collective-permute-start | bytes 92168 | tf_op jit(solution)/shard_map/ppermute | solution.py:554
  0.7 2.3 %pack.1 = (bf16[4,12,32,128]{3,2,1,0:T(8,128)(2,1)S(1)}, bf16[4,12,32,128]{3,2,1,0:T(8,128)(2,1)S(1)}, s32[8,128]{1,0:T(8,128)S(1)}) custom-call(s32[2]{0:T(128)} %bank_blocks.1, bf16[2,30,64,100]{3,2,1,0:T(8,128)(2,1)} %bitcast.3, s32[30,2,64]{2,1,0:T(2,128)} %bitcast.4, s32[30,2,64]{2,1,0:T(2,128)} %bitcast.5), custom_call_target="tpu_custom_call" | custom-call | flops 2000000000 | bytes 2000000 | tf_op jit(solution)/shard_map/pack/pallas_call | solution.py:100
  3.0 0.0 collective-permute-done.partner
  3.0 0.1 collective-permute-start.4
  3.1 0.0 copy-done
  3.1 2.4 %collective-permute-start.2 = (bf16[2,30,512]{2,1,0:T(8,128)(2,1)S(1)}, bf16[2,30,512]{2,1,0:T(8,128)(2,1)S(1)}, u32[]{:S(2)}, u32[]{:S(2)}) collective-permute-start(bf16[2,30,512]{2,1,0:T(8,128)(2,1)S(1)} %pair_waves.1.pair), channel_id=1, source_target_pairs={{0,24},{4,20},{8,16},{12,28},{16,8},{20,4},{24,0},{28,12},{1,25},{... | collective-permute-start | bytes 184328 | tf_op jit(solution)/shard_map/ppermute | solution.py:575
  5.5 1.3 %collective-permute-start.1 = (bf16[30,512]{1,0:T(8,128)(2,1)S(1)}, bf16[30,512]{1,0:T(8,128)(2,1)S(1)}, u32[]{:S(2)}, u32[]{:S(2)}) collective-permute-start(bf16[30,512]{1,0:T(8,128)(2,1)S(1)} %copy-done), channel_id=1, source_target_pairs={{0,8},{4,12},{8,0},{12,4},{16,24},{20,28},{24,16},{28,20},{1,9},{5... | collective-permute-start | bytes 92168 | tf_op jit(solution)/shard_map/ppermute | solution.py:557
  6.8 0.0 collective-permute-done.4.other
  6.8 0.2 merge.1
  7.0 1.4 %collective-permute-start.5 = (bf16[12,32,128]{2,1,0:T(8,128)(2,1)S(1)}, bf16[12,32,128]{2,1,0:T(8,128)(2,1)S(1)}, u32[]{:S(2)}, u32[]{:S(2)}) collective-permute-start(bf16[12,32,128]{2,1,0:T(8,128)(2,1)S(1)} %get-tuple-element.33), channel_id=1, source_target_pairs={{0,24},{4,28},{8,16},{12,20},{16,8},{20,12},{24,0},{28,4},{1,25},{... | collective-permute-start | bytes 294920 | tf_op jit(solution)/shard_map/ppermute | solution.py:557
  8.4 0.0 collective-permute-start.6
  8.4 2.2 %collective-permute-start.7 = (bf16[12,32,128]{2,1,0:T(8,128)(2,1)S(1)}, bf16[12,32,128]{2,1,0:T(8,128)(2,1)S(1)}, u32[]{:S(2)}, u32[]{:S(2)}) collective-permute-start(bf16[12,32,128]{2,1,0:T(8,128)(2,1)S(1)} %get-tuple-element.35), channel_id=1, source_target_pairs={{0,8},{4,12},{8,0},{12,4},{16,24},{20,28},{24,16},{28,20},{1,9},{5... | collective-permute-start | bytes 294920 | tf_op jit(solution)/shard_map/ppermute | solution.py:557
  10.6 0.0 collective-permute-done.1.beside
  10.6 0.0 collective-permute-done.2.rest_0_
  10.7 1.4 %collective-permute-start.3 = (bf16[3,30,512]{2,1,0:T(8,128)(2,1)S(1)}, bf16[3,30,512]{2,1,0:T(8,128)(2,1)S(1)}, u32[]{:S(2)}, u32[]{:S(2)}) collective-permute-start(bf16[3,30,512]{2,1,0:T(8,128)(2,1)S(1)} %choose_waves.1), channel_id=1, source_target_pairs={{0,4},{4,0},{8,12},{12,8},{16,20},{20,16},{24,28},{28,24},{1,5},{5... | collective-permute-start | bytes 276488 | tf_op jit(solution)/shard_map/ppermute | solution.py:554
  12.1 0.9 %collective-permute-done.3.swapped = bf16[3,30,512]{2,1,0:T(8,128)(2,1)S(1)} collective-permute-done((bf16[3,30,512]{2,1,0:T(8,128)(2,1)S(1)}, bf16[3,30,512]{2,1,0:T(8,128)(2,1)S(1)}, u32[]{:S(2)}, u32[]{:S(2)}) %collective-permute-start.3) | collective-permute-done | bytes 92192 | tf_op jit(solution)/shard_map/ppermute | solution.py:554
  13.0 2.9 %prepare_waves.1 = (bf16[30,272,128]{2,1,0:T(8,128)(2,1)S(1)}, bf16[30,256,256]{2,1,0:T(8,128)(2,1)S(1)}) custom-call(bf16[3,30,512]{2,1,0:T(8,128)(2,1)S(1)} %collective-permute-done.3.swapped, bf16[2,30,512]{2,1,0:T(8,128)(2,1)S(1)} %pair_waves.1.pair, bf16[30,512]{1,0:T(8,128)(2,1)S(1)} %collective-permute-done.1.beside, ...), custom_call_target="tpu_custom_call" | custom-call | flops 50000000 | bytes 50000 | tf_op jit(solution)/shard_map/prepare_waves/pallas_call | solution.py:301
  15.9 0.0 collective-permute-done.5.refs_3_
  15.9 1.7 %collective-permute-done.6.refs_2_ = bf16[12,32,128]{2,1,0:T(8,128)(2,1)S(1)} collective-permute-done((bf16[12,32,128]{2,1,0:T(8,128)(2,1)S(1)}, bf16[12,32,128]{2,1,0:T(8,128)(2,1)S(1)}, u32[]{:S(2)}, u32[]{:S(2)}) %collective-permute-start.6) | collective-permute-done | bytes 98336 | tf_op jit(solution)/shard_map/ppermute | solution.py:557
  17.6 0.0 collective-permute-done.7.refs_1_
  17.6 0.1 choose_piece.1.piece
  17.7 1.8 %collective-permute-start.8 = (bf16[12,32,128]{2,1,0:T(8,128)(2,1)S(1)}, bf16[12,32,128]{2,1,0:T(8,128)(2,1)S(1)}, u32[]{:S(2)}, u32[]{:S(2)}) collective-permute-start(bf16[12,32,128]{2,1,0:T(8,128)(2,1)S(1)} %choose_piece.1.piece), channel_id=1, source_target_pairs={{0,4},{4,0},{8,12},{12,8},{16,20},{20,16},{24,28},{28,24},{1,5},{5... | collective-permute-start | bytes 294920 | tf_op jit(solution)/shard_map/ppermute | solution.py:554
  19.5 2.5 %correlate_first.1.rest_0_ = f32[256,256]{1,0:T(8,128)S(1)} custom-call(bf16[12,32,128]{2,1,0:T(8,128)(2,1)S(1)} %choose_piece.1.piece, bf16[30,272,128]{2,1,0:T(8,128)(2,1)S(1)} %get-tuple-element.41.left_a, bf16[30,256,256]{2,1,0:T(8,128)(2,1)S(1)} %get-tuple-element.42.left_r), custom_call_target="tpu_custom_call" | custom-call | flops 3000000000 | bytes 3000000 | tf_op jit(solution)/shard_map/correlate_first/pallas_call | solution.py:470
  22.0 0.0 collective-permute-done.8.piece
  22.0 2.6 %correlate_second.1 = (bf16[128,256]{1,0:T(8,128)(2,1)S(1)}, bf16[128,256]{1,0:T(8,128)(2,1)S(1)}) custom-call(bf16[12,32,128]{2,1,0:T(8,128)(2,1)S(1)} %collective-permute-done.8.piece, bf16[30,272,128]{2,1,0:T(8,128)(2,1)S(1)} %get-tuple-element.41.left_a, bf16[30,256,256]{2,1,0:T(8,128)(2,1)S(1)} %get-tuple-element.42.left_r, ...), custom_call_target="tpu_custom_call" | custom-call | flops 3000000000 | bytes 3000000 | tf_op jit(solution)/shard_map/correlate_second/pallas_call | solution.py:470
  24.6 4.1 %collective-permute-start.9 = (bf16[128,256]{1,0:T(8,128)(2,1)S(1)}, bf16[128,256]{1,0:T(8,128)(2,1)S(1)}, u32[]{:S(2)}, u32[]{:S(2)}) collective-permute-start(bf16[128,256]{1,0:T(8,128)(2,1)S(1)} %get-tuple-element.43), channel_id=1, source_target_pairs={{0,0},{1,8},{2,4},{3,12},{4,16},{5,24},{6,20},{7,28},{8,1},{9,9},{... | collective-permute-start | bytes 196616 | tf_op jit(solution)/shard_map/ppermute | solution.py:596
  28.7 0.1 collective-permute-start.10
  28.8 4.4 %collective-permute-done.9.refs_0_ = bf16[128,256]{1,0:T(8,128)(2,1)S(1)} collective-permute-done((bf16[128,256]{1,0:T(8,128)(2,1)S(1)}, bf16[128,256]{1,0:T(8,128)(2,1)S(1)}, u32[]{:S(2)}, u32[]{:S(2)}) %collective-permute-start.9) | collective-permute-done | bytes 65568 | tf_op jit(solution)/shard_map/ppermute | solution.py:596
  33.2 1.1 %collective-permute-done.10.refs_1_ = bf16[128,256]{1,0:T(8,128)(2,1)S(1)} collective-permute-done((bf16[128,256]{1,0:T(8,128)(2,1)S(1)}, bf16[128,256]{1,0:T(8,128)(2,1)S(1)}, u32[]{:S(2)}, u32[]{:S(2)}) %collective-permute-start.10) | collective-permute-done | bytes 65568 | tf_op jit(solution)/shard_map/ppermute | solution.py:596
  34.3 0.3 collective-permute-start.11
  34.6 1.0 %collective-permute-done.11.received = f32[64,256]{1,0:T(8,128)S(1)} collective-permute-done((f32[64,256]{1,0:T(8,128)S(1)}, f32[64,256]{1,0:T(8,128)S(1)}, u32[]{:S(2)}, u32[]{:S(2)}) %collective-permute-start.11) | collective-permute-done | bytes 65568 | tf_op jit(solution)/shard_map/ppermute | solution.py:554
  35.6 0.9 %finish.1 = f32[32,512]{1,0:T(8,128)} custom-call(f32[64,256]{1,0:T(8,128)S(1)} %get-tuple-element.45.ours, f32[64,256]{1,0:T(8,128)S(1)} %collective-permute-done.11.received), custom_call_target="tpu_custom_call" | custom-call | flops 1000000000 | bytes 1000000 | tf_op jit(solution)/shard_map/finish/pallas_call | solution.py:533
  (3 shorter events, 0.1 us)
Async XLA Ops:
  0.0 3.1 %copy-start = (bf16[30,512]{1,0:T(8,128)(2,1)S(1)}, bf16[30,512]{1,0:T(8,128)(2,1)}, u32[]{:S(2)}) copy-start(bf16[30,512]{1,0:T(8,128)(2,1)} %own.1) | copy-start | bytes 92164
  0.0 3.0 %collective-permute-start = (bf16[30,512]{1,0:T(8,128)(2,1)}, bf16[30,512]{1,0:T(8,128)(2,1)S(1)}, u32[]{:S(2)}, u32[]{:S(2)}) collective-permute-start(bf16[30,512]{1,0:T(8,128)(2,1)} %own.1), channel_id=1, source_target_pairs={{0,4},{4,0},{8,12},{12,8},{16,20},{20,16},{24,28},{28,24},{1,5},{5... | collective-permute-start | bytes 92168 | tf_op jit(solution)/shard_map/ppermute | solution.py:554
  3.0 3.8 %collective-permute-start.4 = (bf16[4,12,32,128]{3,2,1,0:T(8,128)(2,1)S(1)}, bf16[4,12,32,128]{3,2,1,0:T(8,128)(2,1)S(1)}, u32[]{:S(2)}, u32[]{:S(2)}) collective-permute-start(bf16[4,12,32,128]{3,2,1,0:T(8,128)(2,1)S(1)} %get-tuple-element.32), channel_id=1, source_target_pairs={{0,4},{4,0},{8,12},{12,8},{16,20},{20,16},{24,28},{28,24},{1,5},{5... | collective-permute-start | bytes 1179656 | tf_op jit(solution)/shard_map/ppermute | solution.py:554
  3.1 7.5 %collective-permute-start.2 = (bf16[2,30,512]{2,1,0:T(8,128)(2,1)S(1)}, bf16[2,30,512]{2,1,0:T(8,128)(2,1)S(1)}, u32[]{:S(2)}, u32[]{:S(2)}) collective-permute-start(bf16[2,30,512]{2,1,0:T(8,128)(2,1)S(1)} %pair_waves.1.pair), channel_id=1, source_target_pairs={{0,24},{4,20},{8,16},{12,28},{16,8},{20,4},{24,0},{28,12},{1,25},{... | collective-permute-start | bytes 184328 | tf_op jit(solution)/shard_map/ppermute | solution.py:575
  5.5 5.1 %collective-permute-start.1 = (bf16[30,512]{1,0:T(8,128)(2,1)S(1)}, bf16[30,512]{1,0:T(8,128)(2,1)S(1)}, u32[]{:S(2)}, u32[]{:S(2)}) collective-permute-start(bf16[30,512]{1,0:T(8,128)(2,1)S(1)} %copy-done), channel_id=1, source_target_pairs={{0,8},{4,12},{8,0},{12,4},{16,24},{20,28},{24,16},{28,20},{1,9},{5... | collective-permute-start | bytes 92168 | tf_op jit(solution)/shard_map/ppermute | solution.py:557
  7.0 8.8 %collective-permute-start.5 = (bf16[12,32,128]{2,1,0:T(8,128)(2,1)S(1)}, bf16[12,32,128]{2,1,0:T(8,128)(2,1)S(1)}, u32[]{:S(2)}, u32[]{:S(2)}) collective-permute-start(bf16[12,32,128]{2,1,0:T(8,128)(2,1)S(1)} %get-tuple-element.33), channel_id=1, source_target_pairs={{0,24},{4,28},{8,16},{12,20},{16,8},{20,12},{24,0},{28,4},{1,25},{... | collective-permute-start | bytes 294920 | tf_op jit(solution)/shard_map/ppermute | solution.py:557
  8.4 9.2 %collective-permute-start.6 = (bf16[12,32,128]{2,1,0:T(8,128)(2,1)S(1)}, bf16[12,32,128]{2,1,0:T(8,128)(2,1)S(1)}, u32[]{:S(2)}, u32[]{:S(2)}) collective-permute-start(bf16[12,32,128]{2,1,0:T(8,128)(2,1)S(1)} %get-tuple-element.34), channel_id=1, source_target_pairs={{0,16},{4,20},{8,24},{12,28},{16,0},{20,4},{24,8},{28,12},{1,17},{... | collective-permute-start | bytes 294920 | tf_op jit(solution)/shard_map/ppermute | solution.py:557
  8.4 9.2 %collective-permute-start.7 = (bf16[12,32,128]{2,1,0:T(8,128)(2,1)S(1)}, bf16[12,32,128]{2,1,0:T(8,128)(2,1)S(1)}, u32[]{:S(2)}, u32[]{:S(2)}) collective-permute-start(bf16[12,32,128]{2,1,0:T(8,128)(2,1)S(1)} %get-tuple-element.35), channel_id=1, source_target_pairs={{0,8},{4,12},{8,0},{12,4},{16,24},{20,28},{24,16},{28,20},{1,9},{5... | collective-permute-start | bytes 294920 | tf_op jit(solution)/shard_map/ppermute | solution.py:557
  10.7 2.3 %collective-permute-start.3 = (bf16[3,30,512]{2,1,0:T(8,128)(2,1)S(1)}, bf16[3,30,512]{2,1,0:T(8,128)(2,1)S(1)}, u32[]{:S(2)}, u32[]{:S(2)}) collective-permute-start(bf16[3,30,512]{2,1,0:T(8,128)(2,1)S(1)} %choose_waves.1), channel_id=1, source_target_pairs={{0,4},{4,0},{8,12},{12,8},{16,20},{20,16},{24,28},{28,24},{1,5},{5... | collective-permute-start | bytes 276488 | tf_op jit(solution)/shard_map/ppermute | solution.py:554
  17.7 4.3 %collective-permute-start.8 = (bf16[12,32,128]{2,1,0:T(8,128)(2,1)S(1)}, bf16[12,32,128]{2,1,0:T(8,128)(2,1)S(1)}, u32[]{:S(2)}, u32[]{:S(2)}) collective-permute-start(bf16[12,32,128]{2,1,0:T(8,128)(2,1)S(1)} %choose_piece.1.piece), channel_id=1, source_target_pairs={{0,4},{4,0},{8,12},{12,8},{16,20},{20,16},{24,28},{28,24},{1,5},{5... | collective-permute-start | bytes 294920 | tf_op jit(solution)/shard_map/ppermute | solution.py:554
  24.6 8.6 %collective-permute-start.9 = (bf16[128,256]{1,0:T(8,128)(2,1)S(1)}, bf16[128,256]{1,0:T(8,128)(2,1)S(1)}, u32[]{:S(2)}, u32[]{:S(2)}) collective-permute-start(bf16[128,256]{1,0:T(8,128)(2,1)S(1)} %get-tuple-element.43), channel_id=1, source_target_pairs={{0,0},{1,8},{2,4},{3,12},{4,16},{5,24},{6,20},{7,28},{8,1},{9,9},{... | collective-permute-start | bytes 196616 | tf_op jit(solution)/shard_map/ppermute | solution.py:596
  28.7 5.5 %collective-permute-start.10 = (bf16[128,256]{1,0:T(8,128)(2,1)S(1)}, bf16[128,256]{1,0:T(8,128)(2,1)S(1)}, u32[]{:S(2)}, u32[]{:S(2)}) collective-permute-start(bf16[128,256]{1,0:T(8,128)(2,1)S(1)} %get-tuple-element.44), channel_id=1, source_target_pairs={{0,8},{1,0},{2,12},{3,4},{4,24},{5,16},{6,28},{7,20},{8,9},{9,1},{... | collective-permute-start | bytes 196616 | tf_op jit(solution)/shard_map/ppermute | solution.py:596
  34.3 1.3 %collective-permute-start.11 = (f32[64,256]{1,0:T(8,128)S(1)}, f32[64,256]{1,0:T(8,128)S(1)}, u32[]{:S(2)}, u32[]{:S(2)}) collective-permute-start(f32[64,256]{1,0:T(8,128)S(1)} %get-tuple-element.46), channel_id=1, source_target_pairs={{0,4},{4,0},{8,12},{12,8},{16,20},{20,16},{24,28},{28,24},{1,5},{5... | collective-permute-start | bytes 196616 | tf_op jit(solution)/shard_map/ppermute | solution.py:554

commit v16 on v15

--- a/solution.py
+++ b/solution.py
@@ -426,19 +426,25 @@
                 weight_r[item, 0:LANES, lanes] = pick
                 weight_r[item, LANES : 2 * LANES, lanes] = pick
 
+    def products(item):
+        both = [left_a[base + item, 0:rows, :], left_a[base + item, 16 : rows + 16, :]]
+        corr = jnp.dot(
+            jnp.concatenate(both, axis=1), weight_a[item], preferred_element_type=jnp.float32
+        )
+        factor = jnp.dot(left_r[base + item], weight_r[item], preferred_element_type=jnp.float32)
+        return corr * factor
+
     def apply(number, count):
-        for slot in range(count):
-            item = number * slots + slot
-            both = [left_a[base + item, 0:rows, :], left_a[base + item, 16 : rows + 16, :]]
-            corr = jnp.dot(
-                jnp.concatenate(both, axis=1), weight_a[item], preferred_element_type=jnp.float32
-            )
-            factor = jnp.dot(
-                left_r[base + item], weight_r[item], preferred_element_type=jnp.float32
-            )
-            total[...] += corr * factor
-
-    total[...] = before[...] if side else jnp.zeros_like(total)
+        for item in range(number * slots, number * slots + count, 2):
+            value = products(item)
+            if item + 1 < number * slots + count:
+                value = value + products(item + 1)
+            if item:
+                value = value + total[...]
+            elif side:
+                value = value + before[...]
+            total[...] = value
+
     build(0)
 
     for number in range(1, banks):

time: 36.9 us -> 36.9 us (level)
  no operation moved by 1% of the time
where the time goes in v16:
time: 36.9 us; the launch traced here: 36.5 us
  starting transfers between devices  15.7 us (43%)
  Pallas kernels  11.5 us (31%)
  waiting for transfers between devices  9.19 us (25%)
    ppermute x2, waiting for transfers between devices, shards(): gathered.append(lax.ppermute(parts[step], ('tm', 'sta'), route))  5.47 us
    pallas_call x2, Pallas kernels, correlate(): pl.pallas_call(functools.partial(main_kernel, side, tlen, group), out_sha...  5.05 us
    ppermute x4, starting transfers between devices, across(): lax.ppermute(array, 'tm', [(i, i ^ 2 * step) for i in range(count_tm)])  4.91 us
    ppermute x5, starting transfers between devices, swap(): return lax.ppermute(array, 'tm', [(i, i ^ 1) for i in range(count_tm)])  4.24 us
    ppermute x2, starting transfers between devices, shards(): gathered.append(lax.ppermute(parts[step], ('tm', 'sta'), route))  4.15 us
    pallas_call x1, Pallas kernels, prepare_waves(): pl.pallas_call(functools.partial(waves_kernel, channels, tlen, unroll), o...  2.86 us
    ppermute x1, starting transfers between devices, shards(): far.append(lax.ppermute(pair, 'tm', route))  2.37 us
    pallas_call x1, Pallas kernels, pack(): pl.pallas_call(pack_kernel, out_shape=[jax.ShapeDtypeStruct(shape, jnp.bf...  2.3 us
  transfers between devices with their start and end apart: 12, of which 5 were waited for; matrix products, arithmetic and copies ran while one was open for 0% of the time, Pallas kernels for 22%

profile of v16, /device:TPU:7, one launch (start us, length us, event | category | flops | bytes accessed | tf_op | source)
XLA Modules:
  0.0 36.5 jit_solution(2993030199238231482)
XLA Ops:
  0.0 0.0 copy-start
  0.0 0.7 %collective-permute-start = (bf16[30,512]{1,0:T(8,128)(2,1)}, bf16[30,512]{1,0:T(8,128)(2,1)S(1)}, u32[]{:S(2)}, u32[]{:S(2)}) collective-permute-start(bf16[30,512]{1,0:T(8,128)(2,1)} %own.1), channel_id=1, source_target_pairs={{0,4},{4,0},{8,12},{12,8},{16,20},{20,16},{24,28},{28,24},{1,5},{5... | collective-permute-start | bytes 92168 | tf_op jit(solution)/shard_map/ppermute | solution.py:560
  0.7 2.3 %pack.1 = (bf16[4,12,32,128]{3,2,1,0:T(8,128)(2,1)S(1)}, bf16[4,12,32,128]{3,2,1,0:T(8,128)(2,1)S(1)}, s32[8,128]{1,0:T(8,128)S(1)}) custom-call(s32[2]{0:T(128)} %bank_blocks.1, bf16[2,30,64,100]{3,2,1,0:T(8,128)(2,1)} %bitcast.3, s32[30,2,64]{2,1,0:T(2,128)} %bitcast.4, s32[30,2,64]{2,1,0:T(2,128)} %bitcast.5), custom_call_target="tpu_custom_call" | custom-call | flops 2000000000 | bytes 2000000 | tf_op jit(solution)/shard_map/pack/pallas_call | solution.py:100
  3.0 0.0 collective-permute-done.partner
  3.0 0.1 collective-permute-start.4
  3.1 0.0 copy-done
  3.1 2.4 %collective-permute-start.2 = (bf16[2,30,512]{2,1,0:T(8,128)(2,1)S(1)}, bf16[2,30,512]{2,1,0:T(8,128)(2,1)S(1)}, u32[]{:S(2)}, u32[]{:S(2)}) collective-permute-start(bf16[2,30,512]{2,1,0:T(8,128)(2,1)S(1)} %pair_waves.1.pair), channel_id=1, source_target_pairs={{0,24},{4,20},{8,16},{12,28},{16,8},{20,4},{24,0},{28,12},{1,25},{... | collective-permute-start | bytes 184328 | tf_op jit(solution)/shard_map/ppermute | solution.py:581
  5.5 1.3 %collective-permute-start.1 = (bf16[30,512]{1,0:T(8,128)(2,1)S(1)}, bf16[30,512]{1,0:T(8,128)(2,1)S(1)}, u32[]{:S(2)}, u32[]{:S(2)}) collective-permute-start(bf16[30,512]{1,0:T(8,128)(2,1)S(1)} %copy-done), channel_id=1, source_target_pairs={{0,8},{4,12},{8,0},{12,4},{16,24},{20,28},{24,16},{28,20},{1,9},{5... | collective-permute-start | bytes 92168 | tf_op jit(solution)/shard_map/ppermute | solution.py:563
  6.8 0.0 collective-permute-done.4.other
  6.8 0.2 merge.1
  7.0 1.4 %collective-permute-start.5 = (bf16[12,32,128]{2,1,0:T(8,128)(2,1)S(1)}, bf16[12,32,128]{2,1,0:T(8,128)(2,1)S(1)}, u32[]{:S(2)}, u32[]{:S(2)}) collective-permute-start(bf16[12,32,128]{2,1,0:T(8,128)(2,1)S(1)} %get-tuple-element.33), channel_id=1, source_target_pairs={{0,24},{4,28},{8,16},{12,20},{16,8},{20,12},{24,0},{28,4},{1,25},{... | collective-permute-start | bytes 294920 | tf_op jit(solution)/shard_map/ppermute | solution.py:563
  8.4 0.0 collective-permute-start.6
  8.4 2.2 %collective-permute-start.7 = (bf16[12,32,128]{2,1,0:T(8,128)(2,1)S(1)}, bf16[12,32,128]{2,1,0:T(8,128)(2,1)S(1)}, u32[]{:S(2)}, u32[]{:S(2)}) collective-permute-start(bf16[12,32,128]{2,1,0:T(8,128)(2,1)S(1)} %get-tuple-element.35), channel_id=1, source_target_pairs={{0,8},{4,12},{8,0},{12,4},{16,24},{20,28},{24,16},{28,20},{1,9},{5... | collective-permute-start | bytes 294920 | tf_op jit(solution)/shard_map/ppermute | solution.py:563
  10.6 0.0 collective-permute-done.1.beside
  10.6 0.0 collective-permute-done.2.rest_0_
  10.7 1.4 %collective-permute-start.3 = (bf16[3,30,512]{2,1,0:T(8,128)(2,1)S(1)}, bf16[3,30,512]{2,1,0:T(8,128)(2,1)S(1)}, u32[]{:S(2)}, u32[]{:S(2)}) collective-permute-start(bf16[3,30,512]{2,1,0:T(8,128)(2,1)S(1)} %choose_waves.1), channel_id=1, source_target_pairs={{0,4},{4,0},{8,12},{12,8},{16,20},{20,16},{24,28},{28,24},{1,5},{5... | collective-permute-start | bytes 276488 | tf_op jit(solution)/shard_map/ppermute | solution.py:560
  12.1 0.9 %collective-permute-done.3.swapped = bf16[3,30,512]{2,1,0:T(8,128)(2,1)S(1)} collective-permute-done((bf16[3,30,512]{2,1,0:T(8,128)(2,1)S(1)}, bf16[3,30,512]{2,1,0:T(8,128)(2,1)S(1)}, u32[]{:S(2)}, u32[]{:S(2)}) %collective-permute-start.3) | collective-permute-done | bytes 92192 | tf_op jit(solution)/shard_map/ppermute | solution.py:560
  13.0 2.9 %prepare_waves.1 = (bf16[30,272,128]{2,1,0:T(8,128)(2,1)S(1)}, bf16[30,256,256]{2,1,0:T(8,128)(2,1)S(1)}) custom-call(bf16[3,30,512]{2,1,0:T(8,128)(2,1)S(1)} %collective-permute-done.3.swapped, bf16[2,30,512]{2,1,0:T(8,128)(2,1)S(1)} %pair_waves.1.pair, bf16[30,512]{1,0:T(8,128)(2,1)S(1)} %collective-permute-done.1.beside, ...), custom_call_target="tpu_custom_call" | custom-call | flops 50000000 | bytes 50000 | tf_op jit(solution)/shard_map/prepare_waves/pallas_call | solution.py:301
  15.9 0.0 collective-permute-done.5.refs_3_
  15.9 1.7 %collective-permute-done.6.refs_2_ = bf16[12,32,128]{2,1,0:T(8,128)(2,1)S(1)} collective-permute-done((bf16[12,32,128]{2,1,0:T(8,128)(2,1)S(1)}, bf16[12,32,128]{2,1,0:T(8,128)(2,1)S(1)}, u32[]{:S(2)}, u32[]{:S(2)}) %collective-permute-start.6) | collective-permute-done | bytes 98336 | tf_op jit(solution)/shard_map/ppermute | solution.py:563
  17.6 0.0 collective-permute-done.7.refs_1_
  17.6 0.1 choose_piece.1.piece
  17.7 1.8 %collective-permute-start.8 = (bf16[12,32,128]{2,1,0:T(8,128)(2,1)S(1)}, bf16[12,32,128]{2,1,0:T(8,128)(2,1)S(1)}, u32[]{:S(2)}, u32[]{:S(2)}) collective-permute-start(bf16[12,32,128]{2,1,0:T(8,128)(2,1)S(1)} %choose_piece.1.piece), channel_id=1, source_target_pairs={{0,4},{4,0},{8,12},{12,8},{16,20},{20,16},{24,28},{28,24},{1,5},{5... | collective-permute-start | bytes 294920 | tf_op jit(solution)/shard_map/ppermute | solution.py:560
  19.5 2.5 %correlate_first.1.rest_0_ = f32[256,256]{1,0:T(8,128)S(1)} custom-call(bf16[12,32,128]{2,1,0:T(8,128)(2,1)S(1)} %choose_piece.1.piece, bf16[30,272,128]{2,1,0:T(8,128)(2,1)S(1)} %get-tuple-element.41.left_a, bf16[30,256,256]{2,1,0:T(8,128)(2,1)S(1)} %get-tuple-element.42.left_r), custom_call_target="tpu_custom_call" | custom-call | flops 3000000000 | bytes 3000000 | tf_op jit(solution)/shard_map/correlate_first/pallas_call | solution.py:476
  22.0 0.0 collective-permute-done.8.piece
  22.0 2.5 %correlate_second.1 = (bf16[128,256]{1,0:T(8,128)(2,1)S(1)}, bf16[128,256]{1,0:T(8,128)(2,1)S(1)}) custom-call(bf16[12,32,128]{2,1,0:T(8,128)(2,1)S(1)} %collective-permute-done.8.piece, bf16[30,272,128]{2,1,0:T(8,128)(2,1)S(1)} %get-tuple-element.41.left_a, bf16[30,256,256]{2,1,0:T(8,128)(2,1)S(1)} %get-tuple-element.42.left_r, ...), custom_call_target="tpu_custom_call" | custom-call | flops 3000000000 | bytes 3000000 | tf_op jit(solution)/shard_map/correlate_second/pallas_call | solution.py:476
  24.6 4.1 %collective-permute-start.9 = (bf16[128,256]{1,0:T(8,128)(2,1)S(1)}, bf16[128,256]{1,0:T(8,128)(2,1)S(1)}, u32[]{:S(2)}, u32[]{:S(2)}) collective-permute-start(bf16[128,256]{1,0:T(8,128)(2,1)S(1)} %get-tuple-element.43), channel_id=1, source_target_pairs={{0,0},{1,8},{2,4},{3,12},{4,16},{5,24},{6,20},{7,28},{8,1},{9,9},{... | collective-permute-start | bytes 196616 | tf_op jit(solution)/shard_map/ppermute | solution.py:602
  28.7 0.1 collective-permute-start.10
  28.8 4.4 %collective-permute-done.9.refs_0_ = bf16[128,256]{1,0:T(8,128)(2,1)S(1)} collective-permute-done((bf16[128,256]{1,0:T(8,128)(2,1)S(1)}, bf16[128,256]{1,0:T(8,128)(2,1)S(1)}, u32[]{:S(2)}, u32[]{:S(2)}) %collective-permute-start.9) | collective-permute-done | bytes 65568 | tf_op jit(solution)/shard_map/ppermute | solution.py:602
  33.2 1.1 %collective-permute-done.10.refs_1_ = bf16[128,256]{1,0:T(8,128)(2,1)S(1)} collective-permute-done((bf16[128,256]{1,0:T(8,128)(2,1)S(1)}, bf16[128,256]{1,0:T(8,128)(2,1)S(1)}, u32[]{:S(2)}, u32[]{:S(2)}) %collective-permute-start.10) | collective-permute-done | bytes 65568 | tf_op jit(solution)/shard_map/ppermute | solution.py:602
  34.3 0.3 collective-permute-start.11
  34.6 1.0 %collective-permute-done.11.received = f32[64,256]{1,0:T(8,128)S(1)} collective-permute-done((f32[64,256]{1,0:T(8,128)S(1)}, f32[64,256]{1,0:T(8,128)S(1)}, u32[]{:S(2)}, u32[]{:S(2)}) %collective-permute-start.11) | collective-permute-done | bytes 65568 | tf_op jit(solution)/shard_map/ppermute | solution.py:560
  35.6 0.9 %finish.1 = f32[32,512]{1,0:T(8,128)} custom-call(f32[64,256]{1,0:T(8,128)S(1)} %get-tuple-element.45.ours, f32[64,256]{1,0:T(8,128)S(1)} %collective-permute-done.11.received), custom_call_target="tpu_custom_call" | custom-call | flops 1000000000 | bytes 1000000 | tf_op jit(solution)/shard_map/finish/pallas_call | solution.py:539
  (3 shorter events, 0.1 us)
Async XLA Ops:
  0.0 3.1 %copy-start = (bf16[30,512]{1,0:T(8,128)(2,1)S(1)}, bf16[30,512]{1,0:T(8,128)(2,1)}, u32[]{:S(2)}) copy-start(bf16[30,512]{1,0:T(8,128)(2,1)} %own.1) | copy-start | bytes 92164
  0.0 3.0 %collective-permute-start = (bf16[30,512]{1,0:T(8,128)(2,1)}, bf16[30,512]{1,0:T(8,128)(2,1)S(1)}, u32[]{:S(2)}, u32[]{:S(2)}) collective-permute-start(bf16[30,512]{1,0:T(8,128)(2,1)} %own.1), channel_id=1, source_target_pairs={{0,4},{4,0},{8,12},{12,8},{16,20},{20,16},{24,28},{28,24},{1,5},{5... | collective-permute-start | bytes 92168 | tf_op jit(solution)/shard_map/ppermute | solution.py:560
  3.0 3.8 %collective-permute-start.4 = (bf16[4,12,32,128]{3,2,1,0:T(8,128)(2,1)S(1)}, bf16[4,12,32,128]{3,2,1,0:T(8,128)(2,1)S(1)}, u32[]{:S(2)}, u32[]{:S(2)}) collective-permute-start(bf16[4,12,32,128]{3,2,1,0:T(8,128)(2,1)S(1)} %get-tuple-element.32), channel_id=1, source_target_pairs={{0,4},{4,0},{8,12},{12,8},{16,20},{20,16},{24,28},{28,24},{1,5},{5... | collective-permute-start | bytes 1179656 | tf_op jit(solution)/shard_map/ppermute | solution.py:560
  3.1 7.5 %collective-permute-start.2 = (bf16[2,30,512]{2,1,0:T(8,128)(2,1)S(1)}, bf16[2,30,512]{2,1,0:T(8,128)(2,1)S(1)}, u32[]{:S(2)}, u32[]{:S(2)}) collective-permute-start(bf16[2,30,512]{2,1,0:T(8,128)(2,1)S(1)} %pair_waves.1.pair), channel_id=1, source_target_pairs={{0,24},{4,20},{8,16},{12,28},{16,8},{20,4},{24,0},{28,12},{1,25},{... | collective-permute-start | bytes 184328 | tf_op jit(solution)/shard_map/ppermute | solution.py:581
  5.5 5.1 %collective-permute-start.1 = (bf16[30,512]{1,0:T(8,128)(2,1)S(1)}, bf16[30,512]{1,0:T(8,128)(2,1)S(1)}, u32[]{:S(2)}, u32[]{:S(2)}) collective-permute-start(bf16[30,512]{1,0:T(8,128)(2,1)S(1)} %copy-done), channel_id=1, source_target_pairs={{0,8},{4,12},{8,0},{12,4},{16,24},{20,28},{24,16},{28,20},{1,9},{5... | collective-permute-start | bytes 92168 | tf_op jit(solution)/shard_map/ppermute | solution.py:563
  7.0 8.8 %collective-permute-start.5 = (bf16[12,32,128]{2,1,0:T(8,128)(2,1)S(1)}, bf16[12,32,128]{2,1,0:T(8,128)(2,1)S(1)}, u32[]{:S(2)}, u32[]{:S(2)}) collective-permute-start(bf16[12,32,128]{2,1,0:T(8,128)(2,1)S(1)} %get-tuple-element.33), channel_id=1, source_target_pairs={{0,24},{4,28},{8,16},{12,20},{16,8},{20,12},{24,0},{28,4},{1,25},{... | collective-permute-start | bytes 294920 | tf_op jit(solution)/shard_map/ppermute | solution.py:563
  8.4 9.2 %collective-permute-start.6 = (bf16[12,32,128]{2,1,0:T(8,128)(2,1)S(1)}, bf16[12,32,128]{2,1,0:T(8,128)(2,1)S(1)}, u32[]{:S(2)}, u32[]{:S(2)}) collective-permute-start(bf16[12,32,128]{2,1,0:T(8,128)(2,1)S(1)} %get-tuple-element.34), channel_id=1, source_target_pairs={{0,16},{4,20},{8,24},{12,28},{16,0},{20,4},{24,8},{28,12},{1,17},{... | collective-permute-start | bytes 294920 | tf_op jit(solution)/shard_map/ppermute | solution.py:563
  8.4 9.2 %collective-permute-start.7 = (bf16[12,32,128]{2,1,0:T(8,128)(2,1)S(1)}, bf16[12,32,128]{2,1,0:T(8,128)(2,1)S(1)}, u32[]{:S(2)}, u32[]{:S(2)}) collective-permute-start(bf16[12,32,128]{2,1,0:T(8,128)(2,1)S(1)} %get-tuple-element.35), channel_id=1, source_target_pairs={{0,8},{4,12},{8,0},{12,4},{16,24},{20,28},{24,16},{28,20},{1,9},{5... | collective-permute-start | bytes 294920 | tf_op jit(solution)/shard_map/ppermute | solution.py:563
  10.7 2.3 %collective-permute-start.3 = (bf16[3,30,512]{2,1,0:T(8,128)(2,1)S(1)}, bf16[3,30,512]{2,1,0:T(8,128)(2,1)S(1)}, u32[]{:S(2)}, u32[]{:S(2)}) collective-permute-start(bf16[3,30,512]{2,1,0:T(8,128)(2,1)S(1)} %choose_waves.1), channel_id=1, source_target_pairs={{0,4},{4,0},{8,12},{12,8},{16,20},{20,16},{24,28},{28,24},{1,5},{5... | collective-permute-start | bytes 276488 | tf_op jit(solution)/shard_map/ppermute | solution.py:560
  17.7 4.3 %collective-permute-start.8 = (bf16[12,32,128]{2,1,0:T(8,128)(2,1)S(1)}, bf16[12,32,128]{2,1,0:T(8,128)(2,1)S(1)}, u32[]{:S(2)}, u32[]{:S(2)}) collective-permute-start(bf16[12,32,128]{2,1,0:T(8,128)(2,1)S(1)} %choose_piece.1.piece), channel_id=1, source_target_pairs={{0,4},{4,0},{8,12},{12,8},{16,20},{20,16},{24,28},{28,24},{1,5},{5... | collective-permute-start | bytes 294920 | tf_op jit(solution)/shard_map/ppermute | solution.py:560
  24.6 8.6 %collective-permute-start.9 = (bf16[128,256]{1,0:T(8,128)(2,1)S(1)}, bf16[128,256]{1,0:T(8,128)(2,1)S(1)}, u32[]{:S(2)}, u32[]{:S(2)}) collective-permute-start(bf16[128,256]{1,0:T(8,128)(2,1)S(1)} %get-tuple-element.43), channel_id=1, source_target_pairs={{0,0},{1,8},{2,4},{3,12},{4,16},{5,24},{6,20},{7,28},{8,1},{9,9},{... | collective-permute-start | bytes 196616 | tf_op jit(solution)/shard_map/ppermute | solution.py:602
  28.7 5.5 %collective-permute-start.10 = (bf16[128,256]{1,0:T(8,128)(2,1)S(1)}, bf16[128,256]{1,0:T(8,128)(2,1)S(1)}, u32[]{:S(2)}, u32[]{:S(2)}) collective-permute-start(bf16[128,256]{1,0:T(8,128)(2,1)S(1)} %get-tuple-element.44), channel_id=1, source_target_pairs={{0,8},{1,0},{2,12},{3,4},{4,24},{5,16},{6,28},{7,20},{8,9},{9,1},{... | collective-permute-start | bytes 196616 | tf_op jit(solution)/shard_map/ppermute | solution.py:602
  34.3 1.3 %collective-permute-start.11 = (f32[64,256]{1,0:T(8,128)S(1)}, f32[64,256]{1,0:T(8,128)S(1)}, u32[]{:S(2)}, u32[]{:S(2)}) collective-permute-start(f32[64,256]{1,0:T(8,128)S(1)} %get-tuple-element.46), channel_id=1, source_target_pairs={{0,4},{4,0},{8,12},{12,8},{16,20},{20,16},{24,28},{28,24},{1,5},{5... | collective-permute-start | bytes 196616 | tf_op jit(solution)/shard_map/ppermute | solution.py:560

commit v17 on v16

--- a/solution.py
+++ b/solution.py
@@ -233,8 +233,8 @@
 
 
 def waves_kernel(channels, tlen, unroll, swapped, pair, beside, *rest):
-    far = rest[:-4]
-    left_a, left_r, padded, inverse = rest[-4:]
+    far = rest[:-3]
+    left_a, inverse, padded = rest[-3:]
     samples = beside.shape[1]
     near = swapped.shape[0] - 1
     length = 2 * near * samples
@@ -270,8 +270,13 @@
     second_sum = windows(high) + windows(low)
     variance = (second_sum * tlen - first_sum * first_sum) * (1.0 / tlen**2)
     scale = lax.rsqrt(variance + EPSILON)
-    for tile in range(count):
-        inverse[:, LANES * tile : LANES * (tile + 1)] = scale[32 * tile : 32 * (tile + 1)]
+    for tile in range(length // LANES):
+        part = scale[32 * tile : 32 * (tile + 1)]
+        after = scale[32 * (tile + 1) : 32 * (tile + 2)]
+        inverse[2 * tile] = part
+        lane = lax.broadcasted_iota(jnp.int32, part.shape, 1)
+        both = jnp.where(lane < STRIDE, after, part)
+        inverse[2 * tile + 1] = pltpu.roll(both, LANES - STRIDE, 1)
 
     def interleaved(row, tiles):
         even, odd = lagged(row, 0), lagged(row, STRIDE)
@@ -287,10 +292,6 @@
             channel = step * unroll + item
             value = interleaved(padded[pl.ds(channel, 1), :], length // LANES + 1)
             left_a[channel] = value.astype(jnp.bfloat16)
-            value = interleaved(inverse[pl.ds(channel, 1), :], length // LANES)
-            high = value.astype(jnp.bfloat16)
-            left_r[channel, :, 0:LANES] = high
-            left_r[channel, :, LANES:] = (value - high.astype(jnp.float32)).astype(jnp.bfloat16)
 
 
 def prepare_waves(tlen, swapped, pair, beside, far):
@@ -302,13 +303,12 @@
         functools.partial(waves_kernel, channels, tlen, unroll),
         out_shape=[
             jax.ShapeDtypeStruct((channels, rows + 16, LANES), jnp.bfloat16),
-            jax.ShapeDtypeStruct((channels, rows, 2 * LANES), jnp.bfloat16),
+            jax.ShapeDtypeStruct((length // STRIDE, 32, LANES), jnp.float32),
         ],
         in_specs=[VMEM] * (3 + len(far)),
         out_specs=[VMEM, VMEM],
         scratch_shapes=[
             pltpu.VMEM((32, length + 2 * LANES), jnp.float32),
-            pltpu.VMEM((32, length + 2 * LANES), jnp.float32),
         ],
         compiler_params=params(),
         cost_estimate=cost(0.05),
@@ -316,13 +316,14 @@
     )(swapped, pair, beside, *far)
 
 
-def main_kernel(side, tlen, group, piece, left_a, left_r, *rest):
+def main_kernel(side, tlen, group, piece, left_a, inverse, *rest):
     outs = rest[:-5]
     if side:
         before, outs = outs[0], outs[1:]
-    bank, expand, weight_a, weight_r, total = rest[-5:]
+    bank, expand, weight_a, reach, total = rest[-5:]
     core = lax.axis_index("tm") % 2
-    channels, rows, _ = left_r.shape
+    channels = left_a.shape[0]
+    rows = left_a.shape[1] - 16
     half = channels // 2
     base = half * jnp.where(core == side, 0, 1)
     slots = LANES // group
@@ -396,7 +397,6 @@
         for slot in range(slots):
             spreaded = wide[:, slot * LANES : (slot + 1) * LANES]
             code = spreaded[112:113, :].astype(jnp.int32)
-            usable = code > 0
             shift = code - 1
             moves = shift // 8 + ahead
             taps = spreaded[0:112, :]
@@ -409,30 +409,32 @@
                 )[0:top]
             taps = taps.astype(jnp.bfloat16)
             item = number * slots + slot
-            pick = jnp.logical_and(lag == shift + 8 * ahead, usable)
-            pick = jnp.where(pick, 1.0, 0.0).astype(jnp.bfloat16)
-            for index in range(tile_count):
-                skip = 8 * offset_count * index
-                lanes = slice(LANES * index, LANES * (index + 1))
+            reach[item] = jnp.maximum(shift, 0) + 8 * ahead + 7 - lag[0:8]
+            for tile in range(tile_count):
+                skip = 8 * offset_count * tile
+                lanes = slice(LANES * tile, LANES * (tile + 1))
                 if skip:
                     weight_a[item, 0:skip, lanes] = jnp.zeros((skip, LANES), jnp.bfloat16)
-                    pick = jnp.concatenate(
-                        [jnp.zeros((skip, LANES), jnp.bfloat16), pick[0 : LANES - skip]], axis=0
-                    )
                 weight_a[item, skip : skip + top, lanes] = taps
                 rest = DEPTH - top - skip
                 if rest:
                     weight_a[item, skip + top :, lanes] = jnp.zeros((rest, LANES), jnp.bfloat16)
-                weight_r[item, 0:LANES, lanes] = pick
-                weight_r[item, LANES : 2 * LANES, lanes] = pick
 
     def products(item):
         both = [left_a[base + item, 0:rows, :], left_a[base + item, 16 : rows + 16, :]]
         corr = jnp.dot(
             jnp.concatenate(both, axis=1), weight_a[item], preferred_element_type=jnp.float32
         )
-        factor = jnp.dot(left_r[base + item], weight_r[item], preferred_element_type=jnp.float32)
-        return corr * factor
+        columns = []
+        for tile in range(tile_count):
+            place = reach[item] + 8 * offset_count * tile
+            parts = []
+            for step in range(rows // 8):
+                window = inverse[step, pl.ds(base + item, 1), :]
+                window = jnp.broadcast_to(window, (8, LANES))
+                parts.append(jnp.take_along_axis(window, place, axis=1, mode="promise_in_bounds"))
+            columns.append(jnp.concatenate(parts, axis=0))
+        return corr * jnp.concatenate(columns, axis=1)
 
     def apply(number, count):
         for item in range(number * slots, number * slots + count, 2):
@@ -465,8 +467,9 @@
         )
 
 
-def correlate(side, tlen, group, count, piece, left_a, left_r, *before):
-    channels, rows, _ = left_r.shape
+def correlate(side, tlen, group, count, piece, left_a, inverse, *before):
+    channels = left_a.shape[0]
+    rows = left_a.shape[1] - 16
     width = OFFSETS * group
     half = channels // 2
     if side:
@@ -482,13 +485,13 @@
             pltpu.VMEM(((half + 1) * group // LANES, LANES, LANES), jnp.bfloat16),
             pltpu.VMEM((LANES, LANES // group * LANES), jnp.bfloat16),
             pltpu.VMEM((half + 1, DEPTH, width), jnp.bfloat16),
-            pltpu.VMEM((half + 1, DEPTH, width), jnp.bfloat16),
+            pltpu.VMEM((half + 1, 8, LANES), jnp.int32),
             pltpu.VMEM((rows, width), jnp.float32),
         ],
         compiler_params=params(),
         cost_estimate=cost(3),
         name="correlate_" + ("second" if side else "first"),
-    )(piece, left_a, left_r, *before)
+    )(piece, left_a, inverse, *before)
 
 
 def add_kernel(*refs):
@@ -584,14 +587,14 @@
     pieces = [across(merged[step], step) for step in reversed(range(1, chips))]
     pieces = [merged[0]] + pieces[::-1]
     swapped = swap(choose_waves(pair, beside, far))
-    left_a, left_r = prepare_waves(tlen, swapped, pair, beside, far)
-
-    left_a, left_r, *pieces = lax.optimization_barrier((left_a, left_r, *pieces[::-1]))
+    left_a, inverse = prepare_waves(tlen, swapped, pair, beside, far)
+
+    left_a, inverse, *pieces = lax.optimization_barrier((left_a, inverse, *pieces[::-1]))
     pieces = pieces[::-1]
     first = choose_piece(owners, pieces)
     second = swap(first)
-    total = correlate(0, tlen, group, near, first, left_a, left_r)
-    parts = correlate(1, tlen, group, near, second, left_a, left_r, *total)
+    total = correlate(0, tlen, group, near, first, left_a, inverse)
+    parts = correlate(1, tlen, group, near, second, left_a, inverse, *total)
     gathered = []
     for step in range(near):
         route = []

time: 36.9 us -> 36 us (0.976)
  Pallas kernels: 11.5 us -> 9.46 us
  waiting for transfers between devices: 9.19 us -> 10.3 us
    ppermute x4, waiting for transfers between devices: 1.74 us -> 2.81 us  [across(): lax.ppermute(array, 'tm', [(i, i ^ 2 * step) for i in range(count_tm)])]
    pallas_call x1, Pallas kernels: 2.86 us -> 1.78 us  [prepare_waves(): pl.pallas_call(functools.partial(waves_kernel, channels, tlen, unroll), o...]
    pallas_call x2, Pallas kernels: 5.05 us -> 4.11 us  [correlate(): pl.pallas_call(functools.partial(main_kernel, side, tlen, group), out_sha...]
  transfers between devices with their start and end apart: 12 -> 12, of which waited for: 5 -> 5; matrix products, arithmetic and copies ran while one was open for 0% -> 0% of each run, Pallas kernels for 22% -> 18%
where the time goes in v17:
time: 36 us; the launch traced here: 35.5 us
  starting transfers between devices  15.7 us (44%)
  waiting for transfers between devices  10.3 us (29%)
  Pallas kernels  9.46 us (26%)
    ppermute x2, waiting for transfers between devices, shards(): gathered.append(lax.ppermute(parts[step], ('tm', 'sta'), route))  5.47 us
    ppermute x4, starting transfers between devices, across(): lax.ppermute(array, 'tm', [(i, i ^ 2 * step) for i in range(count_tm)])  4.91 us
    ppermute x5, starting transfers between devices, swap(): return lax.ppermute(array, 'tm', [(i, i ^ 1) for i in range(count_tm)])  4.25 us
    ppermute x2, starting transfers between devices, shards(): gathered.append(lax.ppermute(parts[step], ('tm', 'sta'), route))  4.16 us
    pallas_call x2, Pallas kernels, correlate(): pl.pallas_call(functools.partial(main_kernel, side, tlen, group), out_sha...  4.11 us
    ppermute x4, waiting for transfers between devices, across(): lax.ppermute(array, 'tm', [(i, i ^ 2 * step) for i in range(count_tm)])  2.81 us
    ppermute x1, starting transfers between devices, shards(): far.append(lax.ppermute(pair, 'tm', route))  2.37 us
    pallas_call x1, Pallas kernels, pack(): pl.pallas_call(pack_kernel, out_shape=[jax.ShapeDtypeStruct(shape, jnp.bf...  2.31 us
  transfers between devices with their start and end apart: 12, of which 5 were waited for; matrix products, arithmetic and copies ran while one was open for 0% of the time, Pallas kernels for 18%

profile of v17, /device:TPU:7, one launch (start us, length us, event | category | flops | bytes accessed | tf_op | source)
XLA Modules:
  0.0 35.5 jit_solution(9556834593459001608)
XLA Ops:
  0.0 0.7 %collective-permute-start = (bf16[30,512]{1,0:T(8,128)(2,1)}, bf16[30,512]{1,0:T(8,128)(2,1)S(1)}, u32[]{:S(2)}, u32[]{:S(2)}) collective-permute-start(bf16[30,512]{1,0:T(8,128)(2,1)} %own.1), channel_id=1, source_target_pairs={{0,4},{4,0},{8,12},{12,8},{16,20},{20,16},{24,28},{28,24},{1,5},{5... | collective-permute-start | bytes 92168 | tf_op jit(solution)/shard_map/ppermute | solution.py:563
  0.7 0.0 copy-start
  0.7 2.3 %pack.1 = (bf16[4,12,32,128]{3,2,1,0:T(8,128)(2,1)S(1)}, bf16[4,12,32,128]{3,2,1,0:T(8,128)(2,1)S(1)}, s32[8,128]{1,0:T(8,128)S(1)}) custom-call(s32[2]{0:T(128)} %bank_blocks.1, bf16[2,30,64,100]{3,2,1,0:T(8,128)(2,1)} %bitcast.3, s32[30,2,64]{2,1,0:T(2,128)} %bitcast.4, s32[30,2,64]{2,1,0:T(2,128)} %bitcast.5), custom_call_target="tpu_custom_call" | custom-call | flops 2000000000 | bytes 2000000 | tf_op jit(solution)/shard_map/pack/pallas_call | solution.py:100
  3.0 0.0 collective-permute-done.partner
  3.0 0.1 collective-permute-start.4
  3.1 0.0 copy-done
  3.1 2.4 %collective-permute-start.2 = (bf16[2,30,512]{2,1,0:T(8,128)(2,1)S(1)}, bf16[2,30,512]{2,1,0:T(8,128)(2,1)S(1)}, u32[]{:S(2)}, u32[]{:S(2)}) collective-permute-start(bf16[2,30,512]{2,1,0:T(8,128)(2,1)S(1)} %pair_waves.1.pair), channel_id=1, source_target_pairs={{0,24},{4,20},{8,16},{12,28},{16,8},{20,4},{24,0},{28,12},{1,25},{... | collective-permute-start | bytes 184328 | tf_op jit(solution)/shard_map/ppermute | solution.py:584
  5.5 1.3 %collective-permute-start.1 = (bf16[30,512]{1,0:T(8,128)(2,1)S(1)}, bf16[30,512]{1,0:T(8,128)(2,1)S(1)}, u32[]{:S(2)}, u32[]{:S(2)}) collective-permute-start(bf16[30,512]{1,0:T(8,128)(2,1)S(1)} %copy-done), channel_id=1, source_target_pairs={{0,8},{4,12},{8,0},{12,4},{16,24},{20,28},{24,16},{28,20},{1,9},{5... | collective-permute-start | bytes 92168 | tf_op jit(solution)/shard_map/ppermute | solution.py:566
  6.8 0.0 collective-permute-done.4.other
  6.8 0.2 merge.1
  7.0 1.4 %collective-permute-start.5 = (bf16[12,32,128]{2,1,0:T(8,128)(2,1)S(1)}, bf16[12,32,128]{2,1,0:T(8,128)(2,1)S(1)}, u32[]{:S(2)}, u32[]{:S(2)}) collective-permute-start(bf16[12,32,128]{2,1,0:T(8,128)(2,1)S(1)} %get-tuple-element.33), channel_id=1, source_target_pairs={{0,24},{4,28},{8,16},{12,20},{16,8},{20,12},{24,0},{28,4},{1,25},{... | collective-permute-start | bytes 294920 | tf_op jit(solution)/shard_map/ppermute | solution.py:566
  8.4 0.0 collective-permute-start.6
  8.4 2.2 %collective-permute-start.7 = (bf16[12,32,128]{2,1,0:T(8,128)(2,1)S(1)}, bf16[12,32,128]{2,1,0:T(8,128)(2,1)S(1)}, u32[]{:S(2)}, u32[]{:S(2)}) collective-permute-start(bf16[12,32,128]{2,1,0:T(8,128)(2,1)S(1)} %get-tuple-element.35), channel_id=1, source_target_pairs={{0,8},{4,12},{8,0},{12,4},{16,24},{20,28},{24,16},{28,20},{1,9},{5... | collective-permute-start | bytes 294920 | tf_op jit(solution)/shard_map/ppermute | solution.py:566
  10.6 0.0 collective-permute-done.1.beside
  10.6 0.0 collective-permute-done.2.rest_0_
  10.7 1.4 %collective-permute-start.3 = (bf16[3,30,512]{2,1,0:T(8,128)(2,1)S(1)}, bf16[3,30,512]{2,1,0:T(8,128)(2,1)S(1)}, u32[]{:S(2)}, u32[]{:S(2)}) collective-permute-start(bf16[3,30,512]{2,1,0:T(8,128)(2,1)S(1)} %choose_waves.1), channel_id=1, source_target_pairs={{0,4},{4,0},{8,12},{12,8},{16,20},{20,16},{24,28},{28,24},{1,5},{5... | collective-permute-start | bytes 276488 | tf_op jit(solution)/shard_map/ppermute | solution.py:563
  12.1 0.9 %collective-permute-done.3.swapped = bf16[3,30,512]{2,1,0:T(8,128)(2,1)S(1)} collective-permute-done((bf16[3,30,512]{2,1,0:T(8,128)(2,1)S(1)}, bf16[3,30,512]{2,1,0:T(8,128)(2,1)S(1)}, u32[]{:S(2)}, u32[]{:S(2)}) %collective-permute-start.3) | collective-permute-done | bytes 92192 | tf_op jit(solution)/shard_map/ppermute | solution.py:563
  13.0 1.8 %prepare_waves.1 = (bf16[30,272,128]{2,1,0:T(8,128)(2,1)S(1)}, f32[32,32,128]{2,1,0:T(8,128)S(1)}) custom-call(bf16[3,30,512]{2,1,0:T(8,128)(2,1)S(1)} %collective-permute-done.3.swapped, bf16[2,30,512]{2,1,0:T(8,128)(2,1)S(1)} %pair_waves.1.pair, bf16[30,512]{1,0:T(8,128)(2,1)S(1)} %collective-permute-done.1.beside, ...), custom_call_target="tpu_custom_call" | custom-call | flops 50000000 | bytes 50000 | tf_op jit(solution)/shard_map/prepare_waves/pallas_call | solution.py:302
  14.8 0.0 collective-permute-done.5.refs_3_
  14.8 2.8 %collective-permute-done.6.refs_2_ = bf16[12,32,128]{2,1,0:T(8,128)(2,1)S(1)} collective-permute-done((bf16[12,32,128]{2,1,0:T(8,128)(2,1)S(1)}, bf16[12,32,128]{2,1,0:T(8,128)(2,1)S(1)}, u32[]{:S(2)}, u32[]{:S(2)}) %collective-permute-start.6) | collective-permute-done | bytes 98336 | tf_op jit(solution)/shard_map/ppermute | solution.py:566
  17.6 0.0 collective-permute-done.7.refs_1_
  17.6 0.1 choose_piece.1.piece
  17.7 1.8 %collective-permute-start.8 = (bf16[12,32,128]{2,1,0:T(8,128)(2,1)S(1)}, bf16[12,32,128]{2,1,0:T(8,128)(2,1)S(1)}, u32[]{:S(2)}, u32[]{:S(2)}) collective-permute-start(bf16[12,32,128]{2,1,0:T(8,128)(2,1)S(1)} %choose_piece.1.piece), channel_id=1, source_target_pairs={{0,4},{4,0},{8,12},{12,8},{16,20},{20,16},{24,28},{28,24},{1,5},{5... | collective-permute-start | bytes 294920 | tf_op jit(solution)/shard_map/ppermute | solution.py:563
  19.5 2.0 %correlate_first.1.rest_0_ = f32[256,256]{1,0:T(8,128)S(1)} custom-call(bf16[12,32,128]{2,1,0:T(8,128)(2,1)S(1)} %choose_piece.1.piece, bf16[30,272,128]{2,1,0:T(8,128)(2,1)S(1)} %get-tuple-element.41.left_a, f32[32,32,128]{2,1,0:T(8,128)S(1)} %get-tuple-element.42.inverse), custom_call_target="tpu_custom_call" | custom-call | flops 3000000000 | bytes 3000000 | tf_op jit(solution)/shard_map/correlate_first/pallas_call | solution.py:479
  21.6 0.0 collective-permute-done.8.piece
  21.6 2.1 %correlate_second.1 = (bf16[128,256]{1,0:T(8,128)(2,1)S(1)}, bf16[128,256]{1,0:T(8,128)(2,1)S(1)}) custom-call(bf16[12,32,128]{2,1,0:T(8,128)(2,1)S(1)} %collective-permute-done.8.piece, bf16[30,272,128]{2,1,0:T(8,128)(2,1)S(1)} %get-tuple-element.41.left_a, f32[32,32,128]{2,1,0:T(8,128)S(1)} %get-tuple-element.42.inverse, f32[256,256]{1,0:T(8,128)S(1)} %correlate_first.1.rest_0_), custom_call_target="tpu_custom_call" | custom-call | flops 3000000000 | bytes 3000000 | tf_op jit(solution)/shard_map/correlate_second/pallas_call | solution.py:479
  23.7 4.1 %collective-permute-start.9 = (bf16[128,256]{1,0:T(8,128)(2,1)S(1)}, bf16[128,256]{1,0:T(8,128)(2,1)S(1)}, u32[]{:S(2)}, u32[]{:S(2)}) collective-permute-start(bf16[128,256]{1,0:T(8,128)(2,1)S(1)} %get-tuple-element.43), channel_id=1, source_target_pairs={{0,0},{1,8},{2,4},{3,12},{4,16},{5,24},{6,20},{7,28},{8,1},{9,9},{... | collective-permute-start | bytes 196616 | tf_op jit(solution)/shard_map/ppermute | solution.py:605
  27.8 0.1 collective-permute-start.10
  27.8 4.4 %collective-permute-done.9.refs_0_ = bf16[128,256]{1,0:T(8,128)(2,1)S(1)} collective-permute-done((bf16[128,256]{1,0:T(8,128)(2,1)S(1)}, bf16[128,256]{1,0:T(8,128)(2,1)S(1)}, u32[]{:S(2)}, u32[]{:S(2)}) %collective-permute-start.9) | collective-permute-done | bytes 65568 | tf_op jit(solution)/shard_map/ppermute | solution.py:605
  32.2 1.1 %collective-permute-done.10.refs_1_ = bf16[128,256]{1,0:T(8,128)(2,1)S(1)} collective-permute-done((bf16[128,256]{1,0:T(8,128)(2,1)S(1)}, bf16[128,256]{1,0:T(8,128)(2,1)S(1)}, u32[]{:S(2)}, u32[]{:S(2)}) %collective-permute-start.10) | collective-permute-done | bytes 65568 | tf_op jit(solution)/shard_map/ppermute | solution.py:605
  33.3 0.3 collective-permute-start.11
  33.6 1.0 %collective-permute-done.11.received = f32[64,256]{1,0:T(8,128)S(1)} collective-permute-done((f32[64,256]{1,0:T(8,128)S(1)}, f32[64,256]{1,0:T(8,128)S(1)}, u32[]{:S(2)}, u32[]{:S(2)}) %collective-permute-start.11) | collective-permute-done | bytes 65568 | tf_op jit(solution)/shard_map/ppermute | solution.py:563
  34.6 0.9 %finish.1 = f32[32,512]{1,0:T(8,128)} custom-call(f32[64,256]{1,0:T(8,128)S(1)} %get-tuple-element.45.ours, f32[64,256]{1,0:T(8,128)S(1)} %collective-permute-done.11.received), custom_call_target="tpu_custom_call" | custom-call | flops 1000000000 | bytes 1000000 | tf_op jit(solution)/shard_map/finish/pallas_call | solution.py:542
  (3 shorter events, 0.1 us)
Async XLA Ops:
  0.0 3.0 %collective-permute-start = (bf16[30,512]{1,0:T(8,128)(2,1)}, bf16[30,512]{1,0:T(8,128)(2,1)S(1)}, u32[]{:S(2)}, u32[]{:S(2)}) collective-permute-start(bf16[30,512]{1,0:T(8,128)(2,1)} %own.1), channel_id=1, source_target_pairs={{0,4},{4,0},{8,12},{12,8},{16,20},{20,16},{24,28},{28,24},{1,5},{5... | collective-permute-start | bytes 92168 | tf_op jit(solution)/shard_map/ppermute | solution.py:563
  0.7 2.4 %copy-start = (bf16[30,512]{1,0:T(8,128)(2,1)S(1)}, bf16[30,512]{1,0:T(8,128)(2,1)}, u32[]{:S(2)}) copy-start(bf16[30,512]{1,0:T(8,128)(2,1)} %own.1) | copy-start | bytes 92164
  3.0 3.8 %collective-permute-start.4 = (bf16[4,12,32,128]{3,2,1,0:T(8,128)(2,1)S(1)}, bf16[4,12,32,128]{3,2,1,0:T(8,128)(2,1)S(1)}, u32[]{:S(2)}, u32[]{:S(2)}) collective-permute-start(bf16[4,12,32,128]{3,2,1,0:T(8,128)(2,1)S(1)} %get-tuple-element.32), channel_id=1, source_target_pairs={{0,4},{4,0},{8,12},{12,8},{16,20},{20,16},{24,28},{28,24},{1,5},{5... | collective-permute-start | bytes 1179656 | tf_op jit(solution)/shard_map/ppermute | solution.py:563
  3.1 7.5 %collective-permute-start.2 = (bf16[2,30,512]{2,1,0:T(8,128)(2,1)S(1)}, bf16[2,30,512]{2,1,0:T(8,128)(2,1)S(1)}, u32[]{:S(2)}, u32[]{:S(2)}) collective-permute-start(bf16[2,30,512]{2,1,0:T(8,128)(2,1)S(1)} %pair_waves.1.pair), channel_id=1, source_target_pairs={{0,24},{4,20},{8,16},{12,28},{16,8},{20,4},{24,0},{28,12},{1,25},{... | collective-permute-start | bytes 184328 | tf_op jit(solution)/shard_map/ppermute | solution.py:584
  5.5 5.1 %collective-permute-start.1 = (bf16[30,512]{1,0:T(8,128)(2,1)S(1)}, bf16[30,512]{1,0:T(8,128)(2,1)S(1)}, u32[]{:S(2)}, u32[]{:S(2)}) collective-permute-start(bf16[30,512]{1,0:T(8,128)(2,1)S(1)} %copy-done), channel_id=1, source_target_pairs={{0,8},{4,12},{8,0},{12,4},{16,24},{20,28},{24,16},{28,20},{1,9},{5... | collective-permute-start | bytes 92168 | tf_op jit(solution)/shard_map/ppermute | solution.py:566
  7.0 7.8 %collective-permute-start.5 = (bf16[12,32,128]{2,1,0:T(8,128)(2,1)S(1)}, bf16[12,32,128]{2,1,0:T(8,128)(2,1)S(1)}, u32[]{:S(2)}, u32[]{:S(2)}) collective-permute-start(bf16[12,32,128]{2,1,0:T(8,128)(2,1)S(1)} %get-tuple-element.33), channel_id=1, source_target_pairs={{0,24},{4,28},{8,16},{12,20},{16,8},{20,12},{24,0},{28,4},{1,25},{... | collective-permute-start | bytes 294920 | tf_op jit(solution)/shard_map/ppermute | solution.py:566
  8.4 9.2 %collective-permute-start.6 = (bf16[12,32,128]{2,1,0:T(8,128)(2,1)S(1)}, bf16[12,32,128]{2,1,0:T(8,128)(2,1)S(1)}, u32[]{:S(2)}, u32[]{:S(2)}) collective-permute-start(bf16[12,32,128]{2,1,0:T(8,128)(2,1)S(1)} %get-tuple-element.34), channel_id=1, source_target_pairs={{0,16},{4,20},{8,24},{12,28},{16,0},{20,4},{24,8},{28,12},{1,17},{... | collective-permute-start | bytes 294920 | tf_op jit(solution)/shard_map/ppermute | solution.py:566
  8.4 9.2 %collective-permute-start.7 = (bf16[12,32,128]{2,1,0:T(8,128)(2,1)S(1)}, bf16[12,32,128]{2,1,0:T(8,128)(2,1)S(1)}, u32[]{:S(2)}, u32[]{:S(2)}) collective-permute-start(bf16[12,32,128]{2,1,0:T(8,128)(2,1)S(1)} %get-tuple-element.35), channel_id=1, source_target_pairs={{0,8},{4,12},{8,0},{12,4},{16,24},{20,28},{24,16},{28,20},{1,9},{5... | collective-permute-start | bytes 294920 | tf_op jit(solution)/shard_map/ppermute | solution.py:566
  10.7 2.3 %collective-permute-start.3 = (bf16[3,30,512]{2,1,0:T(8,128)(2,1)S(1)}, bf16[3,30,512]{2,1,0:T(8,128)(2,1)S(1)}, u32[]{:S(2)}, u32[]{:S(2)}) collective-permute-start(bf16[3,30,512]{2,1,0:T(8,128)(2,1)S(1)} %choose_waves.1), channel_id=1, source_target_pairs={{0,4},{4,0},{8,12},{12,8},{16,20},{20,16},{24,28},{28,24},{1,5},{5... | collective-permute-start | bytes 276488 | tf_op jit(solution)/shard_map/ppermute | solution.py:563
  17.7 3.9 %collective-permute-start.8 = (bf16[12,32,128]{2,1,0:T(8,128)(2,1)S(1)}, bf16[12,32,128]{2,1,0:T(8,128)(2,1)S(1)}, u32[]{:S(2)}, u32[]{:S(2)}) collective-permute-start(bf16[12,32,128]{2,1,0:T(8,128)(2,1)S(1)} %choose_piece.1.piece), channel_id=1, source_target_pairs={{0,4},{4,0},{8,12},{12,8},{16,20},{20,16},{24,28},{28,24},{1,5},{5... | collective-permute-start | bytes 294920 | tf_op jit(solution)/shard_map/ppermute | solution.py:563
  23.7 8.6 %collective-permute-start.9 = (bf16[128,256]{1,0:T(8,128)(2,1)S(1)}, bf16[128,256]{1,0:T(8,128)(2,1)S(1)}, u32[]{:S(2)}, u32[]{:S(2)}) collective-permute-start(bf16[128,256]{1,0:T(8,128)(2,1)S(1)} %get-tuple-element.43), channel_id=1, source_target_pairs={{0,0},{1,8},{2,4},{3,12},{4,16},{5,24},{6,20},{7,28},{8,1},{9,9},{... | collective-permute-start | bytes 196616 | tf_op jit(solution)/shard_map/ppermute | solution.py:605
  27.8 5.5 %collective-permute-start.10 = (bf16[128,256]{1,0:T(8,128)(2,1)S(1)}, bf16[128,256]{1,0:T(8,128)(2,1)S(1)}, u32[]{:S(2)}, u32[]{:S(2)}) collective-permute-start(bf16[128,256]{1,0:T(8,128)(2,1)S(1)} %get-tuple-element.44), channel_id=1, source_target_pairs={{0,8},{1,0},{2,12},{3,4},{4,24},{5,16},{6,28},{7,20},{8,9},{9,1},{... | collective-permute-start | bytes 196616 | tf_op jit(solution)/shard_map/ppermute | solution.py:605
  33.3 1.3 %collective-permute-start.11 = (f32[64,256]{1,0:T(8,128)S(1)}, f32[64,256]{1,0:T(8,128)S(1)}, u32[]{:S(2)}, u32[]{:S(2)}) collective-permute-start(f32[64,256]{1,0:T(8,128)S(1)} %get-tuple-element.46), channel_id=1, source_target_pairs={{0,4},{4,0},{8,12},{12,8},{16,20},{20,16},{24,28},{28,24},{1,5},{5... | collective-permute-start | bytes 196616 | tf_op jit(solution)/shard_map/ppermute | solution.py:563

commit v18 on v17

--- a/solution.py
+++ b/solution.py
@@ -54,7 +54,7 @@
     mine[...] = jnp.zeros_like(mine)
     theirs[...] = jnp.zeros_like(theirs)
     square[...] = jnp.zeros_like(square)
-    for copy in fetch[:3]:
+    for copy in fetch:
         copy.wait()
     slots = [chosen[which] % blocks for which in range(2)]
     row = lax.broadcasted_iota(jnp.int32, owners.shape, 0)
@@ -69,8 +69,6 @@
         turned = square[...].T
         later = pltpu.roll(turned, LANES - half, 1)
         codes.append([jnp.where(me == core, turned, later) for core in range(2)])
-    for copy in fetch[3:]:
-        copy.wait()
     for which in range(2):
         for side, out in enumerate((mine, theirs)):
             first = half * jnp.where(me == side, 0, 1)

time: 36 us -> 36.1 us (level)
  no operation moved by 1% of the time
where the time goes in v18:
time: 36.1 us; the launch traced here: 35.7 us
  starting transfers between devices  15.7 us (43%)
  waiting for transfers between devices  10.2 us (28%)
  Pallas kernels  9.63 us (27%)
    ppermute x2, waiting for transfers between devices, shards(): gathered.append(lax.ppermute(parts[step], ('tm', 'sta'), route))  5.47 us
    ppermute x4, starting transfers between devices, across(): lax.ppermute(array, 'tm', [(i, i ^ 2 * step) for i in range(count_tm)])  4.91 us
    ppermute x5, starting transfers between devices, swap(): return lax.ppermute(array, 'tm', [(i, i ^ 1) for i in range(count_tm)])  4.27 us
    ppermute x2, starting transfers between devices, shards(): gathered.append(lax.ppermute(parts[step], ('tm', 'sta'), route))  4.15 us
    pallas_call x2, Pallas kernels, correlate(): pl.pallas_call(functools.partial(main_kernel, side, tlen, group), out_sha...  4.11 us
    ppermute x4, waiting for transfers between devices, across(): lax.ppermute(array, 'tm', [(i, i ^ 2 * step) for i in range(count_tm)])  2.81 us
    pallas_call x1, Pallas kernels, pack(): pl.pallas_call(pack_kernel, out_shape=[jax.ShapeDtypeStruct(shape, jnp.bf...  2.47 us
    ppermute x1, starting transfers between devices, shards(): far.append(lax.ppermute(pair, 'tm', route))  2.37 us
  transfers between devices with their start and end apart: 12, of which 5 were waited for; matrix products, arithmetic and copies ran while one was open for 0% of the time, Pallas kernels for 18%

profile of v18, /device:TPU:7, one launch (start us, length us, event | category | flops | bytes accessed | tf_op | source)
XLA Modules:
  0.0 35.7 jit_solution(3571381938375043160)
XLA Ops:
  0.0 0.7 %collective-permute-start = (bf16[30,512]{1,0:T(8,128)(2,1)}, bf16[30,512]{1,0:T(8,128)(2,1)S(1)}, u32[]{:S(2)}, u32[]{:S(2)}) collective-permute-start(bf16[30,512]{1,0:T(8,128)(2,1)} %own.1), channel_id=1, source_target_pairs={{0,4},{4,0},{8,12},{12,8},{16,20},{20,16},{24,28},{28,24},{1,5},{5... | collective-permute-start | bytes 92168 | tf_op jit(solution)/shard_map/ppermute | solution.py:561
  0.7 0.0 copy-start
  0.7 2.5 %pack.1 = (bf16[4,12,32,128]{3,2,1,0:T(8,128)(2,1)S(1)}, bf16[4,12,32,128]{3,2,1,0:T(8,128)(2,1)S(1)}, s32[8,128]{1,0:T(8,128)S(1)}) custom-call(s32[2]{0:T(128)} %bank_blocks.1, bf16[2,30,64,100]{3,2,1,0:T(8,128)(2,1)} %bitcast.3, s32[30,2,64]{2,1,0:T(2,128)} %bitcast.4, s32[30,2,64]{2,1,0:T(2,128)} %bitcast.5), custom_call_target="tpu_custom_call" | custom-call | flops 2000000000 | bytes 2000000 | tf_op jit(solution)/shard_map/pack/pallas_call | solution.py:98
  3.2 0.0 collective-permute-done.partner
  3.2 0.1 collective-permute-start.4
  3.2 0.0 copy-done
  3.3 2.4 %collective-permute-start.2 = (bf16[2,30,512]{2,1,0:T(8,128)(2,1)S(1)}, bf16[2,30,512]{2,1,0:T(8,128)(2,1)S(1)}, u32[]{:S(2)}, u32[]{:S(2)}) collective-permute-start(bf16[2,30,512]{2,1,0:T(8,128)(2,1)S(1)} %pair_waves.1.pair), channel_id=1, source_target_pairs={{0,24},{4,20},{8,16},{12,28},{16,8},{20,4},{24,0},{28,12},{1,25},{... | collective-permute-start | bytes 184328 | tf_op jit(solution)/shard_map/ppermute | solution.py:582
  5.7 1.3 %collective-permute-start.1 = (bf16[30,512]{1,0:T(8,128)(2,1)S(1)}, bf16[30,512]{1,0:T(8,128)(2,1)S(1)}, u32[]{:S(2)}, u32[]{:S(2)}) collective-permute-start(bf16[30,512]{1,0:T(8,128)(2,1)S(1)} %copy-done), channel_id=1, source_target_pairs={{0,8},{4,12},{8,0},{12,4},{16,24},{20,28},{24,16},{28,20},{1,9},{5... | collective-permute-start | bytes 92168 | tf_op jit(solution)/shard_map/ppermute | solution.py:564
  7.0 0.0 collective-permute-done.4.other
  7.0 0.2 merge.1
  7.2 1.4 %collective-permute-start.5 = (bf16[12,32,128]{2,1,0:T(8,128)(2,1)S(1)}, bf16[12,32,128]{2,1,0:T(8,128)(2,1)S(1)}, u32[]{:S(2)}, u32[]{:S(2)}) collective-permute-start(bf16[12,32,128]{2,1,0:T(8,128)(2,1)S(1)} %get-tuple-element.33), channel_id=1, source_target_pairs={{0,24},{4,28},{8,16},{12,20},{16,8},{20,12},{24,0},{28,4},{1,25},{... | collective-permute-start | bytes 294920 | tf_op jit(solution)/shard_map/ppermute | solution.py:564
  8.6 0.0 collective-permute-start.6
  8.6 2.2 %collective-permute-start.7 = (bf16[12,32,128]{2,1,0:T(8,128)(2,1)S(1)}, bf16[12,32,128]{2,1,0:T(8,128)(2,1)S(1)}, u32[]{:S(2)}, u32[]{:S(2)}) collective-permute-start(bf16[12,32,128]{2,1,0:T(8,128)(2,1)S(1)} %get-tuple-element.35), channel_id=1, source_target_pairs={{0,8},{4,12},{8,0},{12,4},{16,24},{20,28},{24,16},{28,20},{1,9},{5... | collective-permute-start | bytes 294920 | tf_op jit(solution)/shard_map/ppermute | solution.py:564
  10.8 0.0 collective-permute-done.1.beside
  10.8 0.0 collective-permute-done.2.rest_0_
  10.8 1.4 %collective-permute-start.3 = (bf16[3,30,512]{2,1,0:T(8,128)(2,1)S(1)}, bf16[3,30,512]{2,1,0:T(8,128)(2,1)S(1)}, u32[]{:S(2)}, u32[]{:S(2)}) collective-permute-start(bf16[3,30,512]{2,1,0:T(8,128)(2,1)S(1)} %choose_waves.1), channel_id=1, source_target_pairs={{0,4},{4,0},{8,12},{12,8},{16,20},{20,16},{24,28},{28,24},{1,5},{5... | collective-permute-start | bytes 276488 | tf_op jit(solution)/shard_map/ppermute | solution.py:561
  12.2 0.9 %collective-permute-done.3.swapped = bf16[3,30,512]{2,1,0:T(8,128)(2,1)S(1)} collective-permute-done((bf16[3,30,512]{2,1,0:T(8,128)(2,1)S(1)}, bf16[3,30,512]{2,1,0:T(8,128)(2,1)S(1)}, u32[]{:S(2)}, u32[]{:S(2)}) %collective-permute-start.3) | collective-permute-done | bytes 92192 | tf_op jit(solution)/shard_map/ppermute | solution.py:561
  13.2 1.8 %prepare_waves.1 = (bf16[30,272,128]{2,1,0:T(8,128)(2,1)S(1)}, f32[32,32,128]{2,1,0:T(8,128)S(1)}) custom-call(bf16[3,30,512]{2,1,0:T(8,128)(2,1)S(1)} %collective-permute-done.3.swapped, bf16[2,30,512]{2,1,0:T(8,128)(2,1)S(1)} %pair_waves.1.pair, bf16[30,512]{1,0:T(8,128)(2,1)S(1)} %collective-permute-done.1.beside, ...), custom_call_target="tpu_custom_call" | custom-call | flops 50000000 | bytes 50000 | tf_op jit(solution)/shard_map/prepare_waves/pallas_call | solution.py:300
  15.0 0.0 collective-permute-done.5.refs_3_
  15.0 2.8 %collective-permute-done.6.refs_2_ = bf16[12,32,128]{2,1,0:T(8,128)(2,1)S(1)} collective-permute-done((bf16[12,32,128]{2,1,0:T(8,128)(2,1)S(1)}, bf16[12,32,128]{2,1,0:T(8,128)(2,1)S(1)}, u32[]{:S(2)}, u32[]{:S(2)}) %collective-permute-start.6) | collective-permute-done | bytes 98336 | tf_op jit(solution)/shard_map/ppermute | solution.py:564
  17.8 0.0 collective-permute-done.7.refs_1_
  17.8 0.1 choose_piece.1.piece
  17.9 1.8 %collective-permute-start.8 = (bf16[12,32,128]{2,1,0:T(8,128)(2,1)S(1)}, bf16[12,32,128]{2,1,0:T(8,128)(2,1)S(1)}, u32[]{:S(2)}, u32[]{:S(2)}) collective-permute-start(bf16[12,32,128]{2,1,0:T(8,128)(2,1)S(1)} %choose_piece.1.piece), channel_id=1, source_target_pairs={{0,4},{4,0},{8,12},{12,8},{16,20},{20,16},{24,28},{28,24},{1,5},{5... | collective-permute-start | bytes 294920 | tf_op jit(solution)/shard_map/ppermute | solution.py:561
  19.7 2.0 %correlate_first.1.rest_0_ = f32[256,256]{1,0:T(8,128)S(1)} custom-call(bf16[12,32,128]{2,1,0:T(8,128)(2,1)S(1)} %choose_piece.1.piece, bf16[30,272,128]{2,1,0:T(8,128)(2,1)S(1)} %get-tuple-element.41.left_a, f32[32,32,128]{2,1,0:T(8,128)S(1)} %get-tuple-element.42.inverse), custom_call_target="tpu_custom_call" | custom-call | flops 3000000000 | bytes 3000000 | tf_op jit(solution)/shard_map/correlate_first/pallas_call | solution.py:477
  21.7 0.0 collective-permute-done.8.piece
  21.7 2.1 %correlate_second.1 = (bf16[128,256]{1,0:T(8,128)(2,1)S(1)}, bf16[128,256]{1,0:T(8,128)(2,1)S(1)}) custom-call(bf16[12,32,128]{2,1,0:T(8,128)(2,1)S(1)} %collective-permute-done.8.piece, bf16[30,272,128]{2,1,0:T(8,128)(2,1)S(1)} %get-tuple-element.41.left_a, f32[32,32,128]{2,1,0:T(8,128)S(1)} %get-tuple-element.42.inverse, f32[256,256]{1,0:T(8,128)S(1)} %correlate_first.1.rest_0_), custom_call_target="tpu_custom_call" | custom-call | flops 3000000000 | bytes 3000000 | tf_op jit(solution)/shard_map/correlate_second/pallas_call | solution.py:477
  23.8 4.1 %collective-permute-start.9 = (bf16[128,256]{1,0:T(8,128)(2,1)S(1)}, bf16[128,256]{1,0:T(8,128)(2,1)S(1)}, u32[]{:S(2)}, u32[]{:S(2)}) collective-permute-start(bf16[128,256]{1,0:T(8,128)(2,1)S(1)} %get-tuple-element.43), channel_id=1, source_target_pairs={{0,0},{1,8},{2,4},{3,12},{4,16},{5,24},{6,20},{7,28},{8,1},{9,9},{... | collective-permute-start | bytes 196616 | tf_op jit(solution)/shard_map/ppermute | solution.py:603
  27.9 0.1 collective-permute-start.10
  28.0 4.4 %collective-permute-done.9.refs_0_ = bf16[128,256]{1,0:T(8,128)(2,1)S(1)} collective-permute-done((bf16[128,256]{1,0:T(8,128)(2,1)S(1)}, bf16[128,256]{1,0:T(8,128)(2,1)S(1)}, u32[]{:S(2)}, u32[]{:S(2)}) %collective-permute-start.9) | collective-permute-done | bytes 65568 | tf_op jit(solution)/shard_map/ppermute | solution.py:603
  32.4 1.1 %collective-permute-done.10.refs_1_ = bf16[128,256]{1,0:T(8,128)(2,1)S(1)} collective-permute-done((bf16[128,256]{1,0:T(8,128)(2,1)S(1)}, bf16[128,256]{1,0:T(8,128)(2,1)S(1)}, u32[]{:S(2)}, u32[]{:S(2)}) %collective-permute-start.10) | collective-permute-done | bytes 65568 | tf_op jit(solution)/shard_map/ppermute | solution.py:603
  33.5 0.3 collective-permute-start.11
  33.8 1.0 %collective-permute-done.11.received = f32[64,256]{1,0:T(8,128)S(1)} collective-permute-done((f32[64,256]{1,0:T(8,128)S(1)}, f32[64,256]{1,0:T(8,128)S(1)}, u32[]{:S(2)}, u32[]{:S(2)}) %collective-permute-start.11) | collective-permute-done | bytes 65568 | tf_op jit(solution)/shard_map/ppermute | solution.py:561
  34.8 0.9 %finish.1 = f32[32,512]{1,0:T(8,128)} custom-call(f32[64,256]{1,0:T(8,128)S(1)} %get-tuple-element.45.ours, f32[64,256]{1,0:T(8,128)S(1)} %collective-permute-done.11.received), custom_call_target="tpu_custom_call" | custom-call | flops 1000000000 | bytes 1000000 | tf_op jit(solution)/shard_map/finish/pallas_call | solution.py:540
  (3 shorter events, 0.1 us)
Async XLA Ops:
  0.0 3.2 %collective-permute-start = (bf16[30,512]{1,0:T(8,128)(2,1)}, bf16[30,512]{1,0:T(8,128)(2,1)S(1)}, u32[]{:S(2)}, u32[]{:S(2)}) collective-permute-start(bf16[30,512]{1,0:T(8,128)(2,1)} %own.1), channel_id=1, source_target_pairs={{0,4},{4,0},{8,12},{12,8},{16,20},{20,16},{24,28},{28,24},{1,5},{5... | collective-permute-start | bytes 92168 | tf_op jit(solution)/shard_map/ppermute | solution.py:561
  0.7 2.6 %copy-start = (bf16[30,512]{1,0:T(8,128)(2,1)S(1)}, bf16[30,512]{1,0:T(8,128)(2,1)}, u32[]{:S(2)}) copy-start(bf16[30,512]{1,0:T(8,128)(2,1)} %own.1) | copy-start | bytes 92164
  3.2 3.8 %collective-permute-start.4 = (bf16[4,12,32,128]{3,2,1,0:T(8,128)(2,1)S(1)}, bf16[4,12,32,128]{3,2,1,0:T(8,128)(2,1)S(1)}, u32[]{:S(2)}, u32[]{:S(2)}) collective-permute-start(bf16[4,12,32,128]{3,2,1,0:T(8,128)(2,1)S(1)} %get-tuple-element.32), channel_id=1, source_target_pairs={{0,4},{4,0},{8,12},{12,8},{16,20},{20,16},{24,28},{28,24},{1,5},{5... | collective-permute-start | bytes 1179656 | tf_op jit(solution)/shard_map/ppermute | solution.py:561
  3.3 7.5 %collective-permute-start.2 = (bf16[2,30,512]{2,1,0:T(8,128)(2,1)S(1)}, bf16[2,30,512]{2,1,0:T(8,128)(2,1)S(1)}, u32[]{:S(2)}, u32[]{:S(2)}) collective-permute-start(bf16[2,30,512]{2,1,0:T(8,128)(2,1)S(1)} %pair_waves.1.pair), channel_id=1, source_target_pairs={{0,24},{4,20},{8,16},{12,28},{16,8},{20,4},{24,0},{28,12},{1,25},{... | collective-permute-start | bytes 184328 | tf_op jit(solution)/shard_map/ppermute | solution.py:582
  5.7 5.1 %collective-permute-start.1 = (bf16[30,512]{1,0:T(8,128)(2,1)S(1)}, bf16[30,512]{1,0:T(8,128)(2,1)S(1)}, u32[]{:S(2)}, u32[]{:S(2)}) collective-permute-start(bf16[30,512]{1,0:T(8,128)(2,1)S(1)} %copy-done), channel_id=1, source_target_pairs={{0,8},{4,12},{8,0},{12,4},{16,24},{20,28},{24,16},{28,20},{1,9},{5... | collective-permute-start | bytes 92168 | tf_op jit(solution)/shard_map/ppermute | solution.py:564
  7.2 7.8 %collective-permute-start.5 = (bf16[12,32,128]{2,1,0:T(8,128)(2,1)S(1)}, bf16[12,32,128]{2,1,0:T(8,128)(2,1)S(1)}, u32[]{:S(2)}, u32[]{:S(2)}) collective-permute-start(bf16[12,32,128]{2,1,0:T(8,128)(2,1)S(1)} %get-tuple-element.33), channel_id=1, source_target_pairs={{0,24},{4,28},{8,16},{12,20},{16,8},{20,12},{24,0},{28,4},{1,25},{... | collective-permute-start | bytes 294920 | tf_op jit(solution)/shard_map/ppermute | solution.py:564
  8.6 9.2 %collective-permute-start.6 = (bf16[12,32,128]{2,1,0:T(8,128)(2,1)S(1)}, bf16[12,32,128]{2,1,0:T(8,128)(2,1)S(1)}, u32[]{:S(2)}, u32[]{:S(2)}) collective-permute-start(bf16[12,32,128]{2,1,0:T(8,128)(2,1)S(1)} %get-tuple-element.34), channel_id=1, source_target_pairs={{0,16},{4,20},{8,24},{12,28},{16,0},{20,4},{24,8},{28,12},{1,17},{... | collective-permute-start | bytes 294920 | tf_op jit(solution)/shard_map/ppermute | solution.py:564
  8.6 9.2 %collective-permute-start.7 = (bf16[12,32,128]{2,1,0:T(8,128)(2,1)S(1)}, bf16[12,32,128]{2,1,0:T(8,128)(2,1)S(1)}, u32[]{:S(2)}, u32[]{:S(2)}) collective-permute-start(bf16[12,32,128]{2,1,0:T(8,128)(2,1)S(1)} %get-tuple-element.35), channel_id=1, source_target_pairs={{0,8},{4,12},{8,0},{12,4},{16,24},{20,28},{24,16},{28,20},{1,9},{5... | collective-permute-start | bytes 294920 | tf_op jit(solution)/shard_map/ppermute | solution.py:564
  10.8 2.3 %collective-permute-start.3 = (bf16[3,30,512]{2,1,0:T(8,128)(2,1)S(1)}, bf16[3,30,512]{2,1,0:T(8,128)(2,1)S(1)}, u32[]{:S(2)}, u32[]{:S(2)}) collective-permute-start(bf16[3,30,512]{2,1,0:T(8,128)(2,1)S(1)} %choose_waves.1), channel_id=1, source_target_pairs={{0,4},{4,0},{8,12},{12,8},{16,20},{20,16},{24,28},{28,24},{1,5},{5... | collective-permute-start | bytes 276488 | tf_op jit(solution)/shard_map/ppermute | solution.py:561
  17.9 3.9 %collective-permute-start.8 = (bf16[12,32,128]{2,1,0:T(8,128)(2,1)S(1)}, bf16[12,32,128]{2,1,0:T(8,128)(2,1)S(1)}, u32[]{:S(2)}, u32[]{:S(2)}) collective-permute-start(bf16[12,32,128]{2,1,0:T(8,128)(2,1)S(1)} %choose_piece.1.piece), channel_id=1, source_target_pairs={{0,4},{4,0},{8,12},{12,8},{16,20},{20,16},{24,28},{28,24},{1,5},{5... | collective-permute-start | bytes 294920 | tf_op jit(solution)/shard_map/ppermute | solution.py:561
  23.8 8.6 %collective-permute-start.9 = (bf16[128,256]{1,0:T(8,128)(2,1)S(1)}, bf16[128,256]{1,0:T(8,128)(2,1)S(1)}, u32[]{:S(2)}, u32[]{:S(2)}) collective-permute-start(bf16[128,256]{1,0:T(8,128)(2,1)S(1)} %get-tuple-element.43), channel_id=1, source_target_pairs={{0,0},{1,8},{2,4},{3,12},{4,16},{5,24},{6,20},{7,28},{8,1},{9,9},{... | collective-permute-start | bytes 196616 | tf_op jit(solution)/shard_map/ppermute | solution.py:603
  27.9 5.5 %collective-permute-start.10 = (bf16[128,256]{1,0:T(8,128)(2,1)S(1)}, bf16[128,256]{1,0:T(8,128)(2,1)S(1)}, u32[]{:S(2)}, u32[]{:S(2)}) collective-permute-start(bf16[128,256]{1,0:T(8,128)(2,1)S(1)} %get-tuple-element.44), channel_id=1, source_target_pairs={{0,8},{1,0},{2,12},{3,4},{4,24},{5,16},{6,28},{7,20},{8,9},{9,1},{... | collective-permute-start | bytes 196616 | tf_op jit(solution)/shard_map/ppermute | solution.py:603
  33.5 1.3 %collective-permute-start.11 = (f32[64,256]{1,0:T(8,128)S(1)}, f32[64,256]{1,0:T(8,128)S(1)}, u32[]{:S(2)}, u32[]{:S(2)}) collective-permute-start(f32[64,256]{1,0:T(8,128)S(1)} %get-tuple-element.46), channel_id=1, source_target_pairs={{0,4},{4,0},{8,12},{12,8},{16,20},{20,16},{24,28},{28,24},{1,5},{5... | collective-permute-start | bytes 196616 | tf_op jit(solution)/shard_map/ppermute | solution.py:561

commit v19 on v18

--- a/solution.py
+++ b/solution.py
@@ -41,20 +41,20 @@
             ((bank_blocks, chosen), (available, usable), (moveout, shifts))
         )
     ]
-    for block in range(blocks):
-        for part in range(2):
-            place = (block, pl.ds(half * part, half))
+    for side in (1, 0):
+        first = half * jnp.where(me == side, 0, 1)
+        for block in range(blocks):
+            place = (block, pl.ds(first, half))
+            number = 3 + blocks * (1 - side) + block
             fetch.append(
-                pltpu.make_async_copy(
-                    templates.at[place], raw.at[place], sems.at[3 + 2 * block + part]
-                )
+                pltpu.make_async_copy(templates.at[place], raw.at[place], sems.at[number])
             )
     for copy in fetch:
         copy.start()
     mine[...] = jnp.zeros_like(mine)
     theirs[...] = jnp.zeros_like(theirs)
     square[...] = jnp.zeros_like(square)
-    for copy in fetch:
+    for copy in fetch[:3]:
         copy.wait()
     slots = [chosen[which] % blocks for which in range(2)]
     row = lax.broadcasted_iota(jnp.int32, owners.shape, 0)
@@ -69,8 +69,10 @@
         turned = square[...].T
         later = pltpu.roll(turned, LANES - half, 1)
         codes.append([jnp.where(me == core, turned, later) for core in range(2)])
-    for which in range(2):
-        for side, out in enumerate((mine, theirs)):
+    for side, out in ((1, theirs), (0, mine)):
+        for block in range(blocks):
+            fetch[3 + blocks * (1 - side) + block].wait()
+        for which in range(2):
             first = half * jnp.where(me == side, 0, 1)
             code = codes[which][side].astype(jnp.bfloat16)
             for tile in range(TILES):

time: 36.1 us -> 35.8 us (level)
  no operation moved by 1% of the time
where the time goes in v19:
time: 35.8 us; the launch traced here: 35.4 us
  starting transfers between devices  15.7 us (44%)
  waiting for transfers between devices  10.2 us (28%)
  Pallas kernels  9.34 us (26%)
    ppermute x2, waiting for transfers between devices, shards(): gathered.append(lax.ppermute(parts[step], ('tm', 'sta'), route))  5.47 us
    ppermute x4, starting transfers between devices, across(): lax.ppermute(array, 'tm', [(i, i ^ 2 * step) for i in range(count_tm)])  4.91 us
    ppermute x5, starting transfers between devices, swap(): return lax.ppermute(array, 'tm', [(i, i ^ 1) for i in range(count_tm)])  4.27 us
    ppermute x2, starting transfers between devices, shards(): gathered.append(lax.ppermute(parts[step], ('tm', 'sta'), route))  4.16 us
    pallas_call x2, Pallas kernels, correlate(): pl.pallas_call(functools.partial(main_kernel, side, tlen, group), out_sha...  4.11 us
    ppermute x4, waiting for transfers between devices, across(): lax.ppermute(array, 'tm', [(i, i ^ 2 * step) for i in range(count_tm)])  2.81 us
    ppermute x1, starting transfers between devices, shards(): far.append(lax.ppermute(pair, 'tm', route))  2.37 us
    pallas_call x1, Pallas kernels, pack(): pl.pallas_call(pack_kernel, out_shape=[jax.ShapeDtypeStruct(shape, jnp.bf...  2.18 us
  transfers between devices with their start and end apart: 12, of which 5 were waited for; matrix products, arithmetic and copies ran while one was open for 0% of the time, Pallas kernels for 18%

profile of v19, /device:TPU:7, one launch (start us, length us, event | category | flops | bytes accessed | tf_op | source)
XLA Modules:
  0.0 35.4 jit_solution(15490893237995025810)
XLA Ops:
  0.0 0.7 %collective-permute-start = (bf16[30,512]{1,0:T(8,128)(2,1)}, bf16[30,512]{1,0:T(8,128)(2,1)S(1)}, u32[]{:S(2)}, u32[]{:S(2)}) collective-permute-start(bf16[30,512]{1,0:T(8,128)(2,1)} %own.1), channel_id=1, source_target_pairs={{0,4},{4,0},{8,12},{12,8},{16,20},{20,16},{24,28},{28,24},{1,5},{5... | collective-permute-start | bytes 92168 | tf_op jit(solution)/shard_map/ppermute | solution.py:563
  0.7 0.0 copy-start
  0.7 2.2 %pack.1 = (bf16[4,12,32,128]{3,2,1,0:T(8,128)(2,1)S(1)}, bf16[4,12,32,128]{3,2,1,0:T(8,128)(2,1)S(1)}, s32[8,128]{1,0:T(8,128)S(1)}) custom-call(s32[2]{0:T(128)} %bank_blocks.1, bf16[2,30,64,100]{3,2,1,0:T(8,128)(2,1)} %bitcast.3, s32[30,2,64]{2,1,0:T(2,128)} %bitcast.4, s32[30,2,64]{2,1,0:T(2,128)} %bitcast.5), custom_call_target="tpu_custom_call" | custom-call | flops 2000000000 | bytes 2000000 | tf_op jit(solution)/shard_map/pack/pallas_call | solution.py:100
  2.9 0.0 collective-permute-done.partner
  2.9 0.1 collective-permute-start.4
  3.0 0.0 copy-done
  3.0 2.4 %collective-permute-start.2 = (bf16[2,30,512]{2,1,0:T(8,128)(2,1)S(1)}, bf16[2,30,512]{2,1,0:T(8,128)(2,1)S(1)}, u32[]{:S(2)}, u32[]{:S(2)}) collective-permute-start(bf16[2,30,512]{2,1,0:T(8,128)(2,1)S(1)} %pair_waves.1.pair), channel_id=1, source_target_pairs={{0,24},{4,20},{8,16},{12,28},{16,8},{20,4},{24,0},{28,12},{1,25},{... | collective-permute-start | bytes 184328 | tf_op jit(solution)/shard_map/ppermute | solution.py:584
  5.4 1.3 %collective-permute-start.1 = (bf16[30,512]{1,0:T(8,128)(2,1)S(1)}, bf16[30,512]{1,0:T(8,128)(2,1)S(1)}, u32[]{:S(2)}, u32[]{:S(2)}) collective-permute-start(bf16[30,512]{1,0:T(8,128)(2,1)S(1)} %copy-done), channel_id=1, source_target_pairs={{0,8},{4,12},{8,0},{12,4},{16,24},{20,28},{24,16},{28,20},{1,9},{5... | collective-permute-start | bytes 92168 | tf_op jit(solution)/shard_map/ppermute | solution.py:566
  6.7 0.0 collective-permute-done.4.other
  6.7 0.2 merge.1
  6.9 1.4 %collective-permute-start.5 = (bf16[12,32,128]{2,1,0:T(8,128)(2,1)S(1)}, bf16[12,32,128]{2,1,0:T(8,128)(2,1)S(1)}, u32[]{:S(2)}, u32[]{:S(2)}) collective-permute-start(bf16[12,32,128]{2,1,0:T(8,128)(2,1)S(1)} %get-tuple-element.33), channel_id=1, source_target_pairs={{0,24},{4,28},{8,16},{12,20},{16,8},{20,12},{24,0},{28,4},{1,25},{... | collective-permute-start | bytes 294920 | tf_op jit(solution)/shard_map/ppermute | solution.py:566
  8.3 0.0 collective-permute-start.6
  8.3 2.2 %collective-permute-start.7 = (bf16[12,32,128]{2,1,0:T(8,128)(2,1)S(1)}, bf16[12,32,128]{2,1,0:T(8,128)(2,1)S(1)}, u32[]{:S(2)}, u32[]{:S(2)}) collective-permute-start(bf16[12,32,128]{2,1,0:T(8,128)(2,1)S(1)} %get-tuple-element.35), channel_id=1, source_target_pairs={{0,8},{4,12},{8,0},{12,4},{16,24},{20,28},{24,16},{28,20},{1,9},{5... | collective-permute-start | bytes 294920 | tf_op jit(solution)/shard_map/ppermute | solution.py:566
  10.5 0.0 collective-permute-done.1.beside
  10.5 0.0 collective-permute-done.2.rest_0_
  10.5 1.4 %collective-permute-start.3 = (bf16[3,30,512]{2,1,0:T(8,128)(2,1)S(1)}, bf16[3,30,512]{2,1,0:T(8,128)(2,1)S(1)}, u32[]{:S(2)}, u32[]{:S(2)}) collective-permute-start(bf16[3,30,512]{2,1,0:T(8,128)(2,1)S(1)} %choose_waves.1), channel_id=1, source_target_pairs={{0,4},{4,0},{8,12},{12,8},{16,20},{20,16},{24,28},{28,24},{1,5},{5... | collective-permute-start | bytes 276488 | tf_op jit(solution)/shard_map/ppermute | solution.py:563
  11.9 0.9 %collective-permute-done.3.swapped = bf16[3,30,512]{2,1,0:T(8,128)(2,1)S(1)} collective-permute-done((bf16[3,30,512]{2,1,0:T(8,128)(2,1)S(1)}, bf16[3,30,512]{2,1,0:T(8,128)(2,1)S(1)}, u32[]{:S(2)}, u32[]{:S(2)}) %collective-permute-start.3) | collective-permute-done | bytes 92192 | tf_op jit(solution)/shard_map/ppermute | solution.py:563
  12.9 1.8 %prepare_waves.1 = (bf16[30,272,128]{2,1,0:T(8,128)(2,1)S(1)}, f32[32,32,128]{2,1,0:T(8,128)S(1)}) custom-call(bf16[3,30,512]{2,1,0:T(8,128)(2,1)S(1)} %collective-permute-done.3.swapped, bf16[2,30,512]{2,1,0:T(8,128)(2,1)S(1)} %pair_waves.1.pair, bf16[30,512]{1,0:T(8,128)(2,1)S(1)} %collective-permute-done.1.beside, ...), custom_call_target="tpu_custom_call" | custom-call | flops 50000000 | bytes 50000 | tf_op jit(solution)/shard_map/prepare_waves/pallas_call | solution.py:302
  14.7 0.0 collective-permute-done.5.refs_3_
  14.7 2.8 %collective-permute-done.6.refs_2_ = bf16[12,32,128]{2,1,0:T(8,128)(2,1)S(1)} collective-permute-done((bf16[12,32,128]{2,1,0:T(8,128)(2,1)S(1)}, bf16[12,32,128]{2,1,0:T(8,128)(2,1)S(1)}, u32[]{:S(2)}, u32[]{:S(2)}) %collective-permute-start.6) | collective-permute-done | bytes 98336 | tf_op jit(solution)/shard_map/ppermute | solution.py:566
  17.5 0.0 collective-permute-done.7.refs_1_
  17.5 0.1 choose_piece.1.piece
  17.6 1.8 %collective-permute-start.8 = (bf16[12,32,128]{2,1,0:T(8,128)(2,1)S(1)}, bf16[12,32,128]{2,1,0:T(8,128)(2,1)S(1)}, u32[]{:S(2)}, u32[]{:S(2)}) collective-permute-start(bf16[12,32,128]{2,1,0:T(8,128)(2,1)S(1)} %choose_piece.1.piece), channel_id=1, source_target_pairs={{0,4},{4,0},{8,12},{12,8},{16,20},{20,16},{24,28},{28,24},{1,5},{5... | collective-permute-start | bytes 294920 | tf_op jit(solution)/shard_map/ppermute | solution.py:563
  19.4 2.0 %correlate_first.1.rest_0_ = f32[256,256]{1,0:T(8,128)S(1)} custom-call(bf16[12,32,128]{2,1,0:T(8,128)(2,1)S(1)} %choose_piece.1.piece, bf16[30,272,128]{2,1,0:T(8,128)(2,1)S(1)} %get-tuple-element.41.left_a, f32[32,32,128]{2,1,0:T(8,128)S(1)} %get-tuple-element.42.inverse), custom_call_target="tpu_custom_call" | custom-call | flops 3000000000 | bytes 3000000 | tf_op jit(solution)/shard_map/correlate_first/pallas_call | solution.py:479
  21.4 0.0 collective-permute-done.8.piece
  21.4 2.1 %correlate_second.1 = (bf16[128,256]{1,0:T(8,128)(2,1)S(1)}, bf16[128,256]{1,0:T(8,128)(2,1)S(1)}) custom-call(bf16[12,32,128]{2,1,0:T(8,128)(2,1)S(1)} %collective-permute-done.8.piece, bf16[30,272,128]{2,1,0:T(8,128)(2,1)S(1)} %get-tuple-element.41.left_a, f32[32,32,128]{2,1,0:T(8,128)S(1)} %get-tuple-element.42.inverse, f32[256,256]{1,0:T(8,128)S(1)} %correlate_first.1.rest_0_), custom_call_target="tpu_custom_call" | custom-call | flops 3000000000 | bytes 3000000 | tf_op jit(solution)/shard_map/correlate_second/pallas_call | solution.py:479
  23.5 4.1 %collective-permute-start.9 = (bf16[128,256]{1,0:T(8,128)(2,1)S(1)}, bf16[128,256]{1,0:T(8,128)(2,1)S(1)}, u32[]{:S(2)}, u32[]{:S(2)}) collective-permute-start(bf16[128,256]{1,0:T(8,128)(2,1)S(1)} %get-tuple-element.43), channel_id=1, source_target_pairs={{0,0},{1,8},{2,4},{3,12},{4,16},{5,24},{6,20},{7,28},{8,1},{9,9},{... | collective-permute-start | bytes 196616 | tf_op jit(solution)/shard_map/ppermute | solution.py:605
  27.6 0.1 collective-permute-start.10
  27.7 4.4 %collective-permute-done.9.refs_0_ = bf16[128,256]{1,0:T(8,128)(2,1)S(1)} collective-permute-done((bf16[128,256]{1,0:T(8,128)(2,1)S(1)}, bf16[128,256]{1,0:T(8,128)(2,1)S(1)}, u32[]{:S(2)}, u32[]{:S(2)}) %collective-permute-start.9) | collective-permute-done | bytes 65568 | tf_op jit(solution)/shard_map/ppermute | solution.py:605
  32.1 1.1 %collective-permute-done.10.refs_1_ = bf16[128,256]{1,0:T(8,128)(2,1)S(1)} collective-permute-done((bf16[128,256]{1,0:T(8,128)(2,1)S(1)}, bf16[128,256]{1,0:T(8,128)(2,1)S(1)}, u32[]{:S(2)}, u32[]{:S(2)}) %collective-permute-start.10) | collective-permute-done | bytes 65568 | tf_op jit(solution)/shard_map/ppermute | solution.py:605
  33.2 0.3 collective-permute-start.11
  33.5 1.0 %collective-permute-done.11.received = f32[64,256]{1,0:T(8,128)S(1)} collective-permute-done((f32[64,256]{1,0:T(8,128)S(1)}, f32[64,256]{1,0:T(8,128)S(1)}, u32[]{:S(2)}, u32[]{:S(2)}) %collective-permute-start.11) | collective-permute-done | bytes 65568 | tf_op jit(solution)/shard_map/ppermute | solution.py:563
  34.5 0.9 %finish.1 = f32[32,512]{1,0:T(8,128)} custom-call(f32[64,256]{1,0:T(8,128)S(1)} %get-tuple-element.45.ours, f32[64,256]{1,0:T(8,128)S(1)} %collective-permute-done.11.received), custom_call_target="tpu_custom_call" | custom-call | flops 1000000000 | bytes 1000000 | tf_op jit(solution)/shard_map/finish/pallas_call | solution.py:542
  (3 shorter events, 0.1 us)
Async XLA Ops:
  0.0 2.9 %collective-permute-start = (bf16[30,512]{1,0:T(8,128)(2,1)}, bf16[30,512]{1,0:T(8,128)(2,1)S(1)}, u32[]{:S(2)}, u32[]{:S(2)}) collective-permute-start(bf16[30,512]{1,0:T(8,128)(2,1)} %own.1), channel_id=1, source_target_pairs={{0,4},{4,0},{8,12},{12,8},{16,20},{20,16},{24,28},{28,24},{1,5},{5... | collective-permute-start | bytes 92168 | tf_op jit(solution)/shard_map/ppermute | solution.py:563
  0.7 2.3 %copy-start = (bf16[30,512]{1,0:T(8,128)(2,1)S(1)}, bf16[30,512]{1,0:T(8,128)(2,1)}, u32[]{:S(2)}) copy-start(bf16[30,512]{1,0:T(8,128)(2,1)} %own.1) | copy-start | bytes 92164
  2.9 3.8 %collective-permute-start.4 = (bf16[4,12,32,128]{3,2,1,0:T(8,128)(2,1)S(1)}, bf16[4,12,32,128]{3,2,1,0:T(8,128)(2,1)S(1)}, u32[]{:S(2)}, u32[]{:S(2)}) collective-permute-start(bf16[4,12,32,128]{3,2,1,0:T(8,128)(2,1)S(1)} %get-tuple-element.32), channel_id=1, source_target_pairs={{0,4},{4,0},{8,12},{12,8},{16,20},{20,16},{24,28},{28,24},{1,5},{5... | collective-permute-start | bytes 1179656 | tf_op jit(solution)/shard_map/ppermute | solution.py:563
  3.0 7.5 %collective-permute-start.2 = (bf16[2,30,512]{2,1,0:T(8,128)(2,1)S(1)}, bf16[2,30,512]{2,1,0:T(8,128)(2,1)S(1)}, u32[]{:S(2)}, u32[]{:S(2)}) collective-permute-start(bf16[2,30,512]{2,1,0:T(8,128)(2,1)S(1)} %pair_waves.1.pair), channel_id=1, source_target_pairs={{0,24},{4,20},{8,16},{12,28},{16,8},{20,4},{24,0},{28,12},{1,25},{... | collective-permute-start | bytes 184328 | tf_op jit(solution)/shard_map/ppermute | solution.py:584
  5.4 5.1 %collective-permute-start.1 = (bf16[30,512]{1,0:T(8,128)(2,1)S(1)}, bf16[30,512]{1,0:T(8,128)(2,1)S(1)}, u32[]{:S(2)}, u32[]{:S(2)}) collective-permute-start(bf16[30,512]{1,0:T(8,128)(2,1)S(1)} %copy-done), channel_id=1, source_target_pairs={{0,8},{4,12},{8,0},{12,4},{16,24},{20,28},{24,16},{28,20},{1,9},{5... | collective-permute-start | bytes 92168 | tf_op jit(solution)/shard_map/ppermute | solution.py:566
  6.9 7.8 %collective-permute-start.5 = (bf16[12,32,128]{2,1,0:T(8,128)(2,1)S(1)}, bf16[12,32,128]{2,1,0:T(8,128)(2,1)S(1)}, u32[]{:S(2)}, u32[]{:S(2)}) collective-permute-start(bf16[12,32,128]{2,1,0:T(8,128)(2,1)S(1)} %get-tuple-element.33), channel_id=1, source_target_pairs={{0,24},{4,28},{8,16},{12,20},{16,8},{20,12},{24,0},{28,4},{1,25},{... | collective-permute-start | bytes 294920 | tf_op jit(solution)/shard_map/ppermute | solution.py:566
  8.3 9.2 %collective-permute-start.6 = (bf16[12,32,128]{2,1,0:T(8,128)(2,1)S(1)}, bf16[12,32,128]{2,1,0:T(8,128)(2,1)S(1)}, u32[]{:S(2)}, u32[]{:S(2)}) collective-permute-start(bf16[12,32,128]{2,1,0:T(8,128)(2,1)S(1)} %get-tuple-element.34), channel_id=1, source_target_pairs={{0,16},{4,20},{8,24},{12,28},{16,0},{20,4},{24,8},{28,12},{1,17},{... | collective-permute-start | bytes 294920 | tf_op jit(solution)/shard_map/ppermute | solution.py:566
  8.3 9.2 %collective-permute-start.7 = (bf16[12,32,128]{2,1,0:T(8,128)(2,1)S(1)}, bf16[12,32,128]{2,1,0:T(8,128)(2,1)S(1)}, u32[]{:S(2)}, u32[]{:S(2)}) collective-permute-start(bf16[12,32,128]{2,1,0:T(8,128)(2,1)S(1)} %get-tuple-element.35), channel_id=1, source_target_pairs={{0,8},{4,12},{8,0},{12,4},{16,24},{20,28},{24,16},{28,20},{1,9},{5... | collective-permute-start | bytes 294920 | tf_op jit(solution)/shard_map/ppermute | solution.py:566
  10.5 2.3 %collective-permute-start.3 = (bf16[3,30,512]{2,1,0:T(8,128)(2,1)S(1)}, bf16[3,30,512]{2,1,0:T(8,128)(2,1)S(1)}, u32[]{:S(2)}, u32[]{:S(2)}) collective-permute-start(bf16[3,30,512]{2,1,0:T(8,128)(2,1)S(1)} %choose_waves.1), channel_id=1, source_target_pairs={{0,4},{4,0},{8,12},{12,8},{16,20},{20,16},{24,28},{28,24},{1,5},{5... | collective-permute-start | bytes 276488 | tf_op jit(solution)/shard_map/ppermute | solution.py:563
  17.6 3.9 %collective-permute-start.8 = (bf16[12,32,128]{2,1,0:T(8,128)(2,1)S(1)}, bf16[12,32,128]{2,1,0:T(8,128)(2,1)S(1)}, u32[]{:S(2)}, u32[]{:S(2)}) collective-permute-start(bf16[12,32,128]{2,1,0:T(8,128)(2,1)S(1)} %choose_piece.1.piece), channel_id=1, source_target_pairs={{0,4},{4,0},{8,12},{12,8},{16,20},{20,16},{24,28},{28,24},{1,5},{5... | collective-permute-start | bytes 294920 | tf_op jit(solution)/shard_map/ppermute | solution.py:563
  23.5 8.6 %collective-permute-start.9 = (bf16[128,256]{1,0:T(8,128)(2,1)S(1)}, bf16[128,256]{1,0:T(8,128)(2,1)S(1)}, u32[]{:S(2)}, u32[]{:S(2)}) collective-permute-start(bf16[128,256]{1,0:T(8,128)(2,1)S(1)} %get-tuple-element.43), channel_id=1, source_target_pairs={{0,0},{1,8},{2,4},{3,12},{4,16},{5,24},{6,20},{7,28},{8,1},{9,9},{... | collective-permute-start | bytes 196616 | tf_op jit(solution)/shard_map/ppermute | solution.py:605
  27.6 5.5 %collective-permute-start.10 = (bf16[128,256]{1,0:T(8,128)(2,1)S(1)}, bf16[128,256]{1,0:T(8,128)(2,1)S(1)}, u32[]{:S(2)}, u32[]{:S(2)}) collective-permute-start(bf16[128,256]{1,0:T(8,128)(2,1)S(1)} %get-tuple-element.44), channel_id=1, source_target_pairs={{0,8},{1,0},{2,12},{3,4},{4,24},{5,16},{6,28},{7,20},{8,9},{9,1},{... | collective-permute-start | bytes 196616 | tf_op jit(solution)/shard_map/ppermute | solution.py:605
  33.2 1.3 %collective-permute-start.11 = (f32[64,256]{1,0:T(8,128)S(1)}, f32[64,256]{1,0:T(8,128)S(1)}, u32[]{:S(2)}, u32[]{:S(2)}) collective-permute-start(f32[64,256]{1,0:T(8,128)S(1)} %get-tuple-element.46), channel_id=1, source_target_pairs={{0,4},{4,0},{8,12},{12,8},{16,20},{20,16},{24,28},{28,24},{1,5},{5... | collective-permute-start | bytes 196616 | tf_op jit(solution)/shard_map/ppermute | solution.py:563

commit v20 on v19

--- a/solution.py
+++ b/solution.py
@@ -589,8 +589,10 @@
     swapped = swap(choose_waves(pair, beside, far))
     left_a, inverse = prepare_waves(tlen, swapped, pair, beside, far)
 
-    left_a, inverse, *pieces = lax.optimization_barrier((left_a, inverse, *pieces[::-1]))
-    pieces = pieces[::-1]
+    order = sorted(range(chips), key=lambda step: (step < 2, step))
+    placed = lax.optimization_barrier((left_a, inverse, *[pieces[step] for step in order]))
+    left_a, inverse = placed[:2]
+    pieces = [placed[2 + order.index(step)] for step in range(chips)]
     first = choose_piece(owners, pieces)
     second = swap(first)
     total = correlate(0, tlen, group, near, first, left_a, inverse)

time: 35.8 us -> 35.4 us (0.989)
  waiting for transfers between devices: 10.2 us -> 7.84 us
  starting transfers between devices: 15.7 us -> 18 us
    ppermute x5, starting transfers between devices: 4.27 us -> 6.09 us  [swap(): return lax.ppermute(array, 'tm', [(i, i ^ 1) for i in range(count_tm)])]
    ppermute x2, waiting for transfers between devices: 5.47 us -> 3.95 us  [shards(): gathered.append(lax.ppermute(parts[step], ('tm', 'sta'), route))]
    ppermute x2, starting transfers between devices: 4.16 us -> 5.52 us  [shards(): gathered.append(lax.ppermute(parts[step], ('tm', 'sta'), route))]
    ppermute x4, starting transfers between devices: 4.91 us -> 4.01 us  [across(): lax.ppermute(array, 'tm', [(i, i ^ 2 * step) for i in range(count_tm)])]
    ppermute x4, waiting for transfers between devices: 2.81 us -> 2.02 us  [across(): lax.ppermute(array, 'tm', [(i, i ^ 2 * step) for i in range(count_tm)])]
where the time goes in v20:
time: 35.4 us; the launch traced here: 35.3 us
  starting transfers between devices  18 us (51%)
  Pallas kernels  9.34 us (26%)
  waiting for transfers between devices  7.84 us (22%)
    ppermute x5, starting transfers between devices, swap(): return lax.ppermute(array, 'tm', [(i, i ^ 1) for i in range(count_tm)])  6.09 us
    ppermute x2, starting transfers between devices, shards(): gathered.append(lax.ppermute(parts[step], ('tm', 'sta'), route))  5.52 us
    pallas_call x2, Pallas kernels, correlate(): pl.pallas_call(functools.partial(main_kernel, side, tlen, group), out_sha...  4.11 us
    ppermute x4, starting transfers between devices, across(): lax.ppermute(array, 'tm', [(i, i ^ 2 * step) for i in range(count_tm)])  4.01 us
    ppermute x2, waiting for transfers between devices, shards(): gathered.append(lax.ppermute(parts[step], ('tm', 'sta'), route))  3.95 us
    ppermute x1, starting transfers between devices, shards(): far.append(lax.ppermute(pair, 'tm', route))  2.37 us
    pallas_call x1, Pallas kernels, pack(): pl.pallas_call(pack_kernel, out_shape=[jax.ShapeDtypeStruct(shape, jnp.bf...  2.18 us
    ppermute x4, waiting for transfers between devices, across(): lax.ppermute(array, 'tm', [(i, i ^ 2 * step) for i in range(count_tm)])  2.02 us
  transfers between devices with their start and end apart: 12, of which 5 were waited for; matrix products, arithmetic and copies ran while one was open for 0% of the time, Pallas kernels for 18%

profile of v20, /device:TPU:7, one launch (start us, length us, event | category | flops | bytes accessed | tf_op | source)
XLA Modules:
  0.0 35.3 jit_solution(17862406808247987728)
XLA Ops:
  0.0 0.7 %collective-permute-start = (bf16[30,512]{1,0:T(8,128)(2,1)}, bf16[30,512]{1,0:T(8,128)(2,1)S(1)}, u32[]{:S(2)}, u32[]{:S(2)}) collective-permute-start(bf16[30,512]{1,0:T(8,128)(2,1)} %own.1), channel_id=1, source_target_pairs={{0,4},{4,0},{8,12},{12,8},{16,20},{20,16},{24,28},{28,24},{1,5},{5... | collective-permute-start | bytes 92168 | tf_op jit(solution)/shard_map/ppermute | solution.py:563
  0.7 0.0 copy-start
  0.7 2.2 %pack.1 = (bf16[4,12,32,128]{3,2,1,0:T(8,128)(2,1)S(1)}, bf16[4,12,32,128]{3,2,1,0:T(8,128)(2,1)S(1)}, s32[8,128]{1,0:T(8,128)S(1)}) custom-call(s32[2]{0:T(128)} %bank_blocks.1, bf16[2,30,64,100]{3,2,1,0:T(8,128)(2,1)} %bitcast.3, s32[30,2,64]{2,1,0:T(2,128)} %bitcast.4, s32[30,2,64]{2,1,0:T(2,128)} %bitcast.5), custom_call_target="tpu_custom_call" | custom-call | flops 2000000000 | bytes 2000000 | tf_op jit(solution)/shard_map/pack/pallas_call | solution.py:100
  2.9 0.0 collective-permute-done.partner
  2.9 0.1 collective-permute-start.4
  3.0 0.0 copy-done
  3.0 2.4 %collective-permute-start.2 = (bf16[2,30,512]{2,1,0:T(8,128)(2,1)S(1)}, bf16[2,30,512]{2,1,0:T(8,128)(2,1)S(1)}, u32[]{:S(2)}, u32[]{:S(2)}) collective-permute-start(bf16[2,30,512]{2,1,0:T(8,128)(2,1)S(1)} %pair_waves.1.pair), channel_id=1, source_target_pairs={{0,24},{4,20},{8,16},{12,28},{16,8},{20,4},{24,0},{28,12},{1,25},{... | collective-permute-start | bytes 184328 | tf_op jit(solution)/shard_map/ppermute | solution.py:584
  5.4 1.3 %collective-permute-start.1 = (bf16[30,512]{1,0:T(8,128)(2,1)S(1)}, bf16[30,512]{1,0:T(8,128)(2,1)S(1)}, u32[]{:S(2)}, u32[]{:S(2)}) collective-permute-start(bf16[30,512]{1,0:T(8,128)(2,1)S(1)} %copy-done), channel_id=1, source_target_pairs={{0,8},{4,12},{8,0},{12,4},{16,24},{20,28},{24,16},{28,20},{1,9},{5... | collective-permute-start | bytes 92168 | tf_op jit(solution)/shard_map/ppermute | solution.py:566
  6.7 0.0 collective-permute-done.4.other
  6.7 0.2 merge.1
  6.9 0.4 %collective-permute-start.5 = (bf16[12,32,128]{2,1,0:T(8,128)(2,1)S(1)}, bf16[12,32,128]{2,1,0:T(8,128)(2,1)S(1)}, u32[]{:S(2)}, u32[]{:S(2)}) collective-permute-start(bf16[12,32,128]{2,1,0:T(8,128)(2,1)S(1)} %get-tuple-element.33), channel_id=1, source_target_pairs={{0,16},{4,20},{8,24},{12,28},{16,0},{20,4},{24,8},{28,12},{1,17},{... | collective-permute-start | bytes 294920 | tf_op jit(solution)/shard_map/ppermute | solution.py:566
  7.3 1.9 %collective-permute-start.6 = (bf16[12,32,128]{2,1,0:T(8,128)(2,1)S(1)}, bf16[12,32,128]{2,1,0:T(8,128)(2,1)S(1)}, u32[]{:S(2)}, u32[]{:S(2)}) collective-permute-start(bf16[12,32,128]{2,1,0:T(8,128)(2,1)S(1)} %get-tuple-element.34), channel_id=1, source_target_pairs={{0,24},{4,28},{8,16},{12,20},{16,8},{20,12},{24,0},{28,4},{1,25},{... | collective-permute-start | bytes 294920 | tf_op jit(solution)/shard_map/ppermute | solution.py:566
  9.2 0.4 %collective-permute-start.7 = (bf16[12,32,128]{2,1,0:T(8,128)(2,1)S(1)}, bf16[12,32,128]{2,1,0:T(8,128)(2,1)S(1)}, u32[]{:S(2)}, u32[]{:S(2)}) collective-permute-start(bf16[12,32,128]{2,1,0:T(8,128)(2,1)S(1)} %get-tuple-element.36), channel_id=1, source_target_pairs={{0,8},{4,12},{8,0},{12,4},{16,24},{20,28},{24,16},{28,20},{1,9},{5... | collective-permute-start | bytes 294920 | tf_op jit(solution)/shard_map/ppermute | solution.py:566
  9.6 0.0 collective-permute-done.1.beside
  9.6 0.0 collective-permute-done.2.rest_0_
  9.7 2.3 %collective-permute-start.3 = (bf16[3,30,512]{2,1,0:T(8,128)(2,1)S(1)}, bf16[3,30,512]{2,1,0:T(8,128)(2,1)S(1)}, u32[]{:S(2)}, u32[]{:S(2)}) collective-permute-start(bf16[3,30,512]{2,1,0:T(8,128)(2,1)S(1)} %choose_waves.1), channel_id=1, source_target_pairs={{0,4},{4,0},{8,12},{12,8},{16,20},{20,16},{24,28},{28,24},{1,5},{5... | collective-permute-start | bytes 276488 | tf_op jit(solution)/shard_map/ppermute | solution.py:563
  11.9 0.9 %collective-permute-done.3.swapped = bf16[3,30,512]{2,1,0:T(8,128)(2,1)S(1)} collective-permute-done((bf16[3,30,512]{2,1,0:T(8,128)(2,1)S(1)}, bf16[3,30,512]{2,1,0:T(8,128)(2,1)S(1)}, u32[]{:S(2)}, u32[]{:S(2)}) %collective-permute-start.3) | collective-permute-done | bytes 92192 | tf_op jit(solution)/shard_map/ppermute | solution.py:563
  12.9 1.8 %prepare_waves.1 = (bf16[30,272,128]{2,1,0:T(8,128)(2,1)S(1)}, f32[32,32,128]{2,1,0:T(8,128)S(1)}) custom-call(bf16[3,30,512]{2,1,0:T(8,128)(2,1)S(1)} %collective-permute-done.3.swapped, bf16[2,30,512]{2,1,0:T(8,128)(2,1)S(1)} %pair_waves.1.pair, bf16[30,512]{1,0:T(8,128)(2,1)S(1)} %collective-permute-done.1.beside, ...), custom_call_target="tpu_custom_call" | custom-call | flops 50000000 | bytes 50000 | tf_op jit(solution)/shard_map/prepare_waves/pallas_call | solution.py:302
  14.7 2.0 %collective-permute-done.5.refs_2_ = bf16[12,32,128]{2,1,0:T(8,128)(2,1)S(1)} collective-permute-done((bf16[12,32,128]{2,1,0:T(8,128)(2,1)S(1)}, bf16[12,32,128]{2,1,0:T(8,128)(2,1)S(1)}, u32[]{:S(2)}, u32[]{:S(2)}) %collective-permute-start.5) | collective-permute-done | bytes 98336 | tf_op jit(solution)/shard_map/ppermute | solution.py:566
  16.7 0.0 collective-permute-done.6.refs_3_
  16.7 0.0 collective-permute-done.7.refs_1_
  16.7 0.1 choose_piece.1.piece
  16.8 1.6 %collective-permute-start.8 = (bf16[12,32,128]{2,1,0:T(8,128)(2,1)S(1)}, bf16[12,32,128]{2,1,0:T(8,128)(2,1)S(1)}, u32[]{:S(2)}, u32[]{:S(2)}) collective-permute-start(bf16[12,32,128]{2,1,0:T(8,128)(2,1)S(1)} %choose_piece.1.piece), channel_id=1, source_target_pairs={{0,4},{4,0},{8,12},{12,8},{16,20},{20,16},{24,28},{28,24},{1,5},{5... | collective-permute-start | bytes 294920 | tf_op jit(solution)/shard_map/ppermute | solution.py:563
  18.4 2.0 %correlate_first.1.rest_0_ = f32[256,256]{1,0:T(8,128)S(1)} custom-call(bf16[12,32,128]{2,1,0:T(8,128)(2,1)S(1)} %choose_piece.1.piece, bf16[30,272,128]{2,1,0:T(8,128)(2,1)S(1)} %get-tuple-element.41.left_a, f32[32,32,128]{2,1,0:T(8,128)S(1)} %get-tuple-element.42.inverse), custom_call_target="tpu_custom_call" | custom-call | flops 3000000000 | bytes 3000000 | tf_op jit(solution)/shard_map/correlate_first/pallas_call | solution.py:479
  20.4 0.0 collective-permute-done.8.piece
  20.4 2.1 %correlate_second.1 = (bf16[128,256]{1,0:T(8,128)(2,1)S(1)}, bf16[128,256]{1,0:T(8,128)(2,1)S(1)}) custom-call(bf16[12,32,128]{2,1,0:T(8,128)(2,1)S(1)} %collective-permute-done.8.piece, bf16[30,272,128]{2,1,0:T(8,128)(2,1)S(1)} %get-tuple-element.41.left_a, f32[32,32,128]{2,1,0:T(8,128)S(1)} %get-tuple-element.42.inverse, f32[256,256]{1,0:T(8,128)S(1)} %correlate_first.1.rest_0_), custom_call_target="tpu_custom_call" | custom-call | flops 3000000000 | bytes 3000000 | tf_op jit(solution)/shard_map/correlate_second/pallas_call | solution.py:479
  22.5 3.6 %collective-permute-start.9 = (bf16[128,256]{1,0:T(8,128)(2,1)S(1)}, bf16[128,256]{1,0:T(8,128)(2,1)S(1)}, u32[]{:S(2)}, u32[]{:S(2)}) collective-permute-start(bf16[128,256]{1,0:T(8,128)(2,1)S(1)} %get-tuple-element.43), channel_id=1, source_target_pairs={{0,0},{1,8},{2,4},{3,12},{4,16},{5,24},{6,20},{7,28},{8,1},{9,9},{... | collective-permute-start | bytes 196616 | tf_op jit(solution)/shard_map/ppermute | solution.py:607
  26.2 1.9 %collective-permute-start.10 = (bf16[128,256]{1,0:T(8,128)(2,1)S(1)}, bf16[128,256]{1,0:T(8,128)(2,1)S(1)}, u32[]{:S(2)}, u32[]{:S(2)}) collective-permute-start(bf16[128,256]{1,0:T(8,128)(2,1)S(1)} %get-tuple-element.44), channel_id=1, source_target_pairs={{0,8},{1,0},{2,12},{3,4},{4,24},{5,16},{6,28},{7,20},{8,9},{9,1},{... | collective-permute-start | bytes 196616 | tf_op jit(solution)/shard_map/ppermute | solution.py:607
  28.0 3.5 %collective-permute-done.9.refs_0_ = bf16[128,256]{1,0:T(8,128)(2,1)S(1)} collective-permute-done((bf16[128,256]{1,0:T(8,128)(2,1)S(1)}, bf16[128,256]{1,0:T(8,128)(2,1)S(1)}, u32[]{:S(2)}, u32[]{:S(2)}) %collective-permute-start.9) | collective-permute-done | bytes 65568 | tf_op jit(solution)/shard_map/ppermute | solution.py:607
  31.5 0.5 %collective-permute-done.10.refs_1_ = bf16[128,256]{1,0:T(8,128)(2,1)S(1)} collective-permute-done((bf16[128,256]{1,0:T(8,128)(2,1)S(1)}, bf16[128,256]{1,0:T(8,128)(2,1)S(1)}, u32[]{:S(2)}, u32[]{:S(2)}) %collective-permute-start.10) | collective-permute-done | bytes 65568 | tf_op jit(solution)/shard_map/ppermute | solution.py:607
  32.0 1.5 %collective-permute-start.11 = (f32[64,256]{1,0:T(8,128)S(1)}, f32[64,256]{1,0:T(8,128)S(1)}, u32[]{:S(2)}, u32[]{:S(2)}) collective-permute-start(f32[64,256]{1,0:T(8,128)S(1)} %get-tuple-element.46), channel_id=1, source_target_pairs={{0,4},{4,0},{8,12},{12,8},{16,20},{20,16},{24,28},{28,24},{1,5},{5... | collective-permute-start | bytes 196616 | tf_op jit(solution)/shard_map/ppermute | solution.py:563
  33.5 0.9 %collective-permute-done.11.received = f32[64,256]{1,0:T(8,128)S(1)} collective-permute-done((f32[64,256]{1,0:T(8,128)S(1)}, f32[64,256]{1,0:T(8,128)S(1)}, u32[]{:S(2)}, u32[]{:S(2)}) %collective-permute-start.11) | collective-permute-done | bytes 65568 | tf_op jit(solution)/shard_map/ppermute | solution.py:563
  34.4 0.9 %finish.1 = f32[32,512]{1,0:T(8,128)} custom-call(f32[64,256]{1,0:T(8,128)S(1)} %get-tuple-element.45.ours, f32[64,256]{1,0:T(8,128)S(1)} %collective-permute-done.11.received), custom_call_target="tpu_custom_call" | custom-call | flops 1000000000 | bytes 1000000 | tf_op jit(solution)/shard_map/finish/pallas_call | solution.py:542
  (3 shorter events, 0.1 us)
Async XLA Ops:
  0.0 2.9 %collective-permute-start = (bf16[30,512]{1,0:T(8,128)(2,1)}, bf16[30,512]{1,0:T(8,128)(2,1)S(1)}, u32[]{:S(2)}, u32[]{:S(2)}) collective-permute-start(bf16[30,512]{1,0:T(8,128)(2,1)} %own.1), channel_id=1, source_target_pairs={{0,4},{4,0},{8,12},{12,8},{16,20},{20,16},{24,28},{28,24},{1,5},{5... | collective-permute-start | bytes 92168 | tf_op jit(solution)/shard_map/ppermute | solution.py:563
  0.7 2.3 %copy-start = (bf16[30,512]{1,0:T(8,128)(2,1)S(1)}, bf16[30,512]{1,0:T(8,128)(2,1)}, u32[]{:S(2)}) copy-start(bf16[30,512]{1,0:T(8,128)(2,1)} %own.1) | copy-start | bytes 92164
  2.9 3.8 %collective-permute-start.4 = (bf16[4,12,32,128]{3,2,1,0:T(8,128)(2,1)S(1)}, bf16[4,12,32,128]{3,2,1,0:T(8,128)(2,1)S(1)}, u32[]{:S(2)}, u32[]{:S(2)}) collective-permute-start(bf16[4,12,32,128]{3,2,1,0:T(8,128)(2,1)S(1)} %get-tuple-element.32), channel_id=1, source_target_pairs={{0,4},{4,0},{8,12},{12,8},{16,20},{20,16},{24,28},{28,24},{1,5},{5... | collective-permute-start | bytes 1179656 | tf_op jit(solution)/shard_map/ppermute | solution.py:563
  3.0 6.6 %collective-permute-start.2 = (bf16[2,30,512]{2,1,0:T(8,128)(2,1)S(1)}, bf16[2,30,512]{2,1,0:T(8,128)(2,1)S(1)}, u32[]{:S(2)}, u32[]{:S(2)}) collective-permute-start(bf16[2,30,512]{2,1,0:T(8,128)(2,1)S(1)} %pair_waves.1.pair), channel_id=1, source_target_pairs={{0,24},{4,20},{8,16},{12,28},{16,8},{20,4},{24,0},{28,12},{1,25},{... | collective-permute-start | bytes 184328 | tf_op jit(solution)/shard_map/ppermute | solution.py:584
  5.4 4.2 %collective-permute-start.1 = (bf16[30,512]{1,0:T(8,128)(2,1)S(1)}, bf16[30,512]{1,0:T(8,128)(2,1)S(1)}, u32[]{:S(2)}, u32[]{:S(2)}) collective-permute-start(bf16[30,512]{1,0:T(8,128)(2,1)S(1)} %copy-done), channel_id=1, source_target_pairs={{0,8},{4,12},{8,0},{12,4},{16,24},{20,28},{24,16},{28,20},{1,9},{5... | collective-permute-start | bytes 92168 | tf_op jit(solution)/shard_map/ppermute | solution.py:566
  6.9 9.8 %collective-permute-start.5 = (bf16[12,32,128]{2,1,0:T(8,128)(2,1)S(1)}, bf16[12,32,128]{2,1,0:T(8,128)(2,1)S(1)}, u32[]{:S(2)}, u32[]{:S(2)}) collective-permute-start(bf16[12,32,128]{2,1,0:T(8,128)(2,1)S(1)} %get-tuple-element.33), channel_id=1, source_target_pairs={{0,16},{4,20},{8,24},{12,28},{16,0},{20,4},{24,8},{28,12},{1,17},{... | collective-permute-start | bytes 294920 | tf_op jit(solution)/shard_map/ppermute | solution.py:566
  7.3 9.4 %collective-permute-start.6 = (bf16[12,32,128]{2,1,0:T(8,128)(2,1)S(1)}, bf16[12,32,128]{2,1,0:T(8,128)(2,1)S(1)}, u32[]{:S(2)}, u32[]{:S(2)}) collective-permute-start(bf16[12,32,128]{2,1,0:T(8,128)(2,1)S(1)} %get-tuple-element.34), channel_id=1, source_target_pairs={{0,24},{4,28},{8,16},{12,20},{16,8},{20,12},{24,0},{28,4},{1,25},{... | collective-permute-start | bytes 294920 | tf_op jit(solution)/shard_map/ppermute | solution.py:566
  9.2 7.5 %collective-permute-start.7 = (bf16[12,32,128]{2,1,0:T(8,128)(2,1)S(1)}, bf16[12,32,128]{2,1,0:T(8,128)(2,1)S(1)}, u32[]{:S(2)}, u32[]{:S(2)}) collective-permute-start(bf16[12,32,128]{2,1,0:T(8,128)(2,1)S(1)} %get-tuple-element.36), channel_id=1, source_target_pairs={{0,8},{4,12},{8,0},{12,4},{16,24},{20,28},{24,16},{28,20},{1,9},{5... | collective-permute-start | bytes 294920 | tf_op jit(solution)/shard_map/ppermute | solution.py:566
  9.7 3.2 %collective-permute-start.3 = (bf16[3,30,512]{2,1,0:T(8,128)(2,1)S(1)}, bf16[3,30,512]{2,1,0:T(8,128)(2,1)S(1)}, u32[]{:S(2)}, u32[]{:S(2)}) collective-permute-start(bf16[3,30,512]{2,1,0:T(8,128)(2,1)S(1)} %choose_waves.1), channel_id=1, source_target_pairs={{0,4},{4,0},{8,12},{12,8},{16,20},{20,16},{24,28},{28,24},{1,5},{5... | collective-permute-start | bytes 276488 | tf_op jit(solution)/shard_map/ppermute | solution.py:563
  16.8 3.6 %collective-permute-start.8 = (bf16[12,32,128]{2,1,0:T(8,128)(2,1)S(1)}, bf16[12,32,128]{2,1,0:T(8,128)(2,1)S(1)}, u32[]{:S(2)}, u32[]{:S(2)}) collective-permute-start(bf16[12,32,128]{2,1,0:T(8,128)(2,1)S(1)} %choose_piece.1.piece), channel_id=1, source_target_pairs={{0,4},{4,0},{8,12},{12,8},{16,20},{20,16},{24,28},{28,24},{1,5},{5... | collective-permute-start | bytes 294920 | tf_op jit(solution)/shard_map/ppermute | solution.py:563
  22.5 9.0 %collective-permute-start.9 = (bf16[128,256]{1,0:T(8,128)(2,1)S(1)}, bf16[128,256]{1,0:T(8,128)(2,1)S(1)}, u32[]{:S(2)}, u32[]{:S(2)}) collective-permute-start(bf16[128,256]{1,0:T(8,128)(2,1)S(1)} %get-tuple-element.43), channel_id=1, source_target_pairs={{0,0},{1,8},{2,4},{3,12},{4,16},{5,24},{6,20},{7,28},{8,1},{9,9},{... | collective-permute-start | bytes 196616 | tf_op jit(solution)/shard_map/ppermute | solution.py:607
  26.2 5.8 %collective-permute-start.10 = (bf16[128,256]{1,0:T(8,128)(2,1)S(1)}, bf16[128,256]{1,0:T(8,128)(2,1)S(1)}, u32[]{:S(2)}, u32[]{:S(2)}) collective-permute-start(bf16[128,256]{1,0:T(8,128)(2,1)S(1)} %get-tuple-element.44), channel_id=1, source_target_pairs={{0,8},{1,0},{2,12},{3,4},{4,24},{5,16},{6,28},{7,20},{8,9},{9,1},{... | collective-permute-start | bytes 196616 | tf_op jit(solution)/shard_map/ppermute | solution.py:607
  32.0 2.4 %collective-permute-start.11 = (f32[64,256]{1,0:T(8,128)S(1)}, f32[64,256]{1,0:T(8,128)S(1)}, u32[]{:S(2)}, u32[]{:S(2)}) collective-permute-start(f32[64,256]{1,0:T(8,128)S(1)} %get-tuple-element.46), channel_id=1, source_target_pairs={{0,4},{4,0},{8,12},{12,8},{16,20},{20,16},{24,28},{28,24},{1,5},{5... | collective-permute-start | bytes 196616 | tf_op jit(solution)/shard_map/ppermute | solution.py:563

commit v21 on v20

--- a/solution.py
+++ b/solution.py
@@ -459,7 +459,7 @@
         outs[0][...] = total[...]
         return
     rows_out = outs[0].shape[0]
-    station = lax.axis_index("sta") % len(outs)
+    station = lax.axis_index("sta") // 2
     for step, out in enumerate(outs):
         part = jnp.bitwise_xor(station, step)
         out[...] = total[pl.ds(pl.multiple_of(part * rows_out, rows_out), rows_out), :].astype(
@@ -602,8 +602,8 @@
         route = []
         for d in range(count_tm):
             for s in range(count_sta):
-                dest = near * (d % 2) + (s % near ^ step)
-                route.append((d * count_sta + s, (2 * dest + s // near) * count_sta + d // 2))
+                dest = near * (d % 2) + (s // 2 ^ step)
+                route.append((d * count_sta + s, (2 * dest + s % 2) * count_sta + d // 2))
         gathered.append(lax.ppermute(parts[step], ("tm", "sta"), route))
     ours, send = add(gathered)
     return finish(group, samples, ours, swap(send))

time: 35.4 us -> 35.2 us (level)
  no operation moved by 1% of the time
where the time goes in v21:
time: 35.2 us; the launch traced here: 34.9 us
  starting transfers between devices  17.7 us (50%)
  Pallas kernels  9.31 us (26%)
  waiting for transfers between devices  7.87 us (22%)
    ppermute x5, starting transfers between devices, swap(): return lax.ppermute(array, 'tm', [(i, i ^ 1) for i in range(count_tm)])  5.78 us
    ppermute x2, starting transfers between devices, shards(): gathered.append(lax.ppermute(parts[step], ('tm', 'sta'), route))  5.5 us
    pallas_call x2, Pallas kernels, correlate(): pl.pallas_call(functools.partial(main_kernel, side, tlen, group), out_sha...  4.08 us
    ppermute x4, starting transfers between devices, across(): lax.ppermute(array, 'tm', [(i, i ^ 2 * step) for i in range(count_tm)])  4.01 us
    ppermute x2, waiting for transfers between devices, shards(): gathered.append(lax.ppermute(parts[step], ('tm', 'sta'), route))  3.99 us
    ppermute x1, starting transfers between devices, shards(): far.append(lax.ppermute(pair, 'tm', route))  2.37 us
    pallas_call x1, Pallas kernels, pack(): pl.pallas_call(pack_kernel, out_shape=[jax.ShapeDtypeStruct(shape, jnp.bf...  2.18 us
    ppermute x4, waiting for transfers between devices, across(): lax.ppermute(array, 'tm', [(i, i ^ 2 * step) for i in range(count_tm)])  2.02 us
  transfers between devices with their start and end apart: 12, of which 5 were waited for; matrix products, arithmetic and copies ran while one was open for 0% of the time, Pallas kernels for 18%

profile of v21, /device:TPU:7, one launch (start us, length us, event | category | flops | bytes accessed | tf_op | source)
XLA Modules:
  0.0 34.9 jit_solution(9896916892704160922)
XLA Ops:
  0.0 0.7 %collective-permute-start = (bf16[30,512]{1,0:T(8,128)(2,1)}, bf16[30,512]{1,0:T(8,128)(2,1)S(1)}, u32[]{:S(2)}, u32[]{:S(2)}) collective-permute-start(bf16[30,512]{1,0:T(8,128)(2,1)} %own.1), channel_id=1, source_target_pairs={{0,4},{4,0},{8,12},{12,8},{16,20},{20,16},{24,28},{28,24},{1,5},{5... | collective-permute-start | bytes 92168 | tf_op jit(solution)/shard_map/ppermute | solution.py:563
  0.7 0.0 copy-start
  0.7 2.2 %pack.1 = (bf16[4,12,32,128]{3,2,1,0:T(8,128)(2,1)S(1)}, bf16[4,12,32,128]{3,2,1,0:T(8,128)(2,1)S(1)}, s32[8,128]{1,0:T(8,128)S(1)}) custom-call(s32[2]{0:T(128)} %bank_blocks.1, bf16[2,30,64,100]{3,2,1,0:T(8,128)(2,1)} %bitcast.3, s32[30,2,64]{2,1,0:T(2,128)} %bitcast.4, s32[30,2,64]{2,1,0:T(2,128)} %bitcast.5), custom_call_target="tpu_custom_call" | custom-call | flops 2000000000 | bytes 2000000 | tf_op jit(solution)/shard_map/pack/pallas_call | solution.py:100
  2.9 0.0 collective-permute-done.partner
  2.9 0.1 collective-permute-start.4
  3.0 0.0 copy-done
  3.0 2.4 %collective-permute-start.2 = (bf16[2,30,512]{2,1,0:T(8,128)(2,1)S(1)}, bf16[2,30,512]{2,1,0:T(8,128)(2,1)S(1)}, u32[]{:S(2)}, u32[]{:S(2)}) collective-permute-start(bf16[2,30,512]{2,1,0:T(8,128)(2,1)S(1)} %pair_waves.1.pair), channel_id=1, source_target_pairs={{0,24},{4,20},{8,16},{12,28},{16,8},{20,4},{24,0},{28,12},{1,25},{... | collective-permute-start | bytes 184328 | tf_op jit(solution)/shard_map/ppermute | solution.py:584
  5.4 1.3 %collective-permute-start.1 = (bf16[30,512]{1,0:T(8,128)(2,1)S(1)}, bf16[30,512]{1,0:T(8,128)(2,1)S(1)}, u32[]{:S(2)}, u32[]{:S(2)}) collective-permute-start(bf16[30,512]{1,0:T(8,128)(2,1)S(1)} %copy-done), channel_id=1, source_target_pairs={{0,8},{4,12},{8,0},{12,4},{16,24},{20,28},{24,16},{28,20},{1,9},{5... | collective-permute-start | bytes 92168 | tf_op jit(solution)/shard_map/ppermute | solution.py:566
  6.7 0.0 collective-permute-done.4.other
  6.7 0.2 merge.1
  6.9 0.4 %collective-permute-start.5 = (bf16[12,32,128]{2,1,0:T(8,128)(2,1)S(1)}, bf16[12,32,128]{2,1,0:T(8,128)(2,1)S(1)}, u32[]{:S(2)}, u32[]{:S(2)}) collective-permute-start(bf16[12,32,128]{2,1,0:T(8,128)(2,1)S(1)} %get-tuple-element.33), channel_id=1, source_target_pairs={{0,16},{4,20},{8,24},{12,28},{16,0},{20,4},{24,8},{28,12},{1,17},{... | collective-permute-start | bytes 294920 | tf_op jit(solution)/shard_map/ppermute | solution.py:566
  7.3 1.9 %collective-permute-start.6 = (bf16[12,32,128]{2,1,0:T(8,128)(2,1)S(1)}, bf16[12,32,128]{2,1,0:T(8,128)(2,1)S(1)}, u32[]{:S(2)}, u32[]{:S(2)}) collective-permute-start(bf16[12,32,128]{2,1,0:T(8,128)(2,1)S(1)} %get-tuple-element.34), channel_id=1, source_target_pairs={{0,24},{4,28},{8,16},{12,20},{16,8},{20,12},{24,0},{28,4},{1,25},{... | collective-permute-start | bytes 294920 | tf_op jit(solution)/shard_map/ppermute | solution.py:566
  9.2 0.4 %collective-permute-start.7 = (bf16[12,32,128]{2,1,0:T(8,128)(2,1)S(1)}, bf16[12,32,128]{2,1,0:T(8,128)(2,1)S(1)}, u32[]{:S(2)}, u32[]{:S(2)}) collective-permute-start(bf16[12,32,128]{2,1,0:T(8,128)(2,1)S(1)} %get-tuple-element.36), channel_id=1, source_target_pairs={{0,8},{4,12},{8,0},{12,4},{16,24},{20,28},{24,16},{28,20},{1,9},{5... | collective-permute-start | bytes 294920 | tf_op jit(solution)/shard_map/ppermute | solution.py:566
  9.6 0.0 collective-permute-done.1.beside
  9.6 0.0 collective-permute-done.2.rest_0_
  9.7 2.3 %collective-permute-start.3 = (bf16[3,30,512]{2,1,0:T(8,128)(2,1)S(1)}, bf16[3,30,512]{2,1,0:T(8,128)(2,1)S(1)}, u32[]{:S(2)}, u32[]{:S(2)}) collective-permute-start(bf16[3,30,512]{2,1,0:T(8,128)(2,1)S(1)} %choose_waves.1), channel_id=1, source_target_pairs={{0,4},{4,0},{8,12},{12,8},{16,20},{20,16},{24,28},{28,24},{1,5},{5... | collective-permute-start | bytes 276488 | tf_op jit(solution)/shard_map/ppermute | solution.py:563
  11.9 0.9 %collective-permute-done.3.swapped = bf16[3,30,512]{2,1,0:T(8,128)(2,1)S(1)} collective-permute-done((bf16[3,30,512]{2,1,0:T(8,128)(2,1)S(1)}, bf16[3,30,512]{2,1,0:T(8,128)(2,1)S(1)}, u32[]{:S(2)}, u32[]{:S(2)}) %collective-permute-start.3) | collective-permute-done | bytes 92192 | tf_op jit(solution)/shard_map/ppermute | solution.py:563
  12.9 1.8 %prepare_waves.1 = (bf16[30,272,128]{2,1,0:T(8,128)(2,1)S(1)}, f32[32,32,128]{2,1,0:T(8,128)S(1)}) custom-call(bf16[3,30,512]{2,1,0:T(8,128)(2,1)S(1)} %collective-permute-done.3.swapped, bf16[2,30,512]{2,1,0:T(8,128)(2,1)S(1)} %pair_waves.1.pair, bf16[30,512]{1,0:T(8,128)(2,1)S(1)} %collective-permute-done.1.beside, ...), custom_call_target="tpu_custom_call" | custom-call | flops 50000000 | bytes 50000 | tf_op jit(solution)/shard_map/prepare_waves/pallas_call | solution.py:302
  14.7 2.0 %collective-permute-done.5.refs_2_ = bf16[12,32,128]{2,1,0:T(8,128)(2,1)S(1)} collective-permute-done((bf16[12,32,128]{2,1,0:T(8,128)(2,1)S(1)}, bf16[12,32,128]{2,1,0:T(8,128)(2,1)S(1)}, u32[]{:S(2)}, u32[]{:S(2)}) %collective-permute-start.5) | collective-permute-done | bytes 98336 | tf_op jit(solution)/shard_map/ppermute | solution.py:566
  16.7 0.0 collective-permute-done.6.refs_3_
  16.7 0.0 collective-permute-done.7.refs_1_
  16.7 0.1 choose_piece.1.piece
  16.8 1.6 %collective-permute-start.8 = (bf16[12,32,128]{2,1,0:T(8,128)(2,1)S(1)}, bf16[12,32,128]{2,1,0:T(8,128)(2,1)S(1)}, u32[]{:S(2)}, u32[]{:S(2)}) collective-permute-start(bf16[12,32,128]{2,1,0:T(8,128)(2,1)S(1)} %choose_piece.1.piece), channel_id=1, source_target_pairs={{0,4},{4,0},{8,12},{12,8},{16,20},{20,16},{24,28},{28,24},{1,5},{5... | collective-permute-start | bytes 294920 | tf_op jit(solution)/shard_map/ppermute | solution.py:563
  18.4 2.0 %correlate_first.1.rest_0_ = f32[256,256]{1,0:T(8,128)S(1)} custom-call(bf16[12,32,128]{2,1,0:T(8,128)(2,1)S(1)} %choose_piece.1.piece, bf16[30,272,128]{2,1,0:T(8,128)(2,1)S(1)} %get-tuple-element.41.left_a, f32[32,32,128]{2,1,0:T(8,128)S(1)} %get-tuple-element.42.inverse), custom_call_target="tpu_custom_call" | custom-call | flops 3000000000 | bytes 3000000 | tf_op jit(solution)/shard_map/correlate_first/pallas_call | solution.py:479
  20.4 0.0 collective-permute-done.8.piece
  20.4 2.1 %correlate_second.1 = (bf16[128,256]{1,0:T(8,128)(2,1)S(1)}, bf16[128,256]{1,0:T(8,128)(2,1)S(1)}) custom-call(bf16[12,32,128]{2,1,0:T(8,128)(2,1)S(1)} %collective-permute-done.8.piece, bf16[30,272,128]{2,1,0:T(8,128)(2,1)S(1)} %get-tuple-element.41.left_a, f32[32,32,128]{2,1,0:T(8,128)S(1)} %get-tuple-element.42.inverse, f32[256,256]{1,0:T(8,128)S(1)} %correlate_first.1.rest_0_), custom_call_target="tpu_custom_call" | custom-call | flops 3000000000 | bytes 3000000 | tf_op jit(solution)/shard_map/correlate_second/pallas_call | solution.py:479
  22.5 3.6 %collective-permute-start.9 = (bf16[128,256]{1,0:T(8,128)(2,1)S(1)}, bf16[128,256]{1,0:T(8,128)(2,1)S(1)}, u32[]{:S(2)}, u32[]{:S(2)}) collective-permute-start(bf16[128,256]{1,0:T(8,128)(2,1)S(1)} %get-tuple-element.43), channel_id=1, source_target_pairs={{0,0},{1,4},{2,8},{3,12},{4,16},{5,20},{6,24},{7,28},{8,1},{9,5},{... | collective-permute-start | bytes 196616 | tf_op jit(solution)/shard_map/ppermute | solution.py:607
  26.1 1.9 %collective-permute-start.10 = (bf16[128,256]{1,0:T(8,128)(2,1)S(1)}, bf16[128,256]{1,0:T(8,128)(2,1)S(1)}, u32[]{:S(2)}, u32[]{:S(2)}) collective-permute-start(bf16[128,256]{1,0:T(8,128)(2,1)S(1)} %get-tuple-element.44), channel_id=1, source_target_pairs={{0,8},{1,12},{2,0},{3,4},{4,24},{5,28},{6,16},{7,20},{8,9},{9,13},... | collective-permute-start | bytes 196616 | tf_op jit(solution)/shard_map/ppermute | solution.py:607
  28.0 3.5 %collective-permute-done.9.refs_0_ = bf16[128,256]{1,0:T(8,128)(2,1)S(1)} collective-permute-done((bf16[128,256]{1,0:T(8,128)(2,1)S(1)}, bf16[128,256]{1,0:T(8,128)(2,1)S(1)}, u32[]{:S(2)}, u32[]{:S(2)}) %collective-permute-start.9) | collective-permute-done | bytes 65568 | tf_op jit(solution)/shard_map/ppermute | solution.py:607
  31.5 0.5 %collective-permute-done.10.refs_1_ = bf16[128,256]{1,0:T(8,128)(2,1)S(1)} collective-permute-done((bf16[128,256]{1,0:T(8,128)(2,1)S(1)}, bf16[128,256]{1,0:T(8,128)(2,1)S(1)}, u32[]{:S(2)}, u32[]{:S(2)}) %collective-permute-start.10) | collective-permute-done | bytes 65568 | tf_op jit(solution)/shard_map/ppermute | solution.py:607
  32.0 1.2 %collective-permute-start.11 = (f32[64,256]{1,0:T(8,128)S(1)}, f32[64,256]{1,0:T(8,128)S(1)}, u32[]{:S(2)}, u32[]{:S(2)}) collective-permute-start(f32[64,256]{1,0:T(8,128)S(1)} %get-tuple-element.46), channel_id=1, source_target_pairs={{0,4},{4,0},{8,12},{12,8},{16,20},{20,16},{24,28},{28,24},{1,5},{5... | collective-permute-start | bytes 196616 | tf_op jit(solution)/shard_map/ppermute | solution.py:563
  33.1 0.9 %collective-permute-done.11.received = f32[64,256]{1,0:T(8,128)S(1)} collective-permute-done((f32[64,256]{1,0:T(8,128)S(1)}, f32[64,256]{1,0:T(8,128)S(1)}, u32[]{:S(2)}, u32[]{:S(2)}) %collective-permute-start.11) | collective-permute-done | bytes 65568 | tf_op jit(solution)/shard_map/ppermute | solution.py:563
  34.1 0.9 %finish.1 = f32[32,512]{1,0:T(8,128)} custom-call(f32[64,256]{1,0:T(8,128)S(1)} %get-tuple-element.45.ours, f32[64,256]{1,0:T(8,128)S(1)} %collective-permute-done.11.received), custom_call_target="tpu_custom_call" | custom-call | flops 1000000000 | bytes 1000000 | tf_op jit(solution)/shard_map/finish/pallas_call | solution.py:542
  (3 shorter events, 0.1 us)
Async XLA Ops:
  0.0 2.9 %collective-permute-start = (bf16[30,512]{1,0:T(8,128)(2,1)}, bf16[30,512]{1,0:T(8,128)(2,1)S(1)}, u32[]{:S(2)}, u32[]{:S(2)}) collective-permute-start(bf16[30,512]{1,0:T(8,128)(2,1)} %own.1), channel_id=1, source_target_pairs={{0,4},{4,0},{8,12},{12,8},{16,20},{20,16},{24,28},{28,24},{1,5},{5... | collective-permute-start | bytes 92168 | tf_op jit(solution)/shard_map/ppermute | solution.py:563
  0.7 2.3 %copy-start = (bf16[30,512]{1,0:T(8,128)(2,1)S(1)}, bf16[30,512]{1,0:T(8,128)(2,1)}, u32[]{:S(2)}) copy-start(bf16[30,512]{1,0:T(8,128)(2,1)} %own.1) | copy-start | bytes 92164
  2.9 3.8 %collective-permute-start.4 = (bf16[4,12,32,128]{3,2,1,0:T(8,128)(2,1)S(1)}, bf16[4,12,32,128]{3,2,1,0:T(8,128)(2,1)S(1)}, u32[]{:S(2)}, u32[]{:S(2)}) collective-permute-start(bf16[4,12,32,128]{3,2,1,0:T(8,128)(2,1)S(1)} %get-tuple-element.32), channel_id=1, source_target_pairs={{0,4},{4,0},{8,12},{12,8},{16,20},{20,16},{24,28},{28,24},{1,5},{5... | collective-permute-start | bytes 1179656 | tf_op jit(solution)/shard_map/ppermute | solution.py:563
  3.0 6.6 %collective-permute-start.2 = (bf16[2,30,512]{2,1,0:T(8,128)(2,1)S(1)}, bf16[2,30,512]{2,1,0:T(8,128)(2,1)S(1)}, u32[]{:S(2)}, u32[]{:S(2)}) collective-permute-start(bf16[2,30,512]{2,1,0:T(8,128)(2,1)S(1)} %pair_waves.1.pair), channel_id=1, source_target_pairs={{0,24},{4,20},{8,16},{12,28},{16,8},{20,4},{24,0},{28,12},{1,25},{... | collective-permute-start | bytes 184328 | tf_op jit(solution)/shard_map/ppermute | solution.py:584
  5.4 4.2 %collective-permute-start.1 = (bf16[30,512]{1,0:T(8,128)(2,1)S(1)}, bf16[30,512]{1,0:T(8,128)(2,1)S(1)}, u32[]{:S(2)}, u32[]{:S(2)}) collective-permute-start(bf16[30,512]{1,0:T(8,128)(2,1)S(1)} %copy-done), channel_id=1, source_target_pairs={{0,8},{4,12},{8,0},{12,4},{16,24},{20,28},{24,16},{28,20},{1,9},{5... | collective-permute-start | bytes 92168 | tf_op jit(solution)/shard_map/ppermute | solution.py:566
  6.9 9.8 %collective-permute-start.5 = (bf16[12,32,128]{2,1,0:T(8,128)(2,1)S(1)}, bf16[12,32,128]{2,1,0:T(8,128)(2,1)S(1)}, u32[]{:S(2)}, u32[]{:S(2)}) collective-permute-start(bf16[12,32,128]{2,1,0:T(8,128)(2,1)S(1)} %get-tuple-element.33), channel_id=1, source_target_pairs={{0,16},{4,20},{8,24},{12,28},{16,0},{20,4},{24,8},{28,12},{1,17},{... | collective-permute-start | bytes 294920 | tf_op jit(solution)/shard_map/ppermute | solution.py:566
  7.3 9.4 %collective-permute-start.6 = (bf16[12,32,128]{2,1,0:T(8,128)(2,1)S(1)}, bf16[12,32,128]{2,1,0:T(8,128)(2,1)S(1)}, u32[]{:S(2)}, u32[]{:S(2)}) collective-permute-start(bf16[12,32,128]{2,1,0:T(8,128)(2,1)S(1)} %get-tuple-element.34), channel_id=1, source_target_pairs={{0,24},{4,28},{8,16},{12,20},{16,8},{20,12},{24,0},{28,4},{1,25},{... | collective-permute-start | bytes 294920 | tf_op jit(solution)/shard_map/ppermute | solution.py:566
  9.2 7.5 %collective-permute-start.7 = (bf16[12,32,128]{2,1,0:T(8,128)(2,1)S(1)}, bf16[12,32,128]{2,1,0:T(8,128)(2,1)S(1)}, u32[]{:S(2)}, u32[]{:S(2)}) collective-permute-start(bf16[12,32,128]{2,1,0:T(8,128)(2,1)S(1)} %get-tuple-element.36), channel_id=1, source_target_pairs={{0,8},{4,12},{8,0},{12,4},{16,24},{20,28},{24,16},{28,20},{1,9},{5... | collective-permute-start | bytes 294920 | tf_op jit(solution)/shard_map/ppermute | solution.py:566
  9.7 3.2 %collective-permute-start.3 = (bf16[3,30,512]{2,1,0:T(8,128)(2,1)S(1)}, bf16[3,30,512]{2,1,0:T(8,128)(2,1)S(1)}, u32[]{:S(2)}, u32[]{:S(2)}) collective-permute-start(bf16[3,30,512]{2,1,0:T(8,128)(2,1)S(1)} %choose_waves.1), channel_id=1, source_target_pairs={{0,4},{4,0},{8,12},{12,8},{16,20},{20,16},{24,28},{28,24},{1,5},{5... | collective-permute-start | bytes 276488 | tf_op jit(solution)/shard_map/ppermute | solution.py:563
  16.8 3.6 %collective-permute-start.8 = (bf16[12,32,128]{2,1,0:T(8,128)(2,1)S(1)}, bf16[12,32,128]{2,1,0:T(8,128)(2,1)S(1)}, u32[]{:S(2)}, u32[]{:S(2)}) collective-permute-start(bf16[12,32,128]{2,1,0:T(8,128)(2,1)S(1)} %choose_piece.1.piece), channel_id=1, source_target_pairs={{0,4},{4,0},{8,12},{12,8},{16,20},{20,16},{24,28},{28,24},{1,5},{5... | collective-permute-start | bytes 294920 | tf_op jit(solution)/shard_map/ppermute | solution.py:563
  22.5 9.0 %collective-permute-start.9 = (bf16[128,256]{1,0:T(8,128)(2,1)S(1)}, bf16[128,256]{1,0:T(8,128)(2,1)S(1)}, u32[]{:S(2)}, u32[]{:S(2)}) collective-permute-start(bf16[128,256]{1,0:T(8,128)(2,1)S(1)} %get-tuple-element.43), channel_id=1, source_target_pairs={{0,0},{1,4},{2,8},{3,12},{4,16},{5,20},{6,24},{7,28},{8,1},{9,5},{... | collective-permute-start | bytes 196616 | tf_op jit(solution)/shard_map/ppermute | solution.py:607
  26.1 5.8 %collective-permute-start.10 = (bf16[128,256]{1,0:T(8,128)(2,1)S(1)}, bf16[128,256]{1,0:T(8,128)(2,1)S(1)}, u32[]{:S(2)}, u32[]{:S(2)}) collective-permute-start(bf16[128,256]{1,0:T(8,128)(2,1)S(1)} %get-tuple-element.44), channel_id=1, source_target_pairs={{0,8},{1,12},{2,0},{3,4},{4,24},{5,28},{6,16},{7,20},{8,9},{9,13},... | collective-permute-start | bytes 196616 | tf_op jit(solution)/shard_map/ppermute | solution.py:607
  32.0 2.1 %collective-permute-start.11 = (f32[64,256]{1,0:T(8,128)S(1)}, f32[64,256]{1,0:T(8,128)S(1)}, u32[]{:S(2)}, u32[]{:S(2)}) collective-permute-start(f32[64,256]{1,0:T(8,128)S(1)} %get-tuple-element.46), channel_id=1, source_target_pairs={{0,4},{4,0},{8,12},{12,8},{16,20},{20,16},{24,28},{28,24},{1,5},{5... | collective-permute-start | bytes 196616 | tf_op jit(solution)/shard_map/ppermute | solution.py:563

commit v22 on v21

--- a/solution.py
+++ b/solution.py
@@ -461,7 +461,7 @@
     rows_out = outs[0].shape[0]
     station = lax.axis_index("sta") // 2
     for step, out in enumerate(outs):
-        part = jnp.bitwise_xor(station, step)
+        part = jnp.bitwise_xor(station, len(outs) - 1 - step)
         out[...] = total[pl.ds(pl.multiple_of(part * rows_out, rows_out), rows_out), :].astype(
             jnp.bfloat16
         )
@@ -602,7 +602,7 @@
         route = []
         for d in range(count_tm):
             for s in range(count_sta):
-                dest = near * (d % 2) + (s // 2 ^ step)
+                dest = near * (d % 2) + (s // 2 ^ (near - 1 - step))
                 route.append((d * count_sta + s, (2 * dest + s % 2) * count_sta + d // 2))
         gathered.append(lax.ppermute(parts[step], ("tm", "sta"), route))
     ours, send = add(gathered)

time: 35.2 us -> 35.5 us (level)
  waiting for transfers between devices: 7.87 us -> 9.07 us
  starting transfers between devices: 17.7 us -> 16.8 us
    ppermute x5, starting transfers between devices: 5.78 us -> 4.69 us  [swap(): return lax.ppermute(array, 'tm', [(i, i ^ 1) for i in range(count_tm)])]
    ppermute x2, waiting for transfers between devices: 3.99 us -> 4.85 us  [shards(): gathered.append(lax.ppermute(parts[step], ('tm', 'sta'), route))]
where the time goes in v22:
time: 35.5 us; the launch traced here: 35.3 us
  starting transfers between devices  16.8 us (47%)
  Pallas kernels  9.31 us (26%)
  waiting for transfers between devices  9.07 us (26%)
    ppermute x2, starting transfers between devices, shards(): gathered.append(lax.ppermute(parts[step], ('tm', 'sta'), route))  5.75 us
    ppermute x2, waiting for transfers between devices, shards(): gathered.append(lax.ppermute(parts[step], ('tm', 'sta'), route))  4.85 us
    ppermute x5, starting transfers between devices, swap(): return lax.ppermute(array, 'tm', [(i, i ^ 1) for i in range(count_tm)])  4.69 us
    pallas_call x2, Pallas kernels, correlate(): pl.pallas_call(functools.partial(main_kernel, side, tlen, group), out_sha...  4.08 us
    ppermute x4, starting transfers between devices, across(): lax.ppermute(array, 'tm', [(i, i ^ 2 * step) for i in range(count_tm)])  4.01 us
    ppermute x1, starting transfers between devices, shards(): far.append(lax.ppermute(pair, 'tm', route))  2.37 us
    ppermute x5, waiting for transfers between devices, swap(): return lax.ppermute(array, 'tm', [(i, i ^ 1) for i in range(count_tm)])  2.19 us
    pallas_call x1, Pallas kernels, pack(): pl.pallas_call(pack_kernel, out_shape=[jax.ShapeDtypeStruct(shape, jnp.bf...  2.18 us
  transfers between devices with their start and end apart: 12, of which 5 were waited for; matrix products, arithmetic and copies ran while one was open for 0% of the time, Pallas kernels for 18%

profile of v22, /device:TPU:7, one launch (start us, length us, event | category | flops | bytes accessed | tf_op | source)
XLA Modules:
  0.0 35.3 jit_solution(16017987143607637781)
XLA Ops:
  0.0 0.7 %collective-permute-start = (bf16[30,512]{1,0:T(8,128)(2,1)}, bf16[30,512]{1,0:T(8,128)(2,1)S(1)}, u32[]{:S(2)}, u32[]{:S(2)}) collective-permute-start(bf16[30,512]{1,0:T(8,128)(2,1)} %own.1), channel_id=1, source_target_pairs={{0,4},{4,0},{8,12},{12,8},{16,20},{20,16},{24,28},{28,24},{1,5},{5... | collective-permute-start | bytes 92168 | tf_op jit(solution)/shard_map/ppermute | solution.py:563
  0.7 0.0 copy-start
  0.7 2.2 %pack.1 = (bf16[4,12,32,128]{3,2,1,0:T(8,128)(2,1)S(1)}, bf16[4,12,32,128]{3,2,1,0:T(8,128)(2,1)S(1)}, s32[8,128]{1,0:T(8,128)S(1)}) custom-call(s32[2]{0:T(128)} %bank_blocks.1, bf16[2,30,64,100]{3,2,1,0:T(8,128)(2,1)} %bitcast.3, s32[30,2,64]{2,1,0:T(2,128)} %bitcast.4, s32[30,2,64]{2,1,0:T(2,128)} %bitcast.5), custom_call_target="tpu_custom_call" | custom-call | flops 2000000000 | bytes 2000000 | tf_op jit(solution)/shard_map/pack/pallas_call | solution.py:100
  2.9 0.0 collective-permute-done.partner
  2.9 0.1 collective-permute-start.4
  3.0 0.0 copy-done
  3.0 2.4 %collective-permute-start.2 = (bf16[2,30,512]{2,1,0:T(8,128)(2,1)S(1)}, bf16[2,30,512]{2,1,0:T(8,128)(2,1)S(1)}, u32[]{:S(2)}, u32[]{:S(2)}) collective-permute-start(bf16[2,30,512]{2,1,0:T(8,128)(2,1)S(1)} %pair_waves.1.pair), channel_id=1, source_target_pairs={{0,24},{4,20},{8,16},{12,28},{16,8},{20,4},{24,0},{28,12},{1,25},{... | collective-permute-start | bytes 184328 | tf_op jit(solution)/shard_map/ppermute | solution.py:584
  5.4 1.3 %collective-permute-start.1 = (bf16[30,512]{1,0:T(8,128)(2,1)S(1)}, bf16[30,512]{1,0:T(8,128)(2,1)S(1)}, u32[]{:S(2)}, u32[]{:S(2)}) collective-permute-start(bf16[30,512]{1,0:T(8,128)(2,1)S(1)} %copy-done), channel_id=1, source_target_pairs={{0,8},{4,12},{8,0},{12,4},{16,24},{20,28},{24,16},{28,20},{1,9},{5... | collective-permute-start | bytes 92168 | tf_op jit(solution)/shard_map/ppermute | solution.py:566
  6.7 0.0 collective-permute-done.4.other
  6.7 0.2 merge.1
  6.9 0.4 %collective-permute-start.5 = (bf16[12,32,128]{2,1,0:T(8,128)(2,1)S(1)}, bf16[12,32,128]{2,1,0:T(8,128)(2,1)S(1)}, u32[]{:S(2)}, u32[]{:S(2)}) collective-permute-start(bf16[12,32,128]{2,1,0:T(8,128)(2,1)S(1)} %get-tuple-element.33), channel_id=1, source_target_pairs={{0,16},{4,20},{8,24},{12,28},{16,0},{20,4},{24,8},{28,12},{1,17},{... | collective-permute-start | bytes 294920 | tf_op jit(solution)/shard_map/ppermute | solution.py:566
  7.3 1.9 %collective-permute-start.6 = (bf16[12,32,128]{2,1,0:T(8,128)(2,1)S(1)}, bf16[12,32,128]{2,1,0:T(8,128)(2,1)S(1)}, u32[]{:S(2)}, u32[]{:S(2)}) collective-permute-start(bf16[12,32,128]{2,1,0:T(8,128)(2,1)S(1)} %get-tuple-element.34), channel_id=1, source_target_pairs={{0,24},{4,28},{8,16},{12,20},{16,8},{20,12},{24,0},{28,4},{1,25},{... | collective-permute-start | bytes 294920 | tf_op jit(solution)/shard_map/ppermute | solution.py:566
  9.2 0.4 %collective-permute-start.7 = (bf16[12,32,128]{2,1,0:T(8,128)(2,1)S(1)}, bf16[12,32,128]{2,1,0:T(8,128)(2,1)S(1)}, u32[]{:S(2)}, u32[]{:S(2)}) collective-permute-start(bf16[12,32,128]{2,1,0:T(8,128)(2,1)S(1)} %get-tuple-element.36), channel_id=1, source_target_pairs={{0,8},{4,12},{8,0},{12,4},{16,24},{20,28},{24,16},{28,20},{1,9},{5... | collective-permute-start | bytes 294920 | tf_op jit(solution)/shard_map/ppermute | solution.py:566
  9.6 0.0 collective-permute-done.1.beside
  9.6 0.0 collective-permute-done.2.rest_0_
  9.7 2.3 %collective-permute-start.3 = (bf16[3,30,512]{2,1,0:T(8,128)(2,1)S(1)}, bf16[3,30,512]{2,1,0:T(8,128)(2,1)S(1)}, u32[]{:S(2)}, u32[]{:S(2)}) collective-permute-start(bf16[3,30,512]{2,1,0:T(8,128)(2,1)S(1)} %choose_waves.1), channel_id=1, source_target_pairs={{0,4},{4,0},{8,12},{12,8},{16,20},{20,16},{24,28},{28,24},{1,5},{5... | collective-permute-start | bytes 276488 | tf_op jit(solution)/shard_map/ppermute | solution.py:563
  11.9 0.9 %collective-permute-done.3.swapped = bf16[3,30,512]{2,1,0:T(8,128)(2,1)S(1)} collective-permute-done((bf16[3,30,512]{2,1,0:T(8,128)(2,1)S(1)}, bf16[3,30,512]{2,1,0:T(8,128)(2,1)S(1)}, u32[]{:S(2)}, u32[]{:S(2)}) %collective-permute-start.3) | collective-permute-done | bytes 92192 | tf_op jit(solution)/shard_map/ppermute | solution.py:563
  12.9 1.8 %prepare_waves.1 = (bf16[30,272,128]{2,1,0:T(8,128)(2,1)S(1)}, f32[32,32,128]{2,1,0:T(8,128)S(1)}) custom-call(bf16[3,30,512]{2,1,0:T(8,128)(2,1)S(1)} %collective-permute-done.3.swapped, bf16[2,30,512]{2,1,0:T(8,128)(2,1)S(1)} %pair_waves.1.pair, bf16[30,512]{1,0:T(8,128)(2,1)S(1)} %collective-permute-done.1.beside, ...), custom_call_target="tpu_custom_call" | custom-call | flops 50000000 | bytes 50000 | tf_op jit(solution)/shard_map/prepare_waves/pallas_call | solution.py:302
  14.7 2.0 %collective-permute-done.5.refs_2_ = bf16[12,32,128]{2,1,0:T(8,128)(2,1)S(1)} collective-permute-done((bf16[12,32,128]{2,1,0:T(8,128)(2,1)S(1)}, bf16[12,32,128]{2,1,0:T(8,128)(2,1)S(1)}, u32[]{:S(2)}, u32[]{:S(2)}) %collective-permute-start.5) | collective-permute-done | bytes 98336 | tf_op jit(solution)/shard_map/ppermute | solution.py:566
  16.7 0.0 collective-permute-done.6.refs_3_
  16.7 0.0 collective-permute-done.7.refs_1_
  16.7 0.1 choose_piece.1.piece
  16.8 1.6 %collective-permute-start.8 = (bf16[12,32,128]{2,1,0:T(8,128)(2,1)S(1)}, bf16[12,32,128]{2,1,0:T(8,128)(2,1)S(1)}, u32[]{:S(2)}, u32[]{:S(2)}) collective-permute-start(bf16[12,32,128]{2,1,0:T(8,128)(2,1)S(1)} %choose_piece.1.piece), channel_id=1, source_target_pairs={{0,4},{4,0},{8,12},{12,8},{16,20},{20,16},{24,28},{28,24},{1,5},{5... | collective-permute-start | bytes 294920 | tf_op jit(solution)/shard_map/ppermute | solution.py:563
  18.4 2.0 %correlate_first.1.rest_0_ = f32[256,256]{1,0:T(8,128)S(1)} custom-call(bf16[12,32,128]{2,1,0:T(8,128)(2,1)S(1)} %choose_piece.1.piece, bf16[30,272,128]{2,1,0:T(8,128)(2,1)S(1)} %get-tuple-element.41.left_a, f32[32,32,128]{2,1,0:T(8,128)S(1)} %get-tuple-element.42.inverse), custom_call_target="tpu_custom_call" | custom-call | flops 3000000000 | bytes 3000000 | tf_op jit(solution)/shard_map/correlate_first/pallas_call | solution.py:479
  20.4 0.0 collective-permute-done.8.piece
  20.4 2.1 %correlate_second.1 = (bf16[128,256]{1,0:T(8,128)(2,1)S(1)}, bf16[128,256]{1,0:T(8,128)(2,1)S(1)}) custom-call(bf16[12,32,128]{2,1,0:T(8,128)(2,1)S(1)} %collective-permute-done.8.piece, bf16[30,272,128]{2,1,0:T(8,128)(2,1)S(1)} %get-tuple-element.41.left_a, f32[32,32,128]{2,1,0:T(8,128)S(1)} %get-tuple-element.42.inverse, f32[256,256]{1,0:T(8,128)S(1)} %correlate_first.1.rest_0_), custom_call_target="tpu_custom_call" | custom-call | flops 3000000000 | bytes 3000000 | tf_op jit(solution)/shard_map/correlate_second/pallas_call | solution.py:479
  22.5 2.3 %collective-permute-start.9 = (bf16[128,256]{1,0:T(8,128)(2,1)S(1)}, bf16[128,256]{1,0:T(8,128)(2,1)S(1)}, u32[]{:S(2)}, u32[]{:S(2)}) collective-permute-start(bf16[128,256]{1,0:T(8,128)(2,1)S(1)} %get-tuple-element.43), channel_id=1, source_target_pairs={{0,8},{1,12},{2,0},{3,4},{4,24},{5,28},{6,16},{7,20},{8,9},{9,13},... | collective-permute-start | bytes 196616 | tf_op jit(solution)/shard_map/ppermute | solution.py:607
  24.8 3.4 %collective-permute-start.10 = (bf16[128,256]{1,0:T(8,128)(2,1)S(1)}, bf16[128,256]{1,0:T(8,128)(2,1)S(1)}, u32[]{:S(2)}, u32[]{:S(2)}) collective-permute-start(bf16[128,256]{1,0:T(8,128)(2,1)S(1)} %get-tuple-element.44), channel_id=1, source_target_pairs={{0,0},{1,4},{2,8},{3,12},{4,16},{5,20},{6,24},{7,28},{8,1},{9,5},{... | collective-permute-start | bytes 196616 | tf_op jit(solution)/shard_map/ppermute | solution.py:607
  28.2 0.5 %collective-permute-done.9.refs_0_ = bf16[128,256]{1,0:T(8,128)(2,1)S(1)} collective-permute-done((bf16[128,256]{1,0:T(8,128)(2,1)S(1)}, bf16[128,256]{1,0:T(8,128)(2,1)S(1)}, u32[]{:S(2)}, u32[]{:S(2)}) %collective-permute-start.9) | collective-permute-done | bytes 65568 | tf_op jit(solution)/shard_map/ppermute | solution.py:607
  28.8 4.3 %collective-permute-done.10.refs_1_ = bf16[128,256]{1,0:T(8,128)(2,1)S(1)} collective-permute-done((bf16[128,256]{1,0:T(8,128)(2,1)S(1)}, bf16[128,256]{1,0:T(8,128)(2,1)S(1)}, u32[]{:S(2)}, u32[]{:S(2)}) %collective-permute-start.10) | collective-permute-done | bytes 65568 | tf_op jit(solution)/shard_map/ppermute | solution.py:607
  33.1 0.1 collective-permute-start.11
  33.2 1.2 %collective-permute-done.11.received = f32[64,256]{1,0:T(8,128)S(1)} collective-permute-done((f32[64,256]{1,0:T(8,128)S(1)}, f32[64,256]{1,0:T(8,128)S(1)}, u32[]{:S(2)}, u32[]{:S(2)}) %collective-permute-start.11) | collective-permute-done | bytes 65568 | tf_op jit(solution)/shard_map/ppermute | solution.py:563
  34.4 0.9 %finish.1 = f32[32,512]{1,0:T(8,128)} custom-call(f32[64,256]{1,0:T(8,128)S(1)} %get-tuple-element.45.ours, f32[64,256]{1,0:T(8,128)S(1)} %collective-permute-done.11.received), custom_call_target="tpu_custom_call" | custom-call | flops 1000000000 | bytes 1000000 | tf_op jit(solution)/shard_map/finish/pallas_call | solution.py:542
  (3 shorter events, 0.1 us)
Async XLA Ops:
  0.0 2.9 %collective-permute-start = (bf16[30,512]{1,0:T(8,128)(2,1)}, bf16[30,512]{1,0:T(8,128)(2,1)S(1)}, u32[]{:S(2)}, u32[]{:S(2)}) collective-permute-start(bf16[30,512]{1,0:T(8,128)(2,1)} %own.1), channel_id=1, source_target_pairs={{0,4},{4,0},{8,12},{12,8},{16,20},{20,16},{24,28},{28,24},{1,5},{5... | collective-permute-start | bytes 92168 | tf_op jit(solution)/shard_map/ppermute | solution.py:563
  0.7 2.3 %copy-start = (bf16[30,512]{1,0:T(8,128)(2,1)S(1)}, bf16[30,512]{1,0:T(8,128)(2,1)}, u32[]{:S(2)}) copy-start(bf16[30,512]{1,0:T(8,128)(2,1)} %own.1) | copy-start | bytes 92164
  2.9 3.8 %collective-permute-start.4 = (bf16[4,12,32,128]{3,2,1,0:T(8,128)(2,1)S(1)}, bf16[4,12,32,128]{3,2,1,0:T(8,128)(2,1)S(1)}, u32[]{:S(2)}, u32[]{:S(2)}) collective-permute-start(bf16[4,12,32,128]{3,2,1,0:T(8,128)(2,1)S(1)} %get-tuple-element.32), channel_id=1, source_target_pairs={{0,4},{4,0},{8,12},{12,8},{16,20},{20,16},{24,28},{28,24},{1,5},{5... | collective-permute-start | bytes 1179656 | tf_op jit(solution)/shard_map/ppermute | solution.py:563
  3.0 6.6 %collective-permute-start.2 = (bf16[2,30,512]{2,1,0:T(8,128)(2,1)S(1)}, bf16[2,30,512]{2,1,0:T(8,128)(2,1)S(1)}, u32[]{:S(2)}, u32[]{:S(2)}) collective-permute-start(bf16[2,30,512]{2,1,0:T(8,128)(2,1)S(1)} %pair_waves.1.pair), channel_id=1, source_target_pairs={{0,24},{4,20},{8,16},{12,28},{16,8},{20,4},{24,0},{28,12},{1,25},{... | collective-permute-start | bytes 184328 | tf_op jit(solution)/shard_map/ppermute | solution.py:584
  5.4 4.2 %collective-permute-start.1 = (bf16[30,512]{1,0:T(8,128)(2,1)S(1)}, bf16[30,512]{1,0:T(8,128)(2,1)S(1)}, u32[]{:S(2)}, u32[]{:S(2)}) collective-permute-start(bf16[30,512]{1,0:T(8,128)(2,1)S(1)} %copy-done), channel_id=1, source_target_pairs={{0,8},{4,12},{8,0},{12,4},{16,24},{20,28},{24,16},{28,20},{1,9},{5... | collective-permute-start | bytes 92168 | tf_op jit(solution)/shard_map/ppermute | solution.py:566
  6.9 9.8 %collective-permute-start.5 = (bf16[12,32,128]{2,1,0:T(8,128)(2,1)S(1)}, bf16[12,32,128]{2,1,0:T(8,128)(2,1)S(1)}, u32[]{:S(2)}, u32[]{:S(2)}) collective-permute-start(bf16[12,32,128]{2,1,0:T(8,128)(2,1)S(1)} %get-tuple-element.33), channel_id=1, source_target_pairs={{0,16},{4,20},{8,24},{12,28},{16,0},{20,4},{24,8},{28,12},{1,17},{... | collective-permute-start | bytes 294920 | tf_op jit(solution)/shard_map/ppermute | solution.py:566
  7.3 9.4 %collective-permute-start.6 = (bf16[12,32,128]{2,1,0:T(8,128)(2,1)S(1)}, bf16[12,32,128]{2,1,0:T(8,128)(2,1)S(1)}, u32[]{:S(2)}, u32[]{:S(2)}) collective-permute-start(bf16[12,32,128]{2,1,0:T(8,128)(2,1)S(1)} %get-tuple-element.34), channel_id=1, source_target_pairs={{0,24},{4,28},{8,16},{12,20},{16,8},{20,12},{24,0},{28,4},{1,25},{... | collective-permute-start | bytes 294920 | tf_op jit(solution)/shard_map/ppermute | solution.py:566
  9.2 7.5 %collective-permute-start.7 = (bf16[12,32,128]{2,1,0:T(8,128)(2,1)S(1)}, bf16[12,32,128]{2,1,0:T(8,128)(2,1)S(1)}, u32[]{:S(2)}, u32[]{:S(2)}) collective-permute-start(bf16[12,32,128]{2,1,0:T(8,128)(2,1)S(1)} %get-tuple-element.36), channel_id=1, source_target_pairs={{0,8},{4,12},{8,0},{12,4},{16,24},{20,28},{24,16},{28,20},{1,9},{5... | collective-permute-start | bytes 294920 | tf_op jit(solution)/shard_map/ppermute | solution.py:566
  9.7 3.2 %collective-permute-start.3 = (bf16[3,30,512]{2,1,0:T(8,128)(2,1)S(1)}, bf16[3,30,512]{2,1,0:T(8,128)(2,1)S(1)}, u32[]{:S(2)}, u32[]{:S(2)}) collective-permute-start(bf16[3,30,512]{2,1,0:T(8,128)(2,1)S(1)} %choose_waves.1), channel_id=1, source_target_pairs={{0,4},{4,0},{8,12},{12,8},{16,20},{20,16},{24,28},{28,24},{1,5},{5... | collective-permute-start | bytes 276488 | tf_op jit(solution)/shard_map/ppermute | solution.py:563
  16.8 3.6 %collective-permute-start.8 = (bf16[12,32,128]{2,1,0:T(8,128)(2,1)S(1)}, bf16[12,32,128]{2,1,0:T(8,128)(2,1)S(1)}, u32[]{:S(2)}, u32[]{:S(2)}) collective-permute-start(bf16[12,32,128]{2,1,0:T(8,128)(2,1)S(1)} %choose_piece.1.piece), channel_id=1, source_target_pairs={{0,4},{4,0},{8,12},{12,8},{16,20},{20,16},{24,28},{28,24},{1,5},{5... | collective-permute-start | bytes 294920 | tf_op jit(solution)/shard_map/ppermute | solution.py:563
  22.5 6.3 %collective-permute-start.9 = (bf16[128,256]{1,0:T(8,128)(2,1)S(1)}, bf16[128,256]{1,0:T(8,128)(2,1)S(1)}, u32[]{:S(2)}, u32[]{:S(2)}) collective-permute-start(bf16[128,256]{1,0:T(8,128)(2,1)S(1)} %get-tuple-element.43), channel_id=1, source_target_pairs={{0,8},{1,12},{2,0},{3,4},{4,24},{5,28},{6,16},{7,20},{8,9},{9,13},... | collective-permute-start | bytes 196616 | tf_op jit(solution)/shard_map/ppermute | solution.py:607
  24.8 8.3 %collective-permute-start.10 = (bf16[128,256]{1,0:T(8,128)(2,1)S(1)}, bf16[128,256]{1,0:T(8,128)(2,1)S(1)}, u32[]{:S(2)}, u32[]{:S(2)}) collective-permute-start(bf16[128,256]{1,0:T(8,128)(2,1)S(1)} %get-tuple-element.44), channel_id=1, source_target_pairs={{0,0},{1,4},{2,8},{3,12},{4,16},{5,20},{6,24},{7,28},{8,1},{9,5},{... | collective-permute-start | bytes 196616 | tf_op jit(solution)/shard_map/ppermute | solution.py:607
  33.1 1.3 %collective-permute-start.11 = (f32[64,256]{1,0:T(8,128)S(1)}, f32[64,256]{1,0:T(8,128)S(1)}, u32[]{:S(2)}, u32[]{:S(2)}) collective-permute-start(f32[64,256]{1,0:T(8,128)S(1)} %get-tuple-element.46), channel_id=1, source_target_pairs={{0,4},{4,0},{8,12},{12,8},{16,20},{20,16},{24,28},{28,24},{1,5},{5... | collective-permute-start | bytes 196616 | tf_op jit(solution)/shard_map/ppermute | solution.py:563

commit v23 on v21

--- a/solution.py
+++ b/solution.py
@@ -233,8 +233,8 @@
 
 
 def waves_kernel(channels, tlen, unroll, swapped, pair, beside, *rest):
-    far = rest[:-3]
-    left_a, inverse, padded = rest[-3:]
+    far = rest[:-5]
+    left_a, inverse, expand, place, padded = rest[-5:]
     samples = beside.shape[1]
     near = swapped.shape[0] - 1
     length = 2 * near * samples
@@ -251,6 +251,17 @@
     rim = rim[:, 0 : padded.shape[1] - length].astype(jnp.float32)
     padded[0:channels, length:] = jnp.where(core == 0, rim, 0.0)
 
+    group = expand.shape[1] // LANES
+    group = LANES // group
+    row = lax.broadcasted_iota(jnp.int32, expand.shape, 0)
+    lane = lax.broadcasted_iota(jnp.int32, expand.shape, 1)
+    chosen = row == lane % group + lane // LANES * group
+    expand[...] = jnp.where(chosen, 1.0, 0.0).astype(jnp.bfloat16)
+    row = lax.broadcasted_iota(jnp.int32, place.shape, 0) % (place.shape[0] // 2)
+    lane = lax.broadcasted_iota(jnp.int32, place.shape, 1)
+    chosen = jnp.logical_and(lane // STRIDE == row // 8, lane % 8 == 7 - row % 8)
+    place[...] = jnp.where(chosen, 1.0, 0.0).astype(jnp.bfloat16)
+
     rows = 32 * count
     values = [padded[:, LANES * tile : LANES * (tile + 1)] for tile in range(count)]
     values = jnp.concatenate(values + [jnp.zeros((32, LANES), jnp.float32)], axis=0)
@@ -294,7 +305,7 @@
             left_a[channel] = value.astype(jnp.bfloat16)
 
 
-def prepare_waves(tlen, swapped, pair, beside, far):
+def prepare_waves(tlen, group, swapped, pair, beside, far):
     channels, samples = beside.shape
     length = 2 * (swapped.shape[0] - 1) * samples
     rows = length // OFFSETS
@@ -304,9 +315,11 @@
         out_shape=[
             jax.ShapeDtypeStruct((channels, rows + 16, LANES), jnp.bfloat16),
             jax.ShapeDtypeStruct((length // STRIDE, 32, LANES), jnp.float32),
+            jax.ShapeDtypeStruct((LANES, LANES // group * LANES), jnp.bfloat16),
+            jax.ShapeDtypeStruct((2 * samples // OFFSETS, samples), jnp.bfloat16),
         ],
         in_specs=[VMEM] * (3 + len(far)),
-        out_specs=[VMEM, VMEM],
+        out_specs=[VMEM] * 4,
         scratch_shapes=[
             pltpu.VMEM((32, length + 2 * LANES), jnp.float32),
         ],
@@ -316,11 +329,11 @@
     )(swapped, pair, beside, *far)
 
 
-def main_kernel(side, tlen, group, piece, left_a, inverse, *rest):
-    outs = rest[:-5]
+def main_kernel(side, tlen, group, piece, left_a, inverse, expand, *rest):
+    outs = rest[:-4]
     if side:
         before, outs = outs[0], outs[1:]
-    bank, expand, weight_a, reach, total = rest[-5:]
+    bank, weight_a, reach, total = rest[-4:]
     core = lax.axis_index("tm") % 2
     channels = left_a.shape[0]
     rows = left_a.shape[1] - 16
@@ -334,13 +347,9 @@
     top = top + top % 16
 
     lag = lax.broadcasted_iota(jnp.int32, (LANES, LANES), 0)
-    target = lax.broadcasted_iota(jnp.int32, (LANES, LANES), 1)
     lane = lax.broadcasted_iota(jnp.int32, (1, LANES), 1)
     used = lag < tlen
     ahead = lane // group
-    for slot in range(slots):
-        chosen = jnp.where(lag == target % group + slot * group, 1.0, 0.0)
-        expand[:, slot * LANES : (slot + 1) * LANES] = chosen.astype(jnp.bfloat16)
     turned = []
     for index in range(banks):
         count = min(slots, max(TILES - slots * index, 0))
@@ -467,7 +476,7 @@
         )
 
 
-def correlate(side, tlen, group, count, piece, left_a, inverse, *before):
+def correlate(side, tlen, group, count, piece, left_a, inverse, expand, *before):
     channels = left_a.shape[0]
     rows = left_a.shape[1] - 16
     width = OFFSETS * group
@@ -479,11 +488,10 @@
     return pl.pallas_call(
         functools.partial(main_kernel, side, tlen, group),
         out_shape=out,
-        in_specs=[VMEM] * (3 + len(before)),
+        in_specs=[VMEM] * (4 + len(before)),
         out_specs=[VMEM] * len(out),
         scratch_shapes=[
             pltpu.VMEM(((half + 1) * group // LANES, LANES, LANES), jnp.bfloat16),
-            pltpu.VMEM((LANES, LANES // group * LANES), jnp.bfloat16),
             pltpu.VMEM((half + 1, DEPTH, width), jnp.bfloat16),
             pltpu.VMEM((half + 1, 8, LANES), jnp.int32),
             pltpu.VMEM((rows, width), jnp.float32),
@@ -491,7 +499,7 @@
         compiler_params=params(),
         cost_estimate=cost(3),
         name="correlate_" + ("second" if side else "first"),
-    )(piece, left_a, inverse, *before)
+    )(piece, left_a, inverse, expand, *before)
 
 
 def add_kernel(*refs):
@@ -520,17 +528,12 @@
     )(*parts)
 
 
-def finish_kernel(group, ours, received, out):
+def finish_kernel(group, ours, received, place, out):
     samples = out.shape[1]
-    rows = ours.shape[0]
     value = ours[...] + received[...]
     high = value.astype(jnp.bfloat16).astype(jnp.float32)
     both = jnp.concatenate([high, value - high], axis=0).T.astype(jnp.bfloat16)
-    row = lax.broadcasted_iota(jnp.int32, (2 * rows, samples), 0) % rows
-    lane = lax.broadcasted_iota(jnp.int32, (2 * rows, samples), 1)
-    place = jnp.logical_and(lane // STRIDE == row // 8, lane % 8 == 7 - row % 8)
-    place = jnp.where(place, 1.0, 0.0).astype(jnp.bfloat16)
-    wide = jnp.dot(both, place, preferred_element_type=jnp.float32)
+    wide = jnp.dot(both, place[...], preferred_element_type=jnp.float32)
     lane = lax.broadcasted_iota(jnp.int32, (group, samples), 1) // 8 % OFFSETS
     result = jnp.zeros((group, samples), jnp.float32)
     for offset in range(OFFSETS):
@@ -538,16 +541,16 @@
     out[...] = result
 
 
-def finish(group, samples, ours, received):
+def finish(group, samples, ours, received, place):
     return pl.pallas_call(
         functools.partial(finish_kernel, group),
         out_shape=jax.ShapeDtypeStruct((group, samples), jnp.float32),
-        in_specs=[VMEM, VMEM],
+        in_specs=[VMEM] * 3,
         out_specs=VMEM,
         compiler_params=params(),
         cost_estimate=cost(1),
         name="finish",
-    )(ours, received)
+    )(ours, received, place)
 
 
 def shards(waveforms, templates, available, moveout, bank_blocks):
@@ -587,7 +590,7 @@
     pieces = [across(merged[step], step) for step in reversed(range(1, chips))]
     pieces = [merged[0]] + pieces[::-1]
     swapped = swap(choose_waves(pair, beside, far))
-    left_a, inverse = prepare_waves(tlen, swapped, pair, beside, far)
+    left_a, inverse, expand, place = prepare_waves(tlen, group, swapped, pair, beside, far)
 
     order = sorted(range(chips), key=lambda step: (step < 2, step))
     placed = lax.optimization_barrier((left_a, inverse, *[pieces[step] for step in order]))
@@ -595,8 +598,8 @@
     pieces = [placed[2 + order.index(step)] for step in range(chips)]
     first = choose_piece(owners, pieces)
     second = swap(first)
-    total = correlate(0, tlen, group, near, first, left_a, inverse)
-    parts = correlate(1, tlen, group, near, second, left_a, inverse, *total)
+    total = correlate(0, tlen, group, near, first, left_a, inverse, expand)
+    parts = correlate(1, tlen, group, near, second, left_a, inverse, expand, *total)
     gathered = []
     for step in range(near):
         route = []
@@ -606,7 +609,7 @@
                 route.append((d * count_sta + s, (2 * dest + s % 2) * count_sta + d // 2))
         gathered.append(lax.ppermute(parts[step], ("tm", "sta"), route))
     ours, send = add(gathered)
-    return finish(group, samples, ours, swap(send))
+    return finish(group, samples, ours, swap(send), place)
 
 
 def solution(mesh):

time: 35.2 us -> 35.2 us (level)
  no operation moved by 1% of the time
where the time goes in v23:
time: 35.2 us; the launch traced here: 34.9 us
  starting transfers between devices  17.7 us (50%)
  Pallas kernels  9.34 us (27%)
  waiting for transfers between devices  7.83 us (22%)
    ppermute x5, starting transfers between devices, swap(): return lax.ppermute(array, 'tm', [(i, i ^ 1) for i in range(count_tm)])  5.77 us
    ppermute x2, starting transfers between devices, shards(): gathered.append(lax.ppermute(parts[step], ('tm', 'sta'), route))  5.5 us
    pallas_call x2, Pallas kernels, correlate(): pl.pallas_call(functools.partial(main_kernel, side, tlen, group), out_sha...  4.04 us
    ppermute x4, starting transfers between devices, across(): lax.ppermute(array, 'tm', [(i, i ^ 2 * step) for i in range(count_tm)])  4.01 us
    ppermute x2, waiting for transfers between devices, shards(): gathered.append(lax.ppermute(parts[step], ('tm', 'sta'), route))  4 us
    ppermute x1, starting transfers between devices, shards(): far.append(lax.ppermute(pair, 'tm', route))  2.37 us
    pallas_call x1, Pallas kernels, pack(): pl.pallas_call(pack_kernel, out_shape=[jax.ShapeDtypeStruct(shape, jnp.bf...  2.18 us
    ppermute x4, waiting for transfers between devices, across(): lax.ppermute(array, 'tm', [(i, i ^ 2 * step) for i in range(count_tm)])  1.97 us
  transfers between devices with their start and end apart: 12, of which 5 were waited for; matrix products, arithmetic and copies ran while one was open for 0% of the time, Pallas kernels for 18%

profile of v23, /device:TPU:7, one launch (start us, length us, event | category | flops | bytes accessed | tf_op | source)
XLA Modules:
  0.0 34.9 jit_solution(6055953646451882462)
XLA Ops:
  0.0 0.7 %collective-permute-start = (bf16[30,512]{1,0:T(8,128)(2,1)}, bf16[30,512]{1,0:T(8,128)(2,1)S(1)}, u32[]{:S(2)}, u32[]{:S(2)}) collective-permute-start(bf16[30,512]{1,0:T(8,128)(2,1)} %own.1), channel_id=1, source_target_pairs={{0,4},{4,0},{8,12},{12,8},{16,20},{20,16},{24,28},{28,24},{1,5},{5... | collective-permute-start | bytes 92168 | tf_op jit(solution)/shard_map/ppermute | solution.py:566
  0.7 0.0 copy-start
  0.7 2.2 %pack.1 = (bf16[4,12,32,128]{3,2,1,0:T(8,128)(2,1)S(1)}, bf16[4,12,32,128]{3,2,1,0:T(8,128)(2,1)S(1)}, s32[8,128]{1,0:T(8,128)S(1)}) custom-call(s32[2]{0:T(128)} %bank_blocks.1, bf16[2,30,64,100]{3,2,1,0:T(8,128)(2,1)} %bitcast.3, s32[30,2,64]{2,1,0:T(2,128)} %bitcast.4, s32[30,2,64]{2,1,0:T(2,128)} %bitcast.5), custom_call_target="tpu_custom_call" | custom-call | flops 2000000000 | bytes 2000000 | tf_op jit(solution)/shard_map/pack/pallas_call | solution.py:100
  2.9 0.0 collective-permute-done.partner
  2.9 0.1 collective-permute-start.4
  3.0 0.0 copy-done
  3.0 2.4 %collective-permute-start.2 = (bf16[2,30,512]{2,1,0:T(8,128)(2,1)S(1)}, bf16[2,30,512]{2,1,0:T(8,128)(2,1)S(1)}, u32[]{:S(2)}, u32[]{:S(2)}) collective-permute-start(bf16[2,30,512]{2,1,0:T(8,128)(2,1)S(1)} %pair_waves.1.pair), channel_id=1, source_target_pairs={{0,24},{4,20},{8,16},{12,28},{16,8},{20,4},{24,0},{28,12},{1,25},{... | collective-permute-start | bytes 184328 | tf_op jit(solution)/shard_map/ppermute | solution.py:587
  5.4 1.3 %collective-permute-start.1 = (bf16[30,512]{1,0:T(8,128)(2,1)S(1)}, bf16[30,512]{1,0:T(8,128)(2,1)S(1)}, u32[]{:S(2)}, u32[]{:S(2)}) collective-permute-start(bf16[30,512]{1,0:T(8,128)(2,1)S(1)} %copy-done), channel_id=1, source_target_pairs={{0,8},{4,12},{8,0},{12,4},{16,24},{20,28},{24,16},{28,20},{1,9},{5... | collective-permute-start | bytes 92168 | tf_op jit(solution)/shard_map/ppermute | solution.py:569
  6.7 0.0 collective-permute-done.4.other
  6.7 0.2 merge.1
  6.9 0.4 %collective-permute-start.5 = (bf16[12,32,128]{2,1,0:T(8,128)(2,1)S(1)}, bf16[12,32,128]{2,1,0:T(8,128)(2,1)S(1)}, u32[]{:S(2)}, u32[]{:S(2)}) collective-permute-start(bf16[12,32,128]{2,1,0:T(8,128)(2,1)S(1)} %get-tuple-element.35), channel_id=1, source_target_pairs={{0,16},{4,20},{8,24},{12,28},{16,0},{20,4},{24,8},{28,12},{1,17},{... | collective-permute-start | bytes 294920 | tf_op jit(solution)/shard_map/ppermute | solution.py:569
  7.3 1.9 %collective-permute-start.6 = (bf16[12,32,128]{2,1,0:T(8,128)(2,1)S(1)}, bf16[12,32,128]{2,1,0:T(8,128)(2,1)S(1)}, u32[]{:S(2)}, u32[]{:S(2)}) collective-permute-start(bf16[12,32,128]{2,1,0:T(8,128)(2,1)S(1)} %get-tuple-element.36), channel_id=1, source_target_pairs={{0,24},{4,28},{8,16},{12,20},{16,8},{20,12},{24,0},{28,4},{1,25},{... | collective-permute-start | bytes 294920 | tf_op jit(solution)/shard_map/ppermute | solution.py:569
  9.2 0.4 %collective-permute-start.7 = (bf16[12,32,128]{2,1,0:T(8,128)(2,1)S(1)}, bf16[12,32,128]{2,1,0:T(8,128)(2,1)S(1)}, u32[]{:S(2)}, u32[]{:S(2)}) collective-permute-start(bf16[12,32,128]{2,1,0:T(8,128)(2,1)S(1)} %get-tuple-element.38), channel_id=1, source_target_pairs={{0,8},{4,12},{8,0},{12,4},{16,24},{20,28},{24,16},{28,20},{1,9},{5... | collective-permute-start | bytes 294920 | tf_op jit(solution)/shard_map/ppermute | solution.py:569
  9.6 0.0 collective-permute-done.1.beside
  9.6 0.0 collective-permute-done.2.rest_0_
  9.7 2.3 %collective-permute-start.3 = (bf16[3,30,512]{2,1,0:T(8,128)(2,1)S(1)}, bf16[3,30,512]{2,1,0:T(8,128)(2,1)S(1)}, u32[]{:S(2)}, u32[]{:S(2)}) collective-permute-start(bf16[3,30,512]{2,1,0:T(8,128)(2,1)S(1)} %choose_waves.1), channel_id=1, source_target_pairs={{0,4},{4,0},{8,12},{12,8},{16,20},{20,16},{24,28},{28,24},{1,5},{5... | collective-permute-start | bytes 276488 | tf_op jit(solution)/shard_map/ppermute | solution.py:566
  11.9 0.9 %collective-permute-done.3.swapped = bf16[3,30,512]{2,1,0:T(8,128)(2,1)S(1)} collective-permute-done((bf16[3,30,512]{2,1,0:T(8,128)(2,1)S(1)}, bf16[3,30,512]{2,1,0:T(8,128)(2,1)S(1)}, u32[]{:S(2)}, u32[]{:S(2)}) %collective-permute-start.3) | collective-permute-done | bytes 92192 | tf_op jit(solution)/shard_map/ppermute | solution.py:566
  12.9 1.8 %prepare_waves.1 = (bf16[30,272,128]{2,1,0:T(8,128)(2,1)S(1)}, f32[32,32,128]{2,1,0:T(8,128)S(1)}, bf16[128,512]{1,0:T(8,128)(2,1)S(1)}, bf16[128,512]{1,0:T(8,128)(2,1)S(1)}) custom-call(bf16[3,30,512]{2,1,0:T(8,128)(2,1)S(1)} %collective-permute-done.3.swapped, bf16[2,30,512]{2,1,0:T(8,128)(2,1)S(1)} %pair_waves.1.pair, ...), custom_call_target="tpu_custom_call" | custom-call | flops 50000000 | bytes 50000 | tf_op jit(solution)/shard_map/prepare_waves/pallas_call | solution.py:313
  14.7 2.0 %collective-permute-done.5.refs_2_ = bf16[12,32,128]{2,1,0:T(8,128)(2,1)S(1)} collective-permute-done((bf16[12,32,128]{2,1,0:T(8,128)(2,1)S(1)}, bf16[12,32,128]{2,1,0:T(8,128)(2,1)S(1)}, u32[]{:S(2)}, u32[]{:S(2)}) %collective-permute-start.5) | collective-permute-done | bytes 98336 | tf_op jit(solution)/shard_map/ppermute | solution.py:569
  16.7 0.0 collective-permute-done.6.refs_3_
  16.7 0.0 collective-permute-done.7.refs_1_
  16.7 0.1 choose_piece.1.piece
  16.8 1.6 %collective-permute-start.8 = (bf16[12,32,128]{2,1,0:T(8,128)(2,1)S(1)}, bf16[12,32,128]{2,1,0:T(8,128)(2,1)S(1)}, u32[]{:S(2)}, u32[]{:S(2)}) collective-permute-start(bf16[12,32,128]{2,1,0:T(8,128)(2,1)S(1)} %choose_piece.1.piece), channel_id=1, source_target_pairs={{0,4},{4,0},{8,12},{12,8},{16,20},{20,16},{24,28},{28,24},{1,5},{5... | collective-permute-start | bytes 294920 | tf_op jit(solution)/shard_map/ppermute | solution.py:566
  18.4 2.0 %correlate_first.1.rest_0_ = f32[256,256]{1,0:T(8,128)S(1)} custom-call(bf16[12,32,128]{2,1,0:T(8,128)(2,1)S(1)} %choose_piece.1.piece, bf16[30,272,128]{2,1,0:T(8,128)(2,1)S(1)} %get-tuple-element.43.left_a, f32[32,32,128]{2,1,0:T(8,128)S(1)} %get-tuple-element.44.inverse, bf16[128,512]{1,0:T(8,128)(2,1)S(1)} %get-tuple-element.45.expand), custom_call_target="tpu_custom_call" | custom-call | flops 3000000000 | bytes 3000000 | tf_op jit(solution)/shard_map/correlate_first/pallas_call | solution.py:488
  20.4 0.0 collective-permute-done.8.piece
  20.4 2.0 %correlate_second.1 = (bf16[128,256]{1,0:T(8,128)(2,1)S(1)}, bf16[128,256]{1,0:T(8,128)(2,1)S(1)}) custom-call(bf16[12,32,128]{2,1,0:T(8,128)(2,1)S(1)} %collective-permute-done.8.piece, bf16[30,272,128]{2,1,0:T(8,128)(2,1)S(1)} %get-tuple-element.43.left_a, f32[32,32,128]{2,1,0:T(8,128)S(1)} %get-tuple-element.44.inverse, ...), custom_call_target="tpu_custom_call" | custom-call | flops 3000000000 | bytes 3000000 | tf_op jit(solution)/shard_map/correlate_second/pallas_call | solution.py:488
  22.4 3.7 %collective-permute-start.9 = (bf16[128,256]{1,0:T(8,128)(2,1)S(1)}, bf16[128,256]{1,0:T(8,128)(2,1)S(1)}, u32[]{:S(2)}, u32[]{:S(2)}) collective-permute-start(bf16[128,256]{1,0:T(8,128)(2,1)S(1)} %get-tuple-element.46), channel_id=1, source_target_pairs={{0,0},{1,4},{2,8},{3,12},{4,16},{5,20},{6,24},{7,28},{8,1},{9,5},{... | collective-permute-start | bytes 196616 | tf_op jit(solution)/shard_map/ppermute | solution.py:610
  26.1 1.8 %collective-permute-start.10 = (bf16[128,256]{1,0:T(8,128)(2,1)S(1)}, bf16[128,256]{1,0:T(8,128)(2,1)S(1)}, u32[]{:S(2)}, u32[]{:S(2)}) collective-permute-start(bf16[128,256]{1,0:T(8,128)(2,1)S(1)} %get-tuple-element.47), channel_id=1, source_target_pairs={{0,8},{1,12},{2,0},{3,4},{4,24},{5,28},{6,16},{7,20},{8,9},{9,13},... | collective-permute-start | bytes 196616 | tf_op jit(solution)/shard_map/ppermute | solution.py:610
  28.0 3.5 %collective-permute-done.9.refs_0_ = bf16[128,256]{1,0:T(8,128)(2,1)S(1)} collective-permute-done((bf16[128,256]{1,0:T(8,128)(2,1)S(1)}, bf16[128,256]{1,0:T(8,128)(2,1)S(1)}, u32[]{:S(2)}, u32[]{:S(2)}) %collective-permute-start.9) | collective-permute-done | bytes 65568 | tf_op jit(solution)/shard_map/ppermute | solution.py:610
  31.5 0.5 %collective-permute-done.10.refs_1_ = bf16[128,256]{1,0:T(8,128)(2,1)S(1)} collective-permute-done((bf16[128,256]{1,0:T(8,128)(2,1)S(1)}, bf16[128,256]{1,0:T(8,128)(2,1)S(1)}, u32[]{:S(2)}, u32[]{:S(2)}) %collective-permute-start.10) | collective-permute-done | bytes 65568 | tf_op jit(solution)/shard_map/ppermute | solution.py:610
  32.0 1.2 %collective-permute-start.11 = (f32[64,256]{1,0:T(8,128)S(1)}, f32[64,256]{1,0:T(8,128)S(1)}, u32[]{:S(2)}, u32[]{:S(2)}) collective-permute-start(f32[64,256]{1,0:T(8,128)S(1)} %get-tuple-element.49), channel_id=1, source_target_pairs={{0,4},{4,0},{8,12},{12,8},{16,20},{20,16},{24,28},{28,24},{1,5},{5... | collective-permute-start | bytes 196616 | tf_op jit(solution)/shard_map/ppermute | solution.py:566
  33.1 0.9 %collective-permute-done.11.received = f32[64,256]{1,0:T(8,128)S(1)} collective-permute-done((f32[64,256]{1,0:T(8,128)S(1)}, f32[64,256]{1,0:T(8,128)S(1)}, u32[]{:S(2)}, u32[]{:S(2)}) %collective-permute-start.11) | collective-permute-done | bytes 65568 | tf_op jit(solution)/shard_map/ppermute | solution.py:566
  34.0 0.9 %finish.1 = f32[32,512]{1,0:T(8,128)} custom-call(f32[64,256]{1,0:T(8,128)S(1)} %get-tuple-element.48.ours, f32[64,256]{1,0:T(8,128)S(1)} %collective-permute-done.11.received, bf16[128,512]{1,0:T(8,128)(2,1)S(1)} %get-tuple-element.50.place), custom_call_target="tpu_custom_call" | custom-call | flops 1000000000 | bytes 1000000 | tf_op jit(solution)/shard_map/finish/pallas_call | solution.py:545
  (3 shorter events, 0.1 us)
Async XLA Ops:
  0.0 2.9 %collective-permute-start = (bf16[30,512]{1,0:T(8,128)(2,1)}, bf16[30,512]{1,0:T(8,128)(2,1)S(1)}, u32[]{:S(2)}, u32[]{:S(2)}) collective-permute-start(bf16[30,512]{1,0:T(8,128)(2,1)} %own.1), channel_id=1, source_target_pairs={{0,4},{4,0},{8,12},{12,8},{16,20},{20,16},{24,28},{28,24},{1,5},{5... | collective-permute-start | bytes 92168 | tf_op jit(solution)/shard_map/ppermute | solution.py:566
  0.7 2.3 %copy-start = (bf16[30,512]{1,0:T(8,128)(2,1)S(1)}, bf16[30,512]{1,0:T(8,128)(2,1)}, u32[]{:S(2)}) copy-start(bf16[30,512]{1,0:T(8,128)(2,1)} %own.1) | copy-start | bytes 92164
  2.9 3.8 %collective-permute-start.4 = (bf16[4,12,32,128]{3,2,1,0:T(8,128)(2,1)S(1)}, bf16[4,12,32,128]{3,2,1,0:T(8,128)(2,1)S(1)}, u32[]{:S(2)}, u32[]{:S(2)}) collective-permute-start(bf16[4,12,32,128]{3,2,1,0:T(8,128)(2,1)S(1)} %get-tuple-element.34), channel_id=1, source_target_pairs={{0,4},{4,0},{8,12},{12,8},{16,20},{20,16},{24,28},{28,24},{1,5},{5... | collective-permute-start | bytes 1179656 | tf_op jit(solution)/shard_map/ppermute | solution.py:566
  3.0 6.6 %collective-permute-start.2 = (bf16[2,30,512]{2,1,0:T(8,128)(2,1)S(1)}, bf16[2,30,512]{2,1,0:T(8,128)(2,1)S(1)}, u32[]{:S(2)}, u32[]{:S(2)}) collective-permute-start(bf16[2,30,512]{2,1,0:T(8,128)(2,1)S(1)} %pair_waves.1.pair), channel_id=1, source_target_pairs={{0,24},{4,20},{8,16},{12,28},{16,8},{20,4},{24,0},{28,12},{1,25},{... | collective-permute-start | bytes 184328 | tf_op jit(solution)/shard_map/ppermute | solution.py:587
  5.4 4.2 %collective-permute-start.1 = (bf16[30,512]{1,0:T(8,128)(2,1)S(1)}, bf16[30,512]{1,0:T(8,128)(2,1)S(1)}, u32[]{:S(2)}, u32[]{:S(2)}) collective-permute-start(bf16[30,512]{1,0:T(8,128)(2,1)S(1)} %copy-done), channel_id=1, source_target_pairs={{0,8},{4,12},{8,0},{12,4},{16,24},{20,28},{24,16},{28,20},{1,9},{5... | collective-permute-start | bytes 92168 | tf_op jit(solution)/shard_map/ppermute | solution.py:569
  6.9 9.8 %collective-permute-start.5 = (bf16[12,32,128]{2,1,0:T(8,128)(2,1)S(1)}, bf16[12,32,128]{2,1,0:T(8,128)(2,1)S(1)}, u32[]{:S(2)}, u32[]{:S(2)}) collective-permute-start(bf16[12,32,128]{2,1,0:T(8,128)(2,1)S(1)} %get-tuple-element.35), channel_id=1, source_target_pairs={{0,16},{4,20},{8,24},{12,28},{16,0},{20,4},{24,8},{28,12},{1,17},{... | collective-permute-start | bytes 294920 | tf_op jit(solution)/shard_map/ppermute | solution.py:569
  7.3 9.4 %collective-permute-start.6 = (bf16[12,32,128]{2,1,0:T(8,128)(2,1)S(1)}, bf16[12,32,128]{2,1,0:T(8,128)(2,1)S(1)}, u32[]{:S(2)}, u32[]{:S(2)}) collective-permute-start(bf16[12,32,128]{2,1,0:T(8,128)(2,1)S(1)} %get-tuple-element.36), channel_id=1, source_target_pairs={{0,24},{4,28},{8,16},{12,20},{16,8},{20,12},{24,0},{28,4},{1,25},{... | collective-permute-start | bytes 294920 | tf_op jit(solution)/shard_map/ppermute | solution.py:569
  9.2 7.5 %collective-permute-start.7 = (bf16[12,32,128]{2,1,0:T(8,128)(2,1)S(1)}, bf16[12,32,128]{2,1,0:T(8,128)(2,1)S(1)}, u32[]{:S(2)}, u32[]{:S(2)}) collective-permute-start(bf16[12,32,128]{2,1,0:T(8,128)(2,1)S(1)} %get-tuple-element.38), channel_id=1, source_target_pairs={{0,8},{4,12},{8,0},{12,4},{16,24},{20,28},{24,16},{28,20},{1,9},{5... | collective-permute-start | bytes 294920 | tf_op jit(solution)/shard_map/ppermute | solution.py:569
  9.7 3.2 %collective-permute-start.3 = (bf16[3,30,512]{2,1,0:T(8,128)(2,1)S(1)}, bf16[3,30,512]{2,1,0:T(8,128)(2,1)S(1)}, u32[]{:S(2)}, u32[]{:S(2)}) collective-permute-start(bf16[3,30,512]{2,1,0:T(8,128)(2,1)S(1)} %choose_waves.1), channel_id=1, source_target_pairs={{0,4},{4,0},{8,12},{12,8},{16,20},{20,16},{24,28},{28,24},{1,5},{5... | collective-permute-start | bytes 276488 | tf_op jit(solution)/shard_map/ppermute | solution.py:566
  16.8 3.6 %collective-permute-start.8 = (bf16[12,32,128]{2,1,0:T(8,128)(2,1)S(1)}, bf16[12,32,128]{2,1,0:T(8,128)(2,1)S(1)}, u32[]{:S(2)}, u32[]{:S(2)}) collective-permute-start(bf16[12,32,128]{2,1,0:T(8,128)(2,1)S(1)} %choose_piece.1.piece), channel_id=1, source_target_pairs={{0,4},{4,0},{8,12},{12,8},{16,20},{20,16},{24,28},{28,24},{1,5},{5... | collective-permute-start | bytes 294920 | tf_op jit(solution)/shard_map/ppermute | solution.py:566
  22.4 9.0 %collective-permute-start.9 = (bf16[128,256]{1,0:T(8,128)(2,1)S(1)}, bf16[128,256]{1,0:T(8,128)(2,1)S(1)}, u32[]{:S(2)}, u32[]{:S(2)}) collective-permute-start(bf16[128,256]{1,0:T(8,128)(2,1)S(1)} %get-tuple-element.46), channel_id=1, source_target_pairs={{0,0},{1,4},{2,8},{3,12},{4,16},{5,20},{6,24},{7,28},{8,1},{9,5},{... | collective-permute-start | bytes 196616 | tf_op jit(solution)/shard_map/ppermute | solution.py:610
  26.1 5.8 %collective-permute-start.10 = (bf16[128,256]{1,0:T(8,128)(2,1)S(1)}, bf16[128,256]{1,0:T(8,128)(2,1)S(1)}, u32[]{:S(2)}, u32[]{:S(2)}) collective-permute-start(bf16[128,256]{1,0:T(8,128)(2,1)S(1)} %get-tuple-element.47), channel_id=1, source_target_pairs={{0,8},{1,12},{2,0},{3,4},{4,24},{5,28},{6,16},{7,20},{8,9},{9,13},... | collective-permute-start | bytes 196616 | tf_op jit(solution)/shard_map/ppermute | solution.py:610
  32.0 2.1 %collective-permute-start.11 = (f32[64,256]{1,0:T(8,128)S(1)}, f32[64,256]{1,0:T(8,128)S(1)}, u32[]{:S(2)}, u32[]{:S(2)}) collective-permute-start(f32[64,256]{1,0:T(8,128)S(1)} %get-tuple-element.49), channel_id=1, source_target_pairs={{0,4},{4,0},{8,12},{12,8},{16,20},{20,16},{24,28},{28,24},{1,5},{5... | collective-permute-start | bytes 196616 | tf_op jit(solution)/shard_map/ppermute | solution.py:566

commit v24 on v23

--- a/solution.py
+++ b/solution.py
@@ -117,11 +117,19 @@
     )(*held)
 
 
+def step_of(number, chips, core):
+    if number < 2:
+        return number
+    pair, second = divmod(number - 2, 2)
+    high = chips - 1 - 2 * pair
+    return high - 1 + core if second else high - core
+
+
 def merge_kernel(owners, mine, other, *outs):
     chips = len(outs)
     me = lax.axis_index("tm")
-    for step, out in enumerate(outs):
-        dest = jnp.bitwise_xor(me // 2, step)
+    for number, out in enumerate(outs):
+        dest = jnp.bitwise_xor(me // 2, step_of(number, chips, me % 2))
         owner = jnp.where(dest < chips // 2, owners[0, 0], owners[1, 0])
         here = owner % 2 == me % 2
 
@@ -211,12 +219,13 @@
 
 def own_kernel(owners, *refs):
     pieces, out = refs[:-1], refs[-1]
-    chip = lax.axis_index("tm") // 2
-    owner = jnp.where(chip < len(pieces) // 2, owners[0, 0], owners[1, 0])
+    me = lax.axis_index("tm")
+    chip, chips = me // 2, len(pieces)
+    owner = jnp.where(chip < chips // 2, owners[0, 0], owners[1, 0])
     source = jnp.bitwise_xor(owner // 2, chip)
     value = pieces[0][...]
     for number, piece in enumerate(pieces[1:], 1):
-        value = jnp.where(source == number, piece[...], value)
+        value = jnp.where(source == step_of(number, chips, me % 2), piece[...], value)
     out[...] = value
 
 
@@ -587,7 +596,13 @@
         far.append(lax.ppermute(pair, "tm", route))
     beside = across(waveforms, 1)
     merged = list(merge(owners, mine, other))
-    pieces = [across(merged[step], step) for step in reversed(range(1, chips))]
+    def exchange(number):
+        route = [
+            (2 * z + c, 2 * (z ^ step_of(number, chips, c)) + c) for z in range(chips) for c in range(2)
+        ]
+        return lax.ppermute(merged[number], "tm", route)
+
+    pieces = [exchange(number) for number in reversed(range(1, chips))]
     pieces = [merged[0]] + pieces[::-1]
     swapped = swap(choose_waves(pair, beside, far))
     left_a, inverse, expand, place = prepare_waves(tlen, group, swapped, pair, beside, far)

time: 35.2 us -> 36.1 us (1.026); the launches traced: 34.9 us -> 35.4 us
  waiting for transfers between devices: 7.83 us -> 9.38 us
  starting transfers between devices: 17.7 us -> 16.5 us
    ppermute x0 -> x3, starting transfers between devices: none -> 2.71 us  [exchange(): return lax.ppermute(merged[number], 'tm', route)]
    ppermute x4 -> x1, starting transfers between devices: 4.01 us -> 1.3 us  [across(): lax.ppermute(array, 'tm', [(i, i ^ 2 * step) for i in range(count_tm)])]
    ppermute x4 -> x1, waiting for transfers between devices: 1.97 us -> 0.01 us  [across(): lax.ppermute(array, 'tm', [(i, i ^ 2 * step) for i in range(count_tm)])]
    ppermute x0 -> x3, waiting for transfers between devices: none -> 1.86 us  [exchange(): return lax.ppermute(merged[number], 'tm', route)]
    ppermute x2, waiting for transfers between devices: 4 us -> 5.46 us  [shards(): gathered.append(lax.ppermute(parts[step], ('tm', 'sta'), route))]
    ppermute x2, starting transfers between devices: 5.5 us -> 4.16 us  [shards(): gathered.append(lax.ppermute(parts[step], ('tm', 'sta'), route))]
  transfers between devices with their start and end apart: 12 -> 12, of which waited for: 5 -> 6; matrix products, arithmetic and copies ran while one was open for 0% -> 0% of each run, Pallas kernels for 18% -> 18%
where the time goes in v24:
time: 36.1 us; the launch traced here: 35.4 us
  starting transfers between devices  16.5 us (46%)
  waiting for transfers between devices  9.38 us (26%)
  Pallas kernels  9.33 us (26%)
    ppermute x5, starting transfers between devices, swap(): return lax.ppermute(array, 'tm', [(i, i ^ 1) for i in range(count_tm)])  6 us
    ppermute x2, waiting for transfers between devices, shards(): gathered.append(lax.ppermute(parts[step], ('tm', 'sta'), route))  5.46 us
    ppermute x2, starting transfers between devices, shards(): gathered.append(lax.ppermute(parts[step], ('tm', 'sta'), route))  4.16 us
    pallas_call x2, Pallas kernels, correlate(): pl.pallas_call(functools.partial(main_kernel, side, tlen, group), out_sha...  4.04 us
    ppermute x3, starting transfers between devices, exchange(): return lax.ppermute(merged[number], 'tm', route)  2.71 us
    ppermute x1, starting transfers between devices, shards(): far.append(lax.ppermute(pair, 'tm', route))  2.37 us
    pallas_call x1, Pallas kernels, pack(): pl.pallas_call(pack_kernel, out_shape=[jax.ShapeDtypeStruct(shape, jnp.bf...  2.18 us
    ppermute x5, waiting for transfers between devices, swap(): return lax.ppermute(array, 'tm', [(i, i ^ 1) for i in range(count_tm)])  2.06 us
  transfers between devices with their start and end apart: 12, of which 6 were waited for; matrix products, arithmetic and copies ran while one was open for 0% of the time, Pallas kernels for 18%

profile of v24, /device:TPU:7, one launch (start us, length us, event | category | flops | bytes accessed | tf_op | source)
XLA Modules:
  0.0 35.4 jit_solution(14032135943630617291)
XLA Ops:
  0.0 0.7 %collective-permute-start = (bf16[30,512]{1,0:T(8,128)(2,1)}, bf16[30,512]{1,0:T(8,128)(2,1)S(1)}, u32[]{:S(2)}, u32[]{:S(2)}) collective-permute-start(bf16[30,512]{1,0:T(8,128)(2,1)} %own.1), channel_id=1, source_target_pairs={{0,4},{4,0},{8,12},{12,8},{16,20},{20,16},{24,28},{28,24},{1,5},{5... | collective-permute-start | bytes 92168 | tf_op jit(solution)/shard_map/ppermute | solution.py:575
  0.7 0.0 copy-start
  0.7 2.2 %pack.1 = (bf16[4,12,32,128]{3,2,1,0:T(8,128)(2,1)S(1)}, bf16[4,12,32,128]{3,2,1,0:T(8,128)(2,1)S(1)}, s32[8,128]{1,0:T(8,128)S(1)}) custom-call(s32[2]{0:T(128)} %bank_blocks.1, bf16[2,30,64,100]{3,2,1,0:T(8,128)(2,1)} %bitcast.3, s32[30,2,64]{2,1,0:T(2,128)} %bitcast.4, s32[30,2,64]{2,1,0:T(2,128)} %bitcast.5), custom_call_target="tpu_custom_call" | custom-call | flops 2000000000 | bytes 2000000 | tf_op jit(solution)/shard_map/pack/pallas_call | solution.py:100
  2.9 0.0 collective-permute-done.partner
  2.9 0.1 collective-permute-start.4
  3.0 0.0 copy-done
  3.0 2.4 %collective-permute-start.2 = (bf16[2,30,512]{2,1,0:T(8,128)(2,1)S(1)}, bf16[2,30,512]{2,1,0:T(8,128)(2,1)S(1)}, u32[]{:S(2)}, u32[]{:S(2)}) collective-permute-start(bf16[2,30,512]{2,1,0:T(8,128)(2,1)S(1)} %pair_waves.1.pair), channel_id=1, source_target_pairs={{0,24},{4,20},{8,16},{12,28},{16,8},{20,4},{24,0},{28,12},{1,25},{... | collective-permute-start | bytes 184328 | tf_op jit(solution)/shard_map/ppermute | solution.py:596
  5.4 1.3 %collective-permute-start.1 = (bf16[30,512]{1,0:T(8,128)(2,1)S(1)}, bf16[30,512]{1,0:T(8,128)(2,1)S(1)}, u32[]{:S(2)}, u32[]{:S(2)}) collective-permute-start(bf16[30,512]{1,0:T(8,128)(2,1)S(1)} %copy-done), channel_id=1, source_target_pairs={{0,8},{4,12},{8,0},{12,4},{16,24},{20,28},{24,16},{28,20},{1,9},{5... | collective-permute-start | bytes 92168 | tf_op jit(solution)/shard_map/ppermute | solution.py:578
  6.7 0.0 collective-permute-done.4.other
  6.7 0.2 merge.1
  6.9 0.4 %collective-permute-start.5 = (bf16[12,32,128]{2,1,0:T(8,128)(2,1)S(1)}, bf16[12,32,128]{2,1,0:T(8,128)(2,1)S(1)}, u32[]{:S(2)}, u32[]{:S(2)}) collective-permute-start(bf16[12,32,128]{2,1,0:T(8,128)(2,1)S(1)} %get-tuple-element.35), channel_id=1, source_target_pairs={{0,24},{4,20},{8,16},{12,28},{16,8},{20,4},{24,0},{28,12},{1,25},{... | collective-permute-start | bytes 294920 | tf_op jit(solution)/shard_map/ppermute | solution.py:603
  7.3 1.9 %collective-permute-start.6 = (bf16[12,32,128]{2,1,0:T(8,128)(2,1)S(1)}, bf16[12,32,128]{2,1,0:T(8,128)(2,1)S(1)}, u32[]{:S(2)}, u32[]{:S(2)}) collective-permute-start(bf16[12,32,128]{2,1,0:T(8,128)(2,1)S(1)} %get-tuple-element.36), channel_id=1, source_target_pairs={{0,16},{4,28},{8,24},{12,20},{16,0},{20,12},{24,8},{28,4},{1,17},{... | collective-permute-start | bytes 294920 | tf_op jit(solution)/shard_map/ppermute | solution.py:603
  9.2 0.4 %collective-permute-start.7 = (bf16[12,32,128]{2,1,0:T(8,128)(2,1)S(1)}, bf16[12,32,128]{2,1,0:T(8,128)(2,1)S(1)}, u32[]{:S(2)}, u32[]{:S(2)}) collective-permute-start(bf16[12,32,128]{2,1,0:T(8,128)(2,1)S(1)} %get-tuple-element.38), channel_id=1, source_target_pairs={{0,8},{4,12},{8,0},{12,4},{16,24},{20,28},{24,16},{28,20},{1,9},{5... | collective-permute-start | bytes 294920 | tf_op jit(solution)/shard_map/ppermute | solution.py:603
  9.6 0.0 collective-permute-done.1.beside
  9.6 0.0 collective-permute-done.2.rest_0_
  9.7 2.3 %collective-permute-start.3 = (bf16[3,30,512]{2,1,0:T(8,128)(2,1)S(1)}, bf16[3,30,512]{2,1,0:T(8,128)(2,1)S(1)}, u32[]{:S(2)}, u32[]{:S(2)}) collective-permute-start(bf16[3,30,512]{2,1,0:T(8,128)(2,1)S(1)} %choose_waves.1), channel_id=1, source_target_pairs={{0,4},{4,0},{8,12},{12,8},{16,20},{20,16},{24,28},{28,24},{1,5},{5... | collective-permute-start | bytes 276488 | tf_op jit(solution)/shard_map/ppermute | solution.py:575
  11.9 0.9 %collective-permute-done.3.swapped = bf16[3,30,512]{2,1,0:T(8,128)(2,1)S(1)} collective-permute-done((bf16[3,30,512]{2,1,0:T(8,128)(2,1)S(1)}, bf16[3,30,512]{2,1,0:T(8,128)(2,1)S(1)}, u32[]{:S(2)}, u32[]{:S(2)}) %collective-permute-start.3) | collective-permute-done | bytes 92192 | tf_op jit(solution)/shard_map/ppermute | solution.py:575
  12.9 1.8 %prepare_waves.1 = (bf16[30,272,128]{2,1,0:T(8,128)(2,1)S(1)}, f32[32,32,128]{2,1,0:T(8,128)S(1)}, bf16[128,512]{1,0:T(8,128)(2,1)S(1)}, bf16[128,512]{1,0:T(8,128)(2,1)S(1)}) custom-call(bf16[3,30,512]{2,1,0:T(8,128)(2,1)S(1)} %collective-permute-done.3.swapped, bf16[2,30,512]{2,1,0:T(8,128)(2,1)S(1)} %pair_waves.1.pair, ...), custom_call_target="tpu_custom_call" | custom-call | flops 50000000 | bytes 50000 | tf_op jit(solution)/shard_map/prepare_waves/pallas_call | solution.py:322
  14.7 1.5 %collective-permute-done.5.refs_2_ = bf16[12,32,128]{2,1,0:T(8,128)(2,1)S(1)} collective-permute-done((bf16[12,32,128]{2,1,0:T(8,128)(2,1)S(1)}, bf16[12,32,128]{2,1,0:T(8,128)(2,1)S(1)}, u32[]{:S(2)}, u32[]{:S(2)}) %collective-permute-start.5) | collective-permute-done | bytes 98336 | tf_op jit(solution)/shard_map/ppermute | solution.py:603
  16.2 0.0 collective-permute-done.6.refs_3_
  16.2 0.4 %collective-permute-done.7.refs_1_ = bf16[12,32,128]{2,1,0:T(8,128)(2,1)S(1)} collective-permute-done((bf16[12,32,128]{2,1,0:T(8,128)(2,1)S(1)}, bf16[12,32,128]{2,1,0:T(8,128)(2,1)S(1)}, u32[]{:S(2)}, u32[]{:S(2)}) %collective-permute-start.7) | collective-permute-done | bytes 98336 | tf_op jit(solution)/shard_map/ppermute | solution.py:603
  16.6 0.1 choose_piece.1.piece
  16.7 2.8 %collective-permute-start.8 = (bf16[12,32,128]{2,1,0:T(8,128)(2,1)S(1)}, bf16[12,32,128]{2,1,0:T(8,128)(2,1)S(1)}, u32[]{:S(2)}, u32[]{:S(2)}) collective-permute-start(bf16[12,32,128]{2,1,0:T(8,128)(2,1)S(1)} %choose_piece.1.piece), channel_id=1, source_target_pairs={{0,4},{4,0},{8,12},{12,8},{16,20},{20,16},{24,28},{28,24},{1,5},{5... | collective-permute-start | bytes 294920 | tf_op jit(solution)/shard_map/ppermute | solution.py:575
  19.4 2.0 %correlate_first.1.rest_0_ = f32[256,256]{1,0:T(8,128)S(1)} custom-call(bf16[12,32,128]{2,1,0:T(8,128)(2,1)S(1)} %choose_piece.1.piece, bf16[30,272,128]{2,1,0:T(8,128)(2,1)S(1)} %get-tuple-element.43.left_a, f32[32,32,128]{2,1,0:T(8,128)S(1)} %get-tuple-element.44.inverse, bf16[128,512]{1,0:T(8,128)(2,1)S(1)} %get-tuple-element.45.expand), custom_call_target="tpu_custom_call" | custom-call | flops 3000000000 | bytes 3000000 | tf_op jit(solution)/shard_map/correlate_first/pallas_call | solution.py:497
  21.5 0.0 collective-permute-done.8.piece
  21.5 2.0 %correlate_second.1 = (bf16[128,256]{1,0:T(8,128)(2,1)S(1)}, bf16[128,256]{1,0:T(8,128)(2,1)S(1)}) custom-call(bf16[12,32,128]{2,1,0:T(8,128)(2,1)S(1)} %collective-permute-done.8.piece, bf16[30,272,128]{2,1,0:T(8,128)(2,1)S(1)} %get-tuple-element.43.left_a, f32[32,32,128]{2,1,0:T(8,128)S(1)} %get-tuple-element.44.inverse, ...), custom_call_target="tpu_custom_call" | custom-call | flops 3000000000 | bytes 3000000 | tf_op jit(solution)/shard_map/correlate_second/pallas_call | solution.py:497
  23.5 4.1 %collective-permute-start.9 = (bf16[128,256]{1,0:T(8,128)(2,1)S(1)}, bf16[128,256]{1,0:T(8,128)(2,1)S(1)}, u32[]{:S(2)}, u32[]{:S(2)}) collective-permute-start(bf16[128,256]{1,0:T(8,128)(2,1)S(1)} %get-tuple-element.46), channel_id=1, source_target_pairs={{0,0},{1,4},{2,8},{3,12},{4,16},{5,20},{6,24},{7,28},{8,1},{9,5},{... | collective-permute-start | bytes 196616 | tf_op jit(solution)/shard_map/ppermute | solution.py:625
  27.6 0.1 collective-permute-start.10
  27.7 4.4 %collective-permute-done.9.refs_0_ = bf16[128,256]{1,0:T(8,128)(2,1)S(1)} collective-permute-done((bf16[128,256]{1,0:T(8,128)(2,1)S(1)}, bf16[128,256]{1,0:T(8,128)(2,1)S(1)}, u32[]{:S(2)}, u32[]{:S(2)}) %collective-permute-start.9) | collective-permute-done | bytes 65568 | tf_op jit(solution)/shard_map/ppermute | solution.py:625
  32.1 1.1 %collective-permute-done.10.refs_1_ = bf16[128,256]{1,0:T(8,128)(2,1)S(1)} collective-permute-done((bf16[128,256]{1,0:T(8,128)(2,1)S(1)}, bf16[128,256]{1,0:T(8,128)(2,1)S(1)}, u32[]{:S(2)}, u32[]{:S(2)}) %collective-permute-start.10) | collective-permute-done | bytes 65568 | tf_op jit(solution)/shard_map/ppermute | solution.py:625
  33.1 0.2 collective-permute-start.11
  33.4 1.1 %collective-permute-done.11.received = f32[64,256]{1,0:T(8,128)S(1)} collective-permute-done((f32[64,256]{1,0:T(8,128)S(1)}, f32[64,256]{1,0:T(8,128)S(1)}, u32[]{:S(2)}, u32[]{:S(2)}) %collective-permute-start.11) | collective-permute-done | bytes 65568 | tf_op jit(solution)/shard_map/ppermute | solution.py:575
  34.5 0.9 %finish.1 = f32[32,512]{1,0:T(8,128)} custom-call(f32[64,256]{1,0:T(8,128)S(1)} %get-tuple-element.48.ours, f32[64,256]{1,0:T(8,128)S(1)} %collective-permute-done.11.received, bf16[128,512]{1,0:T(8,128)(2,1)S(1)} %get-tuple-element.50.place), custom_call_target="tpu_custom_call" | custom-call | flops 1000000000 | bytes 1000000 | tf_op jit(solution)/shard_map/finish/pallas_call | solution.py:554
  (3 shorter events, 0.1 us)
Async XLA Ops:
  0.0 2.9 %collective-permute-start = (bf16[30,512]{1,0:T(8,128)(2,1)}, bf16[30,512]{1,0:T(8,128)(2,1)S(1)}, u32[]{:S(2)}, u32[]{:S(2)}) collective-permute-start(bf16[30,512]{1,0:T(8,128)(2,1)} %own.1), channel_id=1, source_target_pairs={{0,4},{4,0},{8,12},{12,8},{16,20},{20,16},{24,28},{28,24},{1,5},{5... | collective-permute-start | bytes 92168 | tf_op jit(solution)/shard_map/ppermute | solution.py:575
  0.7 2.3 %copy-start = (bf16[30,512]{1,0:T(8,128)(2,1)S(1)}, bf16[30,512]{1,0:T(8,128)(2,1)}, u32[]{:S(2)}) copy-start(bf16[30,512]{1,0:T(8,128)(2,1)} %own.1) | copy-start | bytes 92164
  2.9 3.8 %collective-permute-start.4 = (bf16[4,12,32,128]{3,2,1,0:T(8,128)(2,1)S(1)}, bf16[4,12,32,128]{3,2,1,0:T(8,128)(2,1)S(1)}, u32[]{:S(2)}, u32[]{:S(2)}) collective-permute-start(bf16[4,12,32,128]{3,2,1,0:T(8,128)(2,1)S(1)} %get-tuple-element.34), channel_id=1, source_target_pairs={{0,4},{4,0},{8,12},{12,8},{16,20},{20,16},{24,28},{28,24},{1,5},{5... | collective-permute-start | bytes 1179656 | tf_op jit(solution)/shard_map/ppermute | solution.py:575
  3.0 6.6 %collective-permute-start.2 = (bf16[2,30,512]{2,1,0:T(8,128)(2,1)S(1)}, bf16[2,30,512]{2,1,0:T(8,128)(2,1)S(1)}, u32[]{:S(2)}, u32[]{:S(2)}) collective-permute-start(bf16[2,30,512]{2,1,0:T(8,128)(2,1)S(1)} %pair_waves.1.pair), channel_id=1, source_target_pairs={{0,24},{4,20},{8,16},{12,28},{16,8},{20,4},{24,0},{28,12},{1,25},{... | collective-permute-start | bytes 184328 | tf_op jit(solution)/shard_map/ppermute | solution.py:596
  5.4 4.2 %collective-permute-start.1 = (bf16[30,512]{1,0:T(8,128)(2,1)S(1)}, bf16[30,512]{1,0:T(8,128)(2,1)S(1)}, u32[]{:S(2)}, u32[]{:S(2)}) collective-permute-start(bf16[30,512]{1,0:T(8,128)(2,1)S(1)} %copy-done), channel_id=1, source_target_pairs={{0,8},{4,12},{8,0},{12,4},{16,24},{20,28},{24,16},{28,20},{1,9},{5... | collective-permute-start | bytes 92168 | tf_op jit(solution)/shard_map/ppermute | solution.py:578
  6.9 9.3 %collective-permute-start.5 = (bf16[12,32,128]{2,1,0:T(8,128)(2,1)S(1)}, bf16[12,32,128]{2,1,0:T(8,128)(2,1)S(1)}, u32[]{:S(2)}, u32[]{:S(2)}) collective-permute-start(bf16[12,32,128]{2,1,0:T(8,128)(2,1)S(1)} %get-tuple-element.35), channel_id=1, source_target_pairs={{0,24},{4,20},{8,16},{12,28},{16,8},{20,4},{24,0},{28,12},{1,25},{... | collective-permute-start | bytes 294920 | tf_op jit(solution)/shard_map/ppermute | solution.py:603
  7.3 8.9 %collective-permute-start.6 = (bf16[12,32,128]{2,1,0:T(8,128)(2,1)S(1)}, bf16[12,32,128]{2,1,0:T(8,128)(2,1)S(1)}, u32[]{:S(2)}, u32[]{:S(2)}) collective-permute-start(bf16[12,32,128]{2,1,0:T(8,128)(2,1)S(1)} %get-tuple-element.36), channel_id=1, source_target_pairs={{0,16},{4,28},{8,24},{12,20},{16,0},{20,12},{24,8},{28,4},{1,17},{... | collective-permute-start | bytes 294920 | tf_op jit(solution)/shard_map/ppermute | solution.py:603
  9.2 7.4 %collective-permute-start.7 = (bf16[12,32,128]{2,1,0:T(8,128)(2,1)S(1)}, bf16[12,32,128]{2,1,0:T(8,128)(2,1)S(1)}, u32[]{:S(2)}, u32[]{:S(2)}) collective-permute-start(bf16[12,32,128]{2,1,0:T(8,128)(2,1)S(1)} %get-tuple-element.38), channel_id=1, source_target_pairs={{0,8},{4,12},{8,0},{12,4},{16,24},{20,28},{24,16},{28,20},{1,9},{5... | collective-permute-start | bytes 294920 | tf_op jit(solution)/shard_map/ppermute | solution.py:603
  9.7 3.2 %collective-permute-start.3 = (bf16[3,30,512]{2,1,0:T(8,128)(2,1)S(1)}, bf16[3,30,512]{2,1,0:T(8,128)(2,1)S(1)}, u32[]{:S(2)}, u32[]{:S(2)}) collective-permute-start(bf16[3,30,512]{2,1,0:T(8,128)(2,1)S(1)} %choose_waves.1), channel_id=1, source_target_pairs={{0,4},{4,0},{8,12},{12,8},{16,20},{20,16},{24,28},{28,24},{1,5},{5... | collective-permute-start | bytes 276488 | tf_op jit(solution)/shard_map/ppermute | solution.py:575
  16.7 4.8 %collective-permute-start.8 = (bf16[12,32,128]{2,1,0:T(8,128)(2,1)S(1)}, bf16[12,32,128]{2,1,0:T(8,128)(2,1)S(1)}, u32[]{:S(2)}, u32[]{:S(2)}) collective-permute-start(bf16[12,32,128]{2,1,0:T(8,128)(2,1)S(1)} %choose_piece.1.piece), channel_id=1, source_target_pairs={{0,4},{4,0},{8,12},{12,8},{16,20},{20,16},{24,28},{28,24},{1,5},{5... | collective-permute-start | bytes 294920 | tf_op jit(solution)/shard_map/ppermute | solution.py:575
  23.5 8.6 %collective-permute-start.9 = (bf16[128,256]{1,0:T(8,128)(2,1)S(1)}, bf16[128,256]{1,0:T(8,128)(2,1)S(1)}, u32[]{:S(2)}, u32[]{:S(2)}) collective-permute-start(bf16[128,256]{1,0:T(8,128)(2,1)S(1)} %get-tuple-element.46), channel_id=1, source_target_pairs={{0,0},{1,4},{2,8},{3,12},{4,16},{5,20},{6,24},{7,28},{8,1},{9,5},{... | collective-permute-start | bytes 196616 | tf_op jit(solution)/shard_map/ppermute | solution.py:625
  27.6 5.5 %collective-permute-start.10 = (bf16[128,256]{1,0:T(8,128)(2,1)S(1)}, bf16[128,256]{1,0:T(8,128)(2,1)S(1)}, u32[]{:S(2)}, u32[]{:S(2)}) collective-permute-start(bf16[128,256]{1,0:T(8,128)(2,1)S(1)} %get-tuple-element.47), channel_id=1, source_target_pairs={{0,8},{1,12},{2,0},{3,4},{4,24},{5,28},{6,16},{7,20},{8,9},{9,13},... | collective-permute-start | bytes 196616 | tf_op jit(solution)/shard_map/ppermute | solution.py:625
  33.1 1.3 %collective-permute-start.11 = (f32[64,256]{1,0:T(8,128)S(1)}, f32[64,256]{1,0:T(8,128)S(1)}, u32[]{:S(2)}, u32[]{:S(2)}) collective-permute-start(f32[64,256]{1,0:T(8,128)S(1)} %get-tuple-element.49), channel_id=1, source_target_pairs={{0,4},{4,0},{8,12},{12,8},{16,20},{20,16},{24,28},{28,24},{1,5},{5... | collective-permute-start | bytes 196616 | tf_op jit(solution)/shard_map/ppermute | solution.py:575

commit v25 on v24

--- a/solution.py
+++ b/solution.py
@@ -122,7 +122,7 @@
         return number
     pair, second = divmod(number - 2, 2)
     high = chips - 1 - 2 * pair
-    return high - 1 + core if second else high - core
+    return high - core if second else high - 1 + core
 
 
 def merge_kernel(owners, mine, other, *outs):

time: 36.1 us -> 35.9 us (level)
  the two profiles are of different devices: /device:TPU:7 before, /device:TPU:5 now
where the time goes in v25:
time: 35.9 us; the launch traced here: 35.7 us
  starting transfers between devices  16.3 us (45%)
  waiting for transfers between devices  9.98 us (28%)
  Pallas kernels  9.33 us (26%)
    ppermute x2, starting transfers between devices, shards(): gathered.append(lax.ppermute(parts[step], ('tm', 'sta'), route))  5.39 us
    ppermute x2, waiting for transfers between devices, shards(): gathered.append(lax.ppermute(parts[step], ('tm', 'sta'), route))  4.71 us
    pallas_call x2, Pallas kernels, correlate(): pl.pallas_call(functools.partial(main_kernel, side, tlen, group), out_sha...  4.04 us
    ppermute x3, starting transfers between devices, exchange(): return lax.ppermute(merged[number], 'tm', route)  3.61 us
    ppermute x5, starting transfers between devices, swap(): return lax.ppermute(array, 'tm', [(i, i ^ 1) for i in range(count_tm)])  3.61 us
    ppermute x3, waiting for transfers between devices, exchange(): return lax.ppermute(merged[number], 'tm', route)  3.07 us
    ppermute x1, starting transfers between devices, shards(): far.append(lax.ppermute(pair, 'tm', route))  2.37 us
    ppermute x5, waiting for transfers between devices, swap(): return lax.ppermute(array, 'tm', [(i, i ^ 1) for i in range(count_tm)])  2.19 us
  transfers between devices with their start and end apart: 12, of which 5 were waited for; matrix products, arithmetic and copies ran while one was open for 0% of the time, Pallas kernels for 18%

profile of v25, /device:TPU:5, one launch (start us, length us, event | category | flops | bytes accessed | tf_op | source)
XLA Modules:
  0.0 35.7 jit_solution(15506677535036864302)
XLA Ops:
  0.0 0.7 %collective-permute-start = (bf16[30,512]{1,0:T(8,128)(2,1)}, bf16[30,512]{1,0:T(8,128)(2,1)S(1)}, u32[]{:S(2)}, u32[]{:S(2)}) collective-permute-start(bf16[30,512]{1,0:T(8,128)(2,1)} %own.1), channel_id=1, source_target_pairs={{0,4},{4,0},{8,12},{12,8},{16,20},{20,16},{24,28},{28,24},{1,5},{5... | collective-permute-start | bytes 92168 | tf_op jit(solution)/shard_map/ppermute | solution.py:575
  0.7 0.0 copy-start
  0.7 2.2 %pack.1 = (bf16[4,12,32,128]{3,2,1,0:T(8,128)(2,1)S(1)}, bf16[4,12,32,128]{3,2,1,0:T(8,128)(2,1)S(1)}, s32[8,128]{1,0:T(8,128)S(1)}) custom-call(s32[2]{0:T(128)} %bank_blocks.1, bf16[2,30,64,100]{3,2,1,0:T(8,128)(2,1)} %bitcast.3, s32[30,2,64]{2,1,0:T(2,128)} %bitcast.4, s32[30,2,64]{2,1,0:T(2,128)} %bitcast.5), custom_call_target="tpu_custom_call" | custom-call | flops 2000000000 | bytes 2000000 | tf_op jit(solution)/shard_map/pack/pallas_call | solution.py:100
  2.9 0.0 collective-permute-done.partner
  2.9 0.1 collective-permute-start.4
  3.0 0.0 copy-done
  3.0 2.4 %collective-permute-start.2 = (bf16[2,30,512]{2,1,0:T(8,128)(2,1)S(1)}, bf16[2,30,512]{2,1,0:T(8,128)(2,1)S(1)}, u32[]{:S(2)}, u32[]{:S(2)}) collective-permute-start(bf16[2,30,512]{2,1,0:T(8,128)(2,1)S(1)} %pair_waves.1.pair), channel_id=1, source_target_pairs={{0,24},{4,20},{8,16},{12,28},{16,8},{20,4},{24,0},{28,12},{1,25},{... | collective-permute-start | bytes 184328 | tf_op jit(solution)/shard_map/ppermute | solution.py:596
  5.4 1.3 %collective-permute-start.1 = (bf16[30,512]{1,0:T(8,128)(2,1)S(1)}, bf16[30,512]{1,0:T(8,128)(2,1)S(1)}, u32[]{:S(2)}, u32[]{:S(2)}) collective-permute-start(bf16[30,512]{1,0:T(8,128)(2,1)S(1)} %copy-done), channel_id=1, source_target_pairs={{0,8},{4,12},{8,0},{12,4},{16,24},{20,28},{24,16},{28,20},{1,9},{5... | collective-permute-start | bytes 92168 | tf_op jit(solution)/shard_map/ppermute | solution.py:578
  6.7 0.0 collective-permute-done.4.other
  6.7 0.2 merge.1
  6.9 1.4 %collective-permute-start.5 = (bf16[12,32,128]{2,1,0:T(8,128)(2,1)S(1)}, bf16[12,32,128]{2,1,0:T(8,128)(2,1)S(1)}, u32[]{:S(2)}, u32[]{:S(2)}) collective-permute-start(bf16[12,32,128]{2,1,0:T(8,128)(2,1)S(1)} %get-tuple-element.35), channel_id=1, source_target_pairs={{0,16},{4,28},{8,24},{12,20},{16,0},{20,12},{24,8},{28,4},{1,17},{... | collective-permute-start | bytes 294920 | tf_op jit(solution)/shard_map/ppermute | solution.py:603
  8.3 0.0 collective-permute-start.6
  8.3 2.2 %collective-permute-start.7 = (bf16[12,32,128]{2,1,0:T(8,128)(2,1)S(1)}, bf16[12,32,128]{2,1,0:T(8,128)(2,1)S(1)}, u32[]{:S(2)}, u32[]{:S(2)}) collective-permute-start(bf16[12,32,128]{2,1,0:T(8,128)(2,1)S(1)} %get-tuple-element.38), channel_id=1, source_target_pairs={{0,8},{4,12},{8,0},{12,4},{16,24},{20,28},{24,16},{28,20},{1,9},{5... | collective-permute-start | bytes 294920 | tf_op jit(solution)/shard_map/ppermute | solution.py:603
  10.5 0.0 collective-permute-done.1.beside
  10.5 0.0 collective-permute-done.2.rest_0_
  10.5 1.4 %collective-permute-start.3 = (bf16[3,30,512]{2,1,0:T(8,128)(2,1)S(1)}, bf16[3,30,512]{2,1,0:T(8,128)(2,1)S(1)}, u32[]{:S(2)}, u32[]{:S(2)}) collective-permute-start(bf16[3,30,512]{2,1,0:T(8,128)(2,1)S(1)} %choose_waves.1), channel_id=1, source_target_pairs={{0,4},{4,0},{8,12},{12,8},{16,20},{20,16},{24,28},{28,24},{1,5},{5... | collective-permute-start | bytes 276488 | tf_op jit(solution)/shard_map/ppermute | solution.py:575
  11.9 0.9 %collective-permute-done.3.swapped = bf16[3,30,512]{2,1,0:T(8,128)(2,1)S(1)} collective-permute-done((bf16[3,30,512]{2,1,0:T(8,128)(2,1)S(1)}, bf16[3,30,512]{2,1,0:T(8,128)(2,1)S(1)}, u32[]{:S(2)}, u32[]{:S(2)}) %collective-permute-start.3) | collective-permute-done | bytes 92192 | tf_op jit(solution)/shard_map/ppermute | solution.py:575
  12.9 1.8 %prepare_waves.1 = (bf16[30,272,128]{2,1,0:T(8,128)(2,1)S(1)}, f32[32,32,128]{2,1,0:T(8,128)S(1)}, bf16[128,512]{1,0:T(8,128)(2,1)S(1)}, bf16[128,512]{1,0:T(8,128)(2,1)S(1)}) custom-call(bf16[3,30,512]{2,1,0:T(8,128)(2,1)S(1)} %collective-permute-done.3.swapped, bf16[2,30,512]{2,1,0:T(8,128)(2,1)S(1)} %pair_waves.1.pair, ...), custom_call_target="tpu_custom_call" | custom-call | flops 50000000 | bytes 50000 | tf_op jit(solution)/shard_map/prepare_waves/pallas_call | solution.py:322
  14.7 0.0 collective-permute-done.5.refs_2_
  14.7 3.1 %collective-permute-done.6.refs_3_ = bf16[12,32,128]{2,1,0:T(8,128)(2,1)S(1)} collective-permute-done((bf16[12,32,128]{2,1,0:T(8,128)(2,1)S(1)}, bf16[12,32,128]{2,1,0:T(8,128)(2,1)S(1)}, u32[]{:S(2)}, u32[]{:S(2)}) %collective-permute-start.6) | collective-permute-done | bytes 98336 | tf_op jit(solution)/shard_map/ppermute | solution.py:603
  17.8 0.0 collective-permute-done.7.refs_1_
  17.8 0.1 choose_piece.1.piece
  17.9 1.4 %collective-permute-start.8 = (bf16[12,32,128]{2,1,0:T(8,128)(2,1)S(1)}, bf16[12,32,128]{2,1,0:T(8,128)(2,1)S(1)}, u32[]{:S(2)}, u32[]{:S(2)}) collective-permute-start(bf16[12,32,128]{2,1,0:T(8,128)(2,1)S(1)} %choose_piece.1.piece), channel_id=1, source_target_pairs={{0,4},{4,0},{8,12},{12,8},{16,20},{20,16},{24,28},{28,24},{1,5},{5... | collective-permute-start | bytes 294920 | tf_op jit(solution)/shard_map/ppermute | solution.py:575
  19.3 2.0 %correlate_first.1.rest_0_ = f32[256,256]{1,0:T(8,128)S(1)} custom-call(bf16[12,32,128]{2,1,0:T(8,128)(2,1)S(1)} %choose_piece.1.piece, bf16[30,272,128]{2,1,0:T(8,128)(2,1)S(1)} %get-tuple-element.43.left_a, f32[32,32,128]{2,1,0:T(8,128)S(1)} %get-tuple-element.44.inverse, bf16[128,512]{1,0:T(8,128)(2,1)S(1)} %get-tuple-element.45.expand), custom_call_target="tpu_custom_call" | custom-call | flops 3000000000 | bytes 3000000 | tf_op jit(solution)/shard_map/correlate_first/pallas_call | solution.py:497
  21.3 0.0 collective-permute-done.8.piece
  21.3 2.0 %correlate_second.1 = (bf16[128,256]{1,0:T(8,128)(2,1)S(1)}, bf16[128,256]{1,0:T(8,128)(2,1)S(1)}) custom-call(bf16[12,32,128]{2,1,0:T(8,128)(2,1)S(1)} %collective-permute-done.8.piece, bf16[30,272,128]{2,1,0:T(8,128)(2,1)S(1)} %get-tuple-element.43.left_a, f32[32,32,128]{2,1,0:T(8,128)S(1)} %get-tuple-element.44.inverse, ...), custom_call_target="tpu_custom_call" | custom-call | flops 3000000000 | bytes 3000000 | tf_op jit(solution)/shard_map/correlate_second/pallas_call | solution.py:497
  23.4 3.9 %collective-permute-start.9 = (bf16[128,256]{1,0:T(8,128)(2,1)S(1)}, bf16[128,256]{1,0:T(8,128)(2,1)S(1)}, u32[]{:S(2)}, u32[]{:S(2)}) collective-permute-start(bf16[128,256]{1,0:T(8,128)(2,1)S(1)} %get-tuple-element.46), channel_id=1, source_target_pairs={{0,0},{1,4},{2,8},{3,12},{4,16},{5,20},{6,24},{7,28},{8,1},{9,5},{... | collective-permute-start | bytes 196616 | tf_op jit(solution)/shard_map/ppermute | solution.py:625
  27.2 1.5 %collective-permute-start.10 = (bf16[128,256]{1,0:T(8,128)(2,1)S(1)}, bf16[128,256]{1,0:T(8,128)(2,1)S(1)}, u32[]{:S(2)}, u32[]{:S(2)}) collective-permute-start(bf16[128,256]{1,0:T(8,128)(2,1)S(1)} %get-tuple-element.47), channel_id=1, source_target_pairs={{0,8},{1,12},{2,0},{3,4},{4,24},{5,28},{6,16},{7,20},{8,9},{9,13},... | collective-permute-start | bytes 196616 | tf_op jit(solution)/shard_map/ppermute | solution.py:625
  28.8 2.9 %collective-permute-done.9.refs_0_ = bf16[128,256]{1,0:T(8,128)(2,1)S(1)} collective-permute-done((bf16[128,256]{1,0:T(8,128)(2,1)S(1)}, bf16[128,256]{1,0:T(8,128)(2,1)S(1)}, u32[]{:S(2)}, u32[]{:S(2)}) %collective-permute-start.9) | collective-permute-done | bytes 65568 | tf_op jit(solution)/shard_map/ppermute | solution.py:625
  31.6 1.8 %collective-permute-done.10.refs_1_ = bf16[128,256]{1,0:T(8,128)(2,1)S(1)} collective-permute-done((bf16[128,256]{1,0:T(8,128)(2,1)S(1)}, bf16[128,256]{1,0:T(8,128)(2,1)S(1)}, u32[]{:S(2)}, u32[]{:S(2)}) %collective-permute-start.10) | collective-permute-done | bytes 65568 | tf_op jit(solution)/shard_map/ppermute | solution.py:625
  33.5 0.1 collective-permute-start.11
  33.6 1.2 %collective-permute-done.11.received = f32[64,256]{1,0:T(8,128)S(1)} collective-permute-done((f32[64,256]{1,0:T(8,128)S(1)}, f32[64,256]{1,0:T(8,128)S(1)}, u32[]{:S(2)}, u32[]{:S(2)}) %collective-permute-start.11) | collective-permute-done | bytes 65568 | tf_op jit(solution)/shard_map/ppermute | solution.py:575
  34.8 0.9 %finish.1 = f32[32,512]{1,0:T(8,128)} custom-call(f32[64,256]{1,0:T(8,128)S(1)} %get-tuple-element.48.ours, f32[64,256]{1,0:T(8,128)S(1)} %collective-permute-done.11.received, bf16[128,512]{1,0:T(8,128)(2,1)S(1)} %get-tuple-element.50.place), custom_call_target="tpu_custom_call" | custom-call | flops 1000000000 | bytes 1000000 | tf_op jit(solution)/shard_map/finish/pallas_call | solution.py:554
  (3 shorter events, 0.1 us)
Async XLA Ops:
  0.0 2.9 %collective-permute-start = (bf16[30,512]{1,0:T(8,128)(2,1)}, bf16[30,512]{1,0:T(8,128)(2,1)S(1)}, u32[]{:S(2)}, u32[]{:S(2)}) collective-permute-start(bf16[30,512]{1,0:T(8,128)(2,1)} %own.1), channel_id=1, source_target_pairs={{0,4},{4,0},{8,12},{12,8},{16,20},{20,16},{24,28},{28,24},{1,5},{5... | collective-permute-start | bytes 92168 | tf_op jit(solution)/shard_map/ppermute | solution.py:575
  0.7 2.3 %copy-start = (bf16[30,512]{1,0:T(8,128)(2,1)S(1)}, bf16[30,512]{1,0:T(8,128)(2,1)}, u32[]{:S(2)}) copy-start(bf16[30,512]{1,0:T(8,128)(2,1)} %own.1) | copy-start | bytes 92164
  2.9 3.8 %collective-permute-start.4 = (bf16[4,12,32,128]{3,2,1,0:T(8,128)(2,1)S(1)}, bf16[4,12,32,128]{3,2,1,0:T(8,128)(2,1)S(1)}, u32[]{:S(2)}, u32[]{:S(2)}) collective-permute-start(bf16[4,12,32,128]{3,2,1,0:T(8,128)(2,1)S(1)} %get-tuple-element.34), channel_id=1, source_target_pairs={{0,4},{4,0},{8,12},{12,8},{16,20},{20,16},{24,28},{28,24},{1,5},{5... | collective-permute-start | bytes 1179656 | tf_op jit(solution)/shard_map/ppermute | solution.py:575
  3.0 7.5 %collective-permute-start.2 = (bf16[2,30,512]{2,1,0:T(8,128)(2,1)S(1)}, bf16[2,30,512]{2,1,0:T(8,128)(2,1)S(1)}, u32[]{:S(2)}, u32[]{:S(2)}) collective-permute-start(bf16[2,30,512]{2,1,0:T(8,128)(2,1)S(1)} %pair_waves.1.pair), channel_id=1, source_target_pairs={{0,24},{4,20},{8,16},{12,28},{16,8},{20,4},{24,0},{28,12},{1,25},{... | collective-permute-start | bytes 184328 | tf_op jit(solution)/shard_map/ppermute | solution.py:596
  5.4 5.1 %collective-permute-start.1 = (bf16[30,512]{1,0:T(8,128)(2,1)S(1)}, bf16[30,512]{1,0:T(8,128)(2,1)S(1)}, u32[]{:S(2)}, u32[]{:S(2)}) collective-permute-start(bf16[30,512]{1,0:T(8,128)(2,1)S(1)} %copy-done), channel_id=1, source_target_pairs={{0,8},{4,12},{8,0},{12,4},{16,24},{20,28},{24,16},{28,20},{1,9},{5... | collective-permute-start | bytes 92168 | tf_op jit(solution)/shard_map/ppermute | solution.py:578
  6.9 7.8 %collective-permute-start.5 = (bf16[12,32,128]{2,1,0:T(8,128)(2,1)S(1)}, bf16[12,32,128]{2,1,0:T(8,128)(2,1)S(1)}, u32[]{:S(2)}, u32[]{:S(2)}) collective-permute-start(bf16[12,32,128]{2,1,0:T(8,128)(2,1)S(1)} %get-tuple-element.35), channel_id=1, source_target_pairs={{0,16},{4,28},{8,24},{12,20},{16,0},{20,12},{24,8},{28,4},{1,17},{... | collective-permute-start | bytes 294920 | tf_op jit(solution)/shard_map/ppermute | solution.py:603
  8.3 9.5 %collective-permute-start.6 = (bf16[12,32,128]{2,1,0:T(8,128)(2,1)S(1)}, bf16[12,32,128]{2,1,0:T(8,128)(2,1)S(1)}, u32[]{:S(2)}, u32[]{:S(2)}) collective-permute-start(bf16[12,32,128]{2,1,0:T(8,128)(2,1)S(1)} %get-tuple-element.36), channel_id=1, source_target_pairs={{0,24},{4,20},{8,16},{12,28},{16,8},{20,4},{24,0},{28,12},{1,25},{... | collective-permute-start | bytes 294920 | tf_op jit(solution)/shard_map/ppermute | solution.py:603
  8.3 9.5 %collective-permute-start.7 = (bf16[12,32,128]{2,1,0:T(8,128)(2,1)S(1)}, bf16[12,32,128]{2,1,0:T(8,128)(2,1)S(1)}, u32[]{:S(2)}, u32[]{:S(2)}) collective-permute-start(bf16[12,32,128]{2,1,0:T(8,128)(2,1)S(1)} %get-tuple-element.38), channel_id=1, source_target_pairs={{0,8},{4,12},{8,0},{12,4},{16,24},{20,28},{24,16},{28,20},{1,9},{5... | collective-permute-start | bytes 294920 | tf_op jit(solution)/shard_map/ppermute | solution.py:603
  10.5 2.3 %collective-permute-start.3 = (bf16[3,30,512]{2,1,0:T(8,128)(2,1)S(1)}, bf16[3,30,512]{2,1,0:T(8,128)(2,1)S(1)}, u32[]{:S(2)}, u32[]{:S(2)}) collective-permute-start(bf16[3,30,512]{2,1,0:T(8,128)(2,1)S(1)} %choose_waves.1), channel_id=1, source_target_pairs={{0,4},{4,0},{8,12},{12,8},{16,20},{20,16},{24,28},{28,24},{1,5},{5... | collective-permute-start | bytes 276488 | tf_op jit(solution)/shard_map/ppermute | solution.py:575
  17.9 3.4 %collective-permute-start.8 = (bf16[12,32,128]{2,1,0:T(8,128)(2,1)S(1)}, bf16[12,32,128]{2,1,0:T(8,128)(2,1)S(1)}, u32[]{:S(2)}, u32[]{:S(2)}) collective-permute-start(bf16[12,32,128]{2,1,0:T(8,128)(2,1)S(1)} %choose_piece.1.piece), channel_id=1, source_target_pairs={{0,4},{4,0},{8,12},{12,8},{16,20},{20,16},{24,28},{28,24},{1,5},{5... | collective-permute-start | bytes 294920 | tf_op jit(solution)/shard_map/ppermute | solution.py:575
  23.4 8.3 %collective-permute-start.9 = (bf16[128,256]{1,0:T(8,128)(2,1)S(1)}, bf16[128,256]{1,0:T(8,128)(2,1)S(1)}, u32[]{:S(2)}, u32[]{:S(2)}) collective-permute-start(bf16[128,256]{1,0:T(8,128)(2,1)S(1)} %get-tuple-element.46), channel_id=1, source_target_pairs={{0,0},{1,4},{2,8},{3,12},{4,16},{5,20},{6,24},{7,28},{8,1},{9,5},{... | collective-permute-start | bytes 196616 | tf_op jit(solution)/shard_map/ppermute | solution.py:625
  27.2 6.2 %collective-permute-start.10 = (bf16[128,256]{1,0:T(8,128)(2,1)S(1)}, bf16[128,256]{1,0:T(8,128)(2,1)S(1)}, u32[]{:S(2)}, u32[]{:S(2)}) collective-permute-start(bf16[128,256]{1,0:T(8,128)(2,1)S(1)} %get-tuple-element.47), channel_id=1, source_target_pairs={{0,8},{1,12},{2,0},{3,4},{4,24},{5,28},{6,16},{7,20},{8,9},{9,13},... | collective-permute-start | bytes 196616 | tf_op jit(solution)/shard_map/ppermute | solution.py:625
  33.5 1.3 %collective-permute-start.11 = (f32[64,256]{1,0:T(8,128)S(1)}, f32[64,256]{1,0:T(8,128)S(1)}, u32[]{:S(2)}, u32[]{:S(2)}) collective-permute-start(f32[64,256]{1,0:T(8,128)S(1)} %get-tuple-element.49), channel_id=1, source_target_pairs={{0,4},{4,0},{8,12},{12,8},{16,20},{20,16},{24,28},{28,24},{1,5},{5... | collective-permute-start | bytes 196616 | tf_op jit(solution)/shard_map/ppermute | solution.py:575
